TPU v7x, 32 devices: a whole 2x2x4 slice. The times are simulated.
32 devices in a mesh: groups: 2 (over y), tp: 4 (over z), pd: 4 (over x, core).
Axes of the slice: x: 2, y: 2, z: 4, core: 2. Of those that a mesh axis runs over, the one named last changes fastest.
Arguments:
- prefill_hidden: bfloat16 [49152, 7168], P(('groups', 'pd'), 'tp'), parts along dimension 0, may hold values from -6 to 6
- draft_hidden: bfloat16 [64, 7168], P(('groups', 'pd'), 'tp'), parts along dimension 0, may hold values from -6 to 6
- kv_down: bfloat16 [7168, 576], P('tp'), may hold values from -0.0625 to 0.0625
- kv_gain: float32 [512], replicated, may hold values from 0.1 to 1.9
- query_latent: bfloat16 [32, 2, 1536], P('groups'), parts along dimension 0, may hold values from -110 to 110, as said below
- q_up: bfloat16 [1536, 24576], P(None, 'tp'), may hold values from -0.15625 to 0.15625
- kv_up: bfloat16 [512, 32768], P(None, 'tp'), may hold values from -0.25 to 0.25
- owners: int32 [32], P('groups'), parts along dimension 0, may hold values from 0 to 3, as said below
- segment_ids: int32 [32, 1536], P('groups'), parts along dimension 0, may hold values from 0 to 3, never falling along the last dimension, each value on 1 to 768 neighbouring positions
- accepted: int32 [32], P('groups'), parts along dimension 0, may hold values from 0 to 1
Outputs:
- owner_decoded: bfloat16 [64, 16384], P(('groups', 'pd'), 'tp'), parts along dimension 0
- owner_cache: bfloat16 [32, 1536, 576], P(('groups', 'pd'), 'tp'), parts along dimension 0
There are 2 independent parts, one for each index of `groups`. A program takes and returns all parts, laid end to end along the dimension named above; an argument that names none is the same for every part. Nothing has to cross between parts.
Inputs may be any that keep to these rules, and one draw needn't show every extreme that they name: Owners are pd indices. Requests p * 4 to p * 4 + 3 belong to prefill rank p, and those 4 requests have 4 different owners; one owner holds a request of every prefill rank. `query_latent`: A few new tokens may have large query latents.
All inputs are finite; a program needn't handle non-finite values.
Results may differ from a plain program's by a relative error of at most 0.0117.
The roundings to bfloat16 on the way count: a program that leaves them out, or rounds other values in their place, can miss the bound.
Values may be sent and summed in bfloat16 or wider, within the bound.
No kernel may reach another device: no remote copies, remote signals or barrier semaphores. Data moves between devices by JAX's collectives and lax.ppermute only.
A program may use at most 192 MiB of HBM per device.

v0:
```python
import functools

import jax
import jax.numpy as jnp
from jax import lax
from jax.experimental import pallas as pl
from jax.experimental.pallas import tpu as pltpu
from jax.sharding import PartitionSpec as P

DN = 128
DR = 64
DV = 128
KVL = 512
QL = 1536
PRE_TOK = 1536
RP = 4
WIDTH = KVL + DR
HALF = DR // 2
CODED = WIDTH + 16
SHARE = PRE_TOK // 4
UNIT = 128
UNITS = SHARE // UNIT
LANES = RP * UNIT
STEPS = 256.0
TOP = 32767.0
BF = jnp.bfloat16
F32 = jnp.float32
I16 = jnp.int16
NT = (((1,), (1,)), ((), ()))
ROOM = pltpu.CompilerParams(vmem_limit_bytes=60 << 20)
ANY = pl.BlockSpec(memory_space=pl.ANY)
VMEM = pl.BlockSpec(memory_space=pltpu.VMEM)
SMEM = pl.BlockSpec(memory_space=pltpu.SMEM)


COST = pl.CostEstimate(flops=1024, bytes_accessed=1024, transcendentals=0)


def rms_latent(comp, gain):
    lat = comp[:, :KVL]
    scale = lax.rsqrt(jnp.mean(lat * lat, axis=-1, keepdims=True) + 1e-06)
    return (lat * scale * gain).astype(jnp.bfloat16)


def rotate(values, position):
    half = values.shape[-1] // 2
    freq = jnp.exp(-jnp.log(10000.0) * jnp.arange(half, dtype=jnp.float32) / half)
    angle = position.astype(jnp.float32)[..., None] * freq
    cosine = jnp.cos(angle)
    sine = jnp.sin(angle)
    first = values[..., :half]
    second = values[..., half:]
    return jnp.concatenate([first * cosine - second * sine, first * sine + second * cosine], -1)


def block_stats(keys, q_lat, q_pos, valid):
    scale = (DN + DR) ** (-0.5)
    scores = jnp.einsum("jhk,tk->jht", q_lat, keys[:, :KVL], preferred_element_type=jnp.float32)
    scores = (
        scores + jnp.einsum("jhk,tk->jht", q_pos, keys[:, KVL:], preferred_element_type=jnp.float32)
    ) * scale
    scores = jnp.where(valid, scores, -1e30)
    top = jnp.max(scores, axis=-1)
    weights = jnp.where(valid, jnp.exp(scores - top[..., None]), 0.0)
    total = jnp.sum(weights, axis=-1)
    numer = jnp.einsum(
        "jht,tk->jhk",
        weights.astype(jnp.bfloat16),
        keys[:, :KVL],
        preferred_element_type=jnp.float32,
    )
    return (top, total, numer)


def combine(left, right):
    top = jnp.maximum(left[0], right[0])
    left_scale = jnp.exp(left[0] - top)
    right_scale = jnp.exp(right[0] - top)
    total = left[1] * left_scale + right[1] * right_scale
    numer = left[2] * left_scale[..., None] + right[2] * right_scale[..., None]
    return (top, total, numer)


def local_general(
    prefill_hidden,
    draft_hidden,
    kv_down,
    kv_gain,
    query_latent,
    q_up,
    kv_up,
    owners,
    segment_ids,
    accepted,
):
    tp_count = lax.axis_size("tp")
    pd_count = lax.axis_size("pd")
    tp_rank = lax.axis_index("tp")
    mine_rank = lax.axis_index("pd")
    requests = owners.shape[0]
    share = PRE_TOK // tp_count
    width = KVL + DR
    local_hidden = prefill_hidden.reshape(RP, PRE_TOK, prefill_hidden.shape[1])
    summed = lax.psum_scatter(
        jnp.einsum(
            "rtd,dw->trw", local_hidden, kv_down, preferred_element_type=jnp.float32
        ).reshape(lax.axis_size("tp") * share, RP * width),
        "tp",
        scatter_dimension=0,
        tiled=True,
    ).reshape(share * RP, width)
    draft_sum = lax.psum(jnp.dot(draft_hidden, kv_down, preferred_element_type=jnp.float32), "tp")
    first_req = mine_rank * RP
    row_pos = jnp.broadcast_to(
        tp_rank * share + jnp.arange(share, dtype=jnp.int32)[:, None], (share, RP)
    )
    page_rows = jnp.concatenate(
        [
            rms_latent(summed, kv_gain),
            rotate(summed[:, KVL:], row_pos.reshape(-1)).astype(jnp.bfloat16),
        ],
        1,
    )
    page_rows = page_rows.reshape(share, RP, width)
    draft_pos = jnp.tile(PRE_TOK + jnp.arange(2, dtype=jnp.int32), RP)
    draft_rows = jnp.concatenate(
        [
            rms_latent(draft_sum, kv_gain),
            rotate(draft_sum[:, KVL:], draft_pos).astype(jnp.bfloat16),
        ],
        1,
    )
    draft_rows = draft_rows.reshape(RP, 2, width)
    my_owners = lax.dynamic_slice_in_dim(owners, first_req, RP, 0)
    routing = (my_owners[None, :] == jnp.arange(pd_count, dtype=jnp.int32)[:, None]).astype(
        jnp.bfloat16
    )
    send_pages = jnp.einsum(
        "dk,tkw->dtw", routing, page_rows, preferred_element_type=jnp.float32
    ).astype(jnp.bfloat16)
    send_drafts = jnp.einsum(
        "dk,kjw->djw", routing, draft_rows, preferred_element_type=jnp.float32
    ).astype(jnp.bfloat16)
    pages, drafts = (
        lax.all_to_all(send_pages, "pd", split_axis=0, concat_axis=0, tiled=True),
        lax.all_to_all(send_drafts, "pd", split_axis=0, concat_axis=0, tiled=True),
    )
    heads_local = q_up.shape[1] // (DN + DR)
    query_full = jnp.dot(
        query_latent.reshape(requests * 2, QL), q_up, preferred_element_type=jnp.float32
    )
    query_full = query_full.reshape(requests, 2, heads_local, DN + DR)
    new_pos = jnp.broadcast_to(PRE_TOK + jnp.arange(2, dtype=jnp.int32)[None, :], (requests, 2))
    q_nope = query_full[..., :DN].astype(jnp.bfloat16)
    q_rot = rotate(query_full[..., DN:], new_pos[:, :, None]).astype(jnp.bfloat16)
    up_heads = kv_up.reshape(KVL, heads_local, DN + DV)
    w_value = up_heads[:, :, DN:]
    q_abs = jnp.einsum(
        "rjhd,khd->rjhk", q_nope, up_heads[:, :, :DN], preferred_element_type=jnp.float32
    ).astype(jnp.bfloat16)
    owner_table = owners.reshape(pd_count, RP) == mine_rank
    holding = jnp.sum(owner_table.astype(jnp.int32), axis=1)
    slot_of = jnp.sum(
        owner_table.astype(jnp.int32) * jnp.arange(RP, dtype=jnp.int32)[None, :], axis=1
    )
    owned_count = jnp.sum(holding)
    order = jnp.argsort((1 - holding) * pd_count + jnp.arange(pd_count, dtype=jnp.int32))
    draft_valid = (jnp.arange(2)[None, :] <= jnp.arange(2)[:, None])[:, None, :]
    empty = jnp.zeros((pd_count, 2, heads_local * DV), jnp.bfloat16)

    def finish(stats, source, request, q_lat, q_pos, result):
        stats = combine(stats, block_stats(drafts[source], q_lat, q_pos, draft_valid))
        attended = (stats[2] / stats[1][..., None]).astype(jnp.bfloat16)
        head_out = jnp.einsum("jhk,khd->jhd", attended, w_value, preferred_element_type=jnp.float32)
        keep = (jnp.arange(2) <= accepted[request]).astype(jnp.float32)[:, None, None]
        answer = (head_out * keep).astype(jnp.bfloat16).reshape(1, 2, heads_local * DV)
        return lax.dynamic_update_slice(result, answer, (source, 0, 0))

    def attend(turn, result):
        source = order[turn]
        request = source * RP + slot_of[source]
        q_lat = q_abs[request]
        q_pos = q_rot[request]
        seg_row = segment_ids[request]
        current = seg_row[PRE_TOK - 1]
        init = (
            jnp.full((2, heads_local), -1e30, jnp.float32),
            jnp.zeros((2, heads_local), jnp.float32),
            jnp.zeros((2, heads_local, KVL), jnp.float32),
        )
        valid = (seg_row == current)[None, None, :]
        stats = combine(
            init,
            block_stats(
                lax.all_gather(pages[source], "tp", axis=0, tiled=True), q_lat, q_pos, valid
            ),
        )
        return finish(stats, source, request, q_lat, q_pos, result)

    result = lax.fori_loop(0, owned_count, attend, empty)
    return (result.reshape(pd_count * 2, heads_local * DV), pages)


def encode(values):
    levels = []
    parts = []
    for first, last in ((0, KVL), (KVL, WIDTH)):
        block = values[first:last]
        top = jnp.maximum(jnp.max(jnp.abs(block), axis=0, keepdims=True), 1e-30)
        level = jnp.ceil(jnp.log2(top) * STEPS)
        codes = jnp.round(block * (jnp.exp2(level * (-1.0 / STEPS)) * TOP))
        parts.append(jnp.clip(codes, -TOP, TOP).astype(jnp.int32).astype(I16))
        levels.append(level.astype(jnp.int32))
    row = lax.broadcasted_iota(jnp.int32, (16, values.shape[1]), 0)
    extra = jnp.where(row == 0, levels[0], jnp.where(row == 1, levels[1], 0))
    return jnp.concatenate([*parts, extra.astype(I16)], 0)


def decode(codes):
    level = codes[WIDTH:CODED].astype(jnp.int32).astype(F32)
    step = jnp.exp2(level * (1.0 / STEPS)) * (1.0 / TOP)
    lat = codes[0:KVL].astype(jnp.int32).astype(F32) * step[0:1]
    rot = codes[KVL:WIDTH].astype(jnp.int32).astype(F32) * step[1:2]
    return jnp.concatenate([lat, rot], 0)


def key_rows(comp, gain, cosine, sine):
    lat = comp[:KVL]
    scale = lax.rsqrt(jnp.mean(lat * lat, axis=0, keepdims=True) + 1e-06)
    first = comp[KVL : KVL + HALF]
    second = comp[KVL + HALF :]
    return jnp.concatenate(
        [
            lat * scale * gain,
            first * cosine - second * sine,
            first * sine + second * cosine,
        ],
        0,
    )


def project_kernel(table, hid_ref, down_ref, *refs):
    *_, sum_ref, one_ref, two_ref = refs
    step = pl.program_id(0)
    total = lax.dot_general(down_ref[...], hid_ref[0], NT, preferred_element_type=F32)
    sum_ref[0] = total
    for i, ref in enumerate((one_ref, two_ref)):

        @pl.when((step == i) & (table[6] == 1))
        def _(ref=ref):
            for first in range(0, SHARE, UNIT):
                lanes = slice(first, first + UNIT)
                ref[0, :, lanes] = encode(total[:, lanes])


def project_pair_kernel(table, hid_ref, down_ref, *refs):
    *_, sum_ref, code_ref = refs
    step = pl.program_id(0)
    total = lax.dot_general(down_ref[...], hid_ref[0], NT, preferred_element_type=F32)
    sum_ref[0] = total

    @pl.when((step < 2) & (table[6] == 1))
    def _():
        for first in range(0, SHARE, UNIT):
            lanes = slice(first, first + UNIT)
            code_ref[0, :, lanes] = encode(total[:, lanes])


def project(table, hidden, down_t, request, pair, after):
    depth = hidden.shape[-1]
    if pair:
        codes = [(2, lambda i, table: (jnp.minimum(i, 1), 0, 0))]
    else:
        codes = [(1, lambda i, table: (0, 0, 0))] * 2
    return pl.pallas_call(
        project_pair_kernel if pair else project_kernel,
        grid_spec=pltpu.PrefetchScalarGridSpec(
            num_scalar_prefetch=1,
            grid=(3,),
            in_specs=[
                pl.BlockSpec((1, SHARE, depth), lambda i, table: (request, table[i], 0)),
                pl.BlockSpec((WIDTH, depth), lambda i, table: (0, 0)),
                *([ANY] * len(after)),
            ],
            out_specs=[
                pl.BlockSpec((1, WIDTH, SHARE), lambda i, table: (table[3 + i], 0, 0)),
                *[pl.BlockSpec((1, CODED, SHARE), place) for _, place in codes],
            ],
        ),
        out_shape=[
            jax.ShapeDtypeStruct((3, WIDTH, SHARE), F32),
            *[jax.ShapeDtypeStruct((count, CODED, SHARE), I16) for count, _ in codes],
        ],
        compiler_params=ROOM,
        cost_estimate=COST,
        name="project",
    )(table, hidden, down_t, *after)


def project_last_kernel(table, hid_ref, down_ref, *refs):
    sum_ref, *code_refs = refs[-1 - UNITS :]
    step = pl.program_id(0)
    rows = hid_ref[...].reshape(LANES, hid_ref.shape[-1])
    total = lax.dot_general(down_ref[...], rows, NT, preferred_element_type=F32)
    sum_ref[0] = total
    for u, ref in enumerate(code_refs):

        @pl.when((step == u) & (table[6] == 1))
        def _(ref=ref):
            for first in range(0, LANES, UNIT):
                lanes = slice(first, first + UNIT)
                ref[:, lanes] = encode(total[:, lanes])


def project_last(table, hidden, down_t, after):
    depth = hidden.shape[-1]
    return pl.pallas_call(
        project_last_kernel,
        grid_spec=pltpu.PrefetchScalarGridSpec(
            num_scalar_prefetch=1,
            grid=(UNITS,),
            in_specs=[
                pl.BlockSpec((RP, UNIT, depth), lambda i, table: (0, UNITS + i, 0)),
                pl.BlockSpec((WIDTH, depth), lambda i, table: (0, 0)),
                *([ANY] * len(after)),
            ],
            out_specs=[
                pl.BlockSpec((1, WIDTH, LANES), lambda i, table: (i, 0, 0)),
                *([pl.BlockSpec((CODED, LANES), lambda i, table: (0, 0))] * UNITS),
            ],
        ),
        out_shape=[
            jax.ShapeDtypeStruct((UNITS, WIDTH, LANES), F32),
            *([jax.ShapeDtypeStruct((CODED, LANES), I16)] * UNITS),
        ],
        compiler_params=ROOM,
        cost_estimate=COST,
        name="project_last",
    )(table, hidden, down_t, *after)


def add_kernel(side_at, table, own_ref, got_ref, *refs):
    out_ref = refs[-1]
    step = pl.program_id(0)
    for i in range(2):

        @pl.when((step == i) & (table[2] > i))
        def _(i=i):
            total = own_ref[0] + decode(got_ref[0])
            if i == side_at:
                total = total + decode(refs[0][0])
            out_ref[0] = encode(total)


def add_on(table, sums, got, side=None, side_at=None, after=()):
    count = got.shape[0]
    block = lambda i, j, table: (i, 0, j)
    extra = []
    if side is not None:
        last = side.shape[0] - 1
        extra = [pl.BlockSpec((1, CODED, UNIT), lambda i, j, table: (last, 0, j))]
    return pl.pallas_call(
        functools.partial(add_kernel, side_at),
        grid_spec=pltpu.PrefetchScalarGridSpec(
            num_scalar_prefetch=1,
            grid=(count, UNITS),
            in_specs=[
                pl.BlockSpec((1, WIDTH, UNIT), lambda i, j, table: (table[i], 0, j)),
                pl.BlockSpec((1, CODED, UNIT), block),
                *extra,
                *([ANY] * len(after)),
            ],
            out_specs=pl.BlockSpec((1, CODED, UNIT), block),
        ),
        out_shape=jax.ShapeDtypeStruct((count, CODED, SHARE), I16),
        compiler_params=ROOM,
        cost_estimate=COST,
        name="add_on",
    )(table, sums, got, *([] if side is None else [side]), *after)


def add_last_kernel(table, own_ref, got_ref, out_ref):
    @pl.when(table[7] == 2)
    def _():
        out_ref[...] = encode(own_ref[0] + decode(got_ref[...]))


def add_last(table, sums, got, unit):
    return pl.pallas_call(
        add_last_kernel,
        grid_spec=pltpu.PrefetchScalarGridSpec(
            num_scalar_prefetch=1,
            grid=(RP,),
            in_specs=[
                pl.BlockSpec((1, WIDTH, UNIT), lambda i, table: (unit, 0, i)),
                pl.BlockSpec((CODED, UNIT), lambda i, table: (0, i)),
            ],
            out_specs=pl.BlockSpec((CODED, UNIT), lambda i, table: (0, i)),
        ),
        out_shape=jax.ShapeDtypeStruct((CODED, LANES), I16),
        compiler_params=ROOM,
        cost_estimate=COST,
        name="add_last",
    )(table, sums, got)


def finish_kernel(table, own_ref, got_ref, mid_ref, sent_ref, gain_ref, cos_ref, sin_ref, *refs):
    midcos_ref, midsin_ref, *_, out_ref = refs
    z = table[7]

    def write(place, comp, cosine, sine):
        rows = key_rows(comp, gain_ref[...], cosine[...], sine[...])
        out_ref[0, place] = rows.astype(BF)

    @pl.when((z == 0) | (z == 3))
    def _():
        write(0, own_ref[0] + decode(got_ref[0]), cos_ref, sin_ref)

    @pl.when(z == 3)
    def _():
        write(1, decode(mid_ref[0]), midcos_ref, midsin_ref)

    @pl.when(z == 2)
    def _():
        write(0, decode(sent_ref[0]), midcos_ref, midsin_ref)


def finish(table, sums, got, mid, sent, gain, tables, held, request, after=()):
    lane = pl.BlockSpec((HALF, UNIT), lambda j, table: (0, j))
    first = pl.BlockSpec((1, CODED, UNIT), lambda j, table: (0, 0, j))
    last = mid.shape[0] - 1
    second = pl.BlockSpec((1, CODED, UNIT), lambda j, table: (last, 0, j))
    return pl.pallas_call(
        finish_kernel,
        grid_spec=pltpu.PrefetchScalarGridSpec(
            num_scalar_prefetch=1,
            grid=(UNITS,),
            in_specs=[
                pl.BlockSpec((1, WIDTH, UNIT), lambda j, table: (table[8], 0, j)),
                first,
                second,
                second,
                pl.BlockSpec((KVL, UNIT), lambda j, table: (0, 0)),
                lane,
                lane,
                lane,
                lane,
                ANY,
                *([ANY] * len(after)),
            ],
            out_specs=pl.BlockSpec((1, 2, WIDTH, UNIT), lambda j, table: (request, 0, 0, j)),
        ),
        out_shape=jax.ShapeDtypeStruct(held.shape, BF),
        input_output_aliases={10: 0},
        compiler_params=ROOM,
        cost_estimate=COST,
        name="finish",
    )(table, sums, got, mid, sent, gain, *tables, held, *after)


def page_kernel(table, slots, has, own_ref, one_ref, two_ref, keys_ref, gain_ref, cos_ref, sin_ref, out_ref):
    slot = pl.program_id(0)

    @pl.when(has[slot] == 0)
    def _():
        out_ref[...] = jnp.zeros_like(out_ref)

    @pl.when((has[slot] > 0) & (table[7] == 1))
    def _():
        comp = own_ref[0] + decode(one_ref[...]) + decode(two_ref[...])
        rows = key_rows(comp, gain_ref[...], cos_ref[...], sin_ref[...])
        out_ref[0] = rows.astype(BF)

    @pl.when((has[slot] > 0) & (table[7] != 1))
    def _():
        out_ref[0] = keys_ref[0, 0]


def pages_of(table, slots, has, sums, one, two, keys, gain, cosine, sine, unit):
    count = slots.shape[0]
    part = pl.BlockSpec((CODED, UNIT), lambda i, table, slots, has: (0, slots[i]))
    lane = pl.BlockSpec((HALF, UNIT), lambda i, *_: (0, unit))
    return pl.pallas_call(
        page_kernel,
        grid_spec=pltpu.PrefetchScalarGridSpec(
            num_scalar_prefetch=3,
            grid=(count,),
            in_specs=[
                pl.BlockSpec((1, WIDTH, UNIT), lambda i, table, slots, has: (unit, 0, slots[i])),
                part,
                part,
                pl.BlockSpec(
                    (1, 1, WIDTH, UNIT), lambda i, table, slots, has: (slots[i], 0, 0, unit)
                ),
                pl.BlockSpec((KVL, UNIT), lambda i, *_: (0, 0)),
                lane,
                lane,
            ],
            out_specs=pl.BlockSpec((1, WIDTH, UNIT), lambda i, *_: (i, 0, 0)),
        ),
        out_shape=jax.ShapeDtypeStruct((count, WIDTH, UNIT), BF),
        compiler_params=ROOM,
        cost_estimate=COST,
        name="pages",
    )(table, slots, has, sums, one, two, keys, gain, cosine, sine)


def query_kernel(lat_ref, up_ref, draft_ref, down_ref, *refs):
    *key_refs, cos_ref, sin_ref, out_ref, split_ref = refs

    @pl.when(pl.program_id(0) == 0)
    def _():
        rest = lax.dot_general(draft_ref[...], down_ref[...], NT, preferred_element_type=F32)
        for n in range(3):
            term = rest.astype(BF).astype(F32)
            split_ref[n] = term
            rest = rest - term
        split_ref[3] = jnp.zeros_like(rest)

    full = jnp.dot(lat_ref[...], up_ref[...], preferred_element_type=F32)
    for h, key_ref in enumerate(key_refs):
        base = h * (DN + DR)
        nope = full[:, base : base + DN].astype(BF)
        first = full[:, base + DN : base + DN + HALF]
        second = full[:, base + DN + HALF : base + DN + DR]
        absorbed = lax.dot_general(nope, key_ref[...], NT, preferred_element_type=F32)
        cosine, sine = cos_ref[...], sin_ref[...]
        out_ref[h] = jnp.concatenate(
            [absorbed, first * cosine - second * sine, first * sine + second * cosine], 1
        )


def queries(latents, q_up, kv_up, draft, down_t, cosine, sine, after):
    rows = latents.shape[0]
    heads = q_up.shape[1] // (DN + DR)
    step = 4
    key_spec = [
        pl.BlockSpec((KVL, DN), lambda i, h=h: (0, 2 * (step * i + h))) for h in range(step)
    ]
    whole = lambda i: (0, 0)
    table = pl.BlockSpec((rows, HALF), whole)
    body = lambda *refs: query_kernel(*refs[:-3], *refs[-2:])
    return pl.pallas_call(
        body,
        grid=(heads // step,),
        in_specs=[
            pl.BlockSpec((rows, QL), whole),
            pl.BlockSpec((QL, step * (DN + DR)), lambda i: (0, i)),
            pl.BlockSpec(draft.shape, whole),
            pl.BlockSpec(down_t.shape, whole),
            *key_spec,
            table,
            table,
            ANY,
        ],
        out_specs=[
            pl.BlockSpec((step, rows, WIDTH), lambda i: (i, 0, 0)),
            pl.BlockSpec((4, rows, WIDTH), lambda i: (0, 0, 0)),
        ],
        out_shape=[
            jax.ShapeDtypeStruct((heads, rows, WIDTH), F32),
            jax.ShapeDtypeStruct((4, rows, WIDTH), F32),
        ],
        compiler_params=ROOM,
        cost_estimate=COST,
        name="queries",
    )(latents, q_up, draft, down_t, *([kv_up] * step), cosine, sine, after)


def attend_kernel(table, q_ref, draft_ref, keys_ref, valid_ref, gain_ref, cos_ref, sin_ref, *out_refs):
    request = pl.program_id(0)

    @pl.when(table[7] == 3)
    def _():
        scale = (DN + DR) ** (-0.5)
        local_rows = out_refs[0].shape[1]
        new = 2 * RP
        comp = 0.0
        for t in range(4):
            terms = draft_ref[t].astype(F32)
            comp = comp + (terms[0:new] + terms[new : 2 * new] + terms[2 * new : 3 * new])
        lat = comp[:, :KVL]
        norm = lax.rsqrt(jnp.mean(lat * lat, axis=-1, keepdims=True) + 1e-06)
        first = comp[:, KVL : KVL + HALF]
        second = comp[:, KVL + HALF :]
        cosine, sine = cos_ref[...], sin_ref[...]
        drafts = jnp.concatenate(
            [
                lat * norm * gain_ref[...],
                first * cosine - second * sine,
                first * sine + second * cosine,
            ],
            1,
        )
        drafts = jnp.concatenate([drafts, jnp.zeros((UNIT - new, WIDTH), F32)], 0).astype(BF)
        query = jnp.concatenate([q_ref[t] for t in range(4)], 0)
        keys = jnp.concatenate([keys_ref[0, 1], keys_ref[0, 0]], 1)
        scores = jnp.dot(query, keys, preferred_element_type=F32) * scale
        scores = jnp.where(valid_ref[0] > 0.0, scores, -1e30)
        fresh = lax.dot_general(query, drafts, NT, preferred_element_type=F32) * scale
        row = lax.broadcasted_iota(jnp.int32, fresh.shape, 0)
        late = (row % local_rows) // (local_rows // 2)
        offset = lax.broadcasted_iota(jnp.int32, fresh.shape, 1) - 2 * request
        fresh = jnp.where((offset >= 0) & (offset <= late), fresh, -1e30)
        top = jnp.maximum(
            jnp.max(scores, axis=1, keepdims=True), jnp.max(fresh, axis=1, keepdims=True)
        )
        weights = jnp.exp(scores - top)
        fresh = jnp.exp(fresh - top)
        total = jnp.sum(weights, axis=1, keepdims=True) + jnp.sum(fresh, axis=1, keepdims=True)
        numer = lax.dot_general(weights.astype(BF), keys[:KVL], NT, preferred_element_type=F32)
        numer = numer + jnp.dot(fresh.astype(BF), drafts[:, :KVL], preferred_element_type=F32)
        result = (numer / total).astype(BF)
        for t, ref in enumerate(out_refs):
            ref[0] = result[t * local_rows : (t + 1) * local_rows]


def attend(table, messages, held, valid, gain, cosine, sine, after):
    new = 2 * RP
    local_rows = (messages.shape[1] - 4 * new) // RP
    last = RP * local_rows // (4 * new)
    out = jax.ShapeDtypeStruct((RP, local_rows, KVL), BF)
    whole = lambda i, table: (0, 0)
    body = lambda *refs: attend_kernel(*refs[:8], *refs[-4:])
    return pl.pallas_call(
        body,
        grid_spec=pltpu.PrefetchScalarGridSpec(
            num_scalar_prefetch=1,
            grid=(RP,),
            in_specs=[
                pl.BlockSpec((4, local_rows, WIDTH), lambda i, table: (0, i, 0)),
                pl.BlockSpec((4, 4 * new, WIDTH), lambda i, table: (0, last, 0)),
                pl.BlockSpec((1, 2, WIDTH, SHARE), lambda i, table: (i, 0, 0, 0)),
                pl.BlockSpec((1, 1, valid.shape[2]), lambda i, table: (i, 0, 0)),
                pl.BlockSpec((1, KVL), whole),
                pl.BlockSpec(cosine.shape, whole),
                pl.BlockSpec(sine.shape, whole),
                *([ANY] * len(after)),
            ],
            out_specs=[pl.BlockSpec((1, local_rows, KVL), lambda i, table: (i, 0, 0))] * 4,
        ),
        out_shape=[out] * 4,
        compiler_params=ROOM,
        cost_estimate=COST,
        name="attend",
    )(table, messages, messages, held, valid, gain, cosine, sine, *after)


def heads_kernel(o_ref, keep_ref, *refs):
    *value_refs, out_ref = refs
    for h, value_ref in enumerate(value_refs):
        row = jnp.dot(o_ref[h].astype(BF), value_ref[...], preferred_element_type=F32)
        out_ref[:, h * DV : (h + 1) * DV] = row * keep_ref[...]


def heads_out(attended, keep, kv_up):
    heads, rows, _ = attended.shape
    step = 8
    value_spec = [
        pl.BlockSpec((KVL, DV), lambda i, h=h: (0, 2 * (step * i + h) + 1)) for h in range(step)
    ]
    return pl.pallas_call(
        heads_kernel,
        grid=(heads // step,),
        in_specs=[
            pl.BlockSpec((step, rows, KVL), lambda i: (i, 0, 0)),
            pl.BlockSpec((rows, DV), lambda i: (0, 0)),
            *value_spec,
        ],
        out_specs=pl.BlockSpec((rows, step * DV), lambda i: (0, i)),
        out_shape=jax.ShapeDtypeStruct((rows, heads * DV), F32),
        compiler_params=ROOM,
        cost_estimate=COST,
        name="heads_out",
    )(attended, keep, *([kv_up] * step))


def rope_tables(position):
    freq = jnp.exp(-jnp.log(10000.0) * jnp.arange(HALF, dtype=F32) / HALF)
    angle = position.astype(F32)[..., None] * freq
    return jnp.cos(angle), jnp.sin(angle)


def local_line(
    prefill_hidden,
    draft_hidden,
    kv_down,
    kv_gain,
    query_latent,
    q_up,
    kv_up,
    owners,
    segment_ids,
    accepted,
):
    pd_count = lax.axis_size("pd")
    z = lax.axis_index("tp")
    p = lax.axis_index("pd")
    first_req = p * RP

    table = jnp.asarray(
        [
            [3, 2, 0, 2, 1, 0, 1, 0, 0],
            [3, 2, 0, 2, 1, 0, 0, 1, 0],
            [3, 2, 0, 2, 1, 0, 0, 2, 1],
            [0, 2, 3, 0, 1, 2, 1, 3, 2],
        ],
        jnp.int32,
    )[z]
    hops = jnp.asarray(
        [
            [[0, 0, 0], [2, 1, 2], [0, 0, 1], [0, 0, 0]],
            [[0, 0, 0], [0, 0, 1], [2, 1, 2], [0, 0, 0]],
            [[0, 0, 0], [2, 2, 1], [0, 0, 1], [0, 0, 0]],
            [[0, 0, 0], [1, 1, 1], [0, 0, 0], [0, 0, 0]],
            [[0, 0, 0], [0, 0, 1], [2, 2, 1], [0, 0, 0]],
            [[0, 0, 0], [0, 0, 0], [1, 1, 1], [0, 0, 0]],
        ],
        jnp.int32,
    )[:, z]

    hidden = prefill_hidden.reshape(RP, PRE_TOK, prefill_hidden.shape[1])
    down_t = kv_down.T
    inward = [(0, 1), (3, 2)]
    last = RP - 1
    sums = [None] * RP
    inner = [None] * RP
    for r in range(RP):
        sums[r], *coded = project(table, hidden, down_t, r, r < last, sums[max(r - 1, 0) : r])
        inner[r] = [lax.ppermute(c, "tp", inward) for c in coded]

    my_segments = lax.dynamic_slice_in_dim(segment_ids, first_req, RP, 0)
    valid = (my_segments == my_segments[:, -1:])[:, PRE_TOK // 2 :].astype(F32)
    valid = valid.reshape(RP, 1, PRE_TOK // 2)
    gain = jnp.broadcast_to(kv_gain[:, None], (KVL, UNIT))
    steps = jnp.arange(SHARE, dtype=jnp.int32)
    tables = [t.T for t in (*rope_tables(z * SHARE + steps), *rope_tables(2 * SHARE + steps))]

    held = jnp.zeros((RP, 2, WIDTH, SHARE), BF)
    across = [None] * RP
    sent = [None] * RP
    outer = [None] * RP

    def first_hop(r, after):
        block = add_on(hops[0], sums[r], inner[r][0], after=after)
        across[r] = lax.ppermute(block, "tp", [(1, 2), (2, 1)])
        return block

    def second_hop(r, after):
        block = add_on(hops[1], sums[r], across[r], inner[r][0], 1, after)
        sent[r] = block
        outer[r] = [lax.ppermute(block, "tp", [(2, 3), (1, 0)])] * 2

    block = first_hop(0, [sums[last]])

    latents = lax.dynamic_slice_in_dim(query_latent, first_req, RP, 0).reshape(RP * 2, QL)
    new_pos = jnp.tile(PRE_TOK + jnp.arange(2, dtype=jnp.int32), RP)
    new_cos, new_sin = rope_tables(new_pos)
    query, terms = queries(
        latents, q_up, kv_up, draft_hidden, down_t, new_cos, new_sin, block
    )
    heads = query.shape[0]
    query = query.reshape(heads, RP, 2, WIDTH).transpose(1, 2, 0, 3)
    message = jnp.concatenate(
        [query.reshape(RP * 2 * heads, WIDTH), terms.reshape(8 * RP, WIDTH)], 0
    ).astype(BF)
    messages = lax.all_gather(message, "tp", axis=0)

    first_hop(1, [query])
    second_hop(0, [])
    first_hop(2, [sent[0], message])
    second_hop(1, [])
    held = finish(table, sums[0], *outer[0], sent[0], gain, tables, held, 0, [sent[1]])

    one = add_on(hops[2], sums[last], inner[last][0], after=[sent[1]])
    sums_last, *coded = project_last(table, hidden, down_t, [one])
    inner_last = [lax.ppermute(c, "tp", inward) for c in coded]
    one = lax.ppermute(one, "tp", [(1, 2), (2, 1)])
    two = add_on(hops[3], sums[last], inner[last][1], after=[held, sums_last, messages])
    two = lax.ppermute(two, "tp", [(1, 2)])
    second_hop(2, [])
    held = finish(table, sums[1], *outer[1], sent[1], gain, tables, held, 1, [sent[2]])
    one = add_on(hops[4], sums[last], one, after=[held])
    one = lax.ppermute(one, "tp", [(2, 3), (1, 0)])
    lasts = [add_last(table, sums_last, inner_last[0], 0)]
    sent[last] = add_on(hops[5], sums[last], two, inner[last][1], 0, [lasts[0]])
    two = lax.ppermute(sent[last], "tp", [(2, 3)])
    lasts.append(add_last(table, sums_last, inner_last[1], 1))
    held = finish(table, sums[2], *outer[2], sent[2], gain, tables, held, 2, [lasts[1]])
    lasts.append(add_last(table, sums_last, inner_last[2], 2))
    held = finish(table, sums[last], one, two, sent[last], gain, tables, held, last, [])
    lasts = [lax.ppermute(block, "tp", [(2, 1)]) for block in lasts]

    result = attend(
        table, messages, held, valid, kv_gain.reshape(1, KVL), new_cos, new_sin, [lasts[0]]
    )
    back = [lax.ppermute(result[t], "tp", [(3, t)]) for t in range(3)]
    attended = jnp.where(z == 3, result[3], back[0] + back[1] + back[2])
    attended = attended.reshape(RP, 2, heads, KVL).transpose(2, 0, 1, 3)
    attended = attended.reshape(heads, RP * 2, KVL).astype(F32)
    my_accepted = lax.dynamic_slice_in_dim(accepted, first_req, RP, 0)
    keep = (jnp.arange(2)[None, :] <= my_accepted[:, None]).astype(F32).reshape(RP * 2, 1)
    answer = heads_out(attended, jnp.broadcast_to(keep, (RP * 2, DV)), kv_up)
    answer = answer.reshape(RP, 2, heads * DV)

    my_owners = lax.dynamic_slice_in_dim(owners, first_req, RP, 0)
    routing = my_owners[None, :] == jnp.arange(pd_count, dtype=jnp.int32)[:, None]
    has = jnp.any(routing, axis=1)
    slots = jnp.sum(routing.astype(jnp.int32) * jnp.arange(RP, dtype=jnp.int32)[None, :], axis=1)
    placed = jnp.where(has[:, None, None], answer[slots], 0.0).astype(BF)
    placed = lax.all_to_all(placed, "pd", split_axis=0, concat_axis=0, tiled=True)

    cache = []
    for u in range(UNITS):
        page = pages_of(
            table,
            slots,
            has.astype(jnp.int32),
            sums_last,
            inner_last[u],
            lasts[u],
            held,
            gain,
            tables[0],
            tables[1],
            u,
        )
        cache.append(lax.all_to_all(page, "pd", split_axis=0, concat_axis=0, tiled=True))
    cache = jnp.swapaxes(jnp.concatenate(cache, 2), 1, 2)
    return (placed.reshape(pd_count * 2, heads * DV), cache)


def solution(mesh):
    placed = (
        P(("groups", "pd"), "tp"),
        P(("groups", "pd"), "tp"),
        P("tp", None),
        P(),
        P("groups", None, None),
        P(None, "tp"),
        P(None, "tp"),
        P("groups"),
        P("groups", None),
        P("groups"),
    )
    return jax.shard_map(
        local_line if mesh.shape["tp"] == 4 else local_general,
        mesh=mesh,
        in_specs=placed,
        out_specs=(P(("groups", "pd"), "tp"), P(("groups", "pd"), "tp", None)),
        check_vma=False,
    )
```

profile of v0, /device:TPU:16, one launch (start us, length us, event | category | flops | bytes accessed | tf_op | source)
XLA Modules:
  0.0 341.7 jit_solution(602601919616115142)
XLA Ops:
  8.5 8.1 %project.4 = (f32[3,576,384]{2,1,0:T(8,128)}, s16[2,592,384]{2,1,0:T(8,128)(2,1)}) custom-call(s32[9]{0:T(128)} %fusion.3.table.refs_0_, bf16[4,1536,1792]{2,1,0:T(8,128)(2,1)} %bitcast.37, bf16[576,1792]{1,0:T(8,128)(2,1)} %bitcast.42), custom_call_target="tpu_custom_call" | custom-call | flops 1024 | bytes 1024 | tf_op jit(solution)/shard_map/project/pallas_call | solution.py:275
  17.9 8.2 %project.5 = (f32[3,576,384]{2,1,0:T(8,128)}, s16[2,592,384]{2,1,0:T(8,128)(2,1)}) custom-call(s32[9]{0:T(128)} %fusion.3.table.refs_0_, bf16[4,1536,1792]{2,1,0:T(8,128)(2,1)} %bitcast.38, bf16[576,1792]{1,0:T(8,128)(2,1)} %bitcast.43, f32[3,576,384]{2,1,0:T(8,128)} %get-tuple-element.21.refs_0_.own_ref), custom_call_target="tpu_custom_call" | custom-call | flops 1024 | bytes 1024 | tf_op jit(solution)/shard_map/project/pallas_call | solution.py:275
  27.3 8.1 %project.6 = (f32[3,576,384]{2,1,0:T(8,128)}, s16[2,592,384]{2,1,0:T(8,128)(2,1)}) custom-call(s32[9]{0:T(128)} %fusion.3.table.refs_0_, bf16[4,1536,1792]{2,1,0:T(8,128)(2,1)} %bitcast.39, bf16[576,1792]{1,0:T(8,128)(2,1)} %bitcast.44, f32[3,576,384]{2,1,0:T(8,128)} %get-tuple-element.23.refs_0_.own_ref), custom_call_target="tpu_custom_call" | custom-call | flops 1024 | bytes 1024 | tf_op jit(solution)/shard_map/project/pallas_call | solution.py:275
  35.5 8.2 %project.7 = (f32[3,576,384]{2,1,0:T(8,128)}, s16[1,592,384]{2,1,0:T(8,128)(2,1)}, s16[1,592,384]{2,1,0:T(8,128)(2,1)}) custom-call(s32[9]{0:T(128)} %fusion.3.table.refs_0_, bf16[4,1536,1792]{2,1,0:T(8,128)(2,1)} %bitcast.40, bf16[576,1792]{1,0:T(8,128)(2,1)} %bitcast.45, f32[3,576,384]{2,1,0:T(8,128)} %get-tuple-element.24.refs_0_.own_ref), custom_call_target="tpu_custom_call" | custom-call | flops 1024 | bytes 1024 | tf_op jit(solution)/shard_map/project/pallas_call | solution.py:275
  47.4 5.5 %add_on.10.refs_10_ = s16[2,592,384]{2,1,0:T(8,128)(2,1)} custom-call(s32[3]{0:T(128)} %get-tuple-element.47.table, f32[3,576,384]{2,1,0:T(8,128)} %get-tuple-element.21.refs_0_.own_ref, s16[2,592,384]{2,1,0:T(8,128)(2,1)} %copy-done.4, f32[3,576,384]{2,1,0:T(8,128)} %get-tuple-element.25.refs_0_.own_ref), custom_call_target="tpu_custom_call" | custom-call | flops 1024 | bytes 1024 | tf_op jit(solution)/shard_map/add_on/pallas_call | solution.py:362
  52.9 13.8 %queries.1 = (f32[32,8,576]{2,1,0:T(8,128)}, f32[4,8,576]{2,1,0:T(8,128)}) custom-call(bf16[8,1536]{1,0:T(8,128)(2,1)} %reshape.146.refs_0_, bf16[1536,6144]{1,0:T(8,128)(2,1)} %refs_1_.2, bf16[8,1792]{1,0:T(8,128)(2,1)} %refs_2_.2, bf16[576,1792]{1,0:T(8,128)(2,1)} %bitcast.46, bf16[512,8192]{1,0:T(8,128)(2,1)} %refs_7_.3, bf16[512,8192]{1,0:T(8,128)(2,1)} %refs_7_.3, ...), custom_call_target="tpu_custom_call" | custom-call | flops 1024 | bytes 1024 | tf_op jit(solution)/shard_map/queries/pallas_call | solution.py:543
  70.0 2.5 collective-permute-start.6
  74.7 5.5 %add_on.11 = s16[2,592,384]{2,1,0:T(8,128)(2,1)} custom-call(s32[3]{0:T(128)} %get-tuple-element.47.table, f32[3,576,384]{2,1,0:T(8,128)} %get-tuple-element.23.refs_0_.own_ref, s16[2,592,384]{2,1,0:T(8,128)(2,1)} %copy-done.6, f32[4,2,32,576]{3,2,1,0:T(8,128)} %bitcast.49), custom_call_target="tpu_custom_call" | custom-call | flops 1024 | bytes 1024 | tf_op jit(solution)/shard_map/add_on/pallas_call | solution.py:362
  80.2 3.6 %collective-permute-start.3 = (s16[2,592,384]{2,1,0:T(8,128)(2,1)}, s16[2,592,384]{2,1,0:T(8,128)(2,1)S(1)}, u32[]{:S(2)}, u32[]{:S(2)}) collective-permute-start(s16[2,592,384]{2,1,0:T(8,128)(2,1)} %add_on.11), channel_id=1, source_target_pairs={{4,8},{8,4},{5,9},{9,5},{6,10},{10,6},{7,11},{11,7},{20,24},{24,20... | collective-permute-start | bytes 2727944 | tf_op jit(solution)/shard_map/ppermute | solution.py:746
  85.2 28.8 %collective-permute-done.6.got_ref = s16[2,592,384]{2,1,0:T(8,128)(2,1)} collective-permute-done((s16[2,592,384]{2,1,0:T(8,128)(2,1)S(1)}, s16[2,592,384]{2,1,0:T(8,128)(2,1)}, u32[]{:S(2)}, u32[]{:S(2)}) %collective-permute-start.6) | collective-permute-done | bytes 909344 | tf_op jit(solution)/shard_map/ppermute | solution.py:746
  113.9 5.8 %add_on.14.sent_ref.refs_0_ = s16[2,592,384]{2,1,0:T(8,128)(2,1)} custom-call(s32[3]{0:T(128)} %get-tuple-element.44.table, f32[3,576,384]{2,1,0:T(8,128)} %get-tuple-element.21.refs_0_.own_ref, s16[2,592,384]{2,1,0:T(8,128)(2,1)} %collective-permute-done.6.got_ref, s16[2,592,384]{2,1,0:T(8,128)(2,1)} %copy-done.4), custom_call_target="tpu_custom_call" | custom-call | flops 1024 | bytes 1024 | tf_op jit(solution)/shard_map/add_on/pallas_call | solution.py:362
  119.8 2.3 collective-permute-start.7
  123.8 5.5 %add_on.15 = s16[2,592,384]{2,1,0:T(8,128)(2,1)} custom-call(s32[3]{0:T(128)} %get-tuple-element.47.table, f32[3,576,384]{2,1,0:T(8,128)} %get-tuple-element.24.refs_0_.own_ref, s16[2,592,384]{2,1,0:T(8,128)(2,1)} %copy-done.7, s16[2,592,384]{2,1,0:T(8,128)(2,1)} %add_on.14.sent_ref.refs_0_, bf16[288,576]{1,0:T(8,128)(2,1)} %pad_maximum_fusion.1.refs_1_), custom_call_target="tpu_custom_call" | custom-call | flops 1024 | bytes 1024 | tf_op jit(solution)/shard_map/add_on/pallas_call | solution.py:362
  131.2 6.9 %collective-permute-done.3.got_ref = s16[2,592,384]{2,1,0:T(8,128)(2,1)S(1)} collective-permute-done((s16[2,592,384]{2,1,0:T(8,128)(2,1)}, s16[2,592,384]{2,1,0:T(8,128)(2,1)S(1)}, u32[]{:S(2)}, u32[]{:S(2)}) %collective-permute-start.3) | collective-permute-done | bytes 909344 | tf_op jit(solution)/shard_map/ppermute | solution.py:746
  139.0 5.9 %add_on.12.refs_0_.refs_3_.sent_ref = s16[2,592,384]{2,1,0:T(8,128)(2,1)} custom-call(s32[3]{0:T(128)} %get-tuple-element.44.table, f32[3,576,384]{2,1,0:T(8,128)} %get-tuple-element.23.refs_0_.own_ref, s16[2,592,384]{2,1,0:T(8,128)(2,1)} %copy-done.17, s16[2,592,384]{2,1,0:T(8,128)(2,1)} %copy-done.6), custom_call_target="tpu_custom_call" | custom-call | flops 1024 | bytes 1024 | tf_op jit(solution)/shard_map/add_on/pallas_call | solution.py:362
  145.7 3.7 %add_on.13.refs_0_ = s16[1,592,384]{2,1,0:T(8,128)(2,1)} custom-call(s32[3]{0:T(128)} %get-tuple-element.45.table, f32[3,576,384]{2,1,0:T(8,128)} %get-tuple-element.25.refs_0_.own_ref, s16[1,592,384]{2,1,0:T(8,128)(2,1)} %copy-done.22, s16[2,592,384]{2,1,0:T(8,128)(2,1)} %add_on.12.refs_0_.refs_3_.sent_ref), custom_call_target="tpu_custom_call" | custom-call | flops 1024 | bytes 1024 | tf_op jit(solution)/shard_map/add_on/pallas_call | solution.py:362
  149.4 9.1 %project_last.1 = (f32[3,576,512]{2,1,0:T(8,128)}, s16[592,512]{1,0:T(8,128)(2,1)}, s16[592,512]{1,0:T(8,128)(2,1)}, s16[592,512]{1,0:T(8,128)(2,1)}) custom-call(s32[9]{0:T(128)} %fusion.3.table.refs_0_, bf16[4,1536,1792]{2,1,0:T(8,128)(2,1)} %bitcast.41, bf16[576,1792]{1,0:T(8,128)(2,1)} %bitcast.47, s16[1,592,384]{2,1,0:T(8,128)(2,1)} %add_on.13.refs_0_), custom_call_target="tpu_custom_call" | custom-call | flops 1024 | bytes 1024 | tf_op jit(solution)/shard_map/project_last/pallas_call | solution.py:317
  159.8 4.6 %collective-permute-start.5 = (s16[2,592,384]{2,1,0:T(8,128)(2,1)S(1)}, s16[2,592,384]{2,1,0:T(8,128)(2,1)S(1)}, u32[]{:S(2)}, u32[]{:S(2)}) collective-permute-start(s16[2,592,384]{2,1,0:T(8,128)(2,1)S(1)} %copy-done.2), channel_id=1, source_target_pairs={{8,12},{4,0},{9,13},{5,1},{10,14},{6,2},{11,15},{7,3},{24,28},{20,... | collective-permute-start | bytes 2727944 | tf_op jit(solution)/shard_map/ppermute | solution.py:752
  166.9 2.3 collective-permute-start.4
  170.0 2.1 broadcast_in_dim.16.refs_2_
  172.1 4.5 %finish.4.refs_2_.refs_0_ = bf16[4,2,576,384]{3,2,1,0:T(8,128)(2,1)} custom-call(s32[9]{0:T(128)} %fusion.3.table.refs_0_, f32[3,576,384]{2,1,0:T(8,128)} %get-tuple-element.21.refs_0_.own_ref, s16[2,592,384]{2,1,0:T(8,128)(2,1)} %collective-permute-done.7.got_ref.mid_ref, ...), custom_call_target="tpu_custom_call", output_to_operand_aliasing={{}: (10, {})} | custom-call | flops 1024 | bytes 1024 | tf_op jit(solution)/shard_map/finish/pallas_call | solution.py:433
  176.6 7.2 %collective-permute-done.11.got_ref.refs_0_ = s16[1,592,384]{2,1,0:T(8,128)(2,1)S(1)} collective-permute-done((s16[1,592,384]{2,1,0:T(8,128)(2,1)S(1)}, s16[1,592,384]{2,1,0:T(8,128)(2,1)S(1)}, u32[]{:S(2)}, u32[]{:S(2)}) %collective-permute-start.11) | collective-permute-done | bytes 454688 | tf_op jit(solution)/shard_map/ppermute | solution.py:730
  184.5 3.5 %add_on.18 = s16[1,592,384]{2,1,0:T(8,128)(2,1)} custom-call(s32[3]{0:T(128)} %get-tuple-element.42.table, f32[3,576,384]{2,1,0:T(8,128)} %get-tuple-element.25.refs_0_.own_ref, s16[1,592,384]{2,1,0:T(8,128)(2,1)} %copy-done.16, bf16[4,2,576,384]{3,2,1,0:T(8,128)(2,1)} %finish.4.refs_2_.refs_0_, f32[3,576,512]{2,1,0:T(8,128)} %get-tuple-element.32.refs_1_.own_ref, ...), custom_call_target="tpu_custom_call" | custom-call | flops 1024 | bytes 1024 | tf_op jit(solution)/shard_map/add_on/pallas_call | solution.py:362
  190.8 5.9 %add_on.16.refs_3_.sent_ref = s16[2,592,384]{2,1,0:T(8,128)(2,1)} custom-call(s32[3]{0:T(128)} %get-tuple-element.44.table, f32[3,576,384]{2,1,0:T(8,128)} %get-tuple-element.24.refs_0_.own_ref, s16[2,592,384]{2,1,0:T(8,128)(2,1)} %collective-permute-done.9.got_ref, s16[2,592,384]{2,1,0:T(8,128)(2,1)} %copy-done.7), custom_call_target="tpu_custom_call" | custom-call | flops 1024 | bytes 1024 | tf_op jit(solution)/shard_map/add_on/pallas_call | solution.py:362
  196.6 4.9 %collective-permute-start.15 = (s16[2,592,384]{2,1,0:T(8,128)(2,1)}, s16[2,592,384]{2,1,0:T(8,128)(2,1)S(1)}, u32[]{:S(2)}, u32[]{:S(2)}) collective-permute-start(s16[2,592,384]{2,1,0:T(8,128)(2,1)} %add_on.16.refs_3_.sent_ref), channel_id=1, source_target_pairs={{8,12},{4,0},{9,13},{5,1},{10,14},{6,2},{11,15},{7,3},{24,28},{20,... | collective-permute-start | bytes 2727944 | tf_op jit(solution)/shard_map/ppermute | solution.py:752
  201.6 4.3 %add_last.3.refs_1_ = s16[592,512]{1,0:T(8,128)(2,1)} custom-call(s32[9]{0:T(128)} %fusion.3.table.refs_0_, f32[3,576,512]{2,1,0:T(8,128)} %get-tuple-element.32.refs_1_.own_ref, s16[592,512]{1,0:T(8,128)(2,1)} %copy-done.12), custom_call_target="tpu_custom_call" | custom-call | flops 1024 | bytes 1024 | tf_op jit(solution)/shard_map/add_last/pallas_call | solution.py:389
  205.9 4.9 %collective-permute-start.17 = (s16[592,512]{1,0:T(8,128)(2,1)}, s16[592,512]{1,0:T(8,128)(2,1)S(1)}, u32[]{:S(2)}, u32[]{:S(2)}) collective-permute-start(s16[592,512]{1,0:T(8,128)(2,1)} %add_last.3.refs_1_), channel_id=1, source_target_pairs={{8,4},{9,5},{10,6},{11,7},{24,20},{25,21},{26,22},{27,23}} | collective-permute-start | bytes 1818632 | tf_op jit(solution)/shard_map/ppermute | solution.py:792
  211.8 4.5 %finish.5.refs_0_.refs_2_ = bf16[4,2,576,384]{3,2,1,0:T(8,128)(2,1)} custom-call(s32[9]{0:T(128)} %fusion.3.table.refs_0_, f32[3,576,384]{2,1,0:T(8,128)} %get-tuple-element.23.refs_0_.own_ref, s16[2,592,384]{2,1,0:T(8,128)(2,1)} %copy-done.8, s16[2,592,384]{2,1,0:T(8,128)(2,1)} %copy-done.8, ...), custom_call_target="tpu_custom_call", output_to_operand_aliasing={{}: (10, {})} | custom-call | flops 1024 | bytes 1024 | tf_op jit(solution)/shard_map/finish/pallas_call | solution.py:433
  216.3 3.7 %add_on.17 = s16[1,592,384]{2,1,0:T(8,128)(2,1)} custom-call(s32[3]{0:T(128)} %get-tuple-element.46.table, f32[3,576,384]{2,1,0:T(8,128)} %get-tuple-element.25.refs_0_.own_ref, s16[1,592,384]{2,1,0:T(8,128)(2,1)} %collective-permute-done.4.got_ref, bf16[4,2,576,384]{3,2,1,0:T(8,128)(2,1)} %finish.5.refs_0_.refs_2_), custom_call_target="tpu_custom_call" | custom-call | flops 1024 | bytes 1024 | tf_op jit(solution)/shard_map/add_on/pallas_call | solution.py:362
  221.5 4.0 %add_on.19.sent_ref = s16[1,592,384]{2,1,0:T(8,128)(2,1)} custom-call(s32[3]{0:T(128)} %get-tuple-element.43.table, f32[3,576,384]{2,1,0:T(8,128)} %get-tuple-element.25.refs_0_.own_ref, s16[1,592,384]{2,1,0:T(8,128)(2,1)} %collective-permute-done.12.got_ref, s16[1,592,384]{2,1,0:T(8,128)(2,1)} %copy-done.16, s16[592,512]{1,0:T(8,128)(2,1)} %add_last.3.refs_1_), custom_call_target="tpu_custom_call" | custom-call | flops 1024 | bytes 1024 | tf_op jit(solution)/shard_map/add_on/pallas_call | solution.py:362
  229.8 4.3 %add_last.4.refs_3_ = s16[592,512]{1,0:T(8,128)(2,1)} custom-call(s32[9]{0:T(128)} %fusion.3.table.refs_0_, f32[3,576,512]{2,1,0:T(8,128)} %get-tuple-element.32.refs_1_.own_ref, s16[592,512]{1,0:T(8,128)(2,1)} %collective-permute-done.16.got_ref.one_ref), custom_call_target="tpu_custom_call" | custom-call | flops 1024 | bytes 1024 | tf_op jit(solution)/shard_map/add_last/pallas_call | solution.py:389
  235.0 4.5 %finish.6.refs_2_ = bf16[4,2,576,384]{3,2,1,0:T(8,128)(2,1)} custom-call(s32[9]{0:T(128)} %fusion.3.table.refs_0_, f32[3,576,384]{2,1,0:T(8,128)} %get-tuple-element.24.refs_0_.own_ref, s16[2,592,384]{2,1,0:T(8,128)(2,1)} %copy-done.9, s16[2,592,384]{2,1,0:T(8,128)(2,1)} %copy-done.9, ...), custom_call_target="tpu_custom_call", output_to_operand_aliasing={{}: (10, {})} | custom-call | flops 1024 | bytes 1024 | tf_op jit(solution)/shard_map/finish/pallas_call | solution.py:433
  241.0 4.5 %finish.7.refs_3_.keys_ref = bf16[4,2,576,384]{3,2,1,0:T(8,128)(2,1)} custom-call(s32[9]{0:T(128)} %fusion.3.table.refs_0_, f32[3,576,384]{2,1,0:T(8,128)} %get-tuple-element.25.refs_0_.own_ref, s16[1,592,384]{2,1,0:T(8,128)(2,1)} %copy-done.20, s16[1,592,384]{2,1,0:T(8,128)(2,1)} %copy-done.21, ...), custom_call_target="tpu_custom_call", output_to_operand_aliasing={{}: (10, {})} | custom-call | flops 1024 | bytes 1024 | tf_op jit(solution)/shard_map/finish/pallas_call | solution.py:433
  246.4 4.9 %attend.1 = (bf16[4,64,512]{2,1,0:T(8,128)(2,1)}, bf16[4,64,512]{2,1,0:T(8,128)(2,1)}, bf16[4,64,512]{2,1,0:T(8,128)(2,1)}, bf16[4,64,512]{2,1,0:T(8,128)(2,1)}) custom-call(s32[9]{0:T(128)} %fusion.3.table.refs_0_, bf16[4,288,576]{2,1,0:T(8,128)(2,1)} %all-gather.2.cloned.1.call-done.refs_2_.refs_1_, ...), custom_call_target="tpu_custom_call" | custom-call | flops 1024 | bytes 1024 | tf_op jit(solution)/shard_map/attend/pallas_call | solution.py:625
  256.5 4.3 %add_last.5 = s16[592,512]{1,0:T(8,128)(2,1)} custom-call(s32[9]{0:T(128)} %fusion.3.table.refs_0_, f32[3,576,512]{2,1,0:T(8,128)} %get-tuple-element.32.refs_1_.own_ref, s16[592,512]{1,0:T(8,128)(2,1)} %copy-done.14), custom_call_target="tpu_custom_call" | custom-call | flops 1024 | bytes 1024 | tf_op jit(solution)/shard_map/add_last/pallas_call | solution.py:389
  262.2 3.5 %collective-permute-done.20 = bf16[4,64,512]{2,1,0:T(8,128)(2,1)S(1)} collective-permute-done((bf16[4,64,512]{2,1,0:T(8,128)(2,1)}, bf16[4,64,512]{2,1,0:T(8,128)(2,1)S(1)}, u32[]{:S(2)}, u32[]{:S(2)}) %collective-permute-start.20) | collective-permute-done | bytes 262176 | tf_op jit(solution)/shard_map/ppermute | solution.py:797
  267.9 4.4 %heads_out.1 = f32[8,4096]{1,0:T(8,128)} custom-call(f32[32,8,512]{2,1,0:T(8,128)} %reshape.158.o_ref, f32[8,128]{1,0:T(8,128)} %broadcast_in_dim.17.keep_ref, bf16[512,8192]{1,0:T(8,128)(2,1)} %refs_7_.3, bf16[512,8192]{1,0:T(8,128)(2,1)} %refs_7_.3, bf16[512,8192]{1,0:T(8,128)(2,1)} %refs_7_.3, bf16[512,8192]{1,0:T(8,128)(2,1)} %refs_7_.3, ...), custom_call_target="tpu_custom_call" | custom-call | flops 1024 | bytes 1024 | tf_op jit(solution)/shard_map/heads_out/pallas_call | solution.py:662
  274.7 3.3 all-to-all-start
  278.5 10.6 %collective-permute-done.23.two_ref = s16[592,512]{1,0:T(8,128)(2,1)S(1)} collective-permute-done((s16[592,512]{1,0:T(8,128)(2,1)}, s16[592,512]{1,0:T(8,128)(2,1)S(1)}, u32[]{:S(2)}, u32[]{:S(2)}) %collective-permute-start.23) | collective-permute-done | bytes 606240 | tf_op jit(solution)/shard_map/ppermute | solution.py:792
  290.0 4.5 %pages.5 = bf16[4,576,128]{2,1,0:T(8,128)(2,1)} custom-call(s32[9]{0:T(128)} %fusion.3.table.refs_0_, s32[4]{0:T(128)} %copy-done.25, s32[4]{0:T(128)} %convert_element_type.92.has, f32[3,576,512]{2,1,0:T(8,128)} %get-tuple-element.32.refs_1_.own_ref, s16[592,512]{1,0:T(8,128)(2,1)} %copy-done.14, s16[592,512]{1,0:T(8,128)(2,1)} %copy-done.19, ...), custom_call_target="tpu_custom_call" | custom-call | flops 1024 | bytes 1024 | tf_op jit(solution)/shard_map/pages/pallas_call | solution.py:483
  294.4 3.5 %all-to-all-start.3 = ((bf16[4,576,128]{2,1,0:T(8,128)(2,1)}), bf16[4,576,128]{2,1,0:T(8,128)(2,1)S(1)}, u32[]{:S(2)}, u32[]{:S(2)}) async-start(bf16[4,576,128]{2,1,0:T(8,128)(2,1)} %pages.5), calls=%async_computation.3 | async-start | bytes 1179648 | tf_op jit(solution)/shard_map/all_to_all | solution.py:828
  298.8 4.5 %pages.4 = bf16[4,576,128]{2,1,0:T(8,128)(2,1)} custom-call(s32[9]{0:T(128)} %fusion.3.table.refs_0_, s32[4]{0:T(128)} %copy-done.25, s32[4]{0:T(128)} %convert_element_type.92.has, f32[3,576,512]{2,1,0:T(8,128)} %get-tuple-element.32.refs_1_.own_ref, s16[592,512]{1,0:T(8,128)(2,1)} %collective-permute-done.16.got_ref.one_ref, s16[592,512]{1,0:T(8,128)(2,1)} %copy-done.18, ...), custom_call_target="tpu_custom_call" | custom-call | flops 1024 | bytes 1024 | tf_op jit(solution)/shard_map/pages/pallas_call | solution.py:483
  303.3 4.1 %all-to-all-done.3 = bf16[4,576,128]{2,1,0:T(8,128)(2,1)S(1)} async-done(((bf16[4,576,128]{2,1,0:T(8,128)(2,1)}), bf16[4,576,128]{2,1,0:T(8,128)(2,1)S(1)}, u32[]{:S(2)}, u32[]{:S(2)}) %all-to-all-start.3) | async-done | bytes 589856 | tf_op jit(solution)/shard_map/all_to_all | solution.py:828
  307.5 3.5 %all-to-all-start.2 = ((bf16[4,576,128]{2,1,0:T(8,128)(2,1)}), bf16[4,576,128]{2,1,0:T(8,128)(2,1)S(1)}, u32[]{:S(2)}, u32[]{:S(2)}) async-start(bf16[4,576,128]{2,1,0:T(8,128)(2,1)} %pages.4), calls=%async_computation.2 | async-start | bytes 1179648 | tf_op jit(solution)/shard_map/all_to_all | solution.py:828
  310.9 4.6 %pages.3 = bf16[4,576,128]{2,1,0:T(8,128)(2,1)} custom-call(s32[9]{0:T(128)} %fusion.3.table.refs_0_, s32[4]{0:T(128)} %copy-done.25, s32[4]{0:T(128)} %convert_element_type.92.has, f32[3,576,512]{2,1,0:T(8,128)} %get-tuple-element.32.refs_1_.own_ref, s16[592,512]{1,0:T(8,128)(2,1)} %copy-done.12, s16[592,512]{1,0:T(8,128)(2,1)} %copy-done.15, ...), custom_call_target="tpu_custom_call" | custom-call | flops 1024 | bytes 1024 | tf_op jit(solution)/shard_map/pages/pallas_call | solution.py:483
  315.6 4.9 %all-to-all-done.2 = bf16[4,576,128]{2,1,0:T(8,128)(2,1)S(1)} async-done(((bf16[4,576,128]{2,1,0:T(8,128)(2,1)}), bf16[4,576,128]{2,1,0:T(8,128)(2,1)S(1)}, u32[]{:S(2)}, u32[]{:S(2)}) %all-to-all-start.2) | async-done | bytes 589856 | tf_op jit(solution)/shard_map/all_to_all | solution.py:828
  320.4 3.5 %all-to-all-start.1 = ((bf16[4,576,128]{2,1,0:T(8,128)(2,1)}), bf16[4,576,128]{2,1,0:T(8,128)(2,1)S(1)}, u32[]{:S(2)}, u32[]{:S(2)}) async-start(bf16[4,576,128]{2,1,0:T(8,128)(2,1)} %pages.3), calls=%async_computation.1 | async-start | bytes 1179648 | tf_op jit(solution)/shard_map/all_to_all | solution.py:828
  324.6 8.9 %all-to-all-done.1 = bf16[4,576,128]{2,1,0:T(8,128)(2,1)S(1)} async-done(((bf16[4,576,128]{2,1,0:T(8,128)(2,1)}), bf16[4,576,128]{2,1,0:T(8,128)(2,1)S(1)}, u32[]{:S(2)}, u32[]{:S(2)}) %all-to-all-start.1) | async-done | bytes 589856 | tf_op jit(solution)/shard_map/all_to_all | solution.py:828
  (137 shorter events, 53.1 us)
Async XLA Ops:
  7.2 36.5 %copy-start = (bf16[16,2,1536]{2,1,0:T(2,128)(2,1)S(1)}, bf16[16,2,1536]{2,1,0:T(2,128)(2,1)}, u32[]{:S(2)}) copy-start(bf16[16,2,1536]{2,1,0:T(2,128)(2,1)} %param.16) | copy-start | bytes 294916
  7.2 176.6 %all-gather.2.cloned.1.call-start = ((), (), s32[]{:S(2)}) async-start(), calls=%async_computation.4 | async-start | bytes 1843200 | tf_op jit(solution)/shard_map/all_gather | solution.py:767
  16.6 29.9 %collective-permute-start = (s16[2,592,384]{2,1,0:T(8,128)(2,1)}, s16[2,592,384]{2,1,0:T(8,128)(2,1)S(1)}, u32[]{:S(2)}, u32[]{:S(2)}) collective-permute-start(s16[2,592,384]{2,1,0:T(8,128)(2,1)} %get-tuple-element.22), channel_id=1, source_target_pairs={{0,4},{12,8},{1,5},{13,9},{2,6},{14,10},{3,7},{15,11},{16,20},{28,... | collective-permute-start | bytes 2727944 | tf_op jit(solution)/shard_map/ppermute | solution.py:730
  26.0 47.7 %collective-permute-start.2 = (s16[2,592,384]{2,1,0:T(8,128)(2,1)}, s16[2,592,384]{2,1,0:T(8,128)(2,1)S(1)}, u32[]{:S(2)}, u32[]{:S(2)}) collective-permute-start(s16[2,592,384]{2,1,0:T(8,128)(2,1)} %get-tuple-element.29), channel_id=1, source_target_pairs={{0,4},{12,8},{1,5},{13,9},{2,6},{14,10},{3,7},{15,11},{16,20},{28,... | collective-permute-start | bytes 2727944 | tf_op jit(solution)/shard_map/ppermute | solution.py:730
  66.8 3.2 copy-start.5
  68.1 5.7 %copy-start.3 = (f32[32,8,576]{2,0,1:T(8,128)}, f32[32,8,576]{2,0,1:T(8,128)S(1)}, u32[]{:S(2)}) copy-start(f32[32,8,576]{2,0,1:T(8,128)S(1)} %copy.24) | copy-start | bytes 1769476
  68.1 1.0 copy-start.10
  70.0 44.0 %collective-permute-start.6 = (s16[2,592,384]{2,1,0:T(8,128)(2,1)S(1)}, s16[2,592,384]{2,1,0:T(8,128)(2,1)}, u32[]{:S(2)}, u32[]{:S(2)}) collective-permute-start(s16[2,592,384]{2,1,0:T(8,128)(2,1)S(1)} %copy-done.5), channel_id=1, source_target_pairs={{4,8},{8,4},{5,9},{9,5},{6,10},{10,6},{7,11},{11,7},{20,24},{24,20... | collective-permute-start | bytes 2727944 | tf_op jit(solution)/shard_map/ppermute | solution.py:746
  72.4 50.4 %collective-permute-start.8 = (s16[2,592,384]{2,1,0:T(8,128)(2,1)}, s16[2,592,384]{2,1,0:T(8,128)(2,1)S(1)}, u32[]{:S(2)}, u32[]{:S(2)}) collective-permute-start(s16[2,592,384]{2,1,0:T(8,128)(2,1)} %get-tuple-element.30), channel_id=1, source_target_pairs={{0,4},{12,8},{1,5},{13,9},{2,6},{14,10},{3,7},{15,11},{16,20},{28,... | collective-permute-start | bytes 2727944 | tf_op jit(solution)/shard_map/ppermute | solution.py:730
  73.8 1.0 copy-start.6
  80.2 41.8 %copy-start.11 = (bf16[4,2,32,576]{3,2,1,0:T(8,128)(2,1)S(1)}, bf16[4,2,32,576]{3,2,1,0:T(8,128)(2,1)}, u32[]{:S(2)}) copy-start(bf16[4,2,32,576]{3,2,1,0:T(8,128)(2,1)} %copy-done.10) | copy-start | bytes 884740
  80.2 57.9 %collective-permute-start.3 = (s16[2,592,384]{2,1,0:T(8,128)(2,1)}, s16[2,592,384]{2,1,0:T(8,128)(2,1)S(1)}, u32[]{:S(2)}, u32[]{:S(2)}) collective-permute-start(s16[2,592,384]{2,1,0:T(8,128)(2,1)} %add_on.11), channel_id=1, source_target_pairs={{4,8},{8,4},{5,9},{9,5},{6,10},{10,6},{7,11},{11,7},{20,24},{24,20... | collective-permute-start | bytes 2727944 | tf_op jit(solution)/shard_map/ppermute | solution.py:746
  83.8 61.0 %collective-permute-start.1 = (s16[1,592,384]{2,1,0:T(8,128)(2,1)}, s16[1,592,384]{2,1,0:T(8,128)(2,1)S(1)}, u32[]{:S(2)}, u32[]{:S(2)}) collective-permute-start(s16[1,592,384]{2,1,0:T(8,128)(2,1)} %get-tuple-element.28), channel_id=1, source_target_pairs={{0,4},{12,8},{1,5},{13,9},{2,6},{14,10},{3,7},{15,11},{16,20},{28,... | collective-permute-start | bytes 1363976 | tf_op jit(solution)/shard_map/ppermute | solution.py:730
  119.8 47.1 %collective-permute-start.7 = (s16[2,592,384]{2,1,0:T(8,128)(2,1)}, s16[2,592,384]{2,1,0:T(8,128)(2,1)}, u32[]{:S(2)}, u32[]{:S(2)}) collective-permute-start(s16[2,592,384]{2,1,0:T(8,128)(2,1)} %add_on.14.sent_ref.refs_0_), channel_id=1, source_target_pairs={{8,12},{4,0},{9,13},{5,1},{10,14},{6,2},{11,15},{7,3},{24,28},{20,... | collective-permute-start | bytes 2727944 | tf_op jit(solution)/shard_map/ppermute | solution.py:752
  122.8 0.9 copy-start.7
  129.3 60.0 %collective-permute-start.9 = (s16[2,592,384]{2,1,0:T(8,128)(2,1)}, s16[2,592,384]{2,1,0:T(8,128)(2,1)}, u32[]{:S(2)}, u32[]{:S(2)}) collective-permute-start(s16[2,592,384]{2,1,0:T(8,128)(2,1)} %add_on.15), channel_id=1, source_target_pairs={{4,8},{8,4},{5,9},{9,5},{6,10},{10,6},{7,11},{11,7},{20,24},{24,20... | collective-permute-start | bytes 2727944 | tf_op jit(solution)/shard_map/ppermute | solution.py:746
  149.4 10.4 %copy-start.2 = (s16[2,592,384]{2,1,0:T(8,128)(2,1)S(1)}, s16[2,592,384]{2,1,0:T(8,128)(2,1)}, u32[]{:S(2)}) copy-start(s16[2,592,384]{2,1,0:T(8,128)(2,1)} %add_on.12.refs_0_.refs_3_.sent_ref) | copy-start | bytes 2727940
  149.4 15.1 %copy-start.26 = (s16[1,592,384]{2,1,0:T(8,128)(2,1)S(1)}, s16[1,592,384]{2,1,0:T(8,128)(2,1)}, u32[]{:S(2)}) copy-start(s16[1,592,384]{2,1,0:T(8,128)(2,1)} %get-tuple-element.31) | copy-start | bytes 1363972
  149.4 19.8 %copy-start.24 = (f32[512]{0:T(512)S(1)}, f32[512]{0:T(512)}, u32[]{:S(2)}) copy-start(f32[512]{0:T(512)} %param.15) | copy-start | bytes 6148
  158.5 38.1 %collective-permute-start.13 = (s16[592,512]{1,0:T(8,128)(2,1)}, s16[592,512]{1,0:T(8,128)(2,1)S(1)}, u32[]{:S(2)}, u32[]{:S(2)}) collective-permute-start(s16[592,512]{1,0:T(8,128)(2,1)} %get-tuple-element.33), channel_id=1, source_target_pairs={{0,4},{12,8},{1,5},{13,9},{2,6},{14,10},{3,7},{15,11},{16,20},{28,... | collective-permute-start | bytes 1818632 | tf_op jit(solution)/shard_map/ppermute | solution.py:777
  159.8 46.1 %collective-permute-start.5 = (s16[2,592,384]{2,1,0:T(8,128)(2,1)S(1)}, s16[2,592,384]{2,1,0:T(8,128)(2,1)S(1)}, u32[]{:S(2)}, u32[]{:S(2)}) collective-permute-start(s16[2,592,384]{2,1,0:T(8,128)(2,1)S(1)} %copy-done.2), channel_id=1, source_target_pairs={{8,12},{4,0},{9,13},{5,1},{10,14},{6,2},{11,15},{7,3},{24,28},{20,... | collective-permute-start | bytes 2727944 | tf_op jit(solution)/shard_map/ppermute | solution.py:752
  164.5 19.3 %collective-permute-start.11 = (s16[1,592,384]{2,1,0:T(8,128)(2,1)S(1)}, s16[1,592,384]{2,1,0:T(8,128)(2,1)S(1)}, u32[]{:S(2)}, u32[]{:S(2)}) collective-permute-start(s16[1,592,384]{2,1,0:T(8,128)(2,1)S(1)} %copy-done.26), channel_id=1, source_target_pairs={{0,4},{12,8},{1,5},{13,9},{2,6},{14,10},{3,7},{15,11},{16,20},{28,... | collective-permute-start | bytes 1363976 | tf_op jit(solution)/shard_map/ppermute | solution.py:730
  166.9 49.4 %collective-permute-start.4 = (s16[1,592,384]{2,1,0:T(8,128)(2,1)}, s16[1,592,384]{2,1,0:T(8,128)(2,1)}, u32[]{:S(2)}, u32[]{:S(2)}) collective-permute-start(s16[1,592,384]{2,1,0:T(8,128)(2,1)} %add_on.13.refs_0_), channel_id=1, source_target_pairs={{4,8},{8,4},{5,9},{9,5},{6,10},{10,6},{7,11},{11,7},{20,24},{24,20... | collective-permute-start | bytes 1363976 | tf_op jit(solution)/shard_map/ppermute | solution.py:778
  188.0 33.5 %collective-permute-start.12 = (s16[1,592,384]{2,1,0:T(8,128)(2,1)}, s16[1,592,384]{2,1,0:T(8,128)(2,1)}, u32[]{:S(2)}, u32[]{:S(2)}) collective-permute-start(s16[1,592,384]{2,1,0:T(8,128)(2,1)} %add_on.18), channel_id=1, source_target_pairs={{4,8},{5,9},{6,10},{7,11},{20,24},{21,25},{22,26},{23,27}} | collective-permute-start | bytes 1363976 | tf_op jit(solution)/shard_map/ppermute | solution.py:780
  189.3 38.3 %collective-permute-start.16 = (s16[592,512]{1,0:T(8,128)(2,1)}, s16[592,512]{1,0:T(8,128)(2,1)}, u32[]{:S(2)}, u32[]{:S(2)}) collective-permute-start(s16[592,512]{1,0:T(8,128)(2,1)} %get-tuple-element.34), channel_id=1, source_target_pairs={{0,4},{12,8},{1,5},{13,9},{2,6},{14,10},{3,7},{15,11},{16,20},{28,... | collective-permute-start | bytes 1818632 | tf_op jit(solution)/shard_map/ppermute | solution.py:777
  196.6 14.2 %copy-start.27 = (s32[16]{0:T(128)S(1)}, s32[16]{0:T(128)}, u32[]{:S(2)}) copy-start(s32[16]{0:T(128)} %param.21) | copy-start | bytes 196
  196.6 5.0 %copy-start.12 = (s16[592,512]{1,0:T(8,128)(2,1)}, s16[592,512]{1,0:T(8,128)(2,1)S(1)}, u32[]{:S(2)}) copy-start(s16[592,512]{1,0:T(8,128)(2,1)S(1)} %collective-permute-done.13.got_ref.one_ref) | copy-start | bytes 1818628
  196.6 37.4 %collective-permute-start.15 = (s16[2,592,384]{2,1,0:T(8,128)(2,1)}, s16[2,592,384]{2,1,0:T(8,128)(2,1)S(1)}, u32[]{:S(2)}, u32[]{:S(2)}) collective-permute-start(s16[2,592,384]{2,1,0:T(8,128)(2,1)} %add_on.16.refs_3_.sent_ref), channel_id=1, source_target_pairs={{8,12},{4,0},{9,13},{5,1},{10,14},{6,2},{11,15},{7,3},{24,28},{20,... | collective-permute-start | bytes 2727944 | tf_op jit(solution)/shard_map/ppermute | solution.py:752
  205.9 5.9 %copy-start.8 = (s16[2,592,384]{2,1,0:T(8,128)(2,1)}, s16[2,592,384]{2,1,0:T(8,128)(2,1)S(1)}, u32[]{:S(2)}) copy-start(s16[2,592,384]{2,1,0:T(8,128)(2,1)S(1)} %collective-permute-done.5.got_ref.mid_ref) | copy-start | bytes 2727940
  205.9 39.6 %collective-permute-start.17 = (s16[592,512]{1,0:T(8,128)(2,1)}, s16[592,512]{1,0:T(8,128)(2,1)S(1)}, u32[]{:S(2)}, u32[]{:S(2)}) collective-permute-start(s16[592,512]{1,0:T(8,128)(2,1)} %add_last.3.refs_1_), channel_id=1, source_target_pairs={{8,4},{9,5},{10,6},{11,7},{24,20},{25,21},{26,22},{27,23}} | collective-permute-start | bytes 1818632 | tf_op jit(solution)/shard_map/ppermute | solution.py:792
  220.0 8.9 %copy-start.28 = (s32[16]{0:T(128)S(1)}, s32[16]{0:T(128)}, u32[]{:S(2)}) copy-start(s32[16]{0:T(128)} %param.19) | copy-start | bytes 196
  220.0 19.4 %collective-permute-start.10 = (s16[1,592,384]{2,1,0:T(8,128)(2,1)}, s16[1,592,384]{2,1,0:T(8,128)(2,1)S(1)}, u32[]{:S(2)}, u32[]{:S(2)}) collective-permute-start(s16[1,592,384]{2,1,0:T(8,128)(2,1)} %add_on.17), channel_id=1, source_target_pairs={{8,12},{4,0},{9,13},{5,1},{10,14},{6,2},{11,15},{7,3},{24,28},{20,... | collective-permute-start | bytes 1363976 | tf_op jit(solution)/shard_map/ppermute | solution.py:784
  225.4 14.0 %collective-permute-start.14 = (s16[1,592,384]{2,1,0:T(8,128)(2,1)}, s16[1,592,384]{2,1,0:T(8,128)(2,1)S(1)}, u32[]{:S(2)}, u32[]{:S(2)}) collective-permute-start(s16[1,592,384]{2,1,0:T(8,128)(2,1)} %add_on.19.sent_ref), channel_id=1, source_target_pairs={{8,12},{9,13},{10,14},{11,15},{24,28},{25,29},{26,30},{27,31}} | collective-permute-start | bytes 1363976 | tf_op jit(solution)/shard_map/ppermute | solution.py:787
  227.6 28.0 %collective-permute-start.22 = (s16[592,512]{1,0:T(8,128)(2,1)}, s16[592,512]{1,0:T(8,128)(2,1)S(1)}, u32[]{:S(2)}, u32[]{:S(2)}) collective-permute-start(s16[592,512]{1,0:T(8,128)(2,1)} %get-tuple-element.39), channel_id=1, source_target_pairs={{0,4},{12,8},{1,5},{13,9},{2,6},{14,10},{3,7},{15,11},{16,20},{28,... | collective-permute-start | bytes 1818632 | tf_op jit(solution)/shard_map/ppermute | solution.py:777
  229.2 24.9 %copy-start.25 = (s32[4]{0:T(128)}, s32[4]{0:T(128)S(1)}, u32[]{:S(2)}) copy-start(s32[4]{0:T(128)S(1)} %select_reduce_fusion.slots) | copy-start | bytes 52
  234.1 0.9 copy-start.9
  246.3 7.9 %copy-start.13 = (s16[592,512]{1,0:T(8,128)(2,1)S(1)}, s16[592,512]{1,0:T(8,128)(2,1)}, u32[]{:S(2)}) copy-start(s16[592,512]{1,0:T(8,128)(2,1)} %add_last.4.refs_3_) | copy-start | bytes 1818628
  251.2 14.5 %copy-start.23 = (bf16[4,64,512]{2,1,0:T(8,128)(2,1)S(1)}, bf16[4,64,512]{2,1,0:T(8,128)(2,1)}, u32[]{:S(2)}) copy-start(bf16[4,64,512]{2,1,0:T(8,128)(2,1)} %get-tuple-element.35) | copy-start | bytes 786436
  251.2 14.4 %collective-permute-start.20 = (bf16[4,64,512]{2,1,0:T(8,128)(2,1)}, bf16[4,64,512]{2,1,0:T(8,128)(2,1)S(1)}, u32[]{:S(2)}, u32[]{:S(2)}) collective-permute-start(bf16[4,64,512]{2,1,0:T(8,128)(2,1)} %get-tuple-element.38), channel_id=1, source_target_pairs={{12,8},{13,9},{14,10},{15,11},{28,24},{29,25},{30,26},{31,27}} | collective-permute-start | bytes 786440 | tf_op jit(solution)/shard_map/ppermute | solution.py:797
  252.7 13.0 %collective-permute-start.18 = (bf16[4,64,512]{2,1,0:T(8,128)(2,1)}, bf16[4,64,512]{2,1,0:T(8,128)(2,1)S(1)}, u32[]{:S(2)}, u32[]{:S(2)}) collective-permute-start(bf16[4,64,512]{2,1,0:T(8,128)(2,1)} %get-tuple-element.36), channel_id=1, source_target_pairs={{12,0},{13,1},{14,2},{15,3},{28,16},{29,17},{30,18},{31,19}} | collective-permute-start | bytes 786440 | tf_op jit(solution)/shard_map/ppermute | solution.py:797
  253.4 12.3 %collective-permute-start.19 = (bf16[4,64,512]{2,1,0:T(8,128)(2,1)}, bf16[4,64,512]{2,1,0:T(8,128)(2,1)S(1)}, u32[]{:S(2)}, u32[]{:S(2)}) collective-permute-start(bf16[4,64,512]{2,1,0:T(8,128)(2,1)} %get-tuple-element.37), channel_id=1, source_target_pairs={{12,4},{13,5},{14,6},{15,7},{28,20},{29,21},{30,22},{31,23}} | collective-permute-start | bytes 786440 | tf_op jit(solution)/shard_map/ppermute | solution.py:797
  254.3 43.6 %collective-permute-start.21 = (s16[592,512]{1,0:T(8,128)(2,1)S(1)}, s16[592,512]{1,0:T(8,128)(2,1)S(1)}, u32[]{:S(2)}, u32[]{:S(2)}) collective-permute-start(s16[592,512]{1,0:T(8,128)(2,1)S(1)} %copy-done.13), channel_id=1, source_target_pairs={{8,4},{9,5},{10,6},{11,7},{24,20},{25,21},{26,22},{27,23}} | collective-permute-start | bytes 1818632 | tf_op jit(solution)/shard_map/ppermute | solution.py:792
  260.8 28.2 %collective-permute-start.23 = (s16[592,512]{1,0:T(8,128)(2,1)}, s16[592,512]{1,0:T(8,128)(2,1)S(1)}, u32[]{:S(2)}, u32[]{:S(2)}) collective-permute-start(s16[592,512]{1,0:T(8,128)(2,1)} %add_last.5), channel_id=1, source_target_pairs={{8,4},{9,5},{10,6},{11,7},{24,20},{25,21},{26,22},{27,23}} | collective-permute-start | bytes 1818632 | tf_op jit(solution)/shard_map/ppermute | solution.py:792
  274.7 19.8 %all-to-all-start = ((bf16[4,2,4096]{2,1,0:T(2,128)(2,1)}), bf16[4,2,4096]{2,1,0:T(2,128)(2,1)S(1)}, u32[]{:S(2)}, u32[]{:S(2)}) async-start(bf16[4,2,4096]{2,1,0:T(2,128)(2,1)} %select_convert_fusion), calls=%async_computation | async-start | bytes 131072 | tf_op jit(solution)/shard_map/all_to_all | solution.py:811
  294.4 13.0 %all-to-all-start.3 = ((bf16[4,576,128]{2,1,0:T(8,128)(2,1)}), bf16[4,576,128]{2,1,0:T(8,128)(2,1)S(1)}, u32[]{:S(2)}, u32[]{:S(2)}) async-start(bf16[4,576,128]{2,1,0:T(8,128)(2,1)} %pages.5), calls=%async_computation.3 | async-start | bytes 1179648 | tf_op jit(solution)/shard_map/all_to_all | solution.py:828
  307.5 13.0 %all-to-all-start.2 = ((bf16[4,576,128]{2,1,0:T(8,128)(2,1)}), bf16[4,576,128]{2,1,0:T(8,128)(2,1)S(1)}, u32[]{:S(2)}, u32[]{:S(2)}) async-start(bf16[4,576,128]{2,1,0:T(8,128)(2,1)} %pages.4), calls=%async_computation.2 | async-start | bytes 1179648 | tf_op jit(solution)/shard_map/all_to_all | solution.py:828
  310.9 24.0 %copy-start.1 = (bf16[16,2,1536]{2,1,0:T(2,128)(2,1)S(1)}, bf16[16,2,1536]{2,1,0:T(2,128)(2,1)}, u32[]{:S(2)}) copy-start(bf16[16,2,1536]{2,1,0:T(2,128)(2,1)} %param.16) | copy-start | bytes 294916
  320.4 13.0 %all-to-all-start.1 = ((bf16[4,576,128]{2,1,0:T(8,128)(2,1)}), bf16[4,576,128]{2,1,0:T(8,128)(2,1)S(1)}, u32[]{:S(2)}, u32[]{:S(2)}) async-start(bf16[4,576,128]{2,1,0:T(8,128)(2,1)} %pages.3), calls=%async_computation.1 | async-start | bytes 1179648 | tf_op jit(solution)/shard_map/all_to_all | solution.py:828
  (10 other events, 8.4 us)
Sparse Core Ops, SparseCore 0:
  70.1 59.5 all-gather.1
where the time goes:
time: 347 us; the launch traced here: 342 us
  Pallas kernels  158 us (46%)
  waiting for transfers between devices  74.9 us (22%)
  starting transfers between devices  60.8 us (18%)
  local copies, waits for them, and re-layouts  24.9 us (7%)
  between operations  14.6 us (4%)
  other arithmetic  8.3 us (2%)
    pallas_call x10, Pallas kernels, add_on(): pl.pallas_call(functools.partial(add_kernel, side_at), grid_spec=pltpu.Pr...  48.9 us
    ppermute x3, waiting for transfers between devices, first_hop(): across[r] = lax.ppermute(block, 'tp', [(1, 2), (2, 1)])  35.7 us
    pallas_call x4, Pallas kernels, project(): pl.pallas_call(project_pair_kernel if pair else project_kernel, grid_spec...  32.6 us
    pallas_call x4, Pallas kernels, finish(): pl.pallas_call(finish_kernel, grid_spec=pltpu.PrefetchScalarGridSpec(num_...  18 us
    all_to_all x3, waiting for transfers between devices, local_line(): lax.all_to_all(page, 'pd', split_axis=0, concat_axis=0, tiled=True)  17.9 us
    pallas_call x1, Pallas kernels, queries(): pl.pallas_call(body, grid=(heads // step,), in_specs=[pl.BlockSpec((rows,...  13.8 us
    pallas_call x3, Pallas kernels, pages_of(): pl.pallas_call(page_kernel, grid_spec=pltpu.PrefetchScalarGridSpec(num_sc...  13.6 us
    pallas_call x3, Pallas kernels, add_last(): pl.pallas_call(add_last_kernel, grid_spec=pltpu.PrefetchScalarGridSpec(nu...  12.9 us
  transfers between devices with their start and end apart: 29, of which 8 were waited for; matrix products, arithmetic and copies ran while one was open for 6% of the time, Pallas kernels for 44%

commit v1 on v0

--- a/solution.py
+++ b/solution.py
@@ -239,270 +239,188 @@
     )
 
 
-def project_kernel(table, hid_ref, down_ref, *refs):
-    *_, sum_ref, one_ref, two_ref = refs
-    step = pl.program_id(0)
+def far(z, i):
+    return jnp.where(z < 2, 3 - i, i)
+
+
+def near(z, i):
+    return jnp.where(z < 2, i, 3 - i)
+
+
+def outer_rank(z):
+    return (z == 0) | (z == 3)
+
+
+def project_far_kernel(rank, hid_ref, down_ref, *refs):
+    sum_ref, code_ref = refs[-2:]
     total = lax.dot_general(down_ref[...], hid_ref[0], NT, preferred_element_type=F32)
-    sum_ref[0] = total
-    for i, ref in enumerate((one_ref, two_ref)):
-
-        @pl.when((step == i) & (table[6] == 1))
-        def _(ref=ref):
-            for first in range(0, SHARE, UNIT):
-                lanes = slice(first, first + UNIT)
-                ref[0, :, lanes] = encode(total[:, lanes])
-
-
-def project_pair_kernel(table, hid_ref, down_ref, *refs):
-    *_, sum_ref, code_ref = refs
-    step = pl.program_id(0)
-    total = lax.dot_general(down_ref[...], hid_ref[0], NT, preferred_element_type=F32)
-    sum_ref[0] = total
-
-    @pl.when((step < 2) & (table[6] == 1))
+    for u in range(UNITS):
+        sum_ref[0, u] = total[:, u * UNIT : (u + 1) * UNIT]
+
+    @pl.when(outer_rank(rank[0]))
     def _():
-        for first in range(0, SHARE, UNIT):
-            lanes = slice(first, first + UNIT)
-            code_ref[0, :, lanes] = encode(total[:, lanes])
-
-
-def project(table, hidden, down_t, request, pair, after):
+        for u in range(UNITS):
+            code_ref[0, u] = encode(total[:, u * UNIT : (u + 1) * UNIT])
+
+
+def project_far(rank, hidden, down_t, request, after):
     depth = hidden.shape[-1]
-    if pair:
-        codes = [(2, lambda i, table: (jnp.minimum(i, 1), 0, 0))]
-    else:
-        codes = [(1, lambda i, table: (0, 0, 0))] * 2
     return pl.pallas_call(
-        project_pair_kernel if pair else project_kernel,
+        project_far_kernel,
         grid_spec=pltpu.PrefetchScalarGridSpec(
             num_scalar_prefetch=1,
-            grid=(3,),
+            grid=(2,),
             in_specs=[
-                pl.BlockSpec((1, SHARE, depth), lambda i, table: (request, table[i], 0)),
-                pl.BlockSpec((WIDTH, depth), lambda i, table: (0, 0)),
+                pl.BlockSpec((1, SHARE, depth), lambda i, rank: (request, far(rank[0], i), 0)),
+                pl.BlockSpec((WIDTH, depth), lambda i, rank: (0, 0)),
                 *([ANY] * len(after)),
             ],
             out_specs=[
-                pl.BlockSpec((1, WIDTH, SHARE), lambda i, table: (table[3 + i], 0, 0)),
-                *[pl.BlockSpec((1, CODED, SHARE), place) for _, place in codes],
+                pl.BlockSpec((1, UNITS, WIDTH, UNIT), lambda i, rank: (i, 0, 0, 0)),
+                pl.BlockSpec((1, UNITS, CODED, UNIT), lambda i, rank: (i, 0, 0, 0)),
             ],
         ),
         out_shape=[
-            jax.ShapeDtypeStruct((3, WIDTH, SHARE), F32),
-            *[jax.ShapeDtypeStruct((count, CODED, SHARE), I16) for count, _ in codes],
+            jax.ShapeDtypeStruct((2, UNITS, WIDTH, UNIT), F32),
+            jax.ShapeDtypeStruct((2, UNITS, CODED, UNIT), I16),
         ],
         compiler_params=ROOM,
         cost_estimate=COST,
-        name="project",
-    )(table, hidden, down_t, *after)
-
-
-def project_last_kernel(table, hid_ref, down_ref, *refs):
-    sum_ref, *code_refs = refs[-1 - UNITS :]
-    step = pl.program_id(0)
+        name="project_far",
+    )(rank, hidden, down_t, *after)
+
+
+def project_near_kernel(rank, hid_ref, down_ref, *refs):
+    sum_ref, *code_refs = refs[-3:]
+    unit = pl.program_id(0)
     rows = hid_ref[...].reshape(LANES, hid_ref.shape[-1])
     total = lax.dot_general(down_ref[...], rows, NT, preferred_element_type=F32)
-    sum_ref[0] = total
-    for u, ref in enumerate(code_refs):
-
-        @pl.when((step == u) & (table[6] == 1))
+    for r in range(RP):
+        sum_ref[0, 0, r] = total[:, r * UNIT : (r + 1) * UNIT]
+    coded = outer_rank(rank[0]) & (pl.program_id(1) == 1)
+    for mine, ref in zip((unit == 0, unit > 0), code_refs):
+
+        @pl.when(coded & mine)
         def _(ref=ref):
-            for first in range(0, LANES, UNIT):
-                lanes = slice(first, first + UNIT)
-                ref[:, lanes] = encode(total[:, lanes])
-
-
-def project_last(table, hidden, down_t, after):
+            for r in range(RP):
+                ref[0, r] = encode(total[:, r * UNIT : (r + 1) * UNIT])
+
+
+def project_near(rank, hidden, down_t, after):
     depth = hidden.shape[-1]
     return pl.pallas_call(
-        project_last_kernel,
+        project_near_kernel,
         grid_spec=pltpu.PrefetchScalarGridSpec(
             num_scalar_prefetch=1,
-            grid=(UNITS,),
+            grid=(UNITS, 2),
             in_specs=[
-                pl.BlockSpec((RP, UNIT, depth), lambda i, table: (0, UNITS + i, 0)),
-                pl.BlockSpec((WIDTH, depth), lambda i, table: (0, 0)),
+                pl.BlockSpec(
+                    (RP, UNIT, depth), lambda u, i, rank: (0, near(rank[0], i) * UNITS + u, 0)
+                ),
+                pl.BlockSpec((WIDTH, depth), lambda u, i, rank: (0, 0)),
                 *([ANY] * len(after)),
             ],
             out_specs=[
-                pl.BlockSpec((1, WIDTH, LANES), lambda i, table: (i, 0, 0)),
-                *([pl.BlockSpec((CODED, LANES), lambda i, table: (0, 0))] * UNITS),
+                pl.BlockSpec((1, 1, RP, WIDTH, UNIT), lambda u, i, rank: (u, i, 0, 0, 0)),
+                pl.BlockSpec((1, RP, CODED, UNIT), lambda u, i, rank: (0, 0, 0, 0)),
+                pl.BlockSpec(
+                    (1, RP, CODED, UNIT), lambda u, i, rank: (jnp.maximum(u, 1) - 1, 0, 0, 0)
+                ),
             ],
         ),
         out_shape=[
-            jax.ShapeDtypeStruct((UNITS, WIDTH, LANES), F32),
-            *([jax.ShapeDtypeStruct((CODED, LANES), I16)] * UNITS),
+            jax.ShapeDtypeStruct((UNITS, 2, RP, WIDTH, UNIT), F32),
+            jax.ShapeDtypeStruct((1, RP, CODED, UNIT), I16),
+            jax.ShapeDtypeStruct((UNITS - 1, RP, CODED, UNIT), I16),
         ],
         compiler_params=ROOM,
         cost_estimate=COST,
-        name="project_last",
-    )(table, hidden, down_t, *after)
-
-
-def add_kernel(side_at, table, own_ref, got_ref, *refs):
-    out_ref = refs[-1]
-    step = pl.program_id(0)
-    for i in range(2):
-
-        @pl.when((step == i) & (table[2] > i))
-        def _(i=i):
-            total = own_ref[0] + decode(got_ref[0])
-            if i == side_at:
-                total = total + decode(refs[0][0])
-            out_ref[0] = encode(total)
-
-
-def add_on(table, sums, got, side=None, side_at=None, after=()):
-    count = got.shape[0]
-    block = lambda i, j, table: (i, 0, j)
-    extra = []
-    if side is not None:
-        last = side.shape[0] - 1
-        extra = [pl.BlockSpec((1, CODED, UNIT), lambda i, j, table: (last, 0, j))]
+        name="project_near",
+    )(rank, hidden, down_t, *after)
+
+
+def add_kernel(rank, own_ref, got_ref, *refs):
+    @pl.when(~outer_rank(rank[0]))
+    def _():
+        for u in range(UNITS):
+            refs[-1][0, u] = encode(own_ref[u] + decode(got_ref[0, u]))
+
+
+def add_on(rank, own, got, request=None, after=()):
+    chunk = lambda i, rank: (i, 0, 0, 0)
+    if request is None:
+        own_spec = pl.BlockSpec((None, UNITS, WIDTH, UNIT), chunk)
+    else:
+        own_spec = pl.BlockSpec(
+            (UNITS, None, None, WIDTH, UNIT), lambda i, rank: (0, i, request, 0, 0)
+        )
     return pl.pallas_call(
-        functools.partial(add_kernel, side_at),
+        add_kernel,
         grid_spec=pltpu.PrefetchScalarGridSpec(
             num_scalar_prefetch=1,
-            grid=(count, UNITS),
+            grid=(2,),
             in_specs=[
-                pl.BlockSpec((1, WIDTH, UNIT), lambda i, j, table: (table[i], 0, j)),
-                pl.BlockSpec((1, CODED, UNIT), block),
-                *extra,
+                own_spec,
+                pl.BlockSpec((1, UNITS, CODED, UNIT), chunk),
                 *([ANY] * len(after)),
             ],
-            out_specs=pl.BlockSpec((1, CODED, UNIT), block),
+            out_specs=pl.BlockSpec((1, UNITS, CODED, UNIT), chunk),
         ),
-        out_shape=jax.ShapeDtypeStruct((count, CODED, SHARE), I16),
+        out_shape=jax.ShapeDtypeStruct((2, UNITS, CODED, UNIT), I16),
         compiler_params=ROOM,
         cost_estimate=COST,
         name="add_on",
-    )(table, sums, got, *([] if side is None else [side]), *after)
-
-
-def add_last_kernel(table, own_ref, got_ref, out_ref):
-    @pl.when(table[7] == 2)
-    def _():
-        out_ref[...] = encode(own_ref[0] + decode(got_ref[...]))
-
-
-def add_last(table, sums, got, unit):
-    return pl.pallas_call(
-        add_last_kernel,
-        grid_spec=pltpu.PrefetchScalarGridSpec(
-            num_scalar_prefetch=1,
-            grid=(RP,),
-            in_specs=[
-                pl.BlockSpec((1, WIDTH, UNIT), lambda i, table: (unit, 0, i)),
-                pl.BlockSpec((CODED, UNIT), lambda i, table: (0, i)),
-            ],
-            out_specs=pl.BlockSpec((CODED, UNIT), lambda i, table: (0, i)),
-        ),
-        out_shape=jax.ShapeDtypeStruct((CODED, LANES), I16),
-        compiler_params=ROOM,
-        cost_estimate=COST,
-        name="add_last",
-    )(table, sums, got)
-
-
-def finish_kernel(table, own_ref, got_ref, mid_ref, sent_ref, gain_ref, cos_ref, sin_ref, *refs):
-    midcos_ref, midsin_ref, *_, out_ref = refs
-    z = table[7]
-
-    def write(place, comp, cosine, sine):
-        rows = key_rows(comp, gain_ref[...], cosine[...], sine[...])
-        out_ref[0, place] = rows.astype(BF)
-
-    @pl.when((z == 0) | (z == 3))
-    def _():
-        write(0, own_ref[0] + decode(got_ref[0]), cos_ref, sin_ref)
-
-    @pl.when(z == 3)
-    def _():
-        write(1, decode(mid_ref[0]), midcos_ref, midsin_ref)
-
-    @pl.when(z == 2)
-    def _():
-        write(0, decode(sent_ref[0]), midcos_ref, midsin_ref)
-
-
-def finish(table, sums, got, mid, sent, gain, tables, held, request, after=()):
-    lane = pl.BlockSpec((HALF, UNIT), lambda j, table: (0, j))
-    first = pl.BlockSpec((1, CODED, UNIT), lambda j, table: (0, 0, j))
-    last = mid.shape[0] - 1
-    second = pl.BlockSpec((1, CODED, UNIT), lambda j, table: (last, 0, j))
-    return pl.pallas_call(
-        finish_kernel,
-        grid_spec=pltpu.PrefetchScalarGridSpec(
-            num_scalar_prefetch=1,
-            grid=(UNITS,),
-            in_specs=[
-                pl.BlockSpec((1, WIDTH, UNIT), lambda j, table: (table[8], 0, j)),
-                first,
-                second,
-                second,
-                pl.BlockSpec((KVL, UNIT), lambda j, table: (0, 0)),
-                lane,
-                lane,
-                lane,
-                lane,
-                ANY,
-                *([ANY] * len(after)),
-            ],
-            out_specs=pl.BlockSpec((1, 2, WIDTH, UNIT), lambda j, table: (request, 0, 0, j)),
-        ),
-        out_shape=jax.ShapeDtypeStruct(held.shape, BF),
-        input_output_aliases={10: 0},
-        compiler_params=ROOM,
-        cost_estimate=COST,
-        name="finish",
-    )(table, sums, got, mid, sent, gain, *tables, held, *after)
-
-
-def page_kernel(table, slots, has, own_ref, one_ref, two_ref, keys_ref, gain_ref, cos_ref, sin_ref, out_ref):
-    slot = pl.program_id(0)
-
-    @pl.when(has[slot] == 0)
-    def _():
-        out_ref[...] = jnp.zeros_like(out_ref)
-
-    @pl.when((has[slot] > 0) & (table[7] == 1))
-    def _():
-        comp = own_ref[0] + decode(one_ref[...]) + decode(two_ref[...])
-        rows = key_rows(comp, gain_ref[...], cos_ref[...], sin_ref[...])
-        out_ref[0] = rows.astype(BF)
-
-    @pl.when((has[slot] > 0) & (table[7] != 1))
-    def _():
-        out_ref[0] = keys_ref[0, 0]
-
-
-def pages_of(table, slots, has, sums, one, two, keys, gain, cosine, sine, unit):
-    count = slots.shape[0]
-    part = pl.BlockSpec((CODED, UNIT), lambda i, table, slots, has: (0, slots[i]))
-    lane = pl.BlockSpec((HALF, UNIT), lambda i, *_: (0, unit))
+    )(rank, own, got, *after)
+
+
+def page_kernel(rank, slot, own_ref, *refs):
+    got_refs, sent_refs, refs = refs[:RP], refs[RP : 2 * RP], refs[2 * RP :]
+    side_ref, gain_ref, cos_ref, sin_ref = refs[:4]
+    out_ref = refs[-1]
+    request = pl.program_id(0)
+
+    def write(comp):
+        out_ref[0] = key_rows(comp, gain_ref[...], cos_ref[0], sin_ref[0]).astype(BF)
+
+    for r in range(RP):
+
+        @pl.when((request == r) & outer_rank(rank[0]))
+        def _(r=r):
+            write(own_ref[...] + decode(got_refs[r][0, 0]))
+
+        @pl.when((request == r) & ~outer_rank(rank[0]))
+        def _(r=r):
+            write(decode(sent_refs[r][0, 0]) + decode(side_ref[...]))
+
+
+def pages_of(rank, slot, own, got, sent, side, place, gain, cosine, sine, count, unit):
+    first = pl.BlockSpec((1, 1, CODED, UNIT), lambda i, *_: (0, unit, 0, 0))
+    second = pl.BlockSpec((1, 1, CODED, UNIT), lambda i, *_: (1, unit, 0, 0))
+    table = pl.BlockSpec((1, HALF, UNIT), lambda i, *_: (unit, 0, 0))
+    base = [jnp.zeros((count, WIDTH, UNIT), BF)] if count > RP else []
     return pl.pallas_call(
         page_kernel,
         grid_spec=pltpu.PrefetchScalarGridSpec(
-            num_scalar_prefetch=3,
-            grid=(count,),
+            num_scalar_prefetch=2,
+            grid=(RP,),
             in_specs=[
-                pl.BlockSpec((1, WIDTH, UNIT), lambda i, table, slots, has: (unit, 0, slots[i])),
-                part,
-                part,
-                pl.BlockSpec(
-                    (1, 1, WIDTH, UNIT), lambda i, table, slots, has: (slots[i], 0, 0, unit)
-                ),
+                pl.BlockSpec((None, None, None, WIDTH, UNIT), lambda i, *_: (unit, 0, i, 0, 0)),
+                *([first] * RP),
+                *([second] * RP),
+                pl.BlockSpec((None, None, CODED, UNIT), lambda i, *_: (place, i, 0, 0)),
                 pl.BlockSpec((KVL, UNIT), lambda i, *_: (0, 0)),
-                lane,
-                lane,
+                table,
+                table,
+                *([ANY] * len(base)),
             ],
-            out_specs=pl.BlockSpec((1, WIDTH, UNIT), lambda i, *_: (i, 0, 0)),
+            out_specs=pl.BlockSpec((1, WIDTH, UNIT), lambda i, rank, slot: (slot[i], 0, 0)),
         ),
         out_shape=jax.ShapeDtypeStruct((count, WIDTH, UNIT), BF),
+        input_output_aliases={7 + 2 * RP: 0} if base else {},
         compiler_params=ROOM,
         cost_estimate=COST,
         name="pages",
-    )(table, slots, has, sums, one, two, keys, gain, cosine, sine)
+    )(rank, slot, own, *got, *sent, side, gain, cosine, sine, *base)
 
 
 def query_kernel(lat_ref, up_ref, draft_ref, down_ref, *refs):
@@ -567,11 +485,28 @@
     )(latents, q_up, draft, down_t, *([kv_up] * step), cosine, sine, after)
 
 
-def attend_kernel(table, q_ref, draft_ref, keys_ref, valid_ref, gain_ref, cos_ref, sin_ref, *out_refs):
+def attend_kernel(rank, q_ref, draft_ref, *refs):
+    own_ref, got_refs, refs = refs[0], refs[1 : 1 + RP], refs[1 + RP :]
+    column_ref, cos_ref, sin_ref, midcos_ref, midsin_ref, refs = *refs[:5], refs[5:]
+    valid_ref, gain_ref, newcos_ref, newsin_ref, refs = *refs[:4], refs[4:]
+    out_refs, keys_ref = refs[-5:-1], refs[-1]
     request = pl.program_id(0)
 
-    @pl.when(table[7] == 3)
+    @pl.when(rank[0] == 3)
     def _():
+        for r in range(RP):
+
+            @pl.when(request == r)
+            def _(r=r):
+                for i, (cosine, sine) in enumerate(
+                    ((cos_ref, sin_ref), (midcos_ref, midsin_ref))
+                ):
+                    for u in range(UNITS):
+                        comp = own_ref[u, i] + decode(got_refs[r][i, u])
+                        rows = key_rows(comp, column_ref[...], cosine[u], sine[u])
+                        start = (1 - i) * SHARE + u * UNIT
+                        keys_ref[:, start : start + UNIT] = rows.astype(BF)
+
         scale = (DN + DR) ** (-0.5)
         local_rows = out_refs[0].shape[1]
         new = 2 * RP
@@ -583,7 +518,7 @@
         norm = lax.rsqrt(jnp.mean(lat * lat, axis=-1, keepdims=True) + 1e-06)
         first = comp[:, KVL : KVL + HALF]
         second = comp[:, KVL + HALF :]
-        cosine, sine = cos_ref[...], sin_ref[...]
+        cosine, sine = newcos_ref[...], newsin_ref[...]
         drafts = jnp.concatenate(
             [
                 lat * norm * gain_ref[...],
@@ -594,8 +529,7 @@
         )
         drafts = jnp.concatenate([drafts, jnp.zeros((UNIT - new, WIDTH), F32)], 0).astype(BF)
         query = jnp.concatenate([q_ref[t] for t in range(4)], 0)
-        keys = jnp.concatenate([keys_ref[0, 1], keys_ref[0, 0]], 1)
-        scores = jnp.dot(query, keys, preferred_element_type=F32) * scale
+        scores = jnp.dot(query, keys_ref[...], preferred_element_type=F32) * scale
         scores = jnp.where(valid_ref[0] > 0.0, scores, -1e30)
         fresh = lax.dot_general(query, drafts, NT, preferred_element_type=F32) * scale
         row = lax.broadcasted_iota(jnp.int32, fresh.shape, 0)
@@ -608,42 +542,50 @@
         weights = jnp.exp(scores - top)
         fresh = jnp.exp(fresh - top)
         total = jnp.sum(weights, axis=1, keepdims=True) + jnp.sum(fresh, axis=1, keepdims=True)
-        numer = lax.dot_general(weights.astype(BF), keys[:KVL], NT, preferred_element_type=F32)
+        numer = lax.dot_general(
+            weights.astype(BF), keys_ref[0:KVL, :], NT, preferred_element_type=F32
+        )
         numer = numer + jnp.dot(fresh.astype(BF), drafts[:, :KVL], preferred_element_type=F32)
         result = (numer / total).astype(BF)
         for t, ref in enumerate(out_refs):
             ref[0] = result[t * local_rows : (t + 1) * local_rows]
 
 
-def attend(table, messages, held, valid, gain, cosine, sine, after):
+def attend(rank, messages, own, got, column, tables, valid, gain, cosine, sine, after):
     new = 2 * RP
     local_rows = (messages.shape[1] - 4 * new) // RP
     last = RP * local_rows // (4 * new)
     out = jax.ShapeDtypeStruct((RP, local_rows, KVL), BF)
-    whole = lambda i, table: (0, 0)
-    body = lambda *refs: attend_kernel(*refs[:8], *refs[-4:])
+    whole = lambda i, rank: (0, 0)
+    whole3 = lambda i, rank: (0, 0, 0)
     return pl.pallas_call(
-        body,
+        attend_kernel,
         grid_spec=pltpu.PrefetchScalarGridSpec(
             num_scalar_prefetch=1,
             grid=(RP,),
             in_specs=[
-                pl.BlockSpec((4, local_rows, WIDTH), lambda i, table: (0, i, 0)),
-                pl.BlockSpec((4, 4 * new, WIDTH), lambda i, table: (0, last, 0)),
-                pl.BlockSpec((1, 2, WIDTH, SHARE), lambda i, table: (i, 0, 0, 0)),
-                pl.BlockSpec((1, 1, valid.shape[2]), lambda i, table: (i, 0, 0)),
+                pl.BlockSpec((4, local_rows, WIDTH), lambda i, rank: (0, i, 0)),
+                pl.BlockSpec((4, 4 * new, WIDTH), lambda i, rank: (0, last, 0)),
+                pl.BlockSpec(
+                    (UNITS, 2, None, WIDTH, UNIT), lambda i, rank: (0, 0, i, 0, 0)
+                ),
+                *([pl.BlockSpec((2, UNITS, CODED, UNIT), lambda i, rank: (0, 0, 0, 0))] * RP),
+                pl.BlockSpec((KVL, UNIT), whole),
+                *([pl.BlockSpec((UNITS, HALF, UNIT), whole3)] * 4),
+                pl.BlockSpec((1, 1, valid.shape[2]), lambda i, rank: (i, 0, 0)),
                 pl.BlockSpec((1, KVL), whole),
                 pl.BlockSpec(cosine.shape, whole),
                 pl.BlockSpec(sine.shape, whole),
                 *([ANY] * len(after)),
             ],
-            out_specs=[pl.BlockSpec((1, local_rows, KVL), lambda i, table: (i, 0, 0))] * 4,
+            out_specs=[pl.BlockSpec((1, local_rows, KVL), lambda i, rank: (i, 0, 0))] * 4,
+            scratch_shapes=[pltpu.VMEM((WIDTH, 2 * SHARE), BF)],
         ),
         out_shape=[out] * 4,
         compiler_params=ROOM,
         cost_estimate=COST,
         name="attend",
-    )(table, messages, messages, held, valid, gain, cosine, sine, *after)
+    )(rank, messages, messages, own, *got, column, *tables, valid, gain, cosine, sine, *after)
 
 
 def heads_kernel(o_ref, keep_ref, *refs):
@@ -698,60 +640,33 @@
     p = lax.axis_index("pd")
     first_req = p * RP
 
-    table = jnp.asarray(
-        [
-            [3, 2, 0, 2, 1, 0, 1, 0, 0],
-            [3, 2, 0, 2, 1, 0, 0, 1, 0],
-            [3, 2, 0, 2, 1, 0, 0, 2, 1],
-            [0, 2, 3, 0, 1, 2, 1, 3, 2],
-        ],
-        jnp.int32,
-    )[z]
-    hops = jnp.asarray(
-        [
-            [[0, 0, 0], [2, 1, 2], [0, 0, 1], [0, 0, 0]],
-            [[0, 0, 0], [0, 0, 1], [2, 1, 2], [0, 0, 0]],
-            [[0, 0, 0], [2, 2, 1], [0, 0, 1], [0, 0, 0]],
-            [[0, 0, 0], [1, 1, 1], [0, 0, 0], [0, 0, 0]],
-            [[0, 0, 0], [0, 0, 1], [2, 2, 1], [0, 0, 0]],
-            [[0, 0, 0], [0, 0, 0], [1, 1, 1], [0, 0, 0]],
-        ],
-        jnp.int32,
-    )[:, z]
-
+    rank = z.astype(jnp.int32).reshape(1)
     hidden = prefill_hidden.reshape(RP, PRE_TOK, prefill_hidden.shape[1])
     down_t = kv_down.T
-    inward = [(0, 1), (3, 2)]
-    last = RP - 1
-    sums = [None] * RP
-    inner = [None] * RP
+    inward, across, outward = [(0, 1), (3, 2)], [(1, 2), (2, 1)], [(2, 3), (1, 0)]
+
+    far_sums, inner = [], []
     for r in range(RP):
-        sums[r], *coded = project(table, hidden, down_t, r, r < last, sums[max(r - 1, 0) : r])
-        inner[r] = [lax.ppermute(c, "tp", inward) for c in coded]
-
-    my_segments = lax.dynamic_slice_in_dim(segment_ids, first_req, RP, 0)
-    valid = (my_segments == my_segments[:, -1:])[:, PRE_TOK // 2 :].astype(F32)
-    valid = valid.reshape(RP, 1, PRE_TOK // 2)
-    gain = jnp.broadcast_to(kv_gain[:, None], (KVL, UNIT))
-    steps = jnp.arange(SHARE, dtype=jnp.int32)
-    tables = [t.T for t in (*rope_tables(z * SHARE + steps), *rope_tables(2 * SHARE + steps))]
-
-    held = jnp.zeros((RP, 2, WIDTH, SHARE), BF)
-    across = [None] * RP
-    sent = [None] * RP
-    outer = [None] * RP
+        total, codes = project_far(rank, hidden, down_t, r, far_sums[-1:])
+        far_sums.append(total)
+        inner.append(lax.ppermute(codes, "tp", inward))
 
     def first_hop(r, after):
-        block = add_on(hops[0], sums[r], inner[r][0], after=after)
-        across[r] = lax.ppermute(block, "tp", [(1, 2), (2, 1)])
+        block = add_on(rank, far_sums[r], inner[r], after=after)
+        crossed.append(lax.ppermute(block, "tp", across))
         return block
 
     def second_hop(r, after):
-        block = add_on(hops[1], sums[r], across[r], inner[r][0], 1, after)
-        sent[r] = block
-        outer[r] = [lax.ppermute(block, "tp", [(2, 3), (1, 0)])] * 2
-
-    block = first_hop(0, [sums[last]])
+        block = add_on(rank, near_sums, crossed[r], r, after)
+        sent.append(block)
+        outer.append(lax.ppermute(block, "tp", outward))
+        return block
+
+    crossed, sent, outer = [], [], []
+    block = first_hop(0, far_sums[-1:])
+    near_sums, *side = project_near(rank, hidden, down_t, [block])
+    first_hop(1, [near_sums])
+    block = second_hop(0, [])
 
     latents = lax.dynamic_slice_in_dim(query_latent, first_req, RP, 0).reshape(RP * 2, QL)
     new_pos = jnp.tile(PRE_TOK + jnp.arange(2, dtype=jnp.int32), RP)
@@ -766,33 +681,35 @@
     ).astype(BF)
     messages = lax.all_gather(message, "tp", axis=0)
 
-    first_hop(1, [query])
-    second_hop(0, [])
-    first_hop(2, [sent[0], message])
-    second_hop(1, [])
-    held = finish(table, sums[0], *outer[0], sent[0], gain, tables, held, 0, [sent[1]])
-
-    one = add_on(hops[2], sums[last], inner[last][0], after=[sent[1]])
-    sums_last, *coded = project_last(table, hidden, down_t, [one])
-    inner_last = [lax.ppermute(c, "tp", inward) for c in coded]
-    one = lax.ppermute(one, "tp", [(1, 2), (2, 1)])
-    two = add_on(hops[3], sums[last], inner[last][1], after=[held, sums_last, messages])
-    two = lax.ppermute(two, "tp", [(1, 2)])
-    second_hop(2, [])
-    held = finish(table, sums[1], *outer[1], sent[1], gain, tables, held, 1, [sent[2]])
-    one = add_on(hops[4], sums[last], one, after=[held])
-    one = lax.ppermute(one, "tp", [(2, 3), (1, 0)])
-    lasts = [add_last(table, sums_last, inner_last[0], 0)]
-    sent[last] = add_on(hops[5], sums[last], two, inner[last][1], 0, [lasts[0]])
-    two = lax.ppermute(sent[last], "tp", [(2, 3)])
-    lasts.append(add_last(table, sums_last, inner_last[1], 1))
-    held = finish(table, sums[2], *outer[2], sent[2], gain, tables, held, 2, [lasts[1]])
-    lasts.append(add_last(table, sums_last, inner_last[2], 2))
-    held = finish(table, sums[last], one, two, sent[last], gain, tables, held, last, [])
-    lasts = [lax.ppermute(block, "tp", [(2, 1)]) for block in lasts]
+    my_segments = lax.dynamic_slice_in_dim(segment_ids, first_req, RP, 0)
+    valid = (my_segments == my_segments[:, -1:])[:, PRE_TOK // 2 :].astype(F32)
+    valid = valid.reshape(RP, 1, PRE_TOK // 2)
+    column = jnp.broadcast_to(kv_gain[:, None], (KVL, UNIT))
+    steps = jnp.arange(SHARE, dtype=jnp.int32).reshape(UNITS, UNIT)
+    tables = [
+        jnp.swapaxes(t, 1, 2)
+        for t in (*rope_tables(z * SHARE + steps), *rope_tables(2 * SHARE + steps))
+    ]
+
+    block = first_hop(2, [message])
+    second_hop(1, [block, outer[0]])
+    block = first_hop(3, [sent[1]])
+    side = [lax.ppermute(codes, "tp", inward) for codes in side]
+    second_hop(2, [block, messages, outer[1]])
+    second_hop(3, [side[0], outer[2]])
 
     result = attend(
-        table, messages, held, valid, kv_gain.reshape(1, KVL), new_cos, new_sin, [lasts[0]]
+        rank,
+        messages,
+        near_sums,
+        outer,
+        column,
+        tables,
+        valid,
+        kv_gain.reshape(1, KVL),
+        new_cos,
+        new_sin,
+        [],
     )
     back = [lax.ppermute(result[t], "tp", [(3, t)]) for t in range(3)]
     attended = jnp.where(z == 3, result[3], back[0] + back[1] + back[2])
@@ -813,16 +730,17 @@
     cache = []
     for u in range(UNITS):
         page = pages_of(
-            table,
-            slots,
-            has.astype(jnp.int32),
-            sums_last,
-            inner_last[u],
-            lasts[u],
-            held,
-            gain,
+            rank,
+            my_owners,
+            near_sums,
+            outer,
+            sent,
+            side[u > 0],
+            max(u - 1, 0),
+            column,
             tables[0],
             tables[1],
+            pd_count,
             u,
         )
         cache.append(lax.all_to_all(page, "pd", split_axis=0, concat_axis=0, tiled=True))

time: 347 us -> 315 us (0.908)
  Pallas kernels: 158 us -> 97.5 us
  waiting for transfers between devices: 74.9 us -> 126 us
  starting transfers between devices: 60.8 us -> 49.7 us
  local copies, waits for them, and re-layouts: 24.9 us -> 16.4 us
    pallas_call x23 -> x14, Pallas kernels: 126 us -> 64.4 us  [the longest x4 22.7 us: project_far(): pl.pallas_call(project_far_kernel, grid_spec=pltpu.PrefetchScalarGridSpec...]
    ppermute x21 -> x14, waiting for transfers between devices: 53.5 us -> 87.6 us  [the longest x4 38.6 us: local_line(): inner.append(lax.ppermute(codes, 'tp', inward))]
    ppermute x3, waiting for transfers between devices: 3.54 us -> 22.6 us  [local_line(): back = [lax.ppermute(result[t], 'tp', [(3, t)]) for t in range(3)]]
    ppermute x21 -> x14, starting transfers between devices: 44.2 us -> 33.3 us  [the longest x4 14.7 us: second_hop(): outer.append(lax.ppermute(block, 'tp', outward))]
    unnamed x58 -> x44, local copies, waits for them, and re-layouts: 11.2 us -> 8.59 us
  transfers between devices with their start and end apart: 29 -> 22, of which waited for: 8 -> 14; matrix products, arithmetic and copies ran while one was open for 6% -> 5% of each run, Pallas kernels for 44% -> 26%
where the time goes in v1:
time: 315 us; the launch traced here: 313 us
  waiting for transfers between devices  126 us (40%)
  Pallas kernels  97.5 us (31%)
  starting transfers between devices  49.7 us (16%)
  local copies, waits for them, and re-layouts  16.4 us (5%)
  between operations  14.4 us (5%)
  other arithmetic  8.73 us (3%)
    ppermute x4, waiting for transfers between devices, local_line(): inner.append(lax.ppermute(codes, 'tp', inward))  38.6 us
    ppermute x4, waiting for transfers between devices, second_hop(): outer.append(lax.ppermute(block, 'tp', outward))  24.1 us
    pallas_call x4, Pallas kernels, project_far(): pl.pallas_call(project_far_kernel, grid_spec=pltpu.PrefetchScalarGridSpec...  22.7 us
    ppermute x3, waiting for transfers between devices, local_line(): back = [lax.ppermute(result[t], 'tp', [(3, t)]) for t in range(3)]  22.6 us
    pallas_call x8, Pallas kernels, add_on(): pl.pallas_call(add_kernel, grid_spec=pltpu.PrefetchScalarGridSpec(num_sca...  22.6 us
    all_to_all x3, waiting for transfers between devices, local_line(): lax.all_to_all(page, 'pd', split_axis=0, concat_axis=0, tiled=True)  15.8 us
    pallas_call x3, Pallas kernels, pages_of(): pl.pallas_call(page_kernel, grid_spec=pltpu.PrefetchScalarGridSpec(num_sc...  14.9 us
    ppermute x4, starting transfers between devices, second_hop(): outer.append(lax.ppermute(block, 'tp', outward))  14.7 us
  transfers between devices with their start and end apart: 22, of which 14 were waited for; matrix products, arithmetic and copies ran while one was open for 5% of the time, Pallas kernels for 26%

profile of v1, /device:TPU:16, one launch (start us, length us, event | category | flops | bytes accessed | tf_op | source)
XLA Modules:
  0.0 312.8 jit_solution(802142985598440746)
XLA Ops:
  7.2 5.6 %project_far.4 = (f32[2,3,576,128]{3,2,1,0:T(8,128)}, s16[2,3,592,128]{3,2,1,0:T(8,128)(2,1)}) custom-call(s32[1]{0:T(128)} %bitcast.rank, bf16[4,1536,1792]{2,1,0:T(8,128)(2,1)} %bitcast.26, bf16[576,1792]{1,0:T(8,128)(2,1)} %bitcast.31), custom_call_target="tpu_custom_call" | custom-call | flops 1024 | bytes 1024 | tf_op jit(solution)/shard_map/project_far/pallas_call | solution.py:268
  14.2 5.6 %project_far.5 = (f32[2,3,576,128]{3,2,1,0:T(8,128)}, s16[2,3,592,128]{3,2,1,0:T(8,128)(2,1)}) custom-call(s32[1]{0:T(128)} %bitcast.rank, bf16[4,1536,1792]{2,1,0:T(8,128)(2,1)} %bitcast.27, bf16[576,1792]{1,0:T(8,128)(2,1)} %bitcast.32, f32[2,3,576,128]{3,2,1,0:T(8,128)} %get-tuple-element.19.refs_0_.own_ref), custom_call_target="tpu_custom_call" | custom-call | flops 1024 | bytes 1024 | tf_op jit(solution)/shard_map/project_far/pallas_call | solution.py:268
  19.8 5.6 %project_far.6 = (f32[2,3,576,128]{3,2,1,0:T(8,128)}, s16[2,3,592,128]{3,2,1,0:T(8,128)(2,1)}) custom-call(s32[1]{0:T(128)} %bitcast.rank, bf16[4,1536,1792]{2,1,0:T(8,128)(2,1)} %bitcast.28, bf16[576,1792]{1,0:T(8,128)(2,1)} %bitcast.33, f32[2,3,576,128]{3,2,1,0:T(8,128)} %get-tuple-element.21.refs_0_.own_ref), custom_call_target="tpu_custom_call" | custom-call | flops 1024 | bytes 1024 | tf_op jit(solution)/shard_map/project_far/pallas_call | solution.py:268
  25.4 5.8 %project_far.7 = (f32[2,3,576,128]{3,2,1,0:T(8,128)}, s16[2,3,592,128]{3,2,1,0:T(8,128)(2,1)}) custom-call(s32[1]{0:T(128)} %bitcast.rank, bf16[4,1536,1792]{2,1,0:T(8,128)(2,1)} %bitcast.29, bf16[576,1792]{1,0:T(8,128)(2,1)} %bitcast.34, f32[2,3,576,128]{3,2,1,0:T(8,128)} %get-tuple-element.22.refs_0_.own_ref), custom_call_target="tpu_custom_call" | custom-call | flops 1024 | bytes 1024 | tf_op jit(solution)/shard_map/project_far/pallas_call | solution.py:268
  31.2 5.7 %collective-permute-done.got_ref = s16[2,3,592,128]{3,2,1,0:T(8,128)(2,1)S(1)} collective-permute-done((s16[2,3,592,128]{3,2,1,0:T(8,128)(2,1)}, s16[2,3,592,128]{3,2,1,0:T(8,128)(2,1)S(1)}, u32[]{:S(2)}, u32[]{:S(2)}) %collective-permute-start) | collective-permute-done | bytes 909344 | tf_op jit(solution)/shard_map/ppermute | solution.py:652
  37.8 2.9 add_on.8.refs_0_
  40.7 2.4 collective-permute-start.1
  43.1 1.3 collective-permute-start.3
  45.9 13.0 %project_near.1 = (f32[3,2,4,576,128]{4,3,2,1,0:T(8,128)}, s16[1,4,592,128]{3,2,1,0:T(8,128)(2,1)}, s16[2,4,592,128]{3,2,1,0:T(8,128)(2,1)}) custom-call(s32[1]{0:T(128)} %bitcast.rank, bf16[4,1536,1792]{2,1,0:T(8,128)(2,1)} %bitcast.30, bf16[576,1792]{1,0:T(8,128)(2,1)} %bitcast.35, s16[2,3,592,128]{3,2,1,0:T(8,128)(2,1)} %add_on.8.refs_0_), custom_call_target="tpu_custom_call" | custom-call | flops 1024 | bytes 1024 | tf_op jit(solution)/shard_map/project_near/pallas_call | solution.py:311
  58.9 4.9 %collective-permute-done.1.got_ref = s16[2,3,592,128]{3,2,1,0:T(8,128)(2,1)S(1)} collective-permute-done((s16[2,3,592,128]{3,2,1,0:T(8,128)(2,1)}, s16[2,3,592,128]{3,2,1,0:T(8,128)(2,1)S(1)}, u32[]{:S(2)}, u32[]{:S(2)}) %collective-permute-start.1) | collective-permute-done | bytes 909344 | tf_op jit(solution)/shard_map/ppermute | solution.py:656
  64.8 2.8 add_on.9.refs_10_.refs_4_
  67.6 13.8 %queries.1 = (f32[32,8,576]{2,1,0:T(8,128)}, f32[4,8,576]{2,1,0:T(8,128)}) custom-call(bf16[8,1536]{1,0:T(8,128)(2,1)} %reshape.164.refs_0_, bf16[1536,6144]{1,0:T(8,128)(2,1)} %refs_1_.2, bf16[8,1792]{1,0:T(8,128)(2,1)} %refs_2_.2, bf16[576,1792]{1,0:T(8,128)(2,1)} %bitcast.36, bf16[512,8192]{1,0:T(8,128)(2,1)} %refs_7_.3, bf16[512,8192]{1,0:T(8,128)(2,1)} %refs_7_.3, ...), custom_call_target="tpu_custom_call" | custom-call | flops 1024 | bytes 1024 | tf_op jit(solution)/shard_map/queries/pallas_call | solution.py:461
  84.3 1.4 collective-permute-start.5
  86.7 2.8 add_on.10
  89.5 2.4 collective-permute-start.4
  91.8 3.5 %collective-permute-start.2 = (s16[2,3,592,128]{3,2,1,0:T(8,128)(2,1)S(1)}, s16[2,3,592,128]{3,2,1,0:T(8,128)(2,1)S(1)}, u32[]{:S(2)}, u32[]{:S(2)}) collective-permute-start(s16[2,3,592,128]{3,2,1,0:T(8,128)(2,1)S(1)} %copy-done.2), channel_id=1, source_target_pairs={{8,12},{4,0},{9,13},{5,1},{10,14},{6,2},{11,15},{7,3},{24,28},{20,... | collective-permute-start | bytes 2727944 | tf_op jit(solution)/shard_map/ppermute | solution.py:662
  97.4 27.0 %collective-permute-done.5.got_ref = s16[2,3,592,128]{3,2,1,0:T(8,128)(2,1)} collective-permute-done((s16[2,3,592,128]{3,2,1,0:T(8,128)(2,1)}, s16[2,3,592,128]{3,2,1,0:T(8,128)(2,1)}, u32[]{:S(2)}, u32[]{:S(2)}) %collective-permute-start.5) | collective-permute-done | bytes 909344 | tf_op jit(solution)/shard_map/ppermute | solution.py:652
  124.4 2.8 add_on.11.refs_0_
  127.2 3.5 %collective-permute-start.7 = (s16[2,3,592,128]{3,2,1,0:T(8,128)(2,1)}, s16[2,3,592,128]{3,2,1,0:T(8,128)(2,1)}, u32[]{:S(2)}, u32[]{:S(2)}) collective-permute-start(s16[2,3,592,128]{3,2,1,0:T(8,128)(2,1)} %add_on.11.refs_0_), channel_id=1, source_target_pairs={{4,8},{8,4},{5,9},{9,5},{6,10},{10,6},{7,11},{11,7},{20,24},{24,20... | collective-permute-start | bytes 2727944 | tf_op jit(solution)/shard_map/ppermute | solution.py:656
  130.7 5.5 %collective-permute-done.4.got_ref = s16[2,3,592,128]{3,2,1,0:T(8,128)(2,1)S(1)} collective-permute-done((s16[2,3,592,128]{3,2,1,0:T(8,128)(2,1)}, s16[2,3,592,128]{3,2,1,0:T(8,128)(2,1)S(1)}, u32[]{:S(2)}, u32[]{:S(2)}) %collective-permute-start.4) | collective-permute-done | bytes 909344 | tf_op jit(solution)/shard_map/ppermute | solution.py:656
  138.0 2.8 add_on.12.refs_0_.refs_5_
  140.8 3.0 collective-permute-start.6
  143.9 5.9 %collective-permute-done.8.got_ref = s16[2,3,592,128]{3,2,1,0:T(8,128)(2,1)S(1)} collective-permute-done((s16[2,3,592,128]{3,2,1,0:T(8,128)(2,1)}, s16[2,3,592,128]{3,2,1,0:T(8,128)(2,1)S(1)}, u32[]{:S(2)}, u32[]{:S(2)}) %collective-permute-start.8) | collective-permute-done | bytes 909344 | tf_op jit(solution)/shard_map/ppermute | solution.py:652
  150.8 2.8 add_on.13.refs_0_
  153.6 2.5 collective-permute-start.10
  156.1 7.0 %collective-permute-done.6.refs_2_.refs_1_ = s16[2,3,592,128]{3,2,1,0:T(8,128)(2,1)S(1)} collective-permute-done((s16[2,3,592,128]{3,2,1,0:T(8,128)(2,1)}, s16[2,3,592,128]{3,2,1,0:T(8,128)(2,1)S(1)}, u32[]{:S(2)}, u32[]{:S(2)}) %collective-permute-start.6) | collective-permute-done | bytes 909344 | tf_op jit(solution)/shard_map/ppermute | solution.py:662
  164.0 2.9 add_on.14.refs_6_
  166.9 4.0 %collective-permute-start.9 = (s16[2,3,592,128]{3,2,1,0:T(8,128)(2,1)}, s16[2,3,592,128]{3,2,1,0:T(8,128)(2,1)S(1)}, u32[]{:S(2)}, u32[]{:S(2)}) collective-permute-start(s16[2,3,592,128]{3,2,1,0:T(8,128)(2,1)} %add_on.14.refs_6_), channel_id=1, source_target_pairs={{8,12},{4,0},{9,13},{5,1},{10,14},{6,2},{11,15},{7,3},{24,28},{20,... | collective-permute-start | bytes 2727944 | tf_op jit(solution)/shard_map/ppermute | solution.py:662
  170.9 1.3 collective-permute-start.11
  173.2 13.3 %collective-permute-done.11.refs_0_.refs_8_ = s16[1,4,592,128]{3,2,1,0:T(8,128)(2,1)S(1)} collective-permute-done((s16[1,4,592,128]{3,2,1,0:T(8,128)(2,1)S(1)}, s16[1,4,592,128]{3,2,1,0:T(8,128)(2,1)S(1)}, u32[]{:S(2)}, u32[]{:S(2)}) %collective-permute-start.11) | collective-permute-done | bytes 606240 | tf_op jit(solution)/shard_map/ppermute | solution.py:697
  186.6 2.6 collective-permute-done.9.refs_1_.refs_3_.refs_2_
  190.2 2.8 add_on.15.refs_7_
  193.0 4.2 %collective-permute-start.12 = (s16[2,3,592,128]{3,2,1,0:T(8,128)(2,1)}, s16[2,3,592,128]{3,2,1,0:T(8,128)(2,1)S(1)}, u32[]{:S(2)}, u32[]{:S(2)}) collective-permute-start(s16[2,3,592,128]{3,2,1,0:T(8,128)(2,1)} %add_on.15.refs_7_), channel_id=1, source_target_pairs={{8,12},{4,0},{9,13},{5,1},{10,14},{6,2},{11,15},{7,3},{24,28},{20,... | collective-permute-start | bytes 2727944 | tf_op jit(solution)/shard_map/ppermute | solution.py:662
  199.8 14.5 %collective-permute-done.12.refs_4_.refs_3_ = s16[2,3,592,128]{3,2,1,0:T(8,128)(2,1)S(1)} collective-permute-done((s16[2,3,592,128]{3,2,1,0:T(8,128)(2,1)}, s16[2,3,592,128]{3,2,1,0:T(8,128)(2,1)S(1)}, u32[]{:S(2)}, u32[]{:S(2)}) %collective-permute-start.12) | collective-permute-done | bytes 909344 | tf_op jit(solution)/shard_map/ppermute | solution.py:662
  215.4 6.1 %attend.1 = (bf16[4,64,512]{2,1,0:T(8,128)(2,1)}, bf16[4,64,512]{2,1,0:T(8,128)(2,1)}, bf16[4,64,512]{2,1,0:T(8,128)(2,1)}, bf16[4,64,512]{2,1,0:T(8,128)(2,1)}) custom-call(s32[1]{0:T(128)} %bitcast.rank, bf16[4,288,576]{2,1,0:T(8,128)(2,1)} %all-gather.2.cloned.1.call-done.refs_1_.q_ref.draft_ref, ...), custom_call_target="tpu_custom_call" | custom-call | flops 1024 | bytes 1024 | tf_op jit(solution)/shard_map/attend/pallas_call | solution.py:561
  225.7 22.6 %collective-permute-done.15 = bf16[4,64,512]{2,1,0:T(8,128)(2,1)S(1)} collective-permute-done((bf16[4,64,512]{2,1,0:T(8,128)(2,1)}, bf16[4,64,512]{2,1,0:T(8,128)(2,1)S(1)}, u32[]{:S(2)}, u32[]{:S(2)}) %collective-permute-start.15) | collective-permute-done | bytes 262176 | tf_op jit(solution)/shard_map/ppermute | solution.py:714
  250.5 4.4 %heads_out.1 = f32[8,4096]{1,0:T(8,128)} custom-call(f32[32,8,512]{2,1,0:T(8,128)} %reshape.179.o_ref, f32[8,128]{1,0:T(8,128)} %broadcast_in_dim.14.keep_ref, bf16[512,8192]{1,0:T(8,128)(2,1)} %refs_7_.3, bf16[512,8192]{1,0:T(8,128)(2,1)} %refs_7_.3, bf16[512,8192]{1,0:T(8,128)(2,1)} %refs_7_.3, bf16[512,8192]{1,0:T(8,128)(2,1)} %refs_7_.3, ...), custom_call_target="tpu_custom_call" | custom-call | flops 1024 | bytes 1024 | tf_op jit(solution)/shard_map/heads_out/pallas_call | solution.py:604
  257.3 3.3 %all-to-all-start = ((bf16[4,2,4096]{2,1,0:T(2,128)(2,1)}), bf16[4,2,4096]{2,1,0:T(2,128)(2,1)S(1)}, u32[]{:S(2)}, u32[]{:S(2)}) async-start(bf16[4,2,4096]{2,1,0:T(2,128)(2,1)} %select_convert_fusion), calls=%async_computation | async-start | bytes 131072 | tf_op jit(solution)/shard_map/all_to_all | solution.py:728
  260.6 5.0 %pages.3 = bf16[4,576,128]{2,1,0:T(8,128)(2,1)} custom-call(s32[1]{0:T(128)} %bitcast.rank, s32[4]{0:T(128)} %copy-done.16, f32[3,2,4,576,128]{4,3,2,1,0:T(8,128)} %get-tuple-element.24.own_ref.refs_0_, s16[2,3,592,128]{3,2,1,0:T(8,128)(2,1)} %copy-done.3, s16[2,3,592,128]{3,2,1,0:T(8,128)(2,1)} %copy-done.4, s16[2,3,592,128]{3,2,1,0:T(8,128)(2,1)} %copy-done.5, ...), custom_call_target="tpu_custom_call" | custom-call | flops 1024 | bytes 1024 | tf_op jit(solution)/shard_map/pages/pallas_call | solution.py:401
  265.5 3.5 %all-to-all-start.1 = ((bf16[4,576,128]{2,1,0:T(8,128)(2,1)}), bf16[4,576,128]{2,1,0:T(8,128)(2,1)S(1)}, u32[]{:S(2)}, u32[]{:S(2)}) async-start(bf16[4,576,128]{2,1,0:T(8,128)(2,1)} %pages.3), calls=%async_computation.1 | async-start | bytes 1179648 | tf_op jit(solution)/shard_map/all_to_all | solution.py:746
  271.2 5.0 %pages.4 = bf16[4,576,128]{2,1,0:T(8,128)(2,1)} custom-call(s32[1]{0:T(128)} %bitcast.rank, s32[4]{0:T(128)} %copy-done.16, f32[3,2,4,576,128]{4,3,2,1,0:T(8,128)} %get-tuple-element.24.own_ref.refs_0_, s16[2,3,592,128]{3,2,1,0:T(8,128)(2,1)} %copy-done.3, s16[2,3,592,128]{3,2,1,0:T(8,128)(2,1)} %copy-done.4, s16[2,3,592,128]{3,2,1,0:T(8,128)(2,1)} %copy-done.5, ...), custom_call_target="tpu_custom_call" | custom-call | flops 1024 | bytes 1024 | tf_op jit(solution)/shard_map/pages/pallas_call | solution.py:401
  276.2 2.4 all-to-all-done.1
  278.5 3.5 %all-to-all-start.2 = ((bf16[4,576,128]{2,1,0:T(8,128)(2,1)}), bf16[4,576,128]{2,1,0:T(8,128)(2,1)S(1)}, u32[]{:S(2)}, u32[]{:S(2)}) async-start(bf16[4,576,128]{2,1,0:T(8,128)(2,1)} %pages.4), calls=%async_computation.2 | async-start | bytes 1179648 | tf_op jit(solution)/shard_map/all_to_all | solution.py:746
  282.0 5.0 %pages.5 = bf16[4,576,128]{2,1,0:T(8,128)(2,1)} custom-call(s32[1]{0:T(128)} %bitcast.rank, s32[4]{0:T(128)} %copy-done.16, f32[3,2,4,576,128]{4,3,2,1,0:T(8,128)} %get-tuple-element.24.own_ref.refs_0_, s16[2,3,592,128]{3,2,1,0:T(8,128)(2,1)} %copy-done.3, s16[2,3,592,128]{3,2,1,0:T(8,128)(2,1)} %copy-done.4, s16[2,3,592,128]{3,2,1,0:T(8,128)(2,1)} %copy-done.5, ...), custom_call_target="tpu_custom_call" | custom-call | flops 1024 | bytes 1024 | tf_op jit(solution)/shard_map/pages/pallas_call | solution.py:401
  287.0 4.5 %all-to-all-done.2 = bf16[4,576,128]{2,1,0:T(8,128)(2,1)S(1)} async-done(((bf16[4,576,128]{2,1,0:T(8,128)(2,1)}), bf16[4,576,128]{2,1,0:T(8,128)(2,1)S(1)}, u32[]{:S(2)}, u32[]{:S(2)}) %all-to-all-start.2) | async-done | bytes 589856 | tf_op jit(solution)/shard_map/all_to_all | solution.py:746
  291.5 3.5 %all-to-all-start.3 = ((bf16[4,576,128]{2,1,0:T(8,128)(2,1)}), bf16[4,576,128]{2,1,0:T(8,128)(2,1)S(1)}, u32[]{:S(2)}, u32[]{:S(2)}) async-start(bf16[4,576,128]{2,1,0:T(8,128)(2,1)} %pages.5), calls=%async_computation.3 | async-start | bytes 1179648 | tf_op jit(solution)/shard_map/all_to_all | solution.py:746
  295.7 8.8 %all-to-all-done.3 = bf16[4,576,128]{2,1,0:T(8,128)(2,1)S(1)} async-done(((bf16[4,576,128]{2,1,0:T(8,128)(2,1)}), bf16[4,576,128]{2,1,0:T(8,128)(2,1)S(1)}, u32[]{:S(2)}, u32[]{:S(2)}) %all-to-all-start.3) | async-done | bytes 589856 | tf_op jit(solution)/shard_map/all_to_all | solution.py:746
  304.5 1.4 maximum_bitcast_fusion
  (96 shorter events, 31.4 us)
Async XLA Ops:
  7.2 37.3 %copy-start = (bf16[16,2,1536]{2,1,0:T(2,128)(2,1)S(1)}, bf16[16,2,1536]{2,1,0:T(2,128)(2,1)}, u32[]{:S(2)}) copy-start(bf16[16,2,1536]{2,1,0:T(2,128)(2,1)} %param.14) | copy-start | bytes 294916
  7.2 155.9 %all-gather.2.cloned.1.call-start = ((), (), s32[]{:S(2)}) async-start(), calls=%async_computation.4 | async-start | bytes 1843200 | tf_op jit(solution)/shard_map/all_gather | solution.py:682
  12.9 24.0 %collective-permute-start = (s16[2,3,592,128]{3,2,1,0:T(8,128)(2,1)}, s16[2,3,592,128]{3,2,1,0:T(8,128)(2,1)S(1)}, u32[]{:S(2)}, u32[]{:S(2)}) collective-permute-start(s16[2,3,592,128]{3,2,1,0:T(8,128)(2,1)} %get-tuple-element.20), channel_id=1, source_target_pairs={{0,4},{12,8},{1,5},{13,9},{2,6},{14,10},{3,7},{15,11},{16,20},{28,... | collective-permute-start | bytes 2727944 | tf_op jit(solution)/shard_map/ppermute | solution.py:652
  36.9 1.0 copy-start.14
  37.8 5.3 %copy-start.18 = (s16[2,3,592,128]{3,2,1,0:T(8,128)(2,1)S(1)}, s16[2,3,592,128]{3,2,1,0:T(8,128)(2,1)}, u32[]{:S(2)}) copy-start(s16[2,3,592,128]{3,2,1,0:T(8,128)(2,1)} %get-tuple-element.27) | copy-start | bytes 2727940
  40.7 23.1 %collective-permute-start.1 = (s16[2,3,592,128]{3,2,1,0:T(8,128)(2,1)}, s16[2,3,592,128]{3,2,1,0:T(8,128)(2,1)S(1)}, u32[]{:S(2)}, u32[]{:S(2)}) collective-permute-start(s16[2,3,592,128]{3,2,1,0:T(8,128)(2,1)} %add_on.8.refs_0_), channel_id=1, source_target_pairs={{4,8},{8,4},{5,9},{9,5},{6,10},{10,6},{7,11},{11,7},{20,24},{24,20... | collective-permute-start | bytes 2727944 | tf_op jit(solution)/shard_map/ppermute | solution.py:656
  43.1 42.6 %collective-permute-start.3 = (s16[2,3,592,128]{3,2,1,0:T(8,128)(2,1)S(1)}, s16[2,3,592,128]{3,2,1,0:T(8,128)(2,1)S(1)}, u32[]{:S(2)}, u32[]{:S(2)}) collective-permute-start(s16[2,3,592,128]{3,2,1,0:T(8,128)(2,1)S(1)} %copy-done.18), channel_id=1, source_target_pairs={{0,4},{12,8},{1,5},{13,9},{2,6},{14,10},{3,7},{15,11},{16,20},{28,... | collective-permute-start | bytes 2727944 | tf_op jit(solution)/shard_map/ppermute | solution.py:652
  63.9 0.9 copy-start.12
  84.3 7.6 %copy-start.2 = (s16[2,3,592,128]{3,2,1,0:T(8,128)(2,1)S(1)}, s16[2,3,592,128]{3,2,1,0:T(8,128)(2,1)}, u32[]{:S(2)}) copy-start(s16[2,3,592,128]{3,2,1,0:T(8,128)(2,1)} %add_on.9.refs_10_.refs_4_) | copy-start | bytes 2727940
  84.3 40.2 %collective-permute-start.5 = (s16[2,3,592,128]{3,2,1,0:T(8,128)(2,1)}, s16[2,3,592,128]{3,2,1,0:T(8,128)(2,1)}, u32[]{:S(2)}, u32[]{:S(2)}) collective-permute-start(s16[2,3,592,128]{3,2,1,0:T(8,128)(2,1)} %get-tuple-element.28), channel_id=1, source_target_pairs={{0,4},{12,8},{1,5},{13,9},{2,6},{14,10},{3,7},{15,11},{16,20},{28,... | collective-permute-start | bytes 2727944 | tf_op jit(solution)/shard_map/ppermute | solution.py:652
  85.7 0.9 copy-start.10
  89.5 46.7 %collective-permute-start.4 = (s16[2,3,592,128]{3,2,1,0:T(8,128)(2,1)}, s16[2,3,592,128]{3,2,1,0:T(8,128)(2,1)S(1)}, u32[]{:S(2)}, u32[]{:S(2)}) collective-permute-start(s16[2,3,592,128]{3,2,1,0:T(8,128)(2,1)} %add_on.10), channel_id=1, source_target_pairs={{4,8},{8,4},{5,9},{9,5},{6,10},{10,6},{7,11},{11,7},{20,24},{24,20... | collective-permute-start | bytes 2727944 | tf_op jit(solution)/shard_map/ppermute | solution.py:656
  91.8 44.3 %collective-permute-start.2 = (s16[2,3,592,128]{3,2,1,0:T(8,128)(2,1)S(1)}, s16[2,3,592,128]{3,2,1,0:T(8,128)(2,1)S(1)}, u32[]{:S(2)}, u32[]{:S(2)}) collective-permute-start(s16[2,3,592,128]{3,2,1,0:T(8,128)(2,1)S(1)} %copy-done.2), channel_id=1, source_target_pairs={{8,12},{4,0},{9,13},{5,1},{10,14},{6,2},{11,15},{7,3},{24,28},{20,... | collective-permute-start | bytes 2727944 | tf_op jit(solution)/shard_map/ppermute | solution.py:662
  95.4 54.4 %collective-permute-start.8 = (s16[2,3,592,128]{3,2,1,0:T(8,128)(2,1)}, s16[2,3,592,128]{3,2,1,0:T(8,128)(2,1)S(1)}, u32[]{:S(2)}, u32[]{:S(2)}) collective-permute-start(s16[2,3,592,128]{3,2,1,0:T(8,128)(2,1)} %get-tuple-element.29), channel_id=1, source_target_pairs={{0,4},{12,8},{1,5},{13,9},{2,6},{14,10},{3,7},{15,11},{16,20},{28,... | collective-permute-start | bytes 2727944 | tf_op jit(solution)/shard_map/ppermute | solution.py:652
  127.2 28.9 %collective-permute-start.7 = (s16[2,3,592,128]{3,2,1,0:T(8,128)(2,1)}, s16[2,3,592,128]{3,2,1,0:T(8,128)(2,1)}, u32[]{:S(2)}, u32[]{:S(2)}) collective-permute-start(s16[2,3,592,128]{3,2,1,0:T(8,128)(2,1)} %add_on.11.refs_0_), channel_id=1, source_target_pairs={{4,8},{8,4},{5,9},{9,5},{6,10},{10,6},{7,11},{11,7},{20,24},{24,20... | collective-permute-start | bytes 2727944 | tf_op jit(solution)/shard_map/ppermute | solution.py:656
  136.2 0.9 copy-start.13
  137.1 0.9 copy-start.3
  140.8 22.3 %collective-permute-start.6 = (s16[2,3,592,128]{3,2,1,0:T(8,128)(2,1)}, s16[2,3,592,128]{3,2,1,0:T(8,128)(2,1)S(1)}, u32[]{:S(2)}, u32[]{:S(2)}) collective-permute-start(s16[2,3,592,128]{3,2,1,0:T(8,128)(2,1)} %add_on.12.refs_0_.refs_5_), channel_id=1, source_target_pairs={{8,12},{4,0},{9,13},{5,1},{10,14},{6,2},{11,15},{7,3},{24,28},{20,... | collective-permute-start | bytes 2727944 | tf_op jit(solution)/shard_map/ppermute | solution.py:662
  149.8 0.9 copy-start.9
  153.6 17.3 %copy-start.19 = (s16[1,4,592,128]{3,2,1,0:T(8,128)(2,1)S(1)}, s16[1,4,592,128]{3,2,1,0:T(8,128)(2,1)}, u32[]{:S(2)}) copy-start(s16[1,4,592,128]{3,2,1,0:T(8,128)(2,1)} %get-tuple-element.30) | copy-start | bytes 1818628
  153.6 18.6 %copy-start.20 = (s32[16]{0:T(128)S(1)}, s32[16]{0:T(128)}, u32[]{:S(2)}) copy-start(s32[16]{0:T(128)} %param.17) | copy-start | bytes 196
  153.6 18.7 %copy-start.21 = (s32[16]{0:T(128)S(1)}, s32[16]{0:T(128)}, u32[]{:S(2)}) copy-start(s32[16]{0:T(128)} %param.19) | copy-start | bytes 196
  153.6 33.0 %collective-permute-start.10 = (s16[2,3,592,128]{3,2,1,0:T(8,128)(2,1)}, s16[2,3,592,128]{3,2,1,0:T(8,128)(2,1)S(1)}, u32[]{:S(2)}, u32[]{:S(2)}) collective-permute-start(s16[2,3,592,128]{3,2,1,0:T(8,128)(2,1)} %add_on.13.refs_0_), channel_id=1, source_target_pairs={{4,8},{8,4},{5,9},{9,5},{6,10},{10,6},{7,11},{11,7},{20,24},{24,20... | collective-permute-start | bytes 2727944 | tf_op jit(solution)/shard_map/ppermute | solution.py:656
  163.1 0.9 copy-start.4
  166.9 22.3 %collective-permute-start.9 = (s16[2,3,592,128]{3,2,1,0:T(8,128)(2,1)}, s16[2,3,592,128]{3,2,1,0:T(8,128)(2,1)S(1)}, u32[]{:S(2)}, u32[]{:S(2)}) collective-permute-start(s16[2,3,592,128]{3,2,1,0:T(8,128)(2,1)} %add_on.14.refs_6_), channel_id=1, source_target_pairs={{8,12},{4,0},{9,13},{5,1},{10,14},{6,2},{11,15},{7,3},{24,28},{20,... | collective-permute-start | bytes 2727944 | tf_op jit(solution)/shard_map/ppermute | solution.py:662
  170.9 15.7 %collective-permute-start.11 = (s16[1,4,592,128]{3,2,1,0:T(8,128)(2,1)S(1)}, s16[1,4,592,128]{3,2,1,0:T(8,128)(2,1)S(1)}, u32[]{:S(2)}, u32[]{:S(2)}) collective-permute-start(s16[1,4,592,128]{3,2,1,0:T(8,128)(2,1)S(1)} %copy-done.19), channel_id=1, source_target_pairs={{0,4},{12,8},{1,5},{13,9},{2,6},{14,10},{3,7},{15,11},{16,20},{28,... | collective-permute-start | bytes 1818632 | tf_op jit(solution)/shard_map/ppermute | solution.py:697
  172.3 52.0 %copy-start.16 = (s32[4]{0:T(128)}, s32[4]{0:T(128)S(1)}, u32[]{:S(2)}) copy-start(s32[4]{0:T(128)S(1)} %dynamic_slice.12.slot) | copy-start | bytes 52
  173.2 41.1 %copy-start.15 = (f32[512]{0:T(512)S(1)}, f32[512]{0:T(512)}, u32[]{:S(2)}) copy-start(f32[512]{0:T(512)} %param.13) | copy-start | bytes 6148
  186.6 2.6 copy-start.8
  186.6 2.6 copy-start.11
  189.2 1.0 copy-start.5
  193.0 21.4 %collective-permute-start.12 = (s16[2,3,592,128]{3,2,1,0:T(8,128)(2,1)}, s16[2,3,592,128]{3,2,1,0:T(8,128)(2,1)S(1)}, u32[]{:S(2)}, u32[]{:S(2)}) collective-permute-start(s16[2,3,592,128]{3,2,1,0:T(8,128)(2,1)} %add_on.15.refs_7_), channel_id=1, source_target_pairs={{8,12},{4,0},{9,13},{5,1},{10,14},{6,2},{11,15},{7,3},{24,28},{20,... | collective-permute-start | bytes 2727944 | tf_op jit(solution)/shard_map/ppermute | solution.py:662
  214.4 1.0 copy-start.6
  215.4 9.0 %copy-start.17 = (s16[2,4,592,128]{3,2,1,0:T(8,128)(2,1)S(1)}, s16[2,4,592,128]{3,2,1,0:T(8,128)(2,1)}, u32[]{:S(2)}) copy-start(s16[2,4,592,128]{3,2,1,0:T(8,128)(2,1)} %get-tuple-element.35) | copy-start | bytes 3637252
  221.5 4.2 %collective-permute-start.13 = (bf16[4,64,512]{2,1,0:T(8,128)(2,1)}, bf16[4,64,512]{2,1,0:T(8,128)(2,1)S(1)}, u32[]{:S(2)}, u32[]{:S(2)}) collective-permute-start(bf16[4,64,512]{2,1,0:T(8,128)(2,1)} %get-tuple-element.32), channel_id=1, source_target_pairs={{12,0},{13,1},{14,2},{15,3},{28,16},{29,17},{30,18},{31,19}} | collective-permute-start | bytes 786440 | tf_op jit(solution)/shard_map/ppermute | solution.py:714
  222.2 3.5 %collective-permute-start.14 = (bf16[4,64,512]{2,1,0:T(8,128)(2,1)}, bf16[4,64,512]{2,1,0:T(8,128)(2,1)S(1)}, u32[]{:S(2)}, u32[]{:S(2)}) collective-permute-start(bf16[4,64,512]{2,1,0:T(8,128)(2,1)} %get-tuple-element.33), channel_id=1, source_target_pairs={{12,4},{13,5},{14,6},{15,7},{28,20},{29,21},{30,22},{31,23}} | collective-permute-start | bytes 786440 | tf_op jit(solution)/shard_map/ppermute | solution.py:714
  222.9 25.4 %collective-permute-start.15 = (bf16[4,64,512]{2,1,0:T(8,128)(2,1)}, bf16[4,64,512]{2,1,0:T(8,128)(2,1)S(1)}, u32[]{:S(2)}, u32[]{:S(2)}) collective-permute-start(bf16[4,64,512]{2,1,0:T(8,128)(2,1)} %get-tuple-element.34), channel_id=1, source_target_pairs={{12,8},{13,9},{14,10},{15,11},{28,24},{29,25},{30,26},{31,27}} | collective-permute-start | bytes 786440 | tf_op jit(solution)/shard_map/ppermute | solution.py:714
  224.4 45.7 %collective-permute-start.16 = (s16[2,4,592,128]{3,2,1,0:T(8,128)(2,1)S(1)}, s16[2,4,592,128]{3,2,1,0:T(8,128)(2,1)S(1)}, u32[]{:S(2)}, u32[]{:S(2)}) collective-permute-start(s16[2,4,592,128]{3,2,1,0:T(8,128)(2,1)S(1)} %copy-done.17), channel_id=1, source_target_pairs={{0,4},{12,8},{1,5},{13,9},{2,6},{14,10},{3,7},{15,11},{16,20},{28,... | collective-permute-start | bytes 3637256 | tf_op jit(solution)/shard_map/ppermute | solution.py:697
  257.3 8.3 %all-to-all-start = ((bf16[4,2,4096]{2,1,0:T(2,128)(2,1)}), bf16[4,2,4096]{2,1,0:T(2,128)(2,1)S(1)}, u32[]{:S(2)}, u32[]{:S(2)}) async-start(bf16[4,2,4096]{2,1,0:T(2,128)(2,1)} %select_convert_fusion), calls=%async_computation | async-start | bytes 131072 | tf_op jit(solution)/shard_map/all_to_all | solution.py:728
  265.5 13.0 %all-to-all-start.1 = ((bf16[4,576,128]{2,1,0:T(8,128)(2,1)}), bf16[4,576,128]{2,1,0:T(8,128)(2,1)S(1)}, u32[]{:S(2)}, u32[]{:S(2)}) async-start(bf16[4,576,128]{2,1,0:T(8,128)(2,1)} %pages.3), calls=%async_computation.1 | async-start | bytes 1179648 | tf_op jit(solution)/shard_map/all_to_all | solution.py:746
  270.2 1.0 copy-start.7
  278.5 13.0 %all-to-all-start.2 = ((bf16[4,576,128]{2,1,0:T(8,128)(2,1)}), bf16[4,576,128]{2,1,0:T(8,128)(2,1)S(1)}, u32[]{:S(2)}, u32[]{:S(2)}) async-start(bf16[4,576,128]{2,1,0:T(8,128)(2,1)} %pages.4), calls=%async_computation.2 | async-start | bytes 1179648 | tf_op jit(solution)/shard_map/all_to_all | solution.py:746
  291.5 13.0 %all-to-all-start.3 = ((bf16[4,576,128]{2,1,0:T(8,128)(2,1)}), bf16[4,576,128]{2,1,0:T(8,128)(2,1)S(1)}, u32[]{:S(2)}, u32[]{:S(2)}) async-start(bf16[4,576,128]{2,1,0:T(8,128)(2,1)} %pages.5), calls=%async_computation.3 | async-start | bytes 1179648 | tf_op jit(solution)/shard_map/all_to_all | solution.py:746
  295.0 11.0 %copy-start.1 = (bf16[16,2,1536]{2,1,0:T(2,128)(2,1)S(1)}, bf16[16,2,1536]{2,1,0:T(2,128)(2,1)}, u32[]{:S(2)}) copy-start(bf16[16,2,1536]{2,1,0:T(2,128)(2,1)} %param.14) | copy-start | bytes 294916
Sparse Core Ops, SparseCore 0:
  84.4 58.2 all-gather.1

commit v2 on v1

--- a/solution.py
+++ b/solution.py
@@ -375,52 +375,56 @@
 
 def page_kernel(rank, slot, own_ref, *refs):
     got_refs, sent_refs, refs = refs[:RP], refs[RP : 2 * RP], refs[2 * RP :]
-    side_ref, gain_ref, cos_ref, sin_ref = refs[:4]
-    out_ref = refs[-1]
+    side_refs, (gain_ref, cos_ref, sin_ref), out_ref = refs[:2], refs[2:5], refs[-1]
     request = pl.program_id(0)
 
-    def write(comp):
-        out_ref[0] = key_rows(comp, gain_ref[...], cos_ref[0], sin_ref[0]).astype(BF)
+    def write(u, comp):
+        rows = key_rows(comp, gain_ref[...], cos_ref[u], sin_ref[u])
+        out_ref[0, :, u * UNIT : (u + 1) * UNIT] = rows.astype(BF)
 
     for r in range(RP):
 
         @pl.when((request == r) & outer_rank(rank[0]))
         def _(r=r):
-            write(own_ref[...] + decode(got_refs[r][0, 0]))
+            for u in range(UNITS):
+                write(u, own_ref[u] + decode(got_refs[r][u]))
 
         @pl.when((request == r) & ~outer_rank(rank[0]))
         def _(r=r):
-            write(decode(sent_refs[r][0, 0]) + decode(side_ref[...]))
-
-
-def pages_of(rank, slot, own, got, sent, side, place, gain, cosine, sine, count, unit):
-    first = pl.BlockSpec((1, 1, CODED, UNIT), lambda i, *_: (0, unit, 0, 0))
-    second = pl.BlockSpec((1, 1, CODED, UNIT), lambda i, *_: (1, unit, 0, 0))
-    table = pl.BlockSpec((1, HALF, UNIT), lambda i, *_: (unit, 0, 0))
-    base = [jnp.zeros((count, WIDTH, UNIT), BF)] if count > RP else []
+            for u in range(UNITS):
+                side = side_refs[u > 0][max(u - 1, 0)]
+                write(u, decode(sent_refs[r][u]) + decode(side))
+
+
+def pages_of(rank, slot, own, got, sent, side, gain, cosine, sine, count):
+    first = pl.BlockSpec((None, UNITS, CODED, UNIT), lambda i, *_: (0, 0, 0, 0))
+    second = pl.BlockSpec((None, UNITS, CODED, UNIT), lambda i, *_: (1, 0, 0, 0))
+    table = pl.BlockSpec((UNITS, HALF, UNIT), lambda i, *_: (0, 0, 0))
+    base = [jnp.zeros((count, WIDTH, SHARE), BF)] if count > RP else []
     return pl.pallas_call(
         page_kernel,
         grid_spec=pltpu.PrefetchScalarGridSpec(
             num_scalar_prefetch=2,
             grid=(RP,),
             in_specs=[
-                pl.BlockSpec((None, None, None, WIDTH, UNIT), lambda i, *_: (unit, 0, i, 0, 0)),
+                pl.BlockSpec((UNITS, None, None, WIDTH, UNIT), lambda i, *_: (0, 0, i, 0, 0)),
                 *([first] * RP),
                 *([second] * RP),
-                pl.BlockSpec((None, None, CODED, UNIT), lambda i, *_: (place, i, 0, 0)),
+                pl.BlockSpec((1, None, CODED, UNIT), lambda i, *_: (0, i, 0, 0)),
+                pl.BlockSpec((UNITS - 1, None, CODED, UNIT), lambda i, *_: (0, i, 0, 0)),
                 pl.BlockSpec((KVL, UNIT), lambda i, *_: (0, 0)),
                 table,
                 table,
                 *([ANY] * len(base)),
             ],
-            out_specs=pl.BlockSpec((1, WIDTH, UNIT), lambda i, rank, slot: (slot[i], 0, 0)),
+            out_specs=pl.BlockSpec((1, WIDTH, SHARE), lambda i, rank, slot: (slot[i], 0, 0)),
         ),
-        out_shape=jax.ShapeDtypeStruct((count, WIDTH, UNIT), BF),
-        input_output_aliases={7 + 2 * RP: 0} if base else {},
+        out_shape=jax.ShapeDtypeStruct((count, WIDTH, SHARE), BF),
+        input_output_aliases={8 + 2 * RP: 0} if base else {},
         compiler_params=ROOM,
         cost_estimate=COST,
         name="pages",
-    )(rank, slot, own, *got, *sent, side, gain, cosine, sine, *base)
+    )(rank, slot, own, *got, *sent, *side, gain, cosine, sine, *base)
 
 
 def query_kernel(lat_ref, up_ref, draft_ref, down_ref, *refs):
@@ -588,33 +592,34 @@
     )(rank, messages, messages, own, *got, column, *tables, valid, gain, cosine, sine, *after)
 
 
-def heads_kernel(o_ref, keep_ref, *refs):
-    *value_refs, out_ref = refs
-    for h, value_ref in enumerate(value_refs):
+def heads_kernel(step, o_ref, keep_ref, *refs):
+    out_ref = refs[-1]
+    for h, value_ref in enumerate(refs[:step]):
         row = jnp.dot(o_ref[h].astype(BF), value_ref[...], preferred_element_type=F32)
         out_ref[:, h * DV : (h + 1) * DV] = row * keep_ref[...]
 
 
-def heads_out(attended, keep, kv_up):
+def heads_out(attended, keep, kv_up, after):
     heads, rows, _ = attended.shape
     step = 8
     value_spec = [
         pl.BlockSpec((KVL, DV), lambda i, h=h: (0, 2 * (step * i + h) + 1)) for h in range(step)
     ]
     return pl.pallas_call(
-        heads_kernel,
+        functools.partial(heads_kernel, step),
         grid=(heads // step,),
         in_specs=[
             pl.BlockSpec((step, rows, KVL), lambda i: (i, 0, 0)),
             pl.BlockSpec((rows, DV), lambda i: (0, 0)),
             *value_spec,
+            *([ANY] * len(after)),
         ],
         out_specs=pl.BlockSpec((rows, step * DV), lambda i: (0, i)),
         out_shape=jax.ShapeDtypeStruct((rows, heads * DV), F32),
         compiler_params=ROOM,
         cost_estimate=COST,
         name="heads_out",
-    )(attended, keep, *([kv_up] * step))
+    )(attended, keep, *([kv_up] * step), *after)
 
 
 def rope_tables(position):
@@ -666,7 +671,9 @@
     block = first_hop(0, far_sums[-1:])
     near_sums, *side = project_near(rank, hidden, down_t, [block])
     first_hop(1, [near_sums])
-    block = second_hop(0, [])
+    second_hop(0, [])
+    first_hop(2, [sent[0]])
+    block = second_hop(1, [outer[0]])
 
     latents = lax.dynamic_slice_in_dim(query_latent, first_req, RP, 0).reshape(RP * 2, QL)
     new_pos = jnp.tile(PRE_TOK + jnp.arange(2, dtype=jnp.int32), RP)
@@ -691,11 +698,9 @@
         for t in (*rope_tables(z * SHARE + steps), *rope_tables(2 * SHARE + steps))
     ]
 
-    block = first_hop(2, [message])
-    second_hop(1, [block, outer[0]])
-    block = first_hop(3, [sent[1]])
+    block = first_hop(3, [message, column, valid, *tables])
     side = [lax.ppermute(codes, "tp", inward) for codes in side]
-    second_hop(2, [block, messages, outer[1]])
+    second_hop(2, [block, outer[1]])
     second_hop(3, [side[0], outer[2]])
 
     result = attend(
@@ -712,39 +717,35 @@
         [],
     )
     back = [lax.ppermute(result[t], "tp", [(3, t)]) for t in range(3)]
+
+    my_owners = lax.dynamic_slice_in_dim(owners, first_req, RP, 0)
+    pages = pages_of(
+        rank,
+        my_owners,
+        near_sums,
+        outer,
+        sent,
+        side,
+        column,
+        tables[0],
+        tables[1],
+        pd_count,
+    )
+    cache = lax.all_to_all(pages, "pd", split_axis=0, concat_axis=0, tiled=True)
+    cache = jnp.swapaxes(cache, 1, 2)
+
     attended = jnp.where(z == 3, result[3], back[0] + back[1] + back[2])
     attended = attended.reshape(RP, 2, heads, KVL).transpose(2, 0, 1, 3)
     attended = attended.reshape(heads, RP * 2, KVL).astype(F32)
     my_accepted = lax.dynamic_slice_in_dim(accepted, first_req, RP, 0)
     keep = (jnp.arange(2)[None, :] <= my_accepted[:, None]).astype(F32).reshape(RP * 2, 1)
-    answer = heads_out(attended, jnp.broadcast_to(keep, (RP * 2, DV)), kv_up)
+    answer = heads_out(attended, jnp.broadcast_to(keep, (RP * 2, DV)), kv_up, [pages])
     answer = answer.reshape(RP, 2, heads * DV)
-
-    my_owners = lax.dynamic_slice_in_dim(owners, first_req, RP, 0)
     routing = my_owners[None, :] == jnp.arange(pd_count, dtype=jnp.int32)[:, None]
     has = jnp.any(routing, axis=1)
     slots = jnp.sum(routing.astype(jnp.int32) * jnp.arange(RP, dtype=jnp.int32)[None, :], axis=1)
     placed = jnp.where(has[:, None, None], answer[slots], 0.0).astype(BF)
     placed = lax.all_to_all(placed, "pd", split_axis=0, concat_axis=0, tiled=True)
-
-    cache = []
-    for u in range(UNITS):
-        page = pages_of(
-            rank,
-            my_owners,
-            near_sums,
-            outer,
-            sent,
-            side[u > 0],
-            max(u - 1, 0),
-            column,
-            tables[0],
-            tables[1],
-            pd_count,
-            u,
-        )
-        cache.append(lax.all_to_all(page, "pd", split_axis=0, concat_axis=0, tiled=True))
-    cache = jnp.swapaxes(jnp.concatenate(cache, 2), 1, 2)
     return (placed.reshape(pd_count * 2, heads * DV), cache)
 
 

time: 315 us -> 274 us (0.87)
  waiting for transfers between devices: 126 us -> 99.5 us
  starting transfers between devices: 49.7 us -> 38.6 us
  Pallas kernels: 97.5 us -> 89.3 us
  blocking collectives: 0 us -> 6.68 us
    ppermute x4, waiting for transfers between devices: 38.6 us -> 6.35 us  [local_line(): inner.append(lax.ppermute(codes, 'tp', inward))]
    ppermute x2, waiting for transfers between devices: 14.5 us -> 29 us  [local_line(): side = [lax.ppermute(codes, 'tp', inward) for codes in side]]
    ppermute x3, waiting for transfers between devices: 22.6 us -> 12.4 us  [local_line(): back = [lax.ppermute(result[t], 'tp', [(3, t)]) for t in range(3)]]
    all_to_all x4 -> x1, starting transfers between devices: 13.7 us -> 3.58 us  [local_line(): cache = lax.all_to_all(pages, 'pd', split_axis=0, concat_axis=0, tiled=True)]
    pallas_call x3 -> x1, Pallas kernels: 14.9 us -> 6.96 us  [pages_of(): pl.pallas_call(page_kernel, grid_spec=pltpu.PrefetchScalarGridSpec(num_sc...]
    all_to_all x0 -> x1, blocking collectives: none -> 6.68 us  [local_line(): lax.all_to_all(placed, 'pd', split_axis=0, concat_axis=0, tiled=True)]
    all_to_all x4 -> x1, waiting for transfers between devices: 15.8 us -> 21.5 us  [local_line(): cache = lax.all_to_all(pages, 'pd', split_axis=0, concat_axis=0, tiled=True)]
    ppermute x4, waiting for transfers between devices: 10.4 us -> 6.84 us  [first_hop(): crossed.append(lax.ppermute(block, 'tp', across))]
  transfers between devices with their start and end apart: 22 -> 19, of which waited for: 14 -> 11; matrix products, arithmetic and copies ran while one was open for 5% -> 4% of each run, Pallas kernels for 26% -> 29%
where the time goes in v2:
time: 274 us; the launch traced here: 273 us
  waiting for transfers between devices  99.5 us (36%)
  Pallas kernels  89.3 us (33%)
  starting transfers between devices  38.6 us (14%)
  local copies, waits for them, and re-layouts  17.7 us (6%)
  between operations  14.4 us (5%)
  other arithmetic  6.73 us (2%)
  blocking collectives  6.68 us (2%)
    ppermute x2, waiting for transfers between devices, local_line(): side = [lax.ppermute(codes, 'tp', inward) for codes in side]  29 us
    ppermute x4, waiting for transfers between devices, second_hop(): outer.append(lax.ppermute(block, 'tp', outward))  23.4 us
    pallas_call x4, Pallas kernels, project_far(): pl.pallas_call(project_far_kernel, grid_spec=pltpu.PrefetchScalarGridSpec...  22.5 us
    pallas_call x8, Pallas kernels, add_on(): pl.pallas_call(add_kernel, grid_spec=pltpu.PrefetchScalarGridSpec(num_sca...  22.4 us
    all_to_all x1, waiting for transfers between devices, local_line(): cache = lax.all_to_all(pages, 'pd', split_axis=0, concat_axis=0, tiled=True)  21.5 us
    pallas_call x1, Pallas kernels, queries(): pl.pallas_call(body, grid=(heads // step,), in_specs=[pl.BlockSpec((rows,...  13.8 us
    pallas_call x1, Pallas kernels, project_near(): pl.pallas_call(project_near_kernel, grid_spec=pltpu.PrefetchScalarGridSpe...  13.1 us
    ppermute x3, waiting for transfers between devices, local_line(): back = [lax.ppermute(result[t], 'tp', [(3, t)]) for t in range(3)]  12.4 us
  transfers between devices with their start and end apart: 19, of which 11 were waited for; matrix products, arithmetic and copies ran while one was open for 4% of the time, Pallas kernels for 29%

profile of v2, /device:TPU:16, one launch (start us, length us, event | category | flops | bytes accessed | tf_op | source)
XLA Modules:
  0.0 273.0 jit_solution(8289288561273994956)
XLA Ops:
  7.2 5.6 %project_far.4 = (f32[2,3,576,128]{3,2,1,0:T(8,128)}, s16[2,3,592,128]{3,2,1,0:T(8,128)(2,1)}) custom-call(s32[1]{0:T(128)} %bitcast.rank, bf16[4,1536,1792]{2,1,0:T(8,128)(2,1)} %bitcast.25, bf16[576,1792]{1,0:T(8,128)(2,1)} %bitcast.30), custom_call_target="tpu_custom_call" | custom-call | flops 1024 | bytes 1024 | tf_op jit(solution)/shard_map/project_far/pallas_call | solution.py:268
  12.9 1.3 collective-permute-start
  14.1 5.7 %project_far.5 = (f32[2,3,576,128]{3,2,1,0:T(8,128)}, s16[2,3,592,128]{3,2,1,0:T(8,128)(2,1)}) custom-call(s32[1]{0:T(128)} %bitcast.rank, bf16[4,1536,1792]{2,1,0:T(8,128)(2,1)} %bitcast.26, bf16[576,1792]{1,0:T(8,128)(2,1)} %bitcast.31, f32[2,3,576,128]{3,2,1,0:T(8,128)} %get-tuple-element.19.refs_0_.own_ref), custom_call_target="tpu_custom_call" | custom-call | flops 1024 | bytes 1024 | tf_op jit(solution)/shard_map/project_far/pallas_call | solution.py:268
  19.8 1.3 collective-permute-start.1
  21.1 5.6 %project_far.6 = (f32[2,3,576,128]{3,2,1,0:T(8,128)}, s16[2,3,592,128]{3,2,1,0:T(8,128)(2,1)}) custom-call(s32[1]{0:T(128)} %bitcast.rank, bf16[4,1536,1792]{2,1,0:T(8,128)(2,1)} %bitcast.27, bf16[576,1792]{1,0:T(8,128)(2,1)} %bitcast.32, f32[2,3,576,128]{3,2,1,0:T(8,128)} %get-tuple-element.21.refs_0_.own_ref), custom_call_target="tpu_custom_call" | custom-call | flops 1024 | bytes 1024 | tf_op jit(solution)/shard_map/project_far/pallas_call | solution.py:268
  26.7 5.6 %project_far.7 = (f32[2,3,576,128]{3,2,1,0:T(8,128)}, s16[2,3,592,128]{3,2,1,0:T(8,128)(2,1)}) custom-call(s32[1]{0:T(128)} %bitcast.rank, bf16[4,1536,1792]{2,1,0:T(8,128)(2,1)} %bitcast.28, bf16[576,1792]{1,0:T(8,128)(2,1)} %bitcast.33, f32[2,3,576,128]{3,2,1,0:T(8,128)} %get-tuple-element.22.refs_0_.own_ref), custom_call_target="tpu_custom_call" | custom-call | flops 1024 | bytes 1024 | tf_op jit(solution)/shard_map/project_far/pallas_call | solution.py:268
  32.3 5.7 %collective-permute-done.got_ref = s16[2,3,592,128]{3,2,1,0:T(8,128)(2,1)S(1)} collective-permute-done((s16[2,3,592,128]{3,2,1,0:T(8,128)(2,1)}, s16[2,3,592,128]{3,2,1,0:T(8,128)(2,1)S(1)}, u32[]{:S(2)}, u32[]{:S(2)}) %collective-permute-start) | collective-permute-done | bytes 909344 | tf_op jit(solution)/shard_map/ppermute | solution.py:657
  39.0 2.8 %add_on.8.refs_0_ = s16[2,3,592,128]{3,2,1,0:T(8,128)(2,1)} custom-call(s32[1]{0:T(128)} %bitcast.rank, f32[2,3,576,128]{3,2,1,0:T(8,128)} %get-tuple-element.19.refs_0_.own_ref, s16[2,3,592,128]{3,2,1,0:T(8,128)(2,1)} %copy-done.13, f32[2,3,576,128]{3,2,1,0:T(8,128)} %get-tuple-element.23.refs_0_.own_ref), custom_call_target="tpu_custom_call" | custom-call | flops 1024 | bytes 1024 | tf_op jit(solution)/shard_map/add_on/pallas_call | solution.py:357
  41.8 2.3 collective-permute-start.3
  44.1 1.3 collective-permute-start.6
  45.4 13.1 %project_near.1 = (f32[3,2,4,576,128]{4,3,2,1,0:T(8,128)}, s16[1,4,592,128]{3,2,1,0:T(8,128)(2,1)}, s16[2,4,592,128]{3,2,1,0:T(8,128)(2,1)}) custom-call(s32[1]{0:T(128)} %bitcast.rank, bf16[4,1536,1792]{2,1,0:T(8,128)(2,1)} %bitcast.29, bf16[576,1792]{1,0:T(8,128)(2,1)} %bitcast.34, s16[2,3,592,128]{3,2,1,0:T(8,128)(2,1)} %add_on.8.refs_0_), custom_call_target="tpu_custom_call" | custom-call | flops 1024 | bytes 1024 | tf_op jit(solution)/shard_map/project_near/pallas_call | solution.py:311
  59.4 2.8 %add_on.9 = s16[2,3,592,128]{3,2,1,0:T(8,128)(2,1)} custom-call(s32[1]{0:T(128)} %bitcast.rank, f32[2,3,576,128]{3,2,1,0:T(8,128)} %get-tuple-element.21.refs_0_.own_ref, s16[2,3,592,128]{3,2,1,0:T(8,128)(2,1)} %copy-done.10, f32[3,2,4,576,128]{4,3,2,1,0:T(8,128)} %get-tuple-element.24.refs_0_.own_ref), custom_call_target="tpu_custom_call" | custom-call | flops 1024 | bytes 1024 | tf_op jit(solution)/shard_map/add_on/pallas_call | solution.py:357
  62.2 3.5 %collective-permute-start.2 = (s16[2,3,592,128]{3,2,1,0:T(8,128)(2,1)}, s16[2,3,592,128]{3,2,1,0:T(8,128)(2,1)}, u32[]{:S(2)}, u32[]{:S(2)}) collective-permute-start(s16[2,3,592,128]{3,2,1,0:T(8,128)(2,1)} %add_on.9), channel_id=1, source_target_pairs={{4,8},{8,4},{5,9},{9,5},{6,10},{10,6},{7,11},{11,7},{20,24},{24,20... | collective-permute-start | bytes 2727944 | tf_op jit(solution)/shard_map/ppermute | solution.py:661
  66.7 2.8 %add_on.10.refs_0_.refs_4_ = s16[2,3,592,128]{3,2,1,0:T(8,128)(2,1)} custom-call(s32[1]{0:T(128)} %bitcast.rank, f32[3,2,4,576,128]{4,3,2,1,0:T(8,128)} %get-tuple-element.24.refs_0_.own_ref, s16[2,3,592,128]{3,2,1,0:T(8,128)(2,1)} %copy-done.12), custom_call_target="tpu_custom_call" | custom-call | flops 1024 | bytes 1024 | tf_op jit(solution)/shard_map/add_on/pallas_call | solution.py:357
  69.5 2.8 %collective-permute-start.4 = (s16[2,3,592,128]{3,2,1,0:T(8,128)(2,1)}, s16[2,3,592,128]{3,2,1,0:T(8,128)(2,1)S(1)}, u32[]{:S(2)}, u32[]{:S(2)}) collective-permute-start(s16[2,3,592,128]{3,2,1,0:T(8,128)(2,1)} %add_on.10.refs_0_.refs_4_), channel_id=1, source_target_pairs={{8,12},{4,0},{9,13},{5,1},{10,14},{6,2},{11,15},{7,3},{24,28},{20,... | collective-permute-start | bytes 2727944 | tf_op jit(solution)/shard_map/ppermute | solution.py:667
  72.3 1.3 collective-permute-start.8
  75.3 1.1 multiply_sine_fusion
  77.9 2.8 %add_on.12 = s16[2,3,592,128]{3,2,1,0:T(8,128)(2,1)} custom-call(s32[1]{0:T(128)} %bitcast.rank, f32[2,3,576,128]{3,2,1,0:T(8,128)} %get-tuple-element.22.refs_0_.own_ref, s16[2,3,592,128]{3,2,1,0:T(8,128)(2,1)} %copy-done.8, s16[2,3,592,128]{3,2,1,0:T(8,128)(2,1)} %add_on.10.refs_0_.refs_4_), custom_call_target="tpu_custom_call" | custom-call | flops 1024 | bytes 1024 | tf_op jit(solution)/shard_map/add_on/pallas_call | solution.py:357
  80.7 2.8 %collective-permute-start.7 = (s16[2,3,592,128]{3,2,1,0:T(8,128)(2,1)}, s16[2,3,592,128]{3,2,1,0:T(8,128)(2,1)}, u32[]{:S(2)}, u32[]{:S(2)}) collective-permute-start(s16[2,3,592,128]{3,2,1,0:T(8,128)(2,1)} %add_on.12), channel_id=1, source_target_pairs={{4,8},{8,4},{5,9},{9,5},{6,10},{10,6},{7,11},{11,7},{20,24},{24,20... | collective-permute-start | bytes 2727944 | tf_op jit(solution)/shard_map/ppermute | solution.py:661
  83.6 1.2 collective-permute-done.2.got_ref
  84.8 4.6 %collective-permute-done.4.refs_0_.refs_1_ = s16[2,3,592,128]{3,2,1,0:T(8,128)(2,1)S(1)} collective-permute-done((s16[2,3,592,128]{3,2,1,0:T(8,128)(2,1)}, s16[2,3,592,128]{3,2,1,0:T(8,128)(2,1)S(1)}, u32[]{:S(2)}, u32[]{:S(2)}) %collective-permute-start.4) | collective-permute-done | bytes 909344 | tf_op jit(solution)/shard_map/ppermute | solution.py:667
  90.3 2.8 %add_on.11.refs_10_.refs_5_ = s16[2,3,592,128]{3,2,1,0:T(8,128)(2,1)} custom-call(s32[1]{0:T(128)} %bitcast.rank, f32[3,2,4,576,128]{4,3,2,1,0:T(8,128)} %get-tuple-element.24.refs_0_.own_ref, s16[2,3,592,128]{3,2,1,0:T(8,128)(2,1)} %collective-permute-done.2.got_ref, s16[2,3,592,128]{3,2,1,0:T(8,128)(2,1)} %copy-done.2), custom_call_target="tpu_custom_call" | custom-call | flops 1024 | bytes 1024 | tf_op jit(solution)/shard_map/add_on/pallas_call | solution.py:357
  93.2 4.0 %collective-permute-start.5 = (s16[2,3,592,128]{3,2,1,0:T(8,128)(2,1)}, s16[2,3,592,128]{3,2,1,0:T(8,128)(2,1)S(1)}, u32[]{:S(2)}, u32[]{:S(2)}) collective-permute-start(s16[2,3,592,128]{3,2,1,0:T(8,128)(2,1)} %add_on.11.refs_10_.refs_5_), channel_id=1, source_target_pairs={{8,12},{4,0},{9,13},{5,1},{10,14},{6,2},{11,15},{7,3},{24,28},{20,... | collective-permute-start | bytes 2727944 | tf_op jit(solution)/shard_map/ppermute | solution.py:667
  97.9 13.8 %queries.1 = (f32[32,8,576]{2,1,0:T(8,128)}, f32[4,8,576]{2,1,0:T(8,128)}) custom-call(bf16[8,1536]{1,0:T(8,128)(2,1)} %reshape.172.refs_0_, bf16[1536,6144]{1,0:T(8,128)(2,1)} %refs_1_.2, bf16[8,1792]{1,0:T(8,128)(2,1)} %refs_2_.2, bf16[576,1792]{1,0:T(8,128)(2,1)} %bitcast.35, bf16[512,8192]{1,0:T(8,128)(2,1)} %refs_7_.3, bf16[512,8192]{1,0:T(8,128)(2,1)} %refs_7_.3, ...), custom_call_target="tpu_custom_call" | custom-call | flops 1024 | bytes 1024 | tf_op jit(solution)/shard_map/queries/pallas_call | solution.py:465
  111.7 1.1 convert.20
  117.9 2.8 %add_on.13.refs_0_ = s16[2,3,592,128]{3,2,1,0:T(8,128)(2,1)} custom-call(s32[1]{0:T(128)} %bitcast.rank, f32[2,3,576,128]{3,2,1,0:T(8,128)} %get-tuple-element.23.refs_0_.own_ref, s16[2,3,592,128]{3,2,1,0:T(8,128)(2,1)} %copy-done.9, bf16[288,576]{1,0:T(8,128)(2,1)} %pad_maximum_fusion.1.refs_0_, f32[512,128]{1,0:T(8,128)} %broadcast_in_dim.13.refs_1_.refs_5_.refs_10_, ...), custom_call_target="tpu_custom_call" | custom-call | flops 1024 | bytes 1024 | tf_op jit(solution)/shard_map/add_on/pallas_call | solution.py:357
  120.7 3.6 %collective-permute-start.10 = (s16[2,3,592,128]{3,2,1,0:T(8,128)(2,1)}, s16[2,3,592,128]{3,2,1,0:T(8,128)(2,1)S(1)}, u32[]{:S(2)}, u32[]{:S(2)}) collective-permute-start(s16[2,3,592,128]{3,2,1,0:T(8,128)(2,1)} %add_on.13.refs_0_), channel_id=1, source_target_pairs={{4,8},{8,4},{5,9},{9,5},{6,10},{10,6},{7,11},{11,7},{20,24},{24,20... | collective-permute-start | bytes 2727944 | tf_op jit(solution)/shard_map/ppermute | solution.py:661
  125.2 2.8 %add_on.14.refs_6_ = s16[2,3,592,128]{3,2,1,0:T(8,128)(2,1)} custom-call(s32[1]{0:T(128)} %bitcast.rank, f32[3,2,4,576,128]{4,3,2,1,0:T(8,128)} %get-tuple-element.24.refs_0_.own_ref, s16[2,3,592,128]{3,2,1,0:T(8,128)(2,1)} %collective-permute-done.7.got_ref, s16[2,3,592,128]{3,2,1,0:T(8,128)(2,1)} %add_on.13.refs_0_, s16[2,3,592,128]{3,2,1,0:T(8,128)(2,1)} %copy-done.3), custom_call_target="tpu_custom_call" | custom-call | flops 1024 | bytes 1024 | tf_op jit(solution)/shard_map/add_on/pallas_call | solution.py:357
  128.0 1.3 collective-permute-start.9
  129.4 1.3 collective-permute-start.11
  130.7 28.4 %collective-permute-done.11.refs_0_.refs_8_ = s16[1,4,592,128]{3,2,1,0:T(8,128)(2,1)S(1)} collective-permute-done((s16[1,4,592,128]{3,2,1,0:T(8,128)(2,1)S(1)}, s16[1,4,592,128]{3,2,1,0:T(8,128)(2,1)S(1)}, u32[]{:S(2)}, u32[]{:S(2)}) %collective-permute-start.11) | collective-permute-done | bytes 606240 | tf_op jit(solution)/shard_map/ppermute | solution.py:702
  159.1 5.6 %collective-permute-done.10.got_ref = s16[2,3,592,128]{3,2,1,0:T(8,128)(2,1)S(1)} collective-permute-done((s16[2,3,592,128]{3,2,1,0:T(8,128)(2,1)}, s16[2,3,592,128]{3,2,1,0:T(8,128)(2,1)S(1)}, u32[]{:S(2)}, u32[]{:S(2)}) %collective-permute-start.10) | collective-permute-done | bytes 909344 | tf_op jit(solution)/shard_map/ppermute | solution.py:661
  164.7 1.8 collective-permute-done.9.refs_1_.refs_3_.refs_2_
  167.5 2.8 %add_on.15.refs_7_ = s16[2,3,592,128]{3,2,1,0:T(8,128)(2,1)} custom-call(s32[1]{0:T(128)} %bitcast.rank, f32[3,2,4,576,128]{4,3,2,1,0:T(8,128)} %get-tuple-element.24.refs_0_.own_ref, s16[2,3,592,128]{3,2,1,0:T(8,128)(2,1)} %copy-done.11, s16[1,4,592,128]{3,2,1,0:T(8,128)(2,1)} %copy-done.6, s16[2,3,592,128]{3,2,1,0:T(8,128)(2,1)} %copy-done.4), custom_call_target="tpu_custom_call" | custom-call | flops 1024 | bytes 1024 | tf_op jit(solution)/shard_map/add_on/pallas_call | solution.py:357
  170.3 4.0 %collective-permute-start.12 = (s16[2,3,592,128]{3,2,1,0:T(8,128)(2,1)}, s16[2,3,592,128]{3,2,1,0:T(8,128)(2,1)S(1)}, u32[]{:S(2)}, u32[]{:S(2)}) collective-permute-start(s16[2,3,592,128]{3,2,1,0:T(8,128)(2,1)} %add_on.15.refs_7_), channel_id=1, source_target_pairs={{8,12},{4,0},{9,13},{5,1},{10,14},{6,2},{11,15},{7,3},{24,28},{20,... | collective-permute-start | bytes 2727944 | tf_op jit(solution)/shard_map/ppermute | solution.py:667
  174.3 1.5 collective-permute-start.16
  176.1 16.9 %collective-permute-done.12.refs_4_.refs_3_ = s16[2,3,592,128]{3,2,1,0:T(8,128)(2,1)S(1)} collective-permute-done((s16[2,3,592,128]{3,2,1,0:T(8,128)(2,1)}, s16[2,3,592,128]{3,2,1,0:T(8,128)(2,1)S(1)}, u32[]{:S(2)}, u32[]{:S(2)}) %collective-permute-start.12) | collective-permute-done | bytes 909344 | tf_op jit(solution)/shard_map/ppermute | solution.py:667
  194.0 6.1 %attend.1 = (bf16[4,64,512]{2,1,0:T(8,128)(2,1)}, bf16[4,64,512]{2,1,0:T(8,128)(2,1)}, bf16[4,64,512]{2,1,0:T(8,128)(2,1)}, bf16[4,64,512]{2,1,0:T(8,128)(2,1)}) custom-call(s32[1]{0:T(128)} %bitcast.rank, bf16[4,288,576]{2,1,0:T(8,128)(2,1)} %all-gather.2.cloned.1.call-done.q_ref.draft_ref, ...), custom_call_target="tpu_custom_call" | custom-call | flops 1024 | bytes 1024 | tf_op jit(solution)/shard_map/attend/pallas_call | solution.py:565
  201.5 1.3 collective-permute-start.15
  203.6 1.1 copy-done.7
  204.8 7.0 %pages.1.refs_8_ = bf16[4,576,384]{2,1,0:T(8,128)(2,1)} custom-call(s32[1]{0:T(128)} %bitcast.rank, s32[4]{0:T(128)} %copy-done.16, f32[3,2,4,576,128]{4,3,2,1,0:T(8,128)} %get-tuple-element.24.refs_0_.own_ref, s16[2,3,592,128]{3,2,1,0:T(8,128)(2,1)} %copy-done.2, s16[2,3,592,128]{3,2,1,0:T(8,128)(2,1)} %copy-done.3, s16[2,3,592,128]{3,2,1,0:T(8,128)(2,1)} %copy-done.4, ...), custom_call_target="tpu_custom_call" | custom-call | flops 1024 | bytes 1024 | tf_op jit(solution)/shard_map/pages/pallas_call | solution.py:404
  211.7 12.4 %collective-permute-done.15 = bf16[4,64,512]{2,1,0:T(8,128)(2,1)S(1)} collective-permute-done((bf16[4,64,512]{2,1,0:T(8,128)(2,1)}, bf16[4,64,512]{2,1,0:T(8,128)(2,1)S(1)}, u32[]{:S(2)}, u32[]{:S(2)}) %collective-permute-start.15) | collective-permute-done | bytes 262176 | tf_op jit(solution)/shard_map/ppermute | solution.py:719
  224.5 1.1 reshape.187.o_ref
  226.3 4.4 %heads_out.1 = f32[8,4096]{1,0:T(8,128)} custom-call(f32[32,8,512]{2,1,0:T(8,128)} %reshape.187.o_ref, f32[8,128]{1,0:T(8,128)} %broadcast_in_dim.14.keep_ref, bf16[512,8192]{1,0:T(8,128)(2,1)} %refs_7_.3, bf16[512,8192]{1,0:T(8,128)(2,1)} %refs_7_.3, bf16[512,8192]{1,0:T(8,128)(2,1)} %refs_7_.3, bf16[512,8192]{1,0:T(8,128)(2,1)} %refs_7_.3, ...), custom_call_target="tpu_custom_call" | custom-call | flops 1024 | bytes 1024 | tf_op jit(solution)/shard_map/heads_out/pallas_call | solution.py:608
  232.5 6.7 %all_to_all.10 = bf16[4,2,4096]{2,1,0:T(2,128)(2,1)S(1)} all-to-all(bf16[4,2,4096]{2,1,0:T(2,128)(2,1)S(1)} %select_convert_fusion), channel_id=1, replica_groups=mesh['groups'=2,'tp'=4,'pd'=4] {'pd'}, dimensions={0} | all-to-all | bytes 131072 | tf_op jit(solution)/shard_map/all_to_all | solution.py:748
  239.2 3.6 %all-to-all-start.1 = ((bf16[4,576,384]{2,1,0:T(8,128)(2,1)}), bf16[4,576,384]{2,1,0:T(8,128)(2,1)S(1)}, u32[]{:S(2)}, u32[]{:S(2)}) async-start(bf16[4,576,384]{2,1,0:T(8,128)(2,1)} %pages.1.refs_8_), calls=%async_computation.1 | async-start | bytes 3538944 | tf_op jit(solution)/shard_map/all_to_all | solution.py:734
  243.4 21.5 %all-to-all-done.1 = bf16[4,576,384]{2,1,0:T(8,128)(2,1)S(1)} async-done(((bf16[4,576,384]{2,1,0:T(8,128)(2,1)}), bf16[4,576,384]{2,1,0:T(8,128)(2,1)S(1)}, u32[]{:S(2)}, u32[]{:S(2)}) %all-to-all-start.1) | async-done | bytes 1769504 | tf_op jit(solution)/shard_map/all_to_all | solution.py:734
  264.9 1.2 copy.24
  (85 shorter events, 21.5 us)
Async XLA Ops:
  7.2 66.5 %copy-start = (bf16[16,2,1536]{2,1,0:T(2,128)(2,1)S(1)}, bf16[16,2,1536]{2,1,0:T(2,128)(2,1)}, u32[]{:S(2)}) copy-start(bf16[16,2,1536]{2,1,0:T(2,128)(2,1)} %param.14) | copy-start | bytes 294916
  7.2 169.0 %all-gather.2.cloned.1.call-start = ((), (), s32[]{:S(2)}) async-start(), calls=%async_computation.2 | async-start | bytes 1843200 | tf_op jit(solution)/shard_map/all_gather | solution.py:689
  12.9 25.2 %collective-permute-start = (s16[2,3,592,128]{3,2,1,0:T(8,128)(2,1)}, s16[2,3,592,128]{3,2,1,0:T(8,128)(2,1)S(1)}, u32[]{:S(2)}, u32[]{:S(2)}) collective-permute-start(s16[2,3,592,128]{3,2,1,0:T(8,128)(2,1)} %get-tuple-element.20), channel_id=1, source_target_pairs={{0,4},{12,8},{1,5},{13,9},{2,6},{14,10},{3,7},{15,11},{16,20},{28,... | collective-permute-start | bytes 2727944 | tf_op jit(solution)/shard_map/ppermute | solution.py:657
  19.8 38.7 %collective-permute-start.1 = (s16[2,3,592,128]{3,2,1,0:T(8,128)(2,1)}, s16[2,3,592,128]{3,2,1,0:T(8,128)(2,1)S(1)}, u32[]{:S(2)}, u32[]{:S(2)}) collective-permute-start(s16[2,3,592,128]{3,2,1,0:T(8,128)(2,1)} %get-tuple-element.25), channel_id=1, source_target_pairs={{0,4},{12,8},{1,5},{13,9},{2,6},{14,10},{3,7},{15,11},{16,20},{28,... | collective-permute-start | bytes 2727944 | tf_op jit(solution)/shard_map/ppermute | solution.py:657
  38.0 0.9 copy-start.13
  41.8 24.0 %collective-permute-start.3 = (s16[2,3,592,128]{3,2,1,0:T(8,128)(2,1)}, s16[2,3,592,128]{3,2,1,0:T(8,128)(2,1)S(1)}, u32[]{:S(2)}, u32[]{:S(2)}) collective-permute-start(s16[2,3,592,128]{3,2,1,0:T(8,128)(2,1)} %add_on.8.refs_0_), channel_id=1, source_target_pairs={{4,8},{8,4},{5,9},{9,5},{6,10},{10,6},{7,11},{11,7},{20,24},{24,20... | collective-permute-start | bytes 2727944 | tf_op jit(solution)/shard_map/ppermute | solution.py:661
  44.1 32.9 %collective-permute-start.6 = (s16[2,3,592,128]{3,2,1,0:T(8,128)(2,1)}, s16[2,3,592,128]{3,2,1,0:T(8,128)(2,1)S(1)}, u32[]{:S(2)}, u32[]{:S(2)}) collective-permute-start(s16[2,3,592,128]{3,2,1,0:T(8,128)(2,1)} %get-tuple-element.28), channel_id=1, source_target_pairs={{0,4},{12,8},{1,5},{13,9},{2,6},{14,10},{3,7},{15,11},{16,20},{28,... | collective-permute-start | bytes 2727944 | tf_op jit(solution)/shard_map/ppermute | solution.py:657
  58.5 0.9 copy-start.10
  62.2 22.5 %collective-permute-start.2 = (s16[2,3,592,128]{3,2,1,0:T(8,128)(2,1)}, s16[2,3,592,128]{3,2,1,0:T(8,128)(2,1)}, u32[]{:S(2)}, u32[]{:S(2)}) collective-permute-start(s16[2,3,592,128]{3,2,1,0:T(8,128)(2,1)} %add_on.9), channel_id=1, source_target_pairs={{4,8},{8,4},{5,9},{9,5},{6,10},{10,6},{7,11},{11,7},{20,24},{24,20... | collective-permute-start | bytes 2727944 | tf_op jit(solution)/shard_map/ppermute | solution.py:661
  65.7 0.9 copy-start.12
  69.5 19.9 %collective-permute-start.4 = (s16[2,3,592,128]{3,2,1,0:T(8,128)(2,1)}, s16[2,3,592,128]{3,2,1,0:T(8,128)(2,1)S(1)}, u32[]{:S(2)}, u32[]{:S(2)}) collective-permute-start(s16[2,3,592,128]{3,2,1,0:T(8,128)(2,1)} %add_on.10.refs_0_.refs_4_), channel_id=1, source_target_pairs={{8,12},{4,0},{9,13},{5,1},{10,14},{6,2},{11,15},{7,3},{24,28},{20,... | collective-permute-start | bytes 2727944 | tf_op jit(solution)/shard_map/ppermute | solution.py:667
  72.3 44.5 %collective-permute-start.8 = (s16[2,3,592,128]{3,2,1,0:T(8,128)(2,1)}, s16[2,3,592,128]{3,2,1,0:T(8,128)(2,1)S(1)}, u32[]{:S(2)}, u32[]{:S(2)}) collective-permute-start(s16[2,3,592,128]{3,2,1,0:T(8,128)(2,1)} %get-tuple-element.29), channel_id=1, source_target_pairs={{0,4},{12,8},{1,5},{13,9},{2,6},{14,10},{3,7},{15,11},{16,20},{28,... | collective-permute-start | bytes 2727944 | tf_op jit(solution)/shard_map/ppermute | solution.py:657
  77.0 0.9 copy-start.8
  80.7 43.5 %collective-permute-start.7 = (s16[2,3,592,128]{3,2,1,0:T(8,128)(2,1)}, s16[2,3,592,128]{3,2,1,0:T(8,128)(2,1)}, u32[]{:S(2)}, u32[]{:S(2)}) collective-permute-start(s16[2,3,592,128]{3,2,1,0:T(8,128)(2,1)} %add_on.12), channel_id=1, source_target_pairs={{4,8},{8,4},{5,9},{9,5},{6,10},{10,6},{7,11},{11,7},{20,24},{24,20... | collective-permute-start | bytes 2727944 | tf_op jit(solution)/shard_map/ppermute | solution.py:661
  89.4 1.0 copy-start.2
  93.2 31.1 %collective-permute-start.5 = (s16[2,3,592,128]{3,2,1,0:T(8,128)(2,1)}, s16[2,3,592,128]{3,2,1,0:T(8,128)(2,1)S(1)}, u32[]{:S(2)}, u32[]{:S(2)}) collective-permute-start(s16[2,3,592,128]{3,2,1,0:T(8,128)(2,1)} %add_on.11.refs_10_.refs_5_), channel_id=1, source_target_pairs={{8,12},{4,0},{9,13},{5,1},{10,14},{6,2},{11,15},{7,3},{24,28},{20,... | collective-permute-start | bytes 2727944 | tf_op jit(solution)/shard_map/ppermute | solution.py:667
  111.7 5.1 %copy-start.15 = (f32[512]{0:T(512)S(1)}, f32[512]{0:T(512)}, u32[]{:S(2)}) copy-start(f32[512]{0:T(512)} %param.13) | copy-start | bytes 6148
  116.8 1.0 copy-start.9
  120.7 8.7 %copy-start.17 = (s16[1,4,592,128]{3,2,1,0:T(8,128)(2,1)S(1)}, s16[1,4,592,128]{3,2,1,0:T(8,128)(2,1)}, u32[]{:S(2)}) copy-start(s16[1,4,592,128]{3,2,1,0:T(8,128)(2,1)} %get-tuple-element.30) | copy-start | bytes 1818628
  120.7 44.1 %collective-permute-start.10 = (s16[2,3,592,128]{3,2,1,0:T(8,128)(2,1)}, s16[2,3,592,128]{3,2,1,0:T(8,128)(2,1)S(1)}, u32[]{:S(2)}, u32[]{:S(2)}) collective-permute-start(s16[2,3,592,128]{3,2,1,0:T(8,128)(2,1)} %add_on.13.refs_0_), channel_id=1, source_target_pairs={{4,8},{8,4},{5,9},{9,5},{6,10},{10,6},{7,11},{11,7},{20,24},{24,20... | collective-permute-start | bytes 2727944 | tf_op jit(solution)/shard_map/ppermute | solution.py:661
  124.3 0.9 copy-start.3
  128.0 38.5 %collective-permute-start.9 = (s16[2,3,592,128]{3,2,1,0:T(8,128)(2,1)}, s16[2,3,592,128]{3,2,1,0:T(8,128)(2,1)S(1)}, u32[]{:S(2)}, u32[]{:S(2)}) collective-permute-start(s16[2,3,592,128]{3,2,1,0:T(8,128)(2,1)} %add_on.14.refs_6_), channel_id=1, source_target_pairs={{8,12},{4,0},{9,13},{5,1},{10,14},{6,2},{11,15},{7,3},{24,28},{20,... | collective-permute-start | bytes 2727944 | tf_op jit(solution)/shard_map/ppermute | solution.py:667
  129.4 46.4 %copy-start.18 = (s32[16]{0:T(128)S(1)}, s32[16]{0:T(128)}, u32[]{:S(2)}) copy-start(s32[16]{0:T(128)} %param.17) | copy-start | bytes 196
  129.4 46.5 %copy-start.19 = (s32[16]{0:T(128)S(1)}, s32[16]{0:T(128)}, u32[]{:S(2)}) copy-start(s32[16]{0:T(128)} %param.19) | copy-start | bytes 196
  129.4 29.7 %collective-permute-start.11 = (s16[1,4,592,128]{3,2,1,0:T(8,128)(2,1)S(1)}, s16[1,4,592,128]{3,2,1,0:T(8,128)(2,1)S(1)}, u32[]{:S(2)}, u32[]{:S(2)}) collective-permute-start(s16[1,4,592,128]{3,2,1,0:T(8,128)(2,1)S(1)} %copy-done.17), channel_id=1, source_target_pairs={{0,4},{12,8},{1,5},{13,9},{2,6},{14,10},{3,7},{15,11},{16,20},{28,... | collective-permute-start | bytes 1818632 | tf_op jit(solution)/shard_map/ppermute | solution.py:702
  159.1 7.5 %copy-start.6 = (s16[1,4,592,128]{3,2,1,0:T(8,128)(2,1)}, s16[1,4,592,128]{3,2,1,0:T(8,128)(2,1)S(1)}, u32[]{:S(2)}) copy-start(s16[1,4,592,128]{3,2,1,0:T(8,128)(2,1)S(1)} %collective-permute-done.11.refs_0_.refs_8_) | copy-start | bytes 1818628
  164.7 1.8 copy-start.11
  166.6 0.9 copy-start.4
  170.3 22.8 %collective-permute-start.12 = (s16[2,3,592,128]{3,2,1,0:T(8,128)(2,1)}, s16[2,3,592,128]{3,2,1,0:T(8,128)(2,1)S(1)}, u32[]{:S(2)}, u32[]{:S(2)}) collective-permute-start(s16[2,3,592,128]{3,2,1,0:T(8,128)(2,1)} %add_on.15.refs_7_), channel_id=1, source_target_pairs={{8,12},{4,0},{9,13},{5,1},{10,14},{6,2},{11,15},{7,3},{24,28},{20,... | collective-permute-start | bytes 2727944 | tf_op jit(solution)/shard_map/ppermute | solution.py:667
  174.3 29.3 %collective-permute-start.16 = (s16[2,4,592,128]{3,2,1,0:T(8,128)(2,1)}, s16[2,4,592,128]{3,2,1,0:T(8,128)(2,1)S(1)}, u32[]{:S(2)}, u32[]{:S(2)}) collective-permute-start(s16[2,4,592,128]{3,2,1,0:T(8,128)(2,1)} %get-tuple-element.35), channel_id=1, source_target_pairs={{0,4},{12,8},{1,5},{13,9},{2,6},{14,10},{3,7},{15,11},{16,20},{28,... | collective-permute-start | bytes 3637256 | tf_op jit(solution)/shard_map/ppermute | solution.py:702
  175.9 27.0 %copy-start.16 = (s32[4]{0:T(128)}, s32[4]{0:T(128)S(1)}, u32[]{:S(2)}) copy-start(s32[4]{0:T(128)S(1)} %dynamic_slice.12.slot) | copy-start | bytes 52
  193.1 0.9 copy-start.5
  200.1 11.6 %collective-permute-start.13 = (bf16[4,64,512]{2,1,0:T(8,128)(2,1)}, bf16[4,64,512]{2,1,0:T(8,128)(2,1)S(1)}, u32[]{:S(2)}, u32[]{:S(2)}) collective-permute-start(bf16[4,64,512]{2,1,0:T(8,128)(2,1)} %get-tuple-element.32), channel_id=1, source_target_pairs={{12,0},{13,1},{14,2},{15,3},{28,16},{29,17},{30,18},{31,19}} | collective-permute-start | bytes 786440 | tf_op jit(solution)/shard_map/ppermute | solution.py:719
  200.8 11.0 %collective-permute-start.14 = (bf16[4,64,512]{2,1,0:T(8,128)(2,1)}, bf16[4,64,512]{2,1,0:T(8,128)(2,1)S(1)}, u32[]{:S(2)}, u32[]{:S(2)}) collective-permute-start(bf16[4,64,512]{2,1,0:T(8,128)(2,1)} %get-tuple-element.33), channel_id=1, source_target_pairs={{12,4},{13,5},{14,6},{15,7},{28,20},{29,21},{30,22},{31,23}} | collective-permute-start | bytes 786440 | tf_op jit(solution)/shard_map/ppermute | solution.py:719
  201.5 22.7 %collective-permute-start.15 = (bf16[4,64,512]{2,1,0:T(8,128)(2,1)}, bf16[4,64,512]{2,1,0:T(8,128)(2,1)S(1)}, u32[]{:S(2)}, u32[]{:S(2)}) collective-permute-start(bf16[4,64,512]{2,1,0:T(8,128)(2,1)} %get-tuple-element.34), channel_id=1, source_target_pairs={{12,8},{13,9},{14,10},{15,11},{28,24},{29,25},{30,26},{31,27}} | collective-permute-start | bytes 786440 | tf_op jit(solution)/shard_map/ppermute | solution.py:719
  203.0 21.2 %copy-start.14 = (bf16[4,64,512]{2,1,0:T(8,128)(2,1)S(1)}, bf16[4,64,512]{2,1,0:T(8,128)(2,1)}, u32[]{:S(2)}) copy-start(bf16[4,64,512]{2,1,0:T(8,128)(2,1)} %get-tuple-element.31) | copy-start | bytes 786436
  203.6 1.1 copy-start.7
  239.2 25.7 %all-to-all-start.1 = ((bf16[4,576,384]{2,1,0:T(8,128)(2,1)}), bf16[4,576,384]{2,1,0:T(8,128)(2,1)S(1)}, u32[]{:S(2)}, u32[]{:S(2)}) async-start(bf16[4,576,384]{2,1,0:T(8,128)(2,1)} %pages.1.refs_8_), calls=%async_computation.1 | async-start | bytes 3538944 | tf_op jit(solution)/shard_map/all_to_all | solution.py:734
  264.9 1.2 copy-start.1
Sparse Core Ops, SparseCore 0:
  114.7 47.5 all-gather.1

commit v3 on v2

--- a/solution.py
+++ b/solution.py
@@ -16,6 +16,7 @@
 RP = 4
 WIDTH = KVL + DR
 HALF = DR // 2
+PART = WIDTH // 2
 CODED = WIDTH + 16
 SHARE = PRE_TOK // 4
 UNIT = 128
@@ -28,6 +29,7 @@
 I16 = jnp.int16
 NT = (((1,), (1,)), ((), ()))
 ROOM = pltpu.CompilerParams(vmem_limit_bytes=60 << 20)
+SOME = pltpu.CompilerParams(vmem_limit_bytes=60 << 20)
 ANY = pl.BlockSpec(memory_space=pl.ANY)
 VMEM = pl.BlockSpec(memory_space=pltpu.VMEM)
 SMEM = pl.BlockSpec(memory_space=pltpu.SMEM)
@@ -367,64 +369,73 @@
             out_specs=pl.BlockSpec((1, UNITS, CODED, UNIT), chunk),
         ),
         out_shape=jax.ShapeDtypeStruct((2, UNITS, CODED, UNIT), I16),
-        compiler_params=ROOM,
+        compiler_params=SOME,
         cost_estimate=COST,
         name="add_on",
     )(rank, own, got, *after)
 
 
-def page_kernel(rank, slot, own_ref, *refs):
-    got_refs, sent_refs, refs = refs[:RP], refs[RP : 2 * RP], refs[2 * RP :]
-    side_refs, (gain_ref, cos_ref, sin_ref), out_ref = refs[:2], refs[2:5], refs[-1]
-    request = pl.program_id(0)
+def page_kernel(requests, rank, slot, own_ref, *refs):
+    count = len(requests)
+    got_refs, sent_refs, refs = refs[:count], refs[count : 2 * count], refs[2 * count :]
+    side_refs, (gain_ref, cos_ref, sin_ref), out_refs = refs[:2], refs[2:5], refs[-2:]
+    step = pl.program_id(0)
 
     def write(u, comp):
-        rows = key_rows(comp, gain_ref[...], cos_ref[u], sin_ref[u])
-        out_ref[0, :, u * UNIT : (u + 1) * UNIT] = rows.astype(BF)
-
-    for r in range(RP):
-
-        @pl.when((request == r) & outer_rank(rank[0]))
-        def _(r=r):
+        rows = key_rows(comp, gain_ref[...], cos_ref[u], sin_ref[u]).astype(BF)
+        for n, ref in enumerate(out_refs):
+            part = rows[n * PART : (n + 1) * PART]
+            ref[0, :, u * UNIT : (u + 1) * UNIT] = part
+
+    for k in range(count):
+
+        @pl.when((step == k) & outer_rank(rank[0]))
+        def _(k=k):
             for u in range(UNITS):
-                write(u, own_ref[u] + decode(got_refs[r][u]))
-
-        @pl.when((request == r) & ~outer_rank(rank[0]))
-        def _(r=r):
+                write(u, own_ref[u] + decode(got_refs[k][u]))
+
+        @pl.when((step == k) & ~outer_rank(rank[0]))
+        def _(k=k):
             for u in range(UNITS):
                 side = side_refs[u > 0][max(u - 1, 0)]
-                write(u, decode(sent_refs[r][u]) + decode(side))
-
-
-def pages_of(rank, slot, own, got, sent, side, gain, cosine, sine, count):
+                write(u, decode(sent_refs[k][u]) + decode(side))
+
+
+def pages_of(requests, rank, slot, own, got, sent, side, gain, cosine, sine, base, count, after):
     first = pl.BlockSpec((None, UNITS, CODED, UNIT), lambda i, *_: (0, 0, 0, 0))
     second = pl.BlockSpec((None, UNITS, CODED, UNIT), lambda i, *_: (1, 0, 0, 0))
     table = pl.BlockSpec((UNITS, HALF, UNIT), lambda i, *_: (0, 0, 0))
-    base = [jnp.zeros((count, WIDTH, SHARE), BF)] if count > RP else []
+    start, total = requests[0], len(requests)
+    got, sent = got[start : start + total], sent[start : start + total]
     return pl.pallas_call(
-        page_kernel,
+        functools.partial(page_kernel, requests),
         grid_spec=pltpu.PrefetchScalarGridSpec(
             num_scalar_prefetch=2,
-            grid=(RP,),
+            grid=(total,),
             in_specs=[
-                pl.BlockSpec((UNITS, None, None, WIDTH, UNIT), lambda i, *_: (0, 0, i, 0, 0)),
-                *([first] * RP),
-                *([second] * RP),
-                pl.BlockSpec((1, None, CODED, UNIT), lambda i, *_: (0, i, 0, 0)),
-                pl.BlockSpec((UNITS - 1, None, CODED, UNIT), lambda i, *_: (0, i, 0, 0)),
+                pl.BlockSpec(
+                    (UNITS, None, None, WIDTH, UNIT), lambda i, *_: (0, 0, i + start, 0, 0)
+                ),
+                *([first] * total),
+                *([second] * total),
+                pl.BlockSpec((1, None, CODED, UNIT), lambda i, *_: (0, i + start, 0, 0)),
+                pl.BlockSpec((UNITS - 1, None, CODED, UNIT), lambda i, *_: (0, i + start, 0, 0)),
                 pl.BlockSpec((KVL, UNIT), lambda i, *_: (0, 0)),
                 table,
                 table,
-                *([ANY] * len(base)),
+                *([ANY] * (len(base) + len(after))),
             ],
-            out_specs=pl.BlockSpec((1, WIDTH, SHARE), lambda i, rank, slot: (slot[i], 0, 0)),
+            out_specs=[
+                pl.BlockSpec((1, PART, SHARE), lambda i, rank, slot: (slot[i + start], 0, 0))
+            ]
+            * 2,
         ),
-        out_shape=jax.ShapeDtypeStruct((count, WIDTH, SHARE), BF),
-        input_output_aliases={8 + 2 * RP: 0} if base else {},
+        out_shape=[jax.ShapeDtypeStruct((count, PART, SHARE), BF)] * 2,
+        input_output_aliases={8 + 2 * total + n: n for n in range(len(base))},
         compiler_params=ROOM,
         cost_estimate=COST,
         name="pages",
-    )(rank, slot, own, *got, *sent, *side, gain, cosine, sine, *base)
+    )(rank, slot, own, *got, *sent, *side, gain, cosine, sine, *base, *after)
 
 
 def query_kernel(lat_ref, up_ref, draft_ref, down_ref, *refs):
@@ -489,24 +500,26 @@
     )(latents, q_up, draft, down_t, *([kv_up] * step), cosine, sine, after)
 
 
-def attend_kernel(rank, q_ref, draft_ref, *refs):
-    own_ref, got_refs, refs = refs[0], refs[1 : 1 + RP], refs[1 + RP :]
+def attend_kernel(requests, rank, q_ref, draft_ref, *refs):
+    count = len(requests)
+    own_ref, got_refs, refs = refs[0], refs[1 : 1 + count], refs[1 + count :]
     column_ref, cos_ref, sin_ref, midcos_ref, midsin_ref, refs = *refs[:5], refs[5:]
     valid_ref, gain_ref, newcos_ref, newsin_ref, refs = *refs[:4], refs[4:]
     out_refs, keys_ref = refs[-5:-1], refs[-1]
-    request = pl.program_id(0)
+    step = pl.program_id(0)
+    request = step + requests[0]
 
     @pl.when(rank[0] == 3)
     def _():
-        for r in range(RP):
-
-            @pl.when(request == r)
-            def _(r=r):
+        for k in range(count):
+
+            @pl.when(step == k)
+            def _(k=k):
                 for i, (cosine, sine) in enumerate(
                     ((cos_ref, sin_ref), (midcos_ref, midsin_ref))
                 ):
                     for u in range(UNITS):
-                        comp = own_ref[u, i] + decode(got_refs[r][i, u])
+                        comp = own_ref[u, i] + decode(got_refs[k][i, u])
                         rows = key_rows(comp, column_ref[...], cosine[u], sine[u])
                         start = (1 - i) * SHARE + u * UNIT
                         keys_ref[:, start : start + UNIT] = rows.astype(BF)
@@ -555,28 +568,30 @@
             ref[0] = result[t * local_rows : (t + 1) * local_rows]
 
 
-def attend(rank, messages, own, got, column, tables, valid, gain, cosine, sine, after):
+def attend(requests, rank, messages, own, got, column, tables, valid, gain, cosine, sine, after):
     new = 2 * RP
     local_rows = (messages.shape[1] - 4 * new) // RP
     last = RP * local_rows // (4 * new)
-    out = jax.ShapeDtypeStruct((RP, local_rows, KVL), BF)
+    start, count = requests[0], len(requests)
+    got = got[start : start + count]
+    out = jax.ShapeDtypeStruct((count, local_rows, KVL), BF)
     whole = lambda i, rank: (0, 0)
     whole3 = lambda i, rank: (0, 0, 0)
     return pl.pallas_call(
-        attend_kernel,
+        functools.partial(attend_kernel, requests),
         grid_spec=pltpu.PrefetchScalarGridSpec(
             num_scalar_prefetch=1,
-            grid=(RP,),
+            grid=(count,),
             in_specs=[
-                pl.BlockSpec((4, local_rows, WIDTH), lambda i, rank: (0, i, 0)),
+                pl.BlockSpec((4, local_rows, WIDTH), lambda i, rank: (0, i + start, 0)),
                 pl.BlockSpec((4, 4 * new, WIDTH), lambda i, rank: (0, last, 0)),
                 pl.BlockSpec(
-                    (UNITS, 2, None, WIDTH, UNIT), lambda i, rank: (0, 0, i, 0, 0)
+                    (UNITS, 2, None, WIDTH, UNIT), lambda i, rank: (0, 0, i + start, 0, 0)
                 ),
-                *([pl.BlockSpec((2, UNITS, CODED, UNIT), lambda i, rank: (0, 0, 0, 0))] * RP),
+                *([pl.BlockSpec((2, UNITS, CODED, UNIT), lambda i, rank: (0, 0, 0, 0))] * count),
                 pl.BlockSpec((KVL, UNIT), whole),
                 *([pl.BlockSpec((UNITS, HALF, UNIT), whole3)] * 4),
-                pl.BlockSpec((1, 1, valid.shape[2]), lambda i, rank: (i, 0, 0)),
+                pl.BlockSpec((1, 1, valid.shape[2]), lambda i, rank: (i + start, 0, 0)),
                 pl.BlockSpec((1, KVL), whole),
                 pl.BlockSpec(cosine.shape, whole),
                 pl.BlockSpec(sine.shape, whole),
@@ -622,6 +637,26 @@
     )(attended, keep, *([kv_up] * step), *after)
 
 
+def route_kernel(slot, answer_ref, *refs):
+    out_ref = refs[-1]
+    out_ref[...] = jnp.zeros_like(out_ref)
+    for r in range(RP):
+        out_ref[slot[r]] = answer_ref[2 * r : 2 * r + 2, :]
+
+
+def route(slot, answer, count, after):
+    width = answer.shape[1]
+    return pl.pallas_call(
+        route_kernel,
+        in_specs=[SMEM, VMEM, *([ANY] * len(after))],
+        out_specs=VMEM,
+        out_shape=jax.ShapeDtypeStruct((count, 2, width), F32),
+        compiler_params=SOME,
+        cost_estimate=COST,
+        name="route",
+    )(slot, answer, *after)
+
+
 def rope_tables(position):
     freq = jnp.exp(-jnp.log(10000.0) * jnp.arange(HALF, dtype=F32) / HALF)
     angle = position.astype(F32)[..., None] * freq
@@ -650,9 +685,10 @@
     down_t = kv_down.T
     inward, across, outward = [(0, 1), (3, 2)], [(1, 2), (2, 1)], [(2, 3), (1, 0)]
 
-    far_sums, inner = [], []
-    for r in range(RP):
-        total, codes = project_far(rank, hidden, down_t, r, far_sums[-1:])
+    far_sums, inner, crossed, sent, outer = [], [], [], [], []
+
+    def send_far(r, after):
+        total, codes = project_far(rank, hidden, down_t, r, after)
         far_sums.append(total)
         inner.append(lax.ppermute(codes, "tp", inward))
 
@@ -667,19 +703,14 @@
         outer.append(lax.ppermute(block, "tp", outward))
         return block
 
-    crossed, sent, outer = [], [], []
-    block = first_hop(0, far_sums[-1:])
-    near_sums, *side = project_near(rank, hidden, down_t, [block])
-    first_hop(1, [near_sums])
-    second_hop(0, [])
-    first_hop(2, [sent[0]])
-    block = second_hop(1, [outer[0]])
+    send_far(0, [])
+    send_far(1, far_sums[:1])
 
     latents = lax.dynamic_slice_in_dim(query_latent, first_req, RP, 0).reshape(RP * 2, QL)
     new_pos = jnp.tile(PRE_TOK + jnp.arange(2, dtype=jnp.int32), RP)
     new_cos, new_sin = rope_tables(new_pos)
     query, terms = queries(
-        latents, q_up, kv_up, draft_hidden, down_t, new_cos, new_sin, block
+        latents, q_up, kv_up, draft_hidden, down_t, new_cos, new_sin, far_sums[1]
     )
     heads = query.shape[0]
     query = query.reshape(heads, RP, 2, WIDTH).transpose(1, 2, 0, 3)
@@ -687,6 +718,15 @@
         [query.reshape(RP * 2 * heads, WIDTH), terms.reshape(8 * RP, WIDTH)], 0
     ).astype(BF)
     messages = lax.all_gather(message, "tp", axis=0)
+
+    block = first_hop(0, [message])
+    send_far(2, [block])
+    near_sums, *side = project_near(rank, hidden, down_t, far_sums[2:])
+    block = first_hop(1, [near_sums])
+    block = second_hop(0, [block])
+    send_far(3, [block])
+    block = first_hop(2, far_sums[3:])
+    block = second_hop(1, [block, messages, outer[0]])
 
     my_segments = lax.dynamic_slice_in_dim(segment_ids, first_req, RP, 0)
     valid = (my_segments == my_segments[:, -1:])[:, PRE_TOK // 2 :].astype(F32)
@@ -698,54 +738,68 @@
         for t in (*rope_tables(z * SHARE + steps), *rope_tables(2 * SHARE + steps))
     ]
 
-    block = first_hop(3, [message, column, valid, *tables])
+    block = first_hop(3, [block, column, valid, *tables])
     side = [lax.ppermute(codes, "tp", inward) for codes in side]
     second_hop(2, [block, outer[1]])
-    second_hop(3, [side[0], outer[2]])
-
-    result = attend(
-        rank,
-        messages,
-        near_sums,
-        outer,
-        column,
-        tables,
-        valid,
-        kv_gain.reshape(1, KVL),
-        new_cos,
-        new_sin,
-        [],
-    )
-    back = [lax.ppermute(result[t], "tp", [(3, t)]) for t in range(3)]
+    block = second_hop(3, [side[0], outer[2]])
+
+    def attend_to(requests, after):
+        result = attend(
+            requests,
+            rank,
+            messages,
+            near_sums,
+            outer,
+            column,
+            tables,
+            valid,
+            kv_gain.reshape(1, KVL),
+            new_cos,
+            new_sin,
+            after,
+        )
+        return result, [lax.ppermute(result[t], "tp", [(3, t)]) for t in range(3)]
 
     my_owners = lax.dynamic_slice_in_dim(owners, first_req, RP, 0)
-    pages = pages_of(
-        rank,
-        my_owners,
-        near_sums,
-        outer,
-        sent,
-        side,
-        column,
-        tables[0],
-        tables[1],
-        pd_count,
-    )
-    cache = lax.all_to_all(pages, "pd", split_axis=0, concat_axis=0, tiled=True)
-    cache = jnp.swapaxes(cache, 1, 2)
-
-    attended = jnp.where(z == 3, result[3], back[0] + back[1] + back[2])
-    attended = attended.reshape(RP, 2, heads, KVL).transpose(2, 0, 1, 3)
+    early, late = tuple(range(RP - 1)), (RP - 1,)
+
+    def pages_to(requests, base, after):
+        return pages_of(
+            requests,
+            rank,
+            my_owners,
+            near_sums,
+            outer,
+            sent,
+            side,
+            column,
+            tables[0],
+            tables[1],
+            base,
+            pd_count,
+            after,
+        )
+
+    results, backs = [None] * 2, [None] * 2
+    results[0], backs[0] = attend_to(early, [block])
+    base = [jnp.zeros((pd_count, PART, SHARE), BF)] * 2 if pd_count > RP else []
+    pages = pages_to(early, base, results[0][:1])
+    results[1], backs[1] = attend_to(late, pages[:1])
+    pages = pages_to(late, pages, [*results[1][:1], *backs[0]])
+    cache = [lax.all_to_all(page, "pd", split_axis=0, concat_axis=0, tiled=True) for page in pages]
+
+    attended = [
+        jnp.where(z == 3, result[3], back[0] + back[1] + back[2])
+        for result, back in zip(results, backs)
+    ]
+    attended = jnp.concatenate(attended, 0).reshape(RP, 2, heads, KVL).transpose(2, 0, 1, 3)
     attended = attended.reshape(heads, RP * 2, KVL).astype(F32)
     my_accepted = lax.dynamic_slice_in_dim(accepted, first_req, RP, 0)
     keep = (jnp.arange(2)[None, :] <= my_accepted[:, None]).astype(F32).reshape(RP * 2, 1)
-    answer = heads_out(attended, jnp.broadcast_to(keep, (RP * 2, DV)), kv_up, [pages])
-    answer = answer.reshape(RP, 2, heads * DV)
-    routing = my_owners[None, :] == jnp.arange(pd_count, dtype=jnp.int32)[:, None]
-    has = jnp.any(routing, axis=1)
-    slots = jnp.sum(routing.astype(jnp.int32) * jnp.arange(RP, dtype=jnp.int32)[None, :], axis=1)
-    placed = jnp.where(has[:, None, None], answer[slots], 0.0).astype(BF)
+    answer = heads_out(attended, jnp.broadcast_to(keep, (RP * 2, DV)), kv_up, pages[:1])
+    placed = route(my_owners, answer, pd_count, cache[:1]).astype(BF)
     placed = lax.all_to_all(placed, "pd", split_axis=0, concat_axis=0, tiled=True)
+    cache = jnp.swapaxes(jnp.concatenate(cache, 1), 1, 2)
     return (placed.reshape(pd_count * 2, heads * DV), cache)
 
 

time: 274 us -> 260 us (0.949)
  waiting for transfers between devices: 99.5 us -> 76.1 us
  blocking collectives: 6.68 us -> 0 us
  starting transfers between devices: 38.6 us -> 44.9 us
  Pallas kernels: 89.3 us -> 95.3 us
    ppermute x4, waiting for transfers between devices: 23.4 us -> 3.94 us  [second_hop(): outer.append(lax.ppermute(block, 'tp', outward))]
    all_to_all x1 -> x3, starting transfers between devices: 3.58 us -> 10.4 us  [the longest x2 7.15 us: local_line(): lax.all_to_all(page, 'pd', split_axis=0, concat_axis=0, tiled=True)]
    all_to_all x1 -> x0, blocking collectives: 6.68 us -> none  [local_line(): lax.all_to_all(placed, 'pd', split_axis=0, concat_axis=0, tiled=True)]
    all_to_all x1 -> x3, waiting for transfers between devices: 21.5 us -> 15.3 us  [the longest x2 12.6 us: local_line(): lax.all_to_all(page, 'pd', split_axis=0, concat_axis=0, tiled=True)]
    pallas_call x2 -> x5, Pallas kernels: 13 us -> 18.9 us  [the longest x2 9.48 us: pages_of(): pl.pallas_call(functools.partial(page_kernel, requests), grid_spec=pltpu....]
    ppermute x4, waiting for transfers between devices: 6.84 us -> 11.2 us  [first_hop(): crossed.append(lax.ppermute(block, 'tp', across))]
    ppermute x7 -> x10, starting transfers between devices: 7.79 us -> 10.4 us  [the longest x6 5.25 us: attend_to(): return (result, [lax.ppermute(result[t], 'tp', [(3, t)]) for t in range(3)])]
    unnamed x41 -> x62, local copies, waits for them, and re-layouts: 9.89 us -> 10.5 us
  transfers between devices with their start and end apart: 19 -> 24, of which waited for: 11 -> 12; matrix products, arithmetic and copies ran while one was open for 4% -> 6% of each run, Pallas kernels for 29% -> 33%
where the time goes in v3:
time: 260 us; the launch traced here: 258 us
  Pallas kernels  95.3 us (37%)
  waiting for transfers between devices  76.1 us (29%)
  starting transfers between devices  44.9 us (17%)
  local copies, waits for them, and re-layouts  17.3 us (7%)
  between operations  14.6 us (6%)
  other arithmetic  9.35 us (4%)
    ppermute x2, waiting for transfers between devices, local_line(): side = [lax.ppermute(codes, 'tp', inward) for codes in side]  27.3 us
    pallas_call x4, Pallas kernels, project_far(): pl.pallas_call(project_far_kernel, grid_spec=pltpu.PrefetchScalarGridSpec...  22.6 us
    pallas_call x8, Pallas kernels, add_on(): pl.pallas_call(add_kernel, grid_spec=pltpu.PrefetchScalarGridSpec(num_sca...  22.4 us
    pallas_call x1, Pallas kernels, queries(): pl.pallas_call(body, grid=(heads // step,), in_specs=[pl.BlockSpec((rows,...  13.8 us
    ppermute x4, waiting for transfers between devices, send_far(): inner.append(lax.ppermute(codes, 'tp', inward))  13.3 us
    pallas_call x1, Pallas kernels, project_near(): pl.pallas_call(project_near_kernel, grid_spec=pltpu.PrefetchScalarGridSpe...  13.1 us
    all_to_all x2, waiting for transfers between devices, local_line(): lax.all_to_all(page, 'pd', split_axis=0, concat_axis=0, tiled=True)  12.6 us
    ppermute x4, waiting for transfers between devices, first_hop(): crossed.append(lax.ppermute(block, 'tp', across))  11.2 us
  transfers between devices with their start and end apart: 24, of which 12 were waited for; matrix products, arithmetic and copies ran while one was open for 6% of the time, Pallas kernels for 33%

profile of v3, /device:TPU:16, one launch (start us, length us, event | category | flops | bytes accessed | tf_op | source)
XLA Modules:
  0.0 257.5 jit_solution(15186694649646192962)
XLA Ops:
  7.2 5.6 %project_far.4 = (f32[2,3,576,128]{3,2,1,0:T(8,128)}, s16[2,3,592,128]{3,2,1,0:T(8,128)(2,1)}) custom-call(s32[1]{0:T(128)} %bitcast.rank, bf16[4,1536,1792]{2,1,0:T(8,128)(2,1)} %bitcast.22, bf16[576,1792]{1,0:T(8,128)(2,1)} %bitcast.27), custom_call_target="tpu_custom_call" | custom-call | flops 1024 | bytes 1024 | tf_op jit(solution)/shard_map/project_far/pallas_call | solution.py:270
  14.2 5.6 %project_far.5 = (f32[2,3,576,128]{3,2,1,0:T(8,128)}, s16[2,3,592,128]{3,2,1,0:T(8,128)(2,1)}) custom-call(s32[1]{0:T(128)} %bitcast.rank, bf16[4,1536,1792]{2,1,0:T(8,128)(2,1)} %bitcast.23, bf16[576,1792]{1,0:T(8,128)(2,1)} %bitcast.28, f32[2,3,576,128]{3,2,1,0:T(8,128)} %get-tuple-element.27.refs_0_.own_ref), custom_call_target="tpu_custom_call" | custom-call | flops 1024 | bytes 1024 | tf_op jit(solution)/shard_map/project_far/pallas_call | solution.py:270
  21.3 13.8 %queries.1 = (f32[32,8,576]{2,1,0:T(8,128)}, f32[4,8,576]{2,1,0:T(8,128)}) custom-call(bf16[8,1536]{1,0:T(8,128)(2,1)} %reshape.163.refs_0_, bf16[1536,6144]{1,0:T(8,128)(2,1)} %refs_1_.2, bf16[8,1792]{1,0:T(8,128)(2,1)} %refs_2_.2, bf16[576,1792]{1,0:T(8,128)(2,1)} %bitcast.29, bf16[512,8192]{1,0:T(8,128)(2,1)} %refs_7_.3, bf16[512,8192]{1,0:T(8,128)(2,1)} %refs_7_.3, ...), custom_call_target="tpu_custom_call" | custom-call | flops 1024 | bytes 1024 | tf_op jit(solution)/shard_map/queries/pallas_call | solution.py:476
  38.0 1.3 collective-permute-start.2
  41.0 2.8 %add_on.8.refs_0_ = s16[2,3,592,128]{3,2,1,0:T(8,128)(2,1)} custom-call(s32[1]{0:T(128)} %bitcast.rank, f32[2,3,576,128]{3,2,1,0:T(8,128)} %get-tuple-element.27.refs_0_.own_ref, s16[2,3,592,128]{3,2,1,0:T(8,128)(2,1)} %copy-done.10, bf16[288,576]{1,0:T(8,128)(2,1)} %pad_maximum_fusion.1.refs_0_), custom_call_target="tpu_custom_call" | custom-call | flops 1024 | bytes 1024 | tf_op jit(solution)/shard_map/add_on/pallas_call | solution.py:359
  43.8 2.3 collective-permute-start.1
  46.1 5.7 %project_far.6 = (f32[2,3,576,128]{3,2,1,0:T(8,128)}, s16[2,3,592,128]{3,2,1,0:T(8,128)(2,1)}) custom-call(s32[1]{0:T(128)} %bitcast.rank, bf16[4,1536,1792]{2,1,0:T(8,128)(2,1)} %bitcast.24, bf16[576,1792]{1,0:T(8,128)(2,1)} %bitcast.30, s16[2,3,592,128]{3,2,1,0:T(8,128)(2,1)} %add_on.8.refs_0_), custom_call_target="tpu_custom_call" | custom-call | flops 1024 | bytes 1024 | tf_op jit(solution)/shard_map/project_far/pallas_call | solution.py:270
  51.9 13.1 %project_near.1 = (f32[3,2,4,576,128]{4,3,2,1,0:T(8,128)}, s16[1,4,592,128]{3,2,1,0:T(8,128)(2,1)}, s16[2,4,592,128]{3,2,1,0:T(8,128)(2,1)}) custom-call(s32[1]{0:T(128)} %bitcast.rank, bf16[4,1536,1792]{2,1,0:T(8,128)(2,1)} %bitcast.25, bf16[576,1792]{1,0:T(8,128)(2,1)} %bitcast.31, f32[2,3,576,128]{3,2,1,0:T(8,128)} %get-tuple-element.32.refs_0_.own_ref), custom_call_target="tpu_custom_call" | custom-call | flops 1024 | bytes 1024 | tf_op jit(solution)/shard_map/project_near/pallas_call | solution.py:313
  66.2 9.9 %collective-permute-done.2.got_ref = s16[2,3,592,128]{3,2,1,0:T(8,128)(2,1)S(1)} collective-permute-done((s16[2,3,592,128]{3,2,1,0:T(8,128)(2,1)}, s16[2,3,592,128]{3,2,1,0:T(8,128)(2,1)S(1)}, u32[]{:S(2)}, u32[]{:S(2)}) %collective-permute-start.2) | collective-permute-done | bytes 909344 | tf_op jit(solution)/shard_map/ppermute | solution.py:693
  77.1 2.8 %add_on.9.refs_0_ = s16[2,3,592,128]{3,2,1,0:T(8,128)(2,1)} custom-call(s32[1]{0:T(128)} %bitcast.rank, f32[2,3,576,128]{3,2,1,0:T(8,128)} %get-tuple-element.28.refs_10_.own_ref, s16[2,3,592,128]{3,2,1,0:T(8,128)(2,1)} %copy-done.14, f32[3,2,4,576,128]{4,3,2,1,0:T(8,128)} %get-tuple-element.33.refs_0_.own_ref), custom_call_target="tpu_custom_call" | custom-call | flops 1024 | bytes 1024 | tf_op jit(solution)/shard_map/add_on/pallas_call | solution.py:359
  79.9 3.5 %collective-permute-start.4 = (s16[2,3,592,128]{3,2,1,0:T(8,128)(2,1)}, s16[2,3,592,128]{3,2,1,0:T(8,128)(2,1)}, u32[]{:S(2)}, u32[]{:S(2)}) collective-permute-start(s16[2,3,592,128]{3,2,1,0:T(8,128)(2,1)} %add_on.9.refs_0_), channel_id=1, source_target_pairs={{4,8},{8,4},{5,9},{9,5},{6,10},{10,6},{7,11},{11,7},{20,24},{24,20... | collective-permute-start | bytes 2727944 | tf_op jit(solution)/shard_map/ppermute | solution.py:697
  83.4 8.3 %collective-permute-done.1.got_ref = s16[2,3,592,128]{3,2,1,0:T(8,128)(2,1)S(1)} collective-permute-done((s16[2,3,592,128]{3,2,1,0:T(8,128)(2,1)}, s16[2,3,592,128]{3,2,1,0:T(8,128)(2,1)S(1)}, u32[]{:S(2)}, u32[]{:S(2)}) %collective-permute-start.1) | collective-permute-done | bytes 909344 | tf_op jit(solution)/shard_map/ppermute | solution.py:697
  92.6 2.8 %add_on.10.refs_0_.refs_3_ = s16[2,3,592,128]{3,2,1,0:T(8,128)(2,1)} custom-call(s32[1]{0:T(128)} %bitcast.rank, f32[3,2,4,576,128]{4,3,2,1,0:T(8,128)} %get-tuple-element.33.refs_0_.own_ref, s16[2,3,592,128]{3,2,1,0:T(8,128)(2,1)} %copy-done.16, s16[2,3,592,128]{3,2,1,0:T(8,128)(2,1)} %add_on.9.refs_0_), custom_call_target="tpu_custom_call" | custom-call | flops 1024 | bytes 1024 | tf_op jit(solution)/shard_map/add_on/pallas_call | solution.py:359
  95.4 1.3 collective-permute-start.3
  96.8 5.7 %project_far.7 = (f32[2,3,576,128]{3,2,1,0:T(8,128)}, s16[2,3,592,128]{3,2,1,0:T(8,128)(2,1)}) custom-call(s32[1]{0:T(128)} %bitcast.rank, bf16[4,1536,1792]{2,1,0:T(8,128)(2,1)} %bitcast.26, bf16[576,1792]{1,0:T(8,128)(2,1)} %bitcast.32, s16[2,3,592,128]{3,2,1,0:T(8,128)(2,1)} %add_on.10.refs_0_.refs_3_), custom_call_target="tpu_custom_call" | custom-call | flops 1024 | bytes 1024 | tf_op jit(solution)/shard_map/project_far/pallas_call | solution.py:270
  103.7 3.1 %collective-permute-done.5.got_ref = s16[2,3,592,128]{3,2,1,0:T(8,128)(2,1)S(1)} collective-permute-done((s16[2,3,592,128]{3,2,1,0:T(8,128)(2,1)}, s16[2,3,592,128]{3,2,1,0:T(8,128)(2,1)S(1)}, u32[]{:S(2)}, u32[]{:S(2)}) %collective-permute-start.5) | collective-permute-done | bytes 909344 | tf_op jit(solution)/shard_map/ppermute | solution.py:693
  107.8 2.8 %add_on.11.refs_0_ = s16[2,3,592,128]{3,2,1,0:T(8,128)(2,1)} custom-call(s32[1]{0:T(128)} %bitcast.rank, f32[2,3,576,128]{3,2,1,0:T(8,128)} %get-tuple-element.32.refs_0_.own_ref, s16[2,3,592,128]{3,2,1,0:T(8,128)(2,1)} %copy-done.13, f32[2,3,576,128]{3,2,1,0:T(8,128)} %get-tuple-element.36.refs_0_.own_ref), custom_call_target="tpu_custom_call" | custom-call | flops 1024 | bytes 1024 | tf_op jit(solution)/shard_map/add_on/pallas_call | solution.py:359
  110.5 2.5 collective-permute-start.7
  114.7 2.8 %add_on.12.refs_0_.refs_4_ = s16[2,3,592,128]{3,2,1,0:T(8,128)(2,1)} custom-call(s32[1]{0:T(128)} %bitcast.rank, f32[3,2,4,576,128]{4,3,2,1,0:T(8,128)} %get-tuple-element.33.refs_0_.own_ref, s16[2,3,592,128]{3,2,1,0:T(8,128)(2,1)} %collective-permute-done.4.got_ref, s16[2,3,592,128]{3,2,1,0:T(8,128)(2,1)} %add_on.11.refs_0_, ...), custom_call_target="tpu_custom_call" | custom-call | flops 1024 | bytes 1024 | tf_op jit(solution)/shard_map/add_on/pallas_call | solution.py:359
  117.5 4.0 %collective-permute-start.6 = (s16[2,3,592,128]{3,2,1,0:T(8,128)(2,1)}, s16[2,3,592,128]{3,2,1,0:T(8,128)(2,1)S(1)}, u32[]{:S(2)}, u32[]{:S(2)}) collective-permute-start(s16[2,3,592,128]{3,2,1,0:T(8,128)(2,1)} %add_on.12.refs_0_.refs_4_), channel_id=1, source_target_pairs={{8,12},{4,0},{9,13},{5,1},{10,14},{6,2},{11,15},{7,3},{24,28},{20,... | collective-permute-start | bytes 2727944 | tf_op jit(solution)/shard_map/ppermute | solution.py:703
  126.2 2.8 %add_on.13.refs_0_ = s16[2,3,592,128]{3,2,1,0:T(8,128)(2,1)} custom-call(s32[1]{0:T(128)} %bitcast.rank, f32[2,3,576,128]{3,2,1,0:T(8,128)} %get-tuple-element.36.refs_0_.own_ref, s16[2,3,592,128]{3,2,1,0:T(8,128)(2,1)} %copy-done.12, s16[2,3,592,128]{3,2,1,0:T(8,128)(2,1)} %add_on.12.refs_0_.refs_4_, ...), custom_call_target="tpu_custom_call" | custom-call | flops 1024 | bytes 1024 | tf_op jit(solution)/shard_map/add_on/pallas_call | solution.py:359
  129.0 2.4 collective-permute-start.10
  131.3 2.9 %collective-permute-done.7.got_ref = s16[2,3,592,128]{3,2,1,0:T(8,128)(2,1)S(1)} collective-permute-done((s16[2,3,592,128]{3,2,1,0:T(8,128)(2,1)}, s16[2,3,592,128]{3,2,1,0:T(8,128)(2,1)S(1)}, u32[]{:S(2)}, u32[]{:S(2)}) %collective-permute-start.7) | collective-permute-done | bytes 909344 | tf_op jit(solution)/shard_map/ppermute | solution.py:697
  134.2 3.3 %collective-permute-done.6.refs_1_.refs_2_ = s16[2,3,592,128]{3,2,1,0:T(8,128)(2,1)S(1)} collective-permute-done((s16[2,3,592,128]{3,2,1,0:T(8,128)(2,1)}, s16[2,3,592,128]{3,2,1,0:T(8,128)(2,1)S(1)}, u32[]{:S(2)}, u32[]{:S(2)}) %collective-permute-start.6) | collective-permute-done | bytes 909344 | tf_op jit(solution)/shard_map/ppermute | solution.py:703
  138.4 2.8 %add_on.14.refs_5_ = s16[2,3,592,128]{3,2,1,0:T(8,128)(2,1)} custom-call(s32[1]{0:T(128)} %bitcast.rank, f32[3,2,4,576,128]{4,3,2,1,0:T(8,128)} %get-tuple-element.33.refs_0_.own_ref, s16[2,3,592,128]{3,2,1,0:T(8,128)(2,1)} %copy-done.11, s16[2,3,592,128]{3,2,1,0:T(8,128)(2,1)} %add_on.13.refs_0_, s16[2,3,592,128]{3,2,1,0:T(8,128)(2,1)} %copy-done.3), custom_call_target="tpu_custom_call" | custom-call | flops 1024 | bytes 1024 | tf_op jit(solution)/shard_map/add_on/pallas_call | solution.py:359
  141.2 4.0 %collective-permute-start.9 = (s16[2,3,592,128]{3,2,1,0:T(8,128)(2,1)}, s16[2,3,592,128]{3,2,1,0:T(8,128)(2,1)S(1)}, u32[]{:S(2)}, u32[]{:S(2)}) collective-permute-start(s16[2,3,592,128]{3,2,1,0:T(8,128)(2,1)} %add_on.14.refs_5_), channel_id=1, source_target_pairs={{8,12},{4,0},{9,13},{5,1},{10,14},{6,2},{11,15},{7,3},{24,28},{20,... | collective-permute-start | bytes 2727944 | tf_op jit(solution)/shard_map/ppermute | solution.py:703
  145.2 1.3 collective-permute-start.11
  146.5 1.3 collective-permute-start.16
  147.8 16.1 %collective-permute-done.11.refs_0_.refs_6_.refs_2_ = s16[1,4,592,128]{3,2,1,0:T(8,128)(2,1)S(1)} collective-permute-done((s16[1,4,592,128]{3,2,1,0:T(8,128)(2,1)}, s16[1,4,592,128]{3,2,1,0:T(8,128)(2,1)S(1)}, u32[]{:S(2)}, u32[]{:S(2)}) %collective-permute-start.11) | collective-permute-done | bytes 606240 | tf_op jit(solution)/shard_map/ppermute | solution.py:742
  166.0 2.8 %add_on.15.refs_13_.refs_1_ = s16[2,3,592,128]{3,2,1,0:T(8,128)(2,1)} custom-call(s32[1]{0:T(128)} %bitcast.rank, f32[3,2,4,576,128]{4,3,2,1,0:T(8,128)} %get-tuple-element.33.refs_0_.own_ref, s16[2,3,592,128]{3,2,1,0:T(8,128)(2,1)} %copy-done.15, s16[1,4,592,128]{3,2,1,0:T(8,128)(2,1)} %copy-done.7, s16[2,3,592,128]{3,2,1,0:T(8,128)(2,1)} %copy-done.4), custom_call_target="tpu_custom_call" | custom-call | flops 1024 | bytes 1024 | tf_op jit(solution)/shard_map/add_on/pallas_call | solution.py:359
  168.8 1.5 collective-permute-start.15
  170.3 5.1 %attend.2 = (bf16[3,64,512]{2,1,0:T(8,128)(2,1)}, bf16[3,64,512]{2,1,0:T(8,128)(2,1)}, bf16[3,64,512]{2,1,0:T(8,128)(2,1)}, bf16[3,64,512]{2,1,0:T(8,128)(2,1)}) custom-call(s32[1]{0:T(128)} %bitcast.rank, bf16[4,288,576]{2,1,0:T(8,128)(2,1)} %all-gather.2.cloned.1.call-done.refs_1_.q_ref.draft_ref, ...), custom_call_target="tpu_custom_call" | custom-call | flops 1024 | bytes 1024 | tf_op jit(solution)/shard_map/attend/pallas_call | solution.py:580
  176.8 1.3 collective-permute-start.14
  178.8 11.1 %collective-permute-done.16.refs_7_.refs_3_ = s16[2,4,592,128]{3,2,1,0:T(8,128)(2,1)S(1)} collective-permute-done((s16[2,4,592,128]{3,2,1,0:T(8,128)(2,1)}, s16[2,4,592,128]{3,2,1,0:T(8,128)(2,1)S(1)}, u32[]{:S(2)}, u32[]{:S(2)}) %collective-permute-start.16) | collective-permute-done | bytes 1212448 | tf_op jit(solution)/shard_map/ppermute | solution.py:742
  190.9 6.0 %pages.2 = (bf16[4,288,384]{2,1,0:T(8,128)(2,1)}, bf16[4,288,384]{2,1,0:T(8,128)(2,1)}) custom-call(s32[1]{0:T(128)} %bitcast.rank, s32[4]{0:T(128)} %dynamic_slice.12.slot, f32[3,2,4,576,128]{4,3,2,1,0:T(8,128)} %get-tuple-element.33.refs_0_.own_ref, s16[2,3,592,128]{3,2,1,0:T(8,128)(2,1)} %copy-done.2, s16[2,3,592,128]{3,2,1,0:T(8,128)(2,1)} %copy-done.3, ...), custom_call_target="tpu_custom_call" | custom-call | flops 1024 | bytes 1024 | tf_op jit(solution)/shard_map/pages/pallas_call | solution.py:410
  197.8 2.7 %attend.3 = (bf16[1,64,512]{2,1,0:T(8,128)(2,1)}, bf16[1,64,512]{2,1,0:T(8,128)(2,1)}, bf16[1,64,512]{2,1,0:T(8,128)(2,1)}, bf16[1,64,512]{2,1,0:T(8,128)(2,1)}) custom-call(s32[1]{0:T(128)} %bitcast.rank, bf16[4,288,576]{2,1,0:T(8,128)(2,1)} %all-gather.2.cloned.1.call-done.refs_1_.q_ref.draft_ref, ...), custom_call_target="tpu_custom_call" | custom-call | flops 1024 | bytes 1024 | tf_op jit(solution)/shard_map/attend/pallas_call | solution.py:580
  201.3 3.5 %pages.3 = (bf16[4,288,384]{2,1,0:T(8,128)(2,1)}, bf16[4,288,384]{2,1,0:T(8,128)(2,1)}) custom-call(s32[1]{0:T(128)} %bitcast.rank, s32[4]{0:T(128)} %dynamic_slice.12.slot, f32[3,2,4,576,128]{4,3,2,1,0:T(8,128)} %get-tuple-element.33.refs_0_.own_ref, s16[2,3,592,128]{3,2,1,0:T(8,128)(2,1)} %copy-done.9, ...), custom_call_target="tpu_custom_call", output_to_operand_aliasing={{0}: (10, {}), {1}: (11, {})} | custom-call | flops 1024 | bytes 1024 | tf_op jit(solution)/shard_map/pages/pallas_call | solution.py:410
  204.9 3.6 %all-to-all-start = ((bf16[4,288,384]{2,1,0:T(8,128)(2,1)}), bf16[4,288,384]{2,1,0:T(8,128)(2,1)S(1)}, u32[]{:S(2)}, u32[]{:S(2)}) async-start(bf16[4,288,384]{2,1,0:T(8,128)(2,1)} %get-tuple-element.50.refs_8_), calls=%async_computation | async-start | bytes 1769472 | tf_op jit(solution)/shard_map/all_to_all | solution.py:789
  208.6 12.6 %all-to-all-done.refs_0_ = bf16[4,288,384]{2,1,0:T(8,128)(2,1)S(1)} async-done(((bf16[4,288,384]{2,1,0:T(8,128)(2,1)}), bf16[4,288,384]{2,1,0:T(8,128)(2,1)S(1)}, u32[]{:S(2)}, u32[]{:S(2)}) %all-to-all-start) | async-done | bytes 884768 | tf_op jit(solution)/shard_map/all_to_all | solution.py:789
  221.2 3.5 %all-to-all-start.2 = ((bf16[4,288,384]{2,1,0:T(8,128)(2,1)}), bf16[4,288,384]{2,1,0:T(8,128)(2,1)S(1)}, u32[]{:S(2)}, u32[]{:S(2)}) async-start(bf16[4,288,384]{2,1,0:T(8,128)(2,1)} %get-tuple-element.51), calls=%async_computation.2 | async-start | bytes 1769472 | tf_op jit(solution)/shard_map/all_to_all | solution.py:789
  226.2 1.3 collective-permute-start.19
  227.6 5.2 %collective-permute-done.19 = bf16[1,64,512]{2,1,0:T(8,128)(2,1)S(1)} collective-permute-done((bf16[1,64,512]{2,1,0:T(8,128)(2,1)S(1)}, bf16[1,64,512]{2,1,0:T(8,128)(2,1)S(1)}, u32[]{:S(2)}, u32[]{:S(2)}) %collective-permute-start.19) | collective-permute-done | bytes 65568 | tf_op jit(solution)/shard_map/ppermute | solution.py:761
  235.0 4.4 %heads_out.1.answer_ref = f32[8,4096]{1,0:T(8,128)} custom-call(f32[32,8,512]{2,1,0:T(8,128)} %reshape.177.o_ref, f32[8,128]{1,0:T(8,128)} %broadcast_in_dim.5.keep_ref, bf16[512,8192]{1,0:T(8,128)(2,1)} %refs_7_.3, bf16[512,8192]{1,0:T(8,128)(2,1)} %refs_7_.3, bf16[512,8192]{1,0:T(8,128)(2,1)} %refs_7_.3, bf16[512,8192]{1,0:T(8,128)(2,1)} %refs_7_.3, ...), custom_call_target="tpu_custom_call" | custom-call | flops 1024 | bytes 1024 | tf_op jit(solution)/shard_map/heads_out/pallas_call | solution.py:623
  239.4 1.7 route.1
  241.1 1.6 convert_element_type.89
  242.7 3.3 %all-to-all-start.1 = ((bf16[4,2,4096]{2,1,0:T(2,128)(2,1)}), bf16[4,2,4096]{2,1,0:T(2,128)(2,1)S(1)}, u32[]{:S(2)}, u32[]{:S(2)}) async-start(bf16[4,2,4096]{2,1,0:T(2,128)(2,1)} %convert_element_type.89), calls=%async_computation.1 | async-start | bytes 131072 | tf_op jit(solution)/shard_map/all_to_all | solution.py:801
  246.0 1.4 maximum_bitcast_fusion
  247.4 2.7 %all-to-all-done.1 = bf16[4,2,4096]{2,1,0:T(2,128)(2,1)S(1)} async-done(((bf16[4,2,4096]{2,1,0:T(2,128)(2,1)}), bf16[4,2,4096]{2,1,0:T(2,128)(2,1)S(1)}, u32[]{:S(2)}, u32[]{:S(2)}) %all-to-all-start.1) | async-done | bytes 65568 | tf_op jit(solution)/shard_map/all_to_all | solution.py:801
  (115 shorter events, 31.2 us)
Async XLA Ops:
  7.2 7.0 %copy-start = (bf16[16,2,1536]{2,1,0:T(2,128)(2,1)S(1)}, bf16[16,2,1536]{2,1,0:T(2,128)(2,1)}, u32[]{:S(2)}) copy-start(bf16[16,2,1536]{2,1,0:T(2,128)(2,1)} %param.14) | copy-start | bytes 294916
  7.2 105.9 %all-gather.2.cloned.1.call-start = ((), (), s32[]{:S(2)}) async-start(), calls=%async_computation.3 | async-start | bytes 1843200 | tf_op jit(solution)/shard_map/all_gather | solution.py:720
  12.8 27.2 %collective-permute-start = (s16[2,3,592,128]{3,2,1,0:T(8,128)(2,1)}, s16[2,3,592,128]{3,2,1,0:T(8,128)(2,1)S(1)}, u32[]{:S(2)}, u32[]{:S(2)}) collective-permute-start(s16[2,3,592,128]{3,2,1,0:T(8,128)(2,1)} %get-tuple-element.31), channel_id=1, source_target_pairs={{0,4},{12,8},{1,5},{13,9},{2,6},{14,10},{3,7},{15,11},{16,20},{28,... | collective-permute-start | bytes 2727944 | tf_op jit(solution)/shard_map/ppermute | solution.py:693
  38.0 38.1 %collective-permute-start.2 = (s16[2,3,592,128]{3,2,1,0:T(8,128)(2,1)}, s16[2,3,592,128]{3,2,1,0:T(8,128)(2,1)S(1)}, u32[]{:S(2)}, u32[]{:S(2)}) collective-permute-start(s16[2,3,592,128]{3,2,1,0:T(8,128)(2,1)} %get-tuple-element.34), channel_id=1, source_target_pairs={{0,4},{12,8},{1,5},{13,9},{2,6},{14,10},{3,7},{15,11},{16,20},{28,... | collective-permute-start | bytes 2727944 | tf_op jit(solution)/shard_map/ppermute | solution.py:693
  43.8 47.9 %collective-permute-start.1 = (s16[2,3,592,128]{3,2,1,0:T(8,128)(2,1)}, s16[2,3,592,128]{3,2,1,0:T(8,128)(2,1)S(1)}, u32[]{:S(2)}, u32[]{:S(2)}) collective-permute-start(s16[2,3,592,128]{3,2,1,0:T(8,128)(2,1)} %add_on.8.refs_0_), channel_id=1, source_target_pairs={{4,8},{8,4},{5,9},{9,5},{6,10},{10,6},{7,11},{11,7},{20,24},{24,20... | collective-permute-start | bytes 2727944 | tf_op jit(solution)/shard_map/ppermute | solution.py:697
  64.9 41.9 %collective-permute-start.5 = (s16[2,3,592,128]{3,2,1,0:T(8,128)(2,1)}, s16[2,3,592,128]{3,2,1,0:T(8,128)(2,1)S(1)}, u32[]{:S(2)}, u32[]{:S(2)}) collective-permute-start(s16[2,3,592,128]{3,2,1,0:T(8,128)(2,1)} %get-tuple-element.35), channel_id=1, source_target_pairs={{0,4},{12,8},{1,5},{13,9},{2,6},{14,10},{3,7},{15,11},{16,20},{28,... | collective-permute-start | bytes 2727944 | tf_op jit(solution)/shard_map/ppermute | solution.py:693
  76.1 1.0 copy-start.14
  79.9 33.1 %collective-permute-start.4 = (s16[2,3,592,128]{3,2,1,0:T(8,128)(2,1)}, s16[2,3,592,128]{3,2,1,0:T(8,128)(2,1)}, u32[]{:S(2)}, u32[]{:S(2)}) collective-permute-start(s16[2,3,592,128]{3,2,1,0:T(8,128)(2,1)} %add_on.9.refs_0_), channel_id=1, source_target_pairs={{4,8},{8,4},{5,9},{9,5},{6,10},{10,6},{7,11},{11,7},{20,24},{24,20... | collective-permute-start | bytes 2727944 | tf_op jit(solution)/shard_map/ppermute | solution.py:697
  91.6 1.0 copy-start.16
  95.4 18.3 %collective-permute-start.3 = (s16[2,3,592,128]{3,2,1,0:T(8,128)(2,1)}, s16[2,3,592,128]{3,2,1,0:T(8,128)(2,1)S(1)}, u32[]{:S(2)}, u32[]{:S(2)}) collective-permute-start(s16[2,3,592,128]{3,2,1,0:T(8,128)(2,1)} %add_on.10.refs_0_.refs_3_), channel_id=1, source_target_pairs={{8,12},{4,0},{9,13},{5,1},{10,14},{6,2},{11,15},{7,3},{24,28},{20,... | collective-permute-start | bytes 2727944 | tf_op jit(solution)/shard_map/ppermute | solution.py:703
  102.5 22.7 %collective-permute-start.8 = (s16[2,3,592,128]{3,2,1,0:T(8,128)(2,1)}, s16[2,3,592,128]{3,2,1,0:T(8,128)(2,1)S(1)}, u32[]{:S(2)}, u32[]{:S(2)}) collective-permute-start(s16[2,3,592,128]{3,2,1,0:T(8,128)(2,1)} %get-tuple-element.37), channel_id=1, source_target_pairs={{0,4},{12,8},{1,5},{13,9},{2,6},{14,10},{3,7},{15,11},{16,20},{28,... | collective-permute-start | bytes 2727944 | tf_op jit(solution)/shard_map/ppermute | solution.py:693
  106.8 0.9 copy-start.13
  110.5 14.6 %copy-start.26 = (f32[512]{0:T(512)S(1)}, f32[512]{0:T(512)}, u32[]{:S(2)}) copy-start(f32[512]{0:T(512)} %param.13) | copy-start | bytes 6148
  110.5 23.7 %collective-permute-start.7 = (s16[2,3,592,128]{3,2,1,0:T(8,128)(2,1)}, s16[2,3,592,128]{3,2,1,0:T(8,128)(2,1)S(1)}, u32[]{:S(2)}, u32[]{:S(2)}) collective-permute-start(s16[2,3,592,128]{3,2,1,0:T(8,128)(2,1)} %add_on.11.refs_0_), channel_id=1, source_target_pairs={{4,8},{8,4},{5,9},{9,5},{6,10},{10,6},{7,11},{11,7},{20,24},{24,20... | collective-permute-start | bytes 2727944 | tf_op jit(solution)/shard_map/ppermute | solution.py:697
  117.5 20.0 %collective-permute-start.6 = (s16[2,3,592,128]{3,2,1,0:T(8,128)(2,1)}, s16[2,3,592,128]{3,2,1,0:T(8,128)(2,1)S(1)}, u32[]{:S(2)}, u32[]{:S(2)}) collective-permute-start(s16[2,3,592,128]{3,2,1,0:T(8,128)(2,1)} %add_on.12.refs_0_.refs_4_), channel_id=1, source_target_pairs={{8,12},{4,0},{9,13},{5,1},{10,14},{6,2},{11,15},{7,3},{24,28},{20,... | collective-permute-start | bytes 2727944 | tf_op jit(solution)/shard_map/ppermute | solution.py:703
  125.2 1.0 copy-start.12
  129.0 35.0 %collective-permute-start.10 = (s16[2,3,592,128]{3,2,1,0:T(8,128)(2,1)}, s16[2,3,592,128]{3,2,1,0:T(8,128)(2,1)S(1)}, u32[]{:S(2)}, u32[]{:S(2)}) collective-permute-start(s16[2,3,592,128]{3,2,1,0:T(8,128)(2,1)} %add_on.13.refs_0_), channel_id=1, source_target_pairs={{4,8},{8,4},{5,9},{9,5},{6,10},{10,6},{7,11},{11,7},{20,24},{24,20... | collective-permute-start | bytes 2727944 | tf_op jit(solution)/shard_map/ppermute | solution.py:697
  134.2 3.3 %copy-start.11 = (s16[2,3,592,128]{3,2,1,0:T(8,128)(2,1)}, s16[2,3,592,128]{3,2,1,0:T(8,128)(2,1)S(1)}, u32[]{:S(2)}) copy-start(s16[2,3,592,128]{3,2,1,0:T(8,128)(2,1)S(1)} %collective-permute-done.7.got_ref) | copy-start | bytes 2727940
  137.5 0.9 copy-start.3
  141.2 22.7 %collective-permute-start.9 = (s16[2,3,592,128]{3,2,1,0:T(8,128)(2,1)}, s16[2,3,592,128]{3,2,1,0:T(8,128)(2,1)S(1)}, u32[]{:S(2)}, u32[]{:S(2)}) collective-permute-start(s16[2,3,592,128]{3,2,1,0:T(8,128)(2,1)} %add_on.14.refs_5_), channel_id=1, source_target_pairs={{8,12},{4,0},{9,13},{5,1},{10,14},{6,2},{11,15},{7,3},{24,28},{20,... | collective-permute-start | bytes 2727944 | tf_op jit(solution)/shard_map/ppermute | solution.py:703
  145.2 18.7 %collective-permute-start.11 = (s16[1,4,592,128]{3,2,1,0:T(8,128)(2,1)}, s16[1,4,592,128]{3,2,1,0:T(8,128)(2,1)S(1)}, u32[]{:S(2)}, u32[]{:S(2)}) collective-permute-start(s16[1,4,592,128]{3,2,1,0:T(8,128)(2,1)} %get-tuple-element.38), channel_id=1, source_target_pairs={{0,4},{12,8},{1,5},{13,9},{2,6},{14,10},{3,7},{15,11},{16,20},{28,... | collective-permute-start | bytes 1818632 | tf_op jit(solution)/shard_map/ppermute | solution.py:742
  146.5 43.4 %collective-permute-start.16 = (s16[2,4,592,128]{3,2,1,0:T(8,128)(2,1)}, s16[2,4,592,128]{3,2,1,0:T(8,128)(2,1)S(1)}, u32[]{:S(2)}, u32[]{:S(2)}) collective-permute-start(s16[2,4,592,128]{3,2,1,0:T(8,128)(2,1)} %get-tuple-element.43), channel_id=1, source_target_pairs={{0,4},{12,8},{1,5},{13,9},{2,6},{14,10},{3,7},{15,11},{16,20},{28,... | collective-permute-start | bytes 3637256 | tf_op jit(solution)/shard_map/ppermute | solution.py:742
  163.9 1.1 copy-start.15
  165.0 1.0 copy-start.4
  168.8 28.1 %collective-permute-start.15 = (s16[2,3,592,128]{3,2,1,0:T(8,128)(2,1)}, s16[2,3,592,128]{3,2,1,0:T(8,128)(2,1)S(1)}, u32[]{:S(2)}, u32[]{:S(2)}) collective-permute-start(s16[2,3,592,128]{3,2,1,0:T(8,128)(2,1)} %add_on.15.refs_13_.refs_1_), channel_id=1, source_target_pairs={{8,12},{4,0},{9,13},{5,1},{10,14},{6,2},{11,15},{7,3},{24,28},{20,... | collective-permute-start | bytes 2727944 | tf_op jit(solution)/shard_map/ppermute | solution.py:703
  170.3 7.8 %copy-start.29 = (s32[16]{0:T(128)S(1)}, s32[16]{0:T(128)}, u32[]{:S(2)}) copy-start(s32[16]{0:T(128)} %param.17) | copy-start | bytes 196
  175.5 25.0 %collective-permute-start.12 = (bf16[3,64,512]{2,1,0:T(8,128)(2,1)}, bf16[3,64,512]{2,1,0:T(8,128)(2,1)S(1)}, u32[]{:S(2)}, u32[]{:S(2)}) collective-permute-start(bf16[3,64,512]{2,1,0:T(8,128)(2,1)} %get-tuple-element.40.refs_11_), channel_id=1, source_target_pairs={{12,0},{13,1},{14,2},{15,3},{28,16},{29,17},{30,18},{31,19}} | collective-permute-start | bytes 589832 | tf_op jit(solution)/shard_map/ppermute | solution.py:761
  176.1 24.4 %collective-permute-start.13 = (bf16[3,64,512]{2,1,0:T(8,128)(2,1)}, bf16[3,64,512]{2,1,0:T(8,128)(2,1)S(1)}, u32[]{:S(2)}, u32[]{:S(2)}) collective-permute-start(bf16[3,64,512]{2,1,0:T(8,128)(2,1)} %get-tuple-element.41), channel_id=1, source_target_pairs={{12,4},{13,5},{14,6},{15,7},{28,20},{29,21},{30,22},{31,23}} | collective-permute-start | bytes 589832 | tf_op jit(solution)/shard_map/ppermute | solution.py:761
  176.8 23.7 %collective-permute-start.14 = (bf16[3,64,512]{2,1,0:T(8,128)(2,1)}, bf16[3,64,512]{2,1,0:T(8,128)(2,1)S(1)}, u32[]{:S(2)}, u32[]{:S(2)}) collective-permute-start(bf16[3,64,512]{2,1,0:T(8,128)(2,1)} %get-tuple-element.42), channel_id=1, source_target_pairs={{12,8},{13,9},{14,10},{15,11},{28,24},{29,25},{30,26},{31,27}} | collective-permute-start | bytes 589832 | tf_op jit(solution)/shard_map/ppermute | solution.py:761
  189.9 1.0 copy-start.8
  204.8 3.7 %copy-start.30 = (s32[16]{0:T(128)S(1)}, s32[16]{0:T(128)}, u32[]{:S(2)}) copy-start(s32[16]{0:T(128)} %param.19) | copy-start | bytes 196
  204.8 20.1 %copy-start.24 = (bf16[1,64,512]{2,1,0:T(8,128)(2,1)S(1)}, bf16[1,64,512]{2,1,0:T(8,128)(2,1)}, u32[]{:S(2)}) copy-start(bf16[1,64,512]{2,1,0:T(8,128)(2,1)} %get-tuple-element.46.refs_9_) | copy-start | bytes 196612
  204.8 20.7 %copy-start.28 = (bf16[1,64,512]{2,1,0:T(8,128)(2,1)S(1)}, bf16[1,64,512]{2,1,0:T(8,128)(2,1)}, u32[]{:S(2)}) copy-start(bf16[1,64,512]{2,1,0:T(8,128)(2,1)} %get-tuple-element.47) | copy-start | bytes 196612
  204.8 21.4 %copy-start.27 = (bf16[1,64,512]{2,1,0:T(8,128)(2,1)S(1)}, bf16[1,64,512]{2,1,0:T(8,128)(2,1)}, u32[]{:S(2)}) copy-start(bf16[1,64,512]{2,1,0:T(8,128)(2,1)} %get-tuple-element.48) | copy-start | bytes 196612
  204.8 22.7 %copy-start.18 = (bf16[3,64,512]{2,1,0:T(8,128)(2,1)S(1)}, bf16[3,64,512]{2,1,0:T(8,128)(2,1)}, u32[]{:S(2)}) copy-start(bf16[3,64,512]{2,1,0:T(8,128)(2,1)} %copy-done.17) | copy-start | bytes 589828
  204.8 22.7 %copy-start.20 = (bf16[3,64,512]{2,1,0:T(8,128)(2,1)S(1)}, bf16[3,64,512]{2,1,0:T(8,128)(2,1)}, u32[]{:S(2)}) copy-start(bf16[3,64,512]{2,1,0:T(8,128)(2,1)} %copy-done.19) | copy-start | bytes 589828
  204.8 22.7 %copy-start.22 = (bf16[3,64,512]{2,1,0:T(8,128)(2,1)S(1)}, bf16[3,64,512]{2,1,0:T(8,128)(2,1)}, u32[]{:S(2)}) copy-start(bf16[3,64,512]{2,1,0:T(8,128)(2,1)} %copy-done.21) | copy-start | bytes 589828
  204.8 22.7 %copy-start.23 = (bf16[3,64,512]{2,1,0:T(8,128)(2,1)S(1)}, bf16[3,64,512]{2,1,0:T(8,128)(2,1)}, u32[]{:S(2)}) copy-start(bf16[3,64,512]{2,1,0:T(8,128)(2,1)} %get-tuple-element.39) | copy-start | bytes 589828
  204.9 16.3 %all-to-all-start = ((bf16[4,288,384]{2,1,0:T(8,128)(2,1)}), bf16[4,288,384]{2,1,0:T(8,128)(2,1)S(1)}, u32[]{:S(2)}, u32[]{:S(2)}) async-start(bf16[4,288,384]{2,1,0:T(8,128)(2,1)} %get-tuple-element.50.refs_8_), calls=%async_computation | async-start | bytes 1769472 | tf_op jit(solution)/shard_map/all_to_all | solution.py:789
  208.5 24.3 %copy-start.25 = (bf16[1,64,512]{2,1,0:T(8,128)(2,1)S(1)}, bf16[1,64,512]{2,1,0:T(8,128)(2,1)}, u32[]{:S(2)}) copy-start(bf16[1,64,512]{2,1,0:T(8,128)(2,1)} %get-tuple-element.45) | copy-start | bytes 196612
  221.2 11.7 %copy-start.5 = (bf16[4,288,384]{2,1,0:T(8,128)(2,1)}, bf16[4,288,384]{2,1,0:T(8,128)(2,1)S(1)}, u32[]{:S(2)}) copy-start(bf16[4,288,384]{2,1,0:T(8,128)(2,1)S(1)} %all-to-all-done.refs_0_) | copy-start | bytes 2654212
  221.2 21.5 %all-to-all-start.2 = ((bf16[4,288,384]{2,1,0:T(8,128)(2,1)}), bf16[4,288,384]{2,1,0:T(8,128)(2,1)S(1)}, u32[]{:S(2)}, u32[]{:S(2)}) async-start(bf16[4,288,384]{2,1,0:T(8,128)(2,1)} %get-tuple-element.51), calls=%async_computation.2 | async-start | bytes 1769472 | tf_op jit(solution)/shard_map/all_to_all | solution.py:789
  224.8 2.7 %collective-permute-start.17 = (bf16[1,64,512]{2,1,0:T(8,128)(2,1)S(1)}, bf16[1,64,512]{2,1,0:T(8,128)(2,1)S(1)}, u32[]{:S(2)}, u32[]{:S(2)}) collective-permute-start(bf16[1,64,512]{2,1,0:T(8,128)(2,1)S(1)} %copy-done.24), channel_id=1, source_target_pairs={{12,0},{13,1},{14,2},{15,3},{28,16},{29,17},{30,18},{31,19}} | collective-permute-start | bytes 196616 | tf_op jit(solution)/shard_map/ppermute | solution.py:761
  225.5 2.1 collective-permute-start.18
  226.2 6.6 %collective-permute-start.19 = (bf16[1,64,512]{2,1,0:T(8,128)(2,1)S(1)}, bf16[1,64,512]{2,1,0:T(8,128)(2,1)S(1)}, u32[]{:S(2)}, u32[]{:S(2)}) collective-permute-start(bf16[1,64,512]{2,1,0:T(8,128)(2,1)S(1)} %copy-done.27), channel_id=1, source_target_pairs={{12,8},{13,9},{14,10},{15,11},{28,24},{29,25},{30,26},{31,27}} | collective-permute-start | bytes 196616 | tf_op jit(solution)/shard_map/ppermute | solution.py:761
  239.4 6.6 %copy-start.6 = (bf16[4,288,384]{2,1,0:T(8,128)(2,1)S(1)}, bf16[4,288,384]{2,1,0:T(8,128)(2,1)}, u32[]{:S(2)}) copy-start(bf16[4,288,384]{2,1,0:T(8,128)(2,1)} %copy-done.5) | copy-start | bytes 2654212
  242.7 7.4 %all-to-all-start.1 = ((bf16[4,2,4096]{2,1,0:T(2,128)(2,1)}), bf16[4,2,4096]{2,1,0:T(2,128)(2,1)S(1)}, u32[]{:S(2)}, u32[]{:S(2)}) async-start(bf16[4,2,4096]{2,1,0:T(2,128)(2,1)} %convert_element_type.89), calls=%async_computation.1 | async-start | bytes 131072 | tf_op jit(solution)/shard_map/all_to_all | solution.py:801
  246.0 4.7 %copy-start.1 = (bf16[16,2,1536]{2,1,0:T(2,128)(2,1)S(1)}, bf16[16,2,1536]{2,1,0:T(2,128)(2,1)}, u32[]{:S(2)}) copy-start(bf16[16,2,1536]{2,1,0:T(2,128)(2,1)} %param.14) | copy-start | bytes 294916
  (7 other events, 5.8 us)
Sparse Core Ops, SparseCore 0:
  38.1 60.7 all-gather.1

commit v4 on v3

--- a/solution.py
+++ b/solution.py
@@ -274,7 +274,7 @@
             grid=(2,),
             in_specs=[
                 pl.BlockSpec((1, SHARE, depth), lambda i, rank: (request, far(rank[0], i), 0)),
-                pl.BlockSpec((WIDTH, depth), lambda i, rank: (0, 0)),
+                VMEM,
                 *([ANY] * len(after)),
             ],
             out_specs=[
@@ -319,7 +319,7 @@
                 pl.BlockSpec(
                     (RP, UNIT, depth), lambda u, i, rank: (0, near(rank[0], i) * UNITS + u, 0)
                 ),
-                pl.BlockSpec((WIDTH, depth), lambda u, i, rank: (0, 0)),
+                VMEM,
                 *([ANY] * len(after)),
             ],
             out_specs=[
@@ -375,15 +375,16 @@
     )(rank, own, got, *after)
 
 
-def page_kernel(requests, rank, slot, own_ref, *refs):
+def page_kernel(requests, halves, rank, slot, own_ref, *refs):
     count = len(requests)
     got_refs, sent_refs, refs = refs[:count], refs[count : 2 * count], refs[2 * count :]
-    side_refs, (gain_ref, cos_ref, sin_ref), out_refs = refs[:2], refs[2:5], refs[-2:]
+    side_refs, (gain_ref, cos_ref, sin_ref) = refs[:2], refs[2:5]
+    out_refs = refs[-len(halves) :]
     step = pl.program_id(0)
 
     def write(u, comp):
         rows = key_rows(comp, gain_ref[...], cos_ref[u], sin_ref[u]).astype(BF)
-        for n, ref in enumerate(out_refs):
+        for n, ref in zip(halves, out_refs):
             part = rows[n * PART : (n + 1) * PART]
             ref[0, :, u * UNIT : (u + 1) * UNIT] = part
 
@@ -401,14 +402,14 @@
                 write(u, decode(sent_refs[k][u]) + decode(side))
 
 
-def pages_of(requests, rank, slot, own, got, sent, side, gain, cosine, sine, base, count, after):
+def pages_of(requests, halves, rank, slot, own, got, sent, side, gain, cosine, sine, base, count, after):
     first = pl.BlockSpec((None, UNITS, CODED, UNIT), lambda i, *_: (0, 0, 0, 0))
     second = pl.BlockSpec((None, UNITS, CODED, UNIT), lambda i, *_: (1, 0, 0, 0))
     table = pl.BlockSpec((UNITS, HALF, UNIT), lambda i, *_: (0, 0, 0))
     start, total = requests[0], len(requests)
     got, sent = got[start : start + total], sent[start : start + total]
     return pl.pallas_call(
-        functools.partial(page_kernel, requests),
+        functools.partial(page_kernel, requests, halves),
         grid_spec=pltpu.PrefetchScalarGridSpec(
             num_scalar_prefetch=2,
             grid=(total,),
@@ -428,9 +429,9 @@
             out_specs=[
                 pl.BlockSpec((1, PART, SHARE), lambda i, rank, slot: (slot[i + start], 0, 0))
             ]
-            * 2,
+            * len(halves),
         ),
-        out_shape=[jax.ShapeDtypeStruct((count, PART, SHARE), BF)] * 2,
+        out_shape=[jax.ShapeDtypeStruct((count, PART, SHARE), BF)] * len(halves),
         input_output_aliases={8 + 2 * total + n: n for n in range(len(base))},
         compiler_params=ROOM,
         cost_estimate=COST,
@@ -500,8 +501,9 @@
     )(latents, q_up, draft, down_t, *([kv_up] * step), cosine, sine, after)
 
 
-def attend_kernel(requests, rank, q_ref, draft_ref, *refs):
+def attend_kernel(requests, rank, *refs):
     count = len(requests)
+    q_refs, draft_refs, refs = refs[:4], refs[4:8], refs[8:]
     own_ref, got_refs, refs = refs[0], refs[1 : 1 + count], refs[1 + count :]
     column_ref, cos_ref, sin_ref, midcos_ref, midsin_ref, refs = *refs[:5], refs[5:]
     valid_ref, gain_ref, newcos_ref, newsin_ref, refs = *refs[:4], refs[4:]
@@ -528,8 +530,8 @@
         local_rows = out_refs[0].shape[1]
         new = 2 * RP
         comp = 0.0
-        for t in range(4):
-            terms = draft_ref[t].astype(F32)
+        for ref in draft_refs:
+            terms = ref[...].astype(F32)
             comp = comp + (terms[0:new] + terms[new : 2 * new] + terms[2 * new : 3 * new])
         lat = comp[:, :KVL]
         norm = lax.rsqrt(jnp.mean(lat * lat, axis=-1, keepdims=True) + 1e-06)
@@ -545,7 +547,7 @@
             1,
         )
         drafts = jnp.concatenate([drafts, jnp.zeros((UNIT - new, WIDTH), F32)], 0).astype(BF)
-        query = jnp.concatenate([q_ref[t] for t in range(4)], 0)
+        query = jnp.concatenate([ref[...] for ref in q_refs], 0)
         scores = jnp.dot(query, keys_ref[...], preferred_element_type=F32) * scale
         scores = jnp.where(valid_ref[0] > 0.0, scores, -1e30)
         fresh = lax.dot_general(query, drafts, NT, preferred_element_type=F32) * scale
@@ -570,7 +572,7 @@
 
 def attend(requests, rank, messages, own, got, column, tables, valid, gain, cosine, sine, after):
     new = 2 * RP
-    local_rows = (messages.shape[1] - 4 * new) // RP
+    local_rows = (messages[0].shape[0] - 4 * new) // RP
     last = RP * local_rows // (4 * new)
     start, count = requests[0], len(requests)
     got = got[start : start + count]
@@ -583,8 +585,8 @@
             num_scalar_prefetch=1,
             grid=(count,),
             in_specs=[
-                pl.BlockSpec((4, local_rows, WIDTH), lambda i, rank: (0, i + start, 0)),
-                pl.BlockSpec((4, 4 * new, WIDTH), lambda i, rank: (0, last, 0)),
+                *([pl.BlockSpec((local_rows, WIDTH), lambda i, rank: (i + start, 0))] * 4),
+                *([pl.BlockSpec((4 * new, WIDTH), lambda i, rank: (last, 0))] * 4),
                 pl.BlockSpec(
                     (UNITS, 2, None, WIDTH, UNIT), lambda i, rank: (0, 0, i + start, 0, 0)
                 ),
@@ -604,7 +606,7 @@
         compiler_params=ROOM,
         cost_estimate=COST,
         name="attend",
-    )(rank, messages, messages, own, *got, column, *tables, valid, gain, cosine, sine, *after)
+    )(rank, *messages, *messages, own, *got, column, *tables, valid, gain, cosine, sine, *after)
 
 
 def heads_kernel(step, o_ref, keep_ref, *refs):
@@ -717,16 +719,16 @@
     message = jnp.concatenate(
         [query.reshape(RP * 2 * heads, WIDTH), terms.reshape(8 * RP, WIDTH)], 0
     ).astype(BF)
-    messages = lax.all_gather(message, "tp", axis=0)
+    messages = [lax.ppermute(message, "tp", [(t, 3)]) for t in range(3)] + [message]
 
     block = first_hop(0, [message])
     send_far(2, [block])
     near_sums, *side = project_near(rank, hidden, down_t, far_sums[2:])
-    block = first_hop(1, [near_sums])
+    block = first_hop(1, [near_sums, *messages[:3]])
     block = second_hop(0, [block])
     send_far(3, [block])
     block = first_hop(2, far_sums[3:])
-    block = second_hop(1, [block, messages, outer[0]])
+    block = second_hop(1, [block, outer[0]])
 
     my_segments = lax.dynamic_slice_in_dim(segment_ids, first_req, RP, 0)
     valid = (my_segments == my_segments[:, -1:])[:, PRE_TOK // 2 :].astype(F32)
@@ -763,9 +765,10 @@
     my_owners = lax.dynamic_slice_in_dim(owners, first_req, RP, 0)
     early, late = tuple(range(RP - 1)), (RP - 1,)
 
-    def pages_to(requests, base, after):
+    def pages_to(requests, halves, base, after):
         return pages_of(
             requests,
+            halves,
             rank,
             my_owners,
             near_sums,
@@ -783,9 +786,11 @@
     results, backs = [None] * 2, [None] * 2
     results[0], backs[0] = attend_to(early, [block])
     base = [jnp.zeros((pd_count, PART, SHARE), BF)] * 2 if pd_count > RP else []
-    pages = pages_to(early, base, results[0][:1])
+    pages = pages_to(early, (0, 1), base, results[0][:1])
     results[1], backs[1] = attend_to(late, pages[:1])
-    pages = pages_to(late, pages, [*results[1][:1], *backs[0]])
+    first = pages_to(late, (0,), pages[:1], [*results[1][:1], *backs[0]])
+    second = pages_to(late, (1,), pages[1:], [*first, *backs[1]])
+    pages = [*first, *second]
     cache = [lax.all_to_all(page, "pd", split_axis=0, concat_axis=0, tiled=True) for page in pages]
 
     attended = [
@@ -796,7 +801,7 @@
     attended = attended.reshape(heads, RP * 2, KVL).astype(F32)
     my_accepted = lax.dynamic_slice_in_dim(accepted, first_req, RP, 0)
     keep = (jnp.arange(2)[None, :] <= my_accepted[:, None]).astype(F32).reshape(RP * 2, 1)
-    answer = heads_out(attended, jnp.broadcast_to(keep, (RP * 2, DV)), kv_up, pages[:1])
+    answer = heads_out(attended, jnp.broadcast_to(keep, (RP * 2, DV)), kv_up, pages[1:])
     placed = route(my_owners, answer, pd_count, cache[:1]).astype(BF)
     placed = lax.all_to_all(placed, "pd", split_axis=0, concat_axis=0, tiled=True)
     cache = jnp.swapaxes(jnp.concatenate(cache, 1), 1, 2)

time: 260 us -> 254 us (0.977)
  waiting for transfers between devices: 76.1 us -> 60 us
  between operations: 14.6 us -> 1.28 us
  starting transfers between devices: 44.9 us -> 57.6 us
  blocking collectives: 0 us -> 6.88 us
  Pallas kernels: 95.3 us -> 98.9 us
    ppermute x4, waiting for transfers between devices: 13.3 us -> 0.01 us  [send_far(): inner.append(lax.ppermute(codes, 'tp', inward))]
    ppermute x4, waiting for transfers between devices: 3.94 us -> 14.3 us  [second_hop(): outer.append(lax.ppermute(block, 'tp', outward))]
    ppermute x4, waiting for transfers between devices: 11.2 us -> 1.51 us  [first_hop(): crossed.append(lax.ppermute(block, 'tp', across))]
    ppermute x4, starting transfers between devices: 10.6 us -> 19.4 us  [first_hop(): crossed.append(lax.ppermute(block, 'tp', across))]
    all_to_all x0 -> x1, blocking collectives: none -> 6.88 us  [local_line(): lax.all_to_all(placed, 'pd', split_axis=0, concat_axis=0, tiled=True)]
    ppermute x0 -> x3, starting transfers between devices: none -> 5.72 us  [local_line(): lax.ppermute(message, 'tp', [(t, 3)])]
    pallas_call x2 -> x3, Pallas kernels: 9.48 us -> 12.9 us  [pages_of(): pl.pallas_call(functools.partial(page_kernel, requests, halves), grid_spe...]
    all_to_all x1 -> x0, starting transfers between devices: 3.29 us -> none  [local_line(): lax.all_to_all(placed, 'pd', split_axis=0, concat_axis=0, tiled=True)]
  transfers between devices with their start and end apart: 24 -> 25, of which waited for: 12 -> 7; matrix products, arithmetic and copies ran while one was open for 6% -> 5% of each run, Pallas kernels for 33% -> 35%
where the time goes in v4:
time: 254 us; the launch traced here: 252 us
  Pallas kernels  98.9 us (39%)
  waiting for transfers between devices  60 us (24%)
  starting transfers between devices  57.6 us (23%)
  local copies, waits for them, and re-layouts  18.1 us (7%)
  other arithmetic  8.91 us (4%)
  blocking collectives  6.88 us (3%)
    ppermute x2, waiting for transfers between devices, local_line(): side = [lax.ppermute(codes, 'tp', inward) for codes in side]  27 us
    pallas_call x4, Pallas kernels, project_far(): pl.pallas_call(project_far_kernel, grid_spec=pltpu.PrefetchScalarGridSpec...  22.6 us
    pallas_call x8, Pallas kernels, add_on(): pl.pallas_call(add_kernel, grid_spec=pltpu.PrefetchScalarGridSpec(num_sca...  22.4 us
    ppermute x4, starting transfers between devices, first_hop(): crossed.append(lax.ppermute(block, 'tp', across))  19.4 us
    ppermute x4, waiting for transfers between devices, second_hop(): outer.append(lax.ppermute(block, 'tp', outward))  14.3 us
    pallas_call x1, Pallas kernels, queries(): pl.pallas_call(body, grid=(heads // step,), in_specs=[pl.BlockSpec((rows,...  13.8 us
    pallas_call x1, Pallas kernels, project_near(): pl.pallas_call(project_near_kernel, grid_spec=pltpu.PrefetchScalarGridSpe...  13.1 us
    pallas_call x3, Pallas kernels, pages_of(): pl.pallas_call(functools.partial(page_kernel, requests, halves), grid_spe...  12.9 us
  transfers between devices with their start and end apart: 25, of which 7 were waited for; matrix products, arithmetic and copies ran while one was open for 5% of the time, Pallas kernels for 35%

profile of v4, /device:TPU:16, one launch (start us, length us, event | category | flops | bytes accessed | tf_op | source)
XLA Modules:
  0.0 251.6 jit_solution(8136799558151370755)
XLA Ops:
  0.7 5.7 %project_far.4 = (f32[2,3,576,128]{3,2,1,0:T(8,128)}, s16[2,3,592,128]{3,2,1,0:T(8,128)(2,1)}) custom-call(s32[1]{0:T(128)} %bitcast.rank, bf16[4,1536,1792]{2,1,0:T(8,128)(2,1)} %bitcast.18, bf16[576,1792]{1,0:T(8,128)(2,1)} %bitcast.23), custom_call_target="tpu_custom_call" | custom-call | flops 1024 | bytes 1024 | tf_op jit(solution)/shard_map/project_far/pallas_call | solution.py:270
  6.3 1.3 collective-permute-start.3
  7.6 5.6 %project_far.5 = (f32[2,3,576,128]{3,2,1,0:T(8,128)}, s16[2,3,592,128]{3,2,1,0:T(8,128)(2,1)}) custom-call(s32[1]{0:T(128)} %bitcast.rank, bf16[4,1536,1792]{2,1,0:T(8,128)(2,1)} %bitcast.19, bf16[576,1792]{1,0:T(8,128)(2,1)} %bitcast.24, f32[2,3,576,128]{3,2,1,0:T(8,128)} %get-tuple-element.25.refs_0_.own_ref), custom_call_target="tpu_custom_call" | custom-call | flops 1024 | bytes 1024 | tf_op jit(solution)/shard_map/project_far/pallas_call | solution.py:270
  13.3 1.3 collective-permute-start.5
  16.1 13.8 %queries.1 = (f32[32,8,576]{2,1,0:T(8,128)}, f32[4,8,576]{2,1,0:T(8,128)}) custom-call(bf16[8,1536]{1,0:T(8,128)(2,1)} %reshape.131.refs_0_, bf16[1536,6144]{1,0:T(8,128)(2,1)} %refs_1_.2, bf16[8,1792]{1,0:T(8,128)(2,1)} %refs_2_.2, bf16[576,1792]{1,0:T(8,128)(2,1)} %bitcast.25, bf16[512,8192]{1,0:T(8,128)(2,1)} %refs_7_.3, bf16[512,8192]{1,0:T(8,128)(2,1)} %refs_7_.3, ...), custom_call_target="tpu_custom_call" | custom-call | flops 1024 | bytes 1024 | tf_op jit(solution)/shard_map/queries/pallas_call | solution.py:477
  33.8 2.8 %add_on.8.refs_0_ = s16[2,3,592,128]{3,2,1,0:T(8,128)(2,1)} custom-call(s32[1]{0:T(128)} %bitcast.rank, f32[2,3,576,128]{3,2,1,0:T(8,128)} %get-tuple-element.25.refs_0_.own_ref, s16[2,3,592,128]{3,2,1,0:T(8,128)(2,1)} %copy-done.16, bf16[288,576]{1,0:T(8,128)(2,1)} %pad_maximum_fusion.refs_0_.refs_3_.refs_7_), custom_call_target="tpu_custom_call" | custom-call | flops 1024 | bytes 1024 | tf_op jit(solution)/shard_map/add_on/pallas_call | solution.py:359
  36.6 2.3 collective-permute-start.4
  40.3 4.4 %collective-permute-start.2 = (bf16[288,576]{1,0:T(8,128)(2,1)S(1)}, bf16[288,576]{1,0:T(8,128)(2,1)S(1)}, u32[]{:S(2)}, u32[]{:S(2)}) collective-permute-start(bf16[288,576]{1,0:T(8,128)(2,1)S(1)} %copy-done.2), channel_id=1, source_target_pairs={{8,12},{9,13},{10,14},{11,15},{24,28},{25,29},{26,30},{27,31}} | collective-permute-start | bytes 995336 | tf_op jit(solution)/shard_map/ppermute | solution.py:722
  44.7 5.6 %project_far.6 = (f32[2,3,576,128]{3,2,1,0:T(8,128)}, s16[2,3,592,128]{3,2,1,0:T(8,128)(2,1)}) custom-call(s32[1]{0:T(128)} %bitcast.rank, bf16[4,1536,1792]{2,1,0:T(8,128)(2,1)} %bitcast.20, bf16[576,1792]{1,0:T(8,128)(2,1)} %bitcast.26, s16[2,3,592,128]{3,2,1,0:T(8,128)(2,1)} %add_on.8.refs_0_), custom_call_target="tpu_custom_call" | custom-call | flops 1024 | bytes 1024 | tf_op jit(solution)/shard_map/project_far/pallas_call | solution.py:270
  50.3 13.1 %project_near.1 = (f32[3,2,4,576,128]{4,3,2,1,0:T(8,128)}, s16[1,4,592,128]{3,2,1,0:T(8,128)(2,1)}, s16[2,4,592,128]{3,2,1,0:T(8,128)(2,1)}) custom-call(s32[1]{0:T(128)} %bitcast.rank, bf16[4,1536,1792]{2,1,0:T(8,128)(2,1)} %bitcast.21, bf16[576,1792]{1,0:T(8,128)(2,1)} %bitcast.27, f32[2,3,576,128]{3,2,1,0:T(8,128)} %get-tuple-element.30.refs_0_.own_ref), custom_call_target="tpu_custom_call" | custom-call | flops 1024 | bytes 1024 | tf_op jit(solution)/shard_map/project_near/pallas_call | solution.py:313
  63.4 1.3 collective-permute-start.8
  65.9 2.8 %add_on.9.refs_0_ = s16[2,3,592,128]{3,2,1,0:T(8,128)(2,1)} custom-call(s32[1]{0:T(128)} %bitcast.rank, f32[2,3,576,128]{3,2,1,0:T(8,128)} %get-tuple-element.26.refs_10_.own_ref, s16[2,3,592,128]{3,2,1,0:T(8,128)(2,1)} %copy-done.14, f32[3,2,4,576,128]{4,3,2,1,0:T(8,128)} %get-tuple-element.31.refs_0_.own_ref.refs_8_, bf16[288,576]{1,0:T(8,128)(2,1)} %copy-done.5, ...), custom_call_target="tpu_custom_call" | custom-call | flops 1024 | bytes 1024 | tf_op jit(solution)/shard_map/add_on/pallas_call | solution.py:359
  68.7 13.1 %collective-permute-start.7 = (s16[2,3,592,128]{3,2,1,0:T(8,128)(2,1)}, s16[2,3,592,128]{3,2,1,0:T(8,128)(2,1)}, u32[]{:S(2)}, u32[]{:S(2)}) collective-permute-start(s16[2,3,592,128]{3,2,1,0:T(8,128)(2,1)} %add_on.9.refs_0_), channel_id=1, source_target_pairs={{4,8},{8,4},{5,9},{9,5},{6,10},{10,6},{7,11},{11,7},{20,24},{24,20... | collective-permute-start | bytes 2727944 | tf_op jit(solution)/shard_map/ppermute | solution.py:699
  82.8 2.8 %add_on.10.refs_0_.refs_3_ = s16[2,3,592,128]{3,2,1,0:T(8,128)(2,1)} custom-call(s32[1]{0:T(128)} %bitcast.rank, f32[3,2,4,576,128]{4,3,2,1,0:T(8,128)} %get-tuple-element.31.refs_0_.own_ref.refs_8_, s16[2,3,592,128]{3,2,1,0:T(8,128)(2,1)} %copy-done.18, s16[2,3,592,128]{3,2,1,0:T(8,128)(2,1)} %add_on.9.refs_0_), custom_call_target="tpu_custom_call" | custom-call | flops 1024 | bytes 1024 | tf_op jit(solution)/shard_map/add_on/pallas_call | solution.py:359
  85.5 2.9 %collective-permute-start.6 = (s16[2,3,592,128]{3,2,1,0:T(8,128)(2,1)}, s16[2,3,592,128]{3,2,1,0:T(8,128)(2,1)S(1)}, u32[]{:S(2)}, u32[]{:S(2)}) collective-permute-start(s16[2,3,592,128]{3,2,1,0:T(8,128)(2,1)} %add_on.10.refs_0_.refs_3_), channel_id=1, source_target_pairs={{8,12},{4,0},{9,13},{5,1},{10,14},{6,2},{11,15},{7,3},{24,28},{20,... | collective-permute-start | bytes 2727944 | tf_op jit(solution)/shard_map/ppermute | solution.py:705
  88.4 5.6 %project_far.7 = (f32[2,3,576,128]{3,2,1,0:T(8,128)}, s16[2,3,592,128]{3,2,1,0:T(8,128)(2,1)}) custom-call(s32[1]{0:T(128)} %bitcast.rank, bf16[4,1536,1792]{2,1,0:T(8,128)(2,1)} %bitcast.22, bf16[576,1792]{1,0:T(8,128)(2,1)} %bitcast.28, s16[2,3,592,128]{3,2,1,0:T(8,128)(2,1)} %add_on.10.refs_0_.refs_3_), custom_call_target="tpu_custom_call" | custom-call | flops 1024 | bytes 1024 | tf_op jit(solution)/shard_map/project_far/pallas_call | solution.py:270
  95.3 2.8 %add_on.11.refs_0_ = s16[2,3,592,128]{3,2,1,0:T(8,128)(2,1)} custom-call(s32[1]{0:T(128)} %bitcast.rank, f32[2,3,576,128]{3,2,1,0:T(8,128)} %get-tuple-element.30.refs_0_.own_ref, s16[2,3,592,128]{3,2,1,0:T(8,128)(2,1)} %collective-permute-done.8.got_ref, f32[2,3,576,128]{3,2,1,0:T(8,128)} %get-tuple-element.34.refs_0_.own_ref), custom_call_target="tpu_custom_call" | custom-call | flops 1024 | bytes 1024 | tf_op jit(solution)/shard_map/add_on/pallas_call | solution.py:359
  98.2 2.0 collective-permute-start.10
  100.2 1.5 collective-permute-done.7.got_ref
  101.7 5.5 %collective-permute-done.6.refs_1_.refs_9_.refs_0_ = s16[2,3,592,128]{3,2,1,0:T(8,128)(2,1)S(1)} collective-permute-done((s16[2,3,592,128]{3,2,1,0:T(8,128)(2,1)}, s16[2,3,592,128]{3,2,1,0:T(8,128)(2,1)S(1)}, u32[]{:S(2)}, u32[]{:S(2)}) %collective-permute-start.6) | collective-permute-done | bytes 909344 | tf_op jit(solution)/shard_map/ppermute | solution.py:705
  108.2 2.8 %add_on.12.refs_0_.refs_4_ = s16[2,3,592,128]{3,2,1,0:T(8,128)(2,1)} custom-call(s32[1]{0:T(128)} %bitcast.rank, f32[3,2,4,576,128]{4,3,2,1,0:T(8,128)} %get-tuple-element.31.refs_0_.own_ref.refs_8_, s16[2,3,592,128]{3,2,1,0:T(8,128)(2,1)} %collective-permute-done.7.got_ref, s16[2,3,592,128]{3,2,1,0:T(8,128)(2,1)} %add_on.11.refs_0_, ...), custom_call_target="tpu_custom_call" | custom-call | flops 1024 | bytes 1024 | tf_op jit(solution)/shard_map/add_on/pallas_call | solution.py:359
  111.0 4.0 %collective-permute-start.9 = (s16[2,3,592,128]{3,2,1,0:T(8,128)(2,1)}, s16[2,3,592,128]{3,2,1,0:T(8,128)(2,1)S(1)}, u32[]{:S(2)}, u32[]{:S(2)}) collective-permute-start(s16[2,3,592,128]{3,2,1,0:T(8,128)(2,1)} %add_on.12.refs_0_.refs_4_), channel_id=1, source_target_pairs={{8,12},{4,0},{9,13},{5,1},{10,14},{6,2},{11,15},{7,3},{24,28},{20,... | collective-permute-start | bytes 2727944 | tf_op jit(solution)/shard_map/ppermute | solution.py:705
  119.4 2.8 %add_on.13.refs_0_ = s16[2,3,592,128]{3,2,1,0:T(8,128)(2,1)} custom-call(s32[1]{0:T(128)} %bitcast.rank, f32[2,3,576,128]{3,2,1,0:T(8,128)} %get-tuple-element.34.refs_0_.own_ref, s16[2,3,592,128]{3,2,1,0:T(8,128)(2,1)} %copy-done.17, s16[2,3,592,128]{3,2,1,0:T(8,128)(2,1)} %add_on.12.refs_0_.refs_4_, ...), custom_call_target="tpu_custom_call" | custom-call | flops 1024 | bytes 1024 | tf_op jit(solution)/shard_map/add_on/pallas_call | solution.py:359
  122.2 1.9 collective-permute-start.13
  124.1 8.7 %collective-permute-done.9.refs_1_.refs_10_ = s16[2,3,592,128]{3,2,1,0:T(8,128)(2,1)S(1)} collective-permute-done((s16[2,3,592,128]{3,2,1,0:T(8,128)(2,1)}, s16[2,3,592,128]{3,2,1,0:T(8,128)(2,1)S(1)}, u32[]{:S(2)}, u32[]{:S(2)}) %collective-permute-start.9) | collective-permute-done | bytes 909344 | tf_op jit(solution)/shard_map/ppermute | solution.py:705
  133.8 2.8 %add_on.14.refs_5_ = s16[2,3,592,128]{3,2,1,0:T(8,128)(2,1)} custom-call(s32[1]{0:T(128)} %bitcast.rank, f32[3,2,4,576,128]{4,3,2,1,0:T(8,128)} %get-tuple-element.31.refs_0_.own_ref.refs_8_, s16[2,3,592,128]{3,2,1,0:T(8,128)(2,1)} %copy-done.15, s16[2,3,592,128]{3,2,1,0:T(8,128)(2,1)} %add_on.13.refs_0_, s16[2,3,592,128]{3,2,1,0:T(8,128)(2,1)} %copy-done.10), custom_call_target="tpu_custom_call" | custom-call | flops 1024 | bytes 1024 | tf_op jit(solution)/shard_map/add_on/pallas_call | solution.py:359
  136.6 4.0 %collective-permute-start.12 = (s16[2,3,592,128]{3,2,1,0:T(8,128)(2,1)}, s16[2,3,592,128]{3,2,1,0:T(8,128)(2,1)S(1)}, u32[]{:S(2)}, u32[]{:S(2)}) collective-permute-start(s16[2,3,592,128]{3,2,1,0:T(8,128)(2,1)} %add_on.14.refs_5_), channel_id=1, source_target_pairs={{8,12},{4,0},{9,13},{5,1},{10,14},{6,2},{11,15},{7,3},{24,28},{20,... | collective-permute-start | bytes 2727944 | tf_op jit(solution)/shard_map/ppermute | solution.py:705
  140.6 1.3 collective-permute-start.14
  141.9 1.3 collective-permute-start.19
  143.2 16.1 %collective-permute-done.14.refs_0_.refs_6_.refs_2_ = s16[1,4,592,128]{3,2,1,0:T(8,128)(2,1)S(1)} collective-permute-done((s16[1,4,592,128]{3,2,1,0:T(8,128)(2,1)}, s16[1,4,592,128]{3,2,1,0:T(8,128)(2,1)S(1)}, u32[]{:S(2)}, u32[]{:S(2)}) %collective-permute-start.14) | collective-permute-done | bytes 606240 | tf_op jit(solution)/shard_map/ppermute | solution.py:744
  161.3 2.8 %add_on.15.refs_21_.refs_1_ = s16[2,3,592,128]{3,2,1,0:T(8,128)(2,1)} custom-call(s32[1]{0:T(128)} %bitcast.rank, f32[3,2,4,576,128]{4,3,2,1,0:T(8,128)} %get-tuple-element.31.refs_0_.own_ref.refs_8_, s16[2,3,592,128]{3,2,1,0:T(8,128)(2,1)} %copy-done.19, s16[1,4,592,128]{3,2,1,0:T(8,128)(2,1)} %copy-done.4, s16[2,3,592,128]{3,2,1,0:T(8,128)(2,1)} %copy-done.11), custom_call_target="tpu_custom_call" | custom-call | flops 1024 | bytes 1024 | tf_op jit(solution)/shard_map/add_on/pallas_call | solution.py:359
  164.1 1.5 collective-permute-start.18
  165.7 5.3 %attend.2 = (bf16[3,64,512]{2,1,0:T(8,128)(2,1)}, bf16[3,64,512]{2,1,0:T(8,128)(2,1)}, bf16[3,64,512]{2,1,0:T(8,128)(2,1)}, bf16[3,64,512]{2,1,0:T(8,128)(2,1)}) custom-call(s32[1]{0:T(128)} %bitcast.rank, bf16[288,576]{1,0:T(8,128)(2,1)} %copy-done.5, bf16[288,576]{1,0:T(8,128)(2,1)} %copy-done.6, bf16[288,576]{1,0:T(8,128)(2,1)} %copy-done.7, ...), custom_call_target="tpu_custom_call" | custom-call | flops 1024 | bytes 1024 | tf_op jit(solution)/shard_map/attend/pallas_call | solution.py:582
  172.4 1.3 collective-permute-start.17
  174.4 10.9 %collective-permute-done.19.refs_7_.refs_3_ = s16[2,4,592,128]{3,2,1,0:T(8,128)(2,1)S(1)} collective-permute-done((s16[2,4,592,128]{3,2,1,0:T(8,128)(2,1)}, s16[2,4,592,128]{3,2,1,0:T(8,128)(2,1)S(1)}, u32[]{:S(2)}, u32[]{:S(2)}) %collective-permute-start.19) | collective-permute-done | bytes 1212448 | tf_op jit(solution)/shard_map/ppermute | solution.py:744
  186.3 6.0 %pages.3 = (bf16[4,288,384]{2,1,0:T(8,128)(2,1)}, bf16[4,288,384]{2,1,0:T(8,128)(2,1)}) custom-call(s32[1]{0:T(128)} %bitcast.rank, s32[4]{0:T(128)} %dynamic_slice.12.slot, f32[3,2,4,576,128]{4,3,2,1,0:T(8,128)} %get-tuple-element.31.refs_0_.own_ref.refs_8_, s16[2,3,592,128]{3,2,1,0:T(8,128)(2,1)} %copy-done.8, s16[2,3,592,128]{3,2,1,0:T(8,128)(2,1)} %copy-done.10, ...), custom_call_target="tpu_custom_call" | custom-call | flops 1024 | bytes 1024 | tf_op jit(solution)/shard_map/pages/pallas_call | solution.py:411
  193.3 2.7 %attend.3 = (bf16[1,64,512]{2,1,0:T(8,128)(2,1)}, bf16[1,64,512]{2,1,0:T(8,128)(2,1)}, bf16[1,64,512]{2,1,0:T(8,128)(2,1)}, bf16[1,64,512]{2,1,0:T(8,128)(2,1)}) custom-call(s32[1]{0:T(128)} %bitcast.rank, bf16[288,576]{1,0:T(8,128)(2,1)} %copy-done.5, bf16[288,576]{1,0:T(8,128)(2,1)} %copy-done.6, bf16[288,576]{1,0:T(8,128)(2,1)} %copy-done.7, ...), custom_call_target="tpu_custom_call" | custom-call | flops 1024 | bytes 1024 | tf_op jit(solution)/shard_map/attend/pallas_call | solution.py:582
  196.9 3.3 %pages.4.refs_8_ = bf16[4,288,384]{2,1,0:T(8,128)(2,1)} custom-call(s32[1]{0:T(128)} %bitcast.rank, s32[4]{0:T(128)} %dynamic_slice.12.slot, f32[3,2,4,576,128]{4,3,2,1,0:T(8,128)} %get-tuple-element.31.refs_0_.own_ref.refs_8_, s16[2,3,592,128]{3,2,1,0:T(8,128)(2,1)} %copy-done.9, ...), custom_call_target="tpu_custom_call", output_to_operand_aliasing={{}: (10, {})} | custom-call | flops 1024 | bytes 1024 | tf_op jit(solution)/shard_map/pages/pallas_call | solution.py:411
  200.3 3.6 %all-to-all-start = ((bf16[4,288,384]{2,1,0:T(8,128)(2,1)}), bf16[4,288,384]{2,1,0:T(8,128)(2,1)S(1)}, u32[]{:S(2)}, u32[]{:S(2)}) async-start(bf16[4,288,384]{2,1,0:T(8,128)(2,1)} %pages.4.refs_8_), calls=%async_computation | async-start | bytes 1769472 | tf_op jit(solution)/shard_map/all_to_all | solution.py:794
  205.4 1.3 collective-permute-start.22
  206.9 5.2 %collective-permute-done.22.refs_11_ = bf16[1,64,512]{2,1,0:T(8,128)(2,1)S(1)} collective-permute-done((bf16[1,64,512]{2,1,0:T(8,128)(2,1)S(1)}, bf16[1,64,512]{2,1,0:T(8,128)(2,1)S(1)}, u32[]{:S(2)}, u32[]{:S(2)}) %collective-permute-start.22) | collective-permute-done | bytes 65568 | tf_op jit(solution)/shard_map/ppermute | solution.py:763
  212.6 3.5 %pages.5.refs_8_ = bf16[4,288,384]{2,1,0:T(8,128)(2,1)} custom-call(s32[1]{0:T(128)} %bitcast.rank, s32[4]{0:T(128)} %dynamic_slice.12.slot, f32[3,2,4,576,128]{4,3,2,1,0:T(8,128)} %get-tuple-element.31.refs_0_.own_ref.refs_8_, s16[2,3,592,128]{3,2,1,0:T(8,128)(2,1)} %copy-done.9, ...), custom_call_target="tpu_custom_call", output_to_operand_aliasing={{}: (10, {})} | custom-call | flops 1024 | bytes 1024 | tf_op jit(solution)/shard_map/pages/pallas_call | solution.py:411
  219.2 4.4 %heads_out.1.answer_ref = f32[8,4096]{1,0:T(8,128)} custom-call(f32[32,8,512]{2,1,0:T(8,128)} %reshape.145.o_ref, f32[8,128]{1,0:T(8,128)} %broadcast_in_dim.5.keep_ref, bf16[512,8192]{1,0:T(8,128)(2,1)} %refs_7_.3, bf16[512,8192]{1,0:T(8,128)(2,1)} %refs_7_.3, bf16[512,8192]{1,0:T(8,128)(2,1)} %refs_7_.3, bf16[512,8192]{1,0:T(8,128)(2,1)} %refs_7_.3, ...), custom_call_target="tpu_custom_call" | custom-call | flops 1024 | bytes 1024 | tf_op jit(solution)/shard_map/heads_out/pallas_call | solution.py:625
  224.6 1.6 route.1
  227.2 6.9 %all_to_all.15 = bf16[4,2,4096]{2,1,0:T(2,128)(2,1)S(1)} all-to-all(bf16[4,2,4096]{2,1,0:T(2,128)(2,1)S(1)} %convert_element_type.89), channel_id=1, replica_groups=mesh['groups'=2,'tp'=4,'pd'=4] {'pd'}, dimensions={0} | all-to-all | bytes 131072 | tf_op jit(solution)/shard_map/all_to_all | solution.py:806
  234.1 3.5 %all-to-all-start.2 = ((bf16[4,288,384]{2,1,0:T(8,128)(2,1)}), bf16[4,288,384]{2,1,0:T(8,128)(2,1)S(1)}, u32[]{:S(2)}, u32[]{:S(2)}) async-start(bf16[4,288,384]{2,1,0:T(8,128)(2,1)} %pages.5.refs_8_), calls=%async_computation.2 | async-start | bytes 1769472 | tf_op jit(solution)/shard_map/all_to_all | solution.py:794
  238.2 12.0 %all-to-all-done.2 = bf16[4,288,384]{2,1,0:T(8,128)(2,1)S(1)} async-done(((bf16[4,288,384]{2,1,0:T(8,128)(2,1)}), bf16[4,288,384]{2,1,0:T(8,128)(2,1)S(1)}, u32[]{:S(2)}, u32[]{:S(2)}) %all-to-all-start.2) | async-done | bytes 884768 | tf_op jit(solution)/shard_map/all_to_all | solution.py:794
  250.3 1.4 maximum_bitcast_fusion
  (129 shorter events, 31.0 us)
Async XLA Ops:
  0.6 13.9 %copy-start = (bf16[16,2,1536]{2,1,0:T(2,128)(2,1)S(1)}, bf16[16,2,1536]{2,1,0:T(2,128)(2,1)}, u32[]{:S(2)}) copy-start(bf16[16,2,1536]{2,1,0:T(2,128)(2,1)} %param.14) | copy-start | bytes 294916
  6.3 26.4 %collective-permute-start.3 = (s16[2,3,592,128]{3,2,1,0:T(8,128)(2,1)}, s16[2,3,592,128]{3,2,1,0:T(8,128)(2,1)S(1)}, u32[]{:S(2)}, u32[]{:S(2)}) collective-permute-start(s16[2,3,592,128]{3,2,1,0:T(8,128)(2,1)} %get-tuple-element.29), channel_id=1, source_target_pairs={{0,4},{12,8},{1,5},{13,9},{2,6},{14,10},{3,7},{15,11},{16,20},{28,... | collective-permute-start | bytes 2727944 | tf_op jit(solution)/shard_map/ppermute | solution.py:695
  13.3 51.4 %collective-permute-start.5 = (s16[2,3,592,128]{3,2,1,0:T(8,128)(2,1)}, s16[2,3,592,128]{3,2,1,0:T(8,128)(2,1)S(1)}, u32[]{:S(2)}, u32[]{:S(2)}) collective-permute-start(s16[2,3,592,128]{3,2,1,0:T(8,128)(2,1)} %get-tuple-element.32), channel_id=1, source_target_pairs={{0,4},{12,8},{1,5},{13,9},{2,6},{14,10},{3,7},{15,11},{16,20},{28,... | collective-permute-start | bytes 2727944 | tf_op jit(solution)/shard_map/ppermute | solution.py:695
  32.8 6.2 %copy-start.2 = (bf16[288,576]{1,0:T(8,128)(2,1)S(1)}, bf16[288,576]{1,0:T(8,128)(2,1)}, u32[]{:S(2)}) copy-start(bf16[288,576]{1,0:T(8,128)(2,1)} %pad_maximum_fusion.refs_0_.refs_3_.refs_7_) | copy-start | bytes 995332
  36.6 45.3 %collective-permute-start.4 = (s16[2,3,592,128]{3,2,1,0:T(8,128)(2,1)}, s16[2,3,592,128]{3,2,1,0:T(8,128)(2,1)S(1)}, u32[]{:S(2)}, u32[]{:S(2)}) collective-permute-start(s16[2,3,592,128]{3,2,1,0:T(8,128)(2,1)} %add_on.8.refs_0_), channel_id=1, source_target_pairs={{4,8},{8,4},{5,9},{9,5},{6,10},{10,6},{7,11},{11,7},{20,24},{24,20... | collective-permute-start | bytes 2727944 | tf_op jit(solution)/shard_map/ppermute | solution.py:699
  38.9 24.4 %collective-permute-start = (bf16[288,576]{1,0:T(8,128)(2,1)S(1)}, bf16[288,576]{1,0:T(8,128)(2,1)S(1)}, u32[]{:S(2)}, u32[]{:S(2)}) collective-permute-start(bf16[288,576]{1,0:T(8,128)(2,1)S(1)} %copy-done.2), channel_id=1, source_target_pairs={{0,12},{1,13},{2,14},{3,15},{16,28},{17,29},{18,30},{19,31}} | collective-permute-start | bytes 995336 | tf_op jit(solution)/shard_map/ppermute | solution.py:722
  39.6 25.1 %collective-permute-start.1 = (bf16[288,576]{1,0:T(8,128)(2,1)S(1)}, bf16[288,576]{1,0:T(8,128)(2,1)S(1)}, u32[]{:S(2)}, u32[]{:S(2)}) collective-permute-start(bf16[288,576]{1,0:T(8,128)(2,1)S(1)} %copy-done.2), channel_id=1, source_target_pairs={{4,12},{5,13},{6,14},{7,15},{20,28},{21,29},{22,30},{23,31}} | collective-permute-start | bytes 995336 | tf_op jit(solution)/shard_map/ppermute | solution.py:722
  40.3 24.4 %collective-permute-start.2 = (bf16[288,576]{1,0:T(8,128)(2,1)S(1)}, bf16[288,576]{1,0:T(8,128)(2,1)S(1)}, u32[]{:S(2)}, u32[]{:S(2)}) collective-permute-start(bf16[288,576]{1,0:T(8,128)(2,1)S(1)} %copy-done.2), channel_id=1, source_target_pairs={{8,12},{9,13},{10,14},{11,15},{24,28},{25,29},{26,30},{27,31}} | collective-permute-start | bytes 995336 | tf_op jit(solution)/shard_map/ppermute | solution.py:722
  63.4 1.4 copy-start.5
  63.4 32.0 %collective-permute-start.8 = (s16[2,3,592,128]{3,2,1,0:T(8,128)(2,1)}, s16[2,3,592,128]{3,2,1,0:T(8,128)(2,1)}, u32[]{:S(2)}, u32[]{:S(2)}) collective-permute-start(s16[2,3,592,128]{3,2,1,0:T(8,128)(2,1)} %get-tuple-element.33), channel_id=1, source_target_pairs={{0,4},{12,8},{1,5},{13,9},{2,6},{14,10},{3,7},{15,11},{16,20},{28,... | collective-permute-start | bytes 2727944 | tf_op jit(solution)/shard_map/ppermute | solution.py:695
  64.7 1.2 copy-start.14
  68.7 33.0 %collective-permute-start.7 = (s16[2,3,592,128]{3,2,1,0:T(8,128)(2,1)}, s16[2,3,592,128]{3,2,1,0:T(8,128)(2,1)}, u32[]{:S(2)}, u32[]{:S(2)}) collective-permute-start(s16[2,3,592,128]{3,2,1,0:T(8,128)(2,1)} %add_on.9.refs_0_), channel_id=1, source_target_pairs={{4,8},{8,4},{5,9},{9,5},{6,10},{10,6},{7,11},{11,7},{20,24},{24,20... | collective-permute-start | bytes 2727944 | tf_op jit(solution)/shard_map/ppermute | solution.py:699
  85.5 21.7 %collective-permute-start.6 = (s16[2,3,592,128]{3,2,1,0:T(8,128)(2,1)}, s16[2,3,592,128]{3,2,1,0:T(8,128)(2,1)S(1)}, u32[]{:S(2)}, u32[]{:S(2)}) collective-permute-start(s16[2,3,592,128]{3,2,1,0:T(8,128)(2,1)} %add_on.10.refs_0_.refs_3_), channel_id=1, source_target_pairs={{8,12},{4,0},{9,13},{5,1},{10,14},{6,2},{11,15},{7,3},{24,28},{20,... | collective-permute-start | bytes 2727944 | tf_op jit(solution)/shard_map/ppermute | solution.py:705
  94.0 24.3 %collective-permute-start.11 = (s16[2,3,592,128]{3,2,1,0:T(8,128)(2,1)}, s16[2,3,592,128]{3,2,1,0:T(8,128)(2,1)S(1)}, u32[]{:S(2)}, u32[]{:S(2)}) collective-permute-start(s16[2,3,592,128]{3,2,1,0:T(8,128)(2,1)} %get-tuple-element.35), channel_id=1, source_target_pairs={{0,4},{12,8},{1,5},{13,9},{2,6},{14,10},{3,7},{15,11},{16,20},{28,... | collective-permute-start | bytes 2727944 | tf_op jit(solution)/shard_map/ppermute | solution.py:695
  98.2 20.2 %copy-start.32 = (f32[512]{0:T(512)S(1)}, f32[512]{0:T(512)}, u32[]{:S(2)}) copy-start(f32[512]{0:T(512)} %param.13) | copy-start | bytes 6148
  98.2 25.9 %collective-permute-start.10 = (s16[2,3,592,128]{3,2,1,0:T(8,128)(2,1)}, s16[2,3,592,128]{3,2,1,0:T(8,128)(2,1)S(1)}, u32[]{:S(2)}, u32[]{:S(2)}) collective-permute-start(s16[2,3,592,128]{3,2,1,0:T(8,128)(2,1)} %add_on.11.refs_0_), channel_id=1, source_target_pairs={{4,8},{8,4},{5,9},{9,5},{6,10},{10,6},{7,11},{11,7},{20,24},{24,20... | collective-permute-start | bytes 2727944 | tf_op jit(solution)/shard_map/ppermute | solution.py:699
  111.0 21.9 %collective-permute-start.9 = (s16[2,3,592,128]{3,2,1,0:T(8,128)(2,1)}, s16[2,3,592,128]{3,2,1,0:T(8,128)(2,1)S(1)}, u32[]{:S(2)}, u32[]{:S(2)}) collective-permute-start(s16[2,3,592,128]{3,2,1,0:T(8,128)(2,1)} %add_on.12.refs_0_.refs_4_), channel_id=1, source_target_pairs={{8,12},{4,0},{9,13},{5,1},{10,14},{6,2},{11,15},{7,3},{24,28},{20,... | collective-permute-start | bytes 2727944 | tf_op jit(solution)/shard_map/ppermute | solution.py:705
  118.4 1.0 copy-start.17
  122.2 37.1 %collective-permute-start.13 = (s16[2,3,592,128]{3,2,1,0:T(8,128)(2,1)}, s16[2,3,592,128]{3,2,1,0:T(8,128)(2,1)S(1)}, u32[]{:S(2)}, u32[]{:S(2)}) collective-permute-start(s16[2,3,592,128]{3,2,1,0:T(8,128)(2,1)} %add_on.13.refs_0_), channel_id=1, source_target_pairs={{4,8},{8,4},{5,9},{9,5},{6,10},{10,6},{7,11},{11,7},{20,24},{24,20... | collective-permute-start | bytes 2727944 | tf_op jit(solution)/shard_map/ppermute | solution.py:699
  124.1 8.8 %copy-start.15 = (s16[2,3,592,128]{3,2,1,0:T(8,128)(2,1)}, s16[2,3,592,128]{3,2,1,0:T(8,128)(2,1)S(1)}, u32[]{:S(2)}) copy-start(s16[2,3,592,128]{3,2,1,0:T(8,128)(2,1)S(1)} %collective-permute-done.10.got_ref) | copy-start | bytes 2727940
  136.6 22.7 %collective-permute-start.12 = (s16[2,3,592,128]{3,2,1,0:T(8,128)(2,1)}, s16[2,3,592,128]{3,2,1,0:T(8,128)(2,1)S(1)}, u32[]{:S(2)}, u32[]{:S(2)}) collective-permute-start(s16[2,3,592,128]{3,2,1,0:T(8,128)(2,1)} %add_on.14.refs_5_), channel_id=1, source_target_pairs={{8,12},{4,0},{9,13},{5,1},{10,14},{6,2},{11,15},{7,3},{24,28},{20,... | collective-permute-start | bytes 2727944 | tf_op jit(solution)/shard_map/ppermute | solution.py:705
  140.6 18.7 %collective-permute-start.14 = (s16[1,4,592,128]{3,2,1,0:T(8,128)(2,1)}, s16[1,4,592,128]{3,2,1,0:T(8,128)(2,1)S(1)}, u32[]{:S(2)}, u32[]{:S(2)}) collective-permute-start(s16[1,4,592,128]{3,2,1,0:T(8,128)(2,1)} %get-tuple-element.36), channel_id=1, source_target_pairs={{0,4},{12,8},{1,5},{13,9},{2,6},{14,10},{3,7},{15,11},{16,20},{28,... | collective-permute-start | bytes 1818632 | tf_op jit(solution)/shard_map/ppermute | solution.py:744
  141.9 43.4 %collective-permute-start.19 = (s16[2,4,592,128]{3,2,1,0:T(8,128)(2,1)}, s16[2,4,592,128]{3,2,1,0:T(8,128)(2,1)S(1)}, u32[]{:S(2)}, u32[]{:S(2)}) collective-permute-start(s16[2,4,592,128]{3,2,1,0:T(8,128)(2,1)} %get-tuple-element.41), channel_id=1, source_target_pairs={{0,4},{12,8},{1,5},{13,9},{2,6},{14,10},{3,7},{15,11},{16,20},{28,... | collective-permute-start | bytes 3637256 | tf_op jit(solution)/shard_map/ppermute | solution.py:744
  159.3 1.1 copy-start.19
  164.1 28.2 %collective-permute-start.18 = (s16[2,3,592,128]{3,2,1,0:T(8,128)(2,1)}, s16[2,3,592,128]{3,2,1,0:T(8,128)(2,1)S(1)}, u32[]{:S(2)}, u32[]{:S(2)}) collective-permute-start(s16[2,3,592,128]{3,2,1,0:T(8,128)(2,1)} %add_on.15.refs_21_.refs_1_), channel_id=1, source_target_pairs={{8,12},{4,0},{9,13},{5,1},{10,14},{6,2},{11,15},{7,3},{24,28},{20,... | collective-permute-start | bytes 2727944 | tf_op jit(solution)/shard_map/ppermute | solution.py:705
  165.7 8.0 %copy-start.35 = (s32[16]{0:T(128)S(1)}, s32[16]{0:T(128)}, u32[]{:S(2)}) copy-start(s32[16]{0:T(128)} %param.17) | copy-start | bytes 196
  165.7 8.6 %copy-start.36 = (s32[16]{0:T(128)S(1)}, s32[16]{0:T(128)}, u32[]{:S(2)}) copy-start(s32[16]{0:T(128)} %param.19) | copy-start | bytes 196
  171.0 25.0 %collective-permute-start.15 = (bf16[3,64,512]{2,1,0:T(8,128)(2,1)}, bf16[3,64,512]{2,1,0:T(8,128)(2,1)S(1)}, u32[]{:S(2)}, u32[]{:S(2)}) collective-permute-start(bf16[3,64,512]{2,1,0:T(8,128)(2,1)} %get-tuple-element.38.refs_11_), channel_id=1, source_target_pairs={{12,0},{13,1},{14,2},{15,3},{28,16},{29,17},{30,18},{31,19}} | collective-permute-start | bytes 589832 | tf_op jit(solution)/shard_map/ppermute | solution.py:763
  171.7 24.3 %collective-permute-start.16 = (bf16[3,64,512]{2,1,0:T(8,128)(2,1)}, bf16[3,64,512]{2,1,0:T(8,128)(2,1)S(1)}, u32[]{:S(2)}, u32[]{:S(2)}) collective-permute-start(bf16[3,64,512]{2,1,0:T(8,128)(2,1)} %get-tuple-element.39), channel_id=1, source_target_pairs={{12,4},{13,5},{14,6},{15,7},{28,20},{29,21},{30,22},{31,23}} | collective-permute-start | bytes 589832 | tf_op jit(solution)/shard_map/ppermute | solution.py:763
  172.4 23.7 %collective-permute-start.17 = (bf16[3,64,512]{2,1,0:T(8,128)(2,1)}, bf16[3,64,512]{2,1,0:T(8,128)(2,1)S(1)}, u32[]{:S(2)}, u32[]{:S(2)}) collective-permute-start(bf16[3,64,512]{2,1,0:T(8,128)(2,1)} %get-tuple-element.40), channel_id=1, source_target_pairs={{12,8},{13,9},{14,10},{15,11},{28,24},{29,25},{30,26},{31,27}} | collective-permute-start | bytes 589832 | tf_op jit(solution)/shard_map/ppermute | solution.py:763
  185.3 1.0 copy-start.3
  200.2 3.9 %copy-start.30 = (bf16[1,64,512]{2,1,0:T(8,128)(2,1)S(1)}, bf16[1,64,512]{2,1,0:T(8,128)(2,1)}, u32[]{:S(2)}) copy-start(bf16[1,64,512]{2,1,0:T(8,128)(2,1)} %get-tuple-element.44.refs_8_) | copy-start | bytes 196612
  200.2 4.5 %copy-start.34 = (bf16[1,64,512]{2,1,0:T(8,128)(2,1)S(1)}, bf16[1,64,512]{2,1,0:T(8,128)(2,1)}, u32[]{:S(2)}) copy-start(bf16[1,64,512]{2,1,0:T(8,128)(2,1)} %get-tuple-element.45) | copy-start | bytes 196612
  200.2 5.2 %copy-start.33 = (bf16[1,64,512]{2,1,0:T(8,128)(2,1)S(1)}, bf16[1,64,512]{2,1,0:T(8,128)(2,1)}, u32[]{:S(2)}) copy-start(bf16[1,64,512]{2,1,0:T(8,128)(2,1)} %get-tuple-element.46) | copy-start | bytes 196612
  200.2 6.5 %copy-start.21 = (bf16[3,64,512]{2,1,0:T(8,128)(2,1)S(1)}, bf16[3,64,512]{2,1,0:T(8,128)(2,1)}, u32[]{:S(2)}) copy-start(bf16[3,64,512]{2,1,0:T(8,128)(2,1)} %copy-done.20) | copy-start | bytes 589828
  200.2 6.5 %copy-start.23 = (bf16[3,64,512]{2,1,0:T(8,128)(2,1)S(1)}, bf16[3,64,512]{2,1,0:T(8,128)(2,1)}, u32[]{:S(2)}) copy-start(bf16[3,64,512]{2,1,0:T(8,128)(2,1)} %copy-done.22) | copy-start | bytes 589828
  200.2 6.5 %copy-start.25 = (bf16[3,64,512]{2,1,0:T(8,128)(2,1)S(1)}, bf16[3,64,512]{2,1,0:T(8,128)(2,1)}, u32[]{:S(2)}) copy-start(bf16[3,64,512]{2,1,0:T(8,128)(2,1)} %copy-done.24) | copy-start | bytes 589828
  200.3 6.5 %copy-start.29 = (bf16[3,64,512]{2,1,0:T(8,128)(2,1)S(1)}, bf16[3,64,512]{2,1,0:T(8,128)(2,1)}, u32[]{:S(2)}) copy-start(bf16[3,64,512]{2,1,0:T(8,128)(2,1)} %get-tuple-element.37) | copy-start | bytes 589828
  200.3 23.4 %all-to-all-start = ((bf16[4,288,384]{2,1,0:T(8,128)(2,1)}), bf16[4,288,384]{2,1,0:T(8,128)(2,1)S(1)}, u32[]{:S(2)}, u32[]{:S(2)}) async-start(bf16[4,288,384]{2,1,0:T(8,128)(2,1)} %pages.4.refs_8_), calls=%async_computation | async-start | bytes 1769472 | tf_op jit(solution)/shard_map/all_to_all | solution.py:794
  204.1 2.7 %collective-permute-start.20 = (bf16[1,64,512]{2,1,0:T(8,128)(2,1)S(1)}, bf16[1,64,512]{2,1,0:T(8,128)(2,1)S(1)}, u32[]{:S(2)}, u32[]{:S(2)}) collective-permute-start(bf16[1,64,512]{2,1,0:T(8,128)(2,1)S(1)} %copy-done.30), channel_id=1, source_target_pairs={{12,0},{13,1},{14,2},{15,3},{28,16},{29,17},{30,18},{31,19}} | collective-permute-start | bytes 196616 | tf_op jit(solution)/shard_map/ppermute | solution.py:763
  204.8 2.1 collective-permute-start.21
  205.4 6.6 %collective-permute-start.22 = (bf16[1,64,512]{2,1,0:T(8,128)(2,1)S(1)}, bf16[1,64,512]{2,1,0:T(8,128)(2,1)S(1)}, u32[]{:S(2)}, u32[]{:S(2)}) collective-permute-start(bf16[1,64,512]{2,1,0:T(8,128)(2,1)S(1)} %copy-done.33), channel_id=1, source_target_pairs={{12,8},{13,9},{14,10},{15,11},{28,24},{29,25},{30,26},{31,27}} | collective-permute-start | bytes 196616 | tf_op jit(solution)/shard_map/ppermute | solution.py:763
  206.8 5.2 %copy-start.26 = (bf16[1,64,512]{2,1,0:T(8,128)(2,1)}, bf16[1,64,512]{2,1,0:T(8,128)(2,1)S(1)}, u32[]{:S(2)}) copy-start(bf16[1,64,512]{2,1,0:T(8,128)(2,1)S(1)} %collective-permute-done.20.refs_9_) | copy-start | bytes 196612
  206.9 5.2 %copy-start.27 = (bf16[1,64,512]{2,1,0:T(8,128)(2,1)}, bf16[1,64,512]{2,1,0:T(8,128)(2,1)S(1)}, u32[]{:S(2)}) copy-start(bf16[1,64,512]{2,1,0:T(8,128)(2,1)S(1)} %collective-permute-done.21.refs_10_) | copy-start | bytes 196612
  212.6 3.5 %copy-start.31 = (bf16[1,64,512]{2,1,0:T(8,128)(2,1)S(1)}, bf16[1,64,512]{2,1,0:T(8,128)(2,1)}, u32[]{:S(2)}) copy-start(bf16[1,64,512]{2,1,0:T(8,128)(2,1)} %get-tuple-element.43) | copy-start | bytes 196612
  226.2 24.1 %copy-start.13 = (bf16[4,288,384]{2,1,0:T(8,128)(2,1)S(1)}, bf16[4,288,384]{2,1,0:T(8,128)(2,1)}, u32[]{:S(2)}) copy-start(bf16[4,288,384]{2,1,0:T(8,128)(2,1)} %copy-done.12) | copy-start | bytes 2654212
  234.1 16.2 %all-to-all-start.2 = ((bf16[4,288,384]{2,1,0:T(8,128)(2,1)}), bf16[4,288,384]{2,1,0:T(8,128)(2,1)S(1)}, u32[]{:S(2)}, u32[]{:S(2)}) async-start(bf16[4,288,384]{2,1,0:T(8,128)(2,1)} %pages.5.refs_8_), calls=%async_computation.2 | async-start | bytes 1769472 | tf_op jit(solution)/shard_map/all_to_all | solution.py:794
  237.6 14.1 %copy-start.1 = (bf16[16,2,1536]{2,1,0:T(2,128)(2,1)S(1)}, bf16[16,2,1536]{2,1,0:T(2,128)(2,1)}, u32[]{:S(2)}) copy-start(bf16[16,2,1536]{2,1,0:T(2,128)(2,1)} %param.14) | copy-start | bytes 294916
  (14 other events, 11.9 us)

commit v5 on v4

--- a/solution.py
+++ b/solution.py
@@ -16,7 +16,6 @@
 RP = 4
 WIDTH = KVL + DR
 HALF = DR // 2
-PART = WIDTH // 2
 CODED = WIDTH + 16
 SHARE = PRE_TOK // 4
 UNIT = 128
@@ -29,7 +28,6 @@
 I16 = jnp.int16
 NT = (((1,), (1,)), ((), ()))
 ROOM = pltpu.CompilerParams(vmem_limit_bytes=60 << 20)
-SOME = pltpu.CompilerParams(vmem_limit_bytes=60 << 20)
 ANY = pl.BlockSpec(memory_space=pl.ANY)
 VMEM = pl.BlockSpec(memory_space=pltpu.VMEM)
 SMEM = pl.BlockSpec(memory_space=pltpu.SMEM)
@@ -341,14 +339,14 @@
     )(rank, hidden, down_t, *after)
 
 
-def add_kernel(rank, own_ref, got_ref, *refs):
+def add_kernel(out_at, rank, own_ref, got_ref, *refs):
     @pl.when(~outer_rank(rank[0]))
     def _():
         for u in range(UNITS):
-            refs[-1][0, u] = encode(own_ref[u] + decode(got_ref[0, u]))
-
-
-def add_on(rank, own, got, request=None, after=()):
+            refs[out_at][0, u] = encode(own_ref[u] + decode(got_ref[0, u]))
+
+
+def add_on(rank, own, got, request=None, after=(), carried=()):
     chunk = lambda i, rank: (i, 0, 0, 0)
     if request is None:
         own_spec = pl.BlockSpec((None, UNITS, WIDTH, UNIT), chunk)
@@ -357,36 +355,46 @@
             (UNITS, None, None, WIDTH, UNIT), lambda i, rank: (0, i, request, 0, 0)
         )
     return pl.pallas_call(
-        add_kernel,
+        functools.partial(add_kernel, -1 - len(carried)),
         grid_spec=pltpu.PrefetchScalarGridSpec(
             num_scalar_prefetch=1,
             grid=(2,),
             in_specs=[
                 own_spec,
                 pl.BlockSpec((1, UNITS, CODED, UNIT), chunk),
-                *([ANY] * len(after)),
+                *([ANY] * (len(after) + len(carried))),
             ],
-            out_specs=pl.BlockSpec((1, UNITS, CODED, UNIT), chunk),
+            out_specs=[
+                pl.BlockSpec((1, UNITS, CODED, UNIT), chunk),
+                *([ANY] * len(carried)),
+            ],
         ),
-        out_shape=jax.ShapeDtypeStruct((2, UNITS, CODED, UNIT), I16),
-        compiler_params=SOME,
+        out_shape=[
+            jax.ShapeDtypeStruct((2, UNITS, CODED, UNIT), I16),
+            *[jax.ShapeDtypeStruct(c.shape, c.dtype) for c in carried],
+        ],
+        input_output_aliases={3 + len(after) + n: 1 + n for n in range(len(carried))},
+        compiler_params=ROOM,
         cost_estimate=COST,
         name="add_on",
-    )(rank, own, got, *after)
-
-
-def page_kernel(requests, halves, rank, slot, own_ref, *refs):
+    )(rank, own, got, *after, *carried)
+
+
+def gain_column(gain_ref):
+    return jnp.broadcast_to(gain_ref[...], (UNIT, KVL)).T
+
+
+def page_kernel(requests, rank, slot, own_ref, *refs):
     count = len(requests)
     got_refs, sent_refs, refs = refs[:count], refs[count : 2 * count], refs[2 * count :]
     side_refs, (gain_ref, cos_ref, sin_ref) = refs[:2], refs[2:5]
-    out_refs = refs[-len(halves) :]
+    out_ref = refs[-1]
     step = pl.program_id(0)
+    column = gain_column(gain_ref)
 
     def write(u, comp):
-        rows = key_rows(comp, gain_ref[...], cos_ref[u], sin_ref[u]).astype(BF)
-        for n, ref in zip(halves, out_refs):
-            part = rows[n * PART : (n + 1) * PART]
-            ref[0, :, u * UNIT : (u + 1) * UNIT] = part
+        rows = key_rows(comp, column, cos_ref[u], sin_ref[u]).astype(BF)
+        out_ref[0, :, u * UNIT : (u + 1) * UNIT] = rows
 
     for k in range(count):
 
@@ -402,14 +410,14 @@
                 write(u, decode(sent_refs[k][u]) + decode(side))
 
 
-def pages_of(requests, halves, rank, slot, own, got, sent, side, gain, cosine, sine, base, count, after):
+def pages_of(requests, rank, slot, own, got, sent, side, gain, cosine, sine, base, count, after):
     first = pl.BlockSpec((None, UNITS, CODED, UNIT), lambda i, *_: (0, 0, 0, 0))
     second = pl.BlockSpec((None, UNITS, CODED, UNIT), lambda i, *_: (1, 0, 0, 0))
     table = pl.BlockSpec((UNITS, HALF, UNIT), lambda i, *_: (0, 0, 0))
     start, total = requests[0], len(requests)
     got, sent = got[start : start + total], sent[start : start + total]
     return pl.pallas_call(
-        functools.partial(page_kernel, requests, halves),
+        functools.partial(page_kernel, requests),
         grid_spec=pltpu.PrefetchScalarGridSpec(
             num_scalar_prefetch=2,
             grid=(total,),
@@ -421,17 +429,16 @@
                 *([second] * total),
                 pl.BlockSpec((1, None, CODED, UNIT), lambda i, *_: (0, i + start, 0, 0)),
                 pl.BlockSpec((UNITS - 1, None, CODED, UNIT), lambda i, *_: (0, i + start, 0, 0)),
-                pl.BlockSpec((KVL, UNIT), lambda i, *_: (0, 0)),
+                pl.BlockSpec((1, KVL), lambda i, *_: (0, 0)),
                 table,
                 table,
                 *([ANY] * (len(base) + len(after))),
             ],
-            out_specs=[
-                pl.BlockSpec((1, PART, SHARE), lambda i, rank, slot: (slot[i + start], 0, 0))
-            ]
-            * len(halves),
+            out_specs=pl.BlockSpec(
+                (1, WIDTH, SHARE), lambda i, rank, slot: (slot[i + start], 0, 0)
+            ),
         ),
-        out_shape=[jax.ShapeDtypeStruct((count, PART, SHARE), BF)] * len(halves),
+        out_shape=jax.ShapeDtypeStruct((count, WIDTH, SHARE), BF),
         input_output_aliases={8 + 2 * total + n: n for n in range(len(base))},
         compiler_params=ROOM,
         cost_estimate=COST,
@@ -505,14 +512,15 @@
     count = len(requests)
     q_refs, draft_refs, refs = refs[:4], refs[4:8], refs[8:]
     own_ref, got_refs, refs = refs[0], refs[1 : 1 + count], refs[1 + count :]
-    column_ref, cos_ref, sin_ref, midcos_ref, midsin_ref, refs = *refs[:5], refs[5:]
-    valid_ref, gain_ref, newcos_ref, newsin_ref, refs = *refs[:4], refs[4:]
+    cos_ref, sin_ref, midcos_ref, midsin_ref, refs = *refs[:4], refs[4:]
+    segment_ref, gain_ref, newcos_ref, newsin_ref, refs = *refs[:4], refs[4:]
     out_refs, keys_ref = refs[-5:-1], refs[-1]
     step = pl.program_id(0)
     request = step + requests[0]
 
     @pl.when(rank[0] == 3)
     def _():
+        column = gain_column(gain_ref)
         for k in range(count):
 
             @pl.when(step == k)
@@ -522,7 +530,7 @@
                 ):
                     for u in range(UNITS):
                         comp = own_ref[u, i] + decode(got_refs[k][i, u])
-                        rows = key_rows(comp, column_ref[...], cosine[u], sine[u])
+                        rows = key_rows(comp, column, cosine[u], sine[u])
                         start = (1 - i) * SHARE + u * UNIT
                         keys_ref[:, start : start + UNIT] = rows.astype(BF)
 
@@ -549,7 +557,9 @@
         drafts = jnp.concatenate([drafts, jnp.zeros((UNIT - new, WIDTH), F32)], 0).astype(BF)
         query = jnp.concatenate([ref[...] for ref in q_refs], 0)
         scores = jnp.dot(query, keys_ref[...], preferred_element_type=F32) * scale
-        scores = jnp.where(valid_ref[0] > 0.0, scores, -1e30)
+        segments = segment_ref[pl.ds(rank[1] * RP + request, 1), :]
+        valid = segments[:, PRE_TOK // 2 :] == segments[:, PRE_TOK - 1 :]
+        scores = jnp.where(valid, scores, -1e30)
         fresh = lax.dot_general(query, drafts, NT, preferred_element_type=F32) * scale
         row = lax.broadcasted_iota(jnp.int32, fresh.shape, 0)
         late = (row % local_rows) // (local_rows // 2)
@@ -570,7 +580,7 @@
             ref[0] = result[t * local_rows : (t + 1) * local_rows]
 
 
-def attend(requests, rank, messages, own, got, column, tables, valid, gain, cosine, sine, after):
+def attend(requests, rank, messages, own, got, tables, segments, gain, cosine, sine, after):
     new = 2 * RP
     local_rows = (messages[0].shape[0] - 4 * new) // RP
     last = RP * local_rows // (4 * new)
@@ -591,9 +601,8 @@
                     (UNITS, 2, None, WIDTH, UNIT), lambda i, rank: (0, 0, i + start, 0, 0)
                 ),
                 *([pl.BlockSpec((2, UNITS, CODED, UNIT), lambda i, rank: (0, 0, 0, 0))] * count),
-                pl.BlockSpec((KVL, UNIT), whole),
                 *([pl.BlockSpec((UNITS, HALF, UNIT), whole3)] * 4),
-                pl.BlockSpec((1, 1, valid.shape[2]), lambda i, rank: (i + start, 0, 0)),
+                pl.BlockSpec(segments.shape, whole),
                 pl.BlockSpec((1, KVL), whole),
                 pl.BlockSpec(cosine.shape, whole),
                 pl.BlockSpec(sine.shape, whole),
@@ -606,7 +615,7 @@
         compiler_params=ROOM,
         cost_estimate=COST,
         name="attend",
-    )(rank, *messages, *messages, own, *got, column, *tables, valid, gain, cosine, sine, *after)
+    )(rank, *messages, *messages, own, *got, *tables, segments, gain, cosine, sine, *after)
 
 
 def heads_kernel(step, o_ref, keep_ref, *refs):
@@ -653,7 +662,7 @@
         in_specs=[SMEM, VMEM, *([ANY] * len(after))],
         out_specs=VMEM,
         out_shape=jax.ShapeDtypeStruct((count, 2, width), F32),
-        compiler_params=SOME,
+        compiler_params=ROOM,
         cost_estimate=COST,
         name="route",
     )(slot, answer, *after)
@@ -682,7 +691,8 @@
     p = lax.axis_index("pd")
     first_req = p * RP
 
-    rank = z.astype(jnp.int32).reshape(1)
+    gain = kv_gain.reshape(1, KVL)
+    rank = jnp.stack([z, p]).astype(jnp.int32)
     hidden = prefill_hidden.reshape(RP, PRE_TOK, prefill_hidden.shape[1])
     down_t = kv_down.T
     inward, across, outward = [(0, 1), (3, 2)], [(1, 2), (2, 1)], [(2, 3), (1, 0)]
@@ -694,16 +704,16 @@
         far_sums.append(total)
         inner.append(lax.ppermute(codes, "tp", inward))
 
-    def first_hop(r, after):
-        block = add_on(rank, far_sums[r], inner[r], after=after)
+    def first_hop(r, after, carried=()):
+        block, *carried = add_on(rank, far_sums[r], inner[r], after=after, carried=carried)
         crossed.append(lax.ppermute(block, "tp", across))
-        return block
+        return [block, *carried]
 
     def second_hop(r, after):
-        block = add_on(rank, near_sums, crossed[r], r, after)
+        (block,) = add_on(rank, near_sums, crossed[r], r, after)
         sent.append(block)
         outer.append(lax.ppermute(block, "tp", outward))
-        return block
+        return [block]
 
     send_far(0, [])
     send_far(1, far_sums[:1])
@@ -721,29 +731,23 @@
     ).astype(BF)
     messages = [lax.ppermute(message, "tp", [(t, 3)]) for t in range(3)] + [message]
 
-    block = first_hop(0, [message])
-    send_far(2, [block])
+    done = first_hop(0, [message])
+    send_far(2, done)
     near_sums, *side = project_near(rank, hidden, down_t, far_sums[2:])
-    block = first_hop(1, [near_sums, *messages[:3]])
-    block = second_hop(0, [block])
-    send_far(3, [block])
-    block = first_hop(2, far_sums[3:])
-    block = second_hop(1, [block, outer[0]])
-
-    my_segments = lax.dynamic_slice_in_dim(segment_ids, first_req, RP, 0)
-    valid = (my_segments == my_segments[:, -1:])[:, PRE_TOK // 2 :].astype(F32)
-    valid = valid.reshape(RP, 1, PRE_TOK // 2)
-    column = jnp.broadcast_to(kv_gain[:, None], (KVL, UNIT))
+    done = first_hop(1, [near_sums])
+    done = second_hop(0, [*done, *messages[:3]])
+    send_far(3, done)
     steps = jnp.arange(SHARE, dtype=jnp.int32).reshape(UNITS, UNIT)
     tables = [
         jnp.swapaxes(t, 1, 2)
         for t in (*rope_tables(z * SHARE + steps), *rope_tables(2 * SHARE + steps))
     ]
-
-    block = first_hop(3, [block, column, valid, *tables])
+    block, side[0] = first_hop(2, far_sums[3:], side[:1])
     side = [lax.ppermute(codes, "tp", inward) for codes in side]
-    second_hop(2, [block, outer[1]])
-    block = second_hop(3, [side[0], outer[2]])
+    done = second_hop(1, [block, outer[0]])
+    done = first_hop(3, done)
+    done = second_hop(2, [*done, outer[1], side[0], *tables])
+    done = second_hop(3, [*done, outer[2]])
 
     def attend_to(requests, after):
         result = attend(
@@ -752,10 +756,9 @@
             messages,
             near_sums,
             outer,
-            column,
             tables,
-            valid,
-            kv_gain.reshape(1, KVL),
+            segment_ids,
+            gain,
             new_cos,
             new_sin,
             after,
@@ -765,17 +768,16 @@
     my_owners = lax.dynamic_slice_in_dim(owners, first_req, RP, 0)
     early, late = tuple(range(RP - 1)), (RP - 1,)
 
-    def pages_to(requests, halves, base, after):
+    def pages_to(requests, base, after):
         return pages_of(
             requests,
-            halves,
             rank,
             my_owners,
             near_sums,
             outer,
             sent,
             side,
-            column,
+            gain,
             tables[0],
             tables[1],
             base,
@@ -784,14 +786,12 @@
         )
 
     results, backs = [None] * 2, [None] * 2
-    results[0], backs[0] = attend_to(early, [block])
-    base = [jnp.zeros((pd_count, PART, SHARE), BF)] * 2 if pd_count > RP else []
-    pages = pages_to(early, (0, 1), base, results[0][:1])
-    results[1], backs[1] = attend_to(late, pages[:1])
-    first = pages_to(late, (0,), pages[:1], [*results[1][:1], *backs[0]])
-    second = pages_to(late, (1,), pages[1:], [*first, *backs[1]])
-    pages = [*first, *second]
-    cache = [lax.all_to_all(page, "pd", split_axis=0, concat_axis=0, tiled=True) for page in pages]
+    results[0], backs[0] = attend_to(early, done)
+    base = [jnp.zeros((pd_count, WIDTH, SHARE), BF)] if pd_count > RP else []
+    pages = pages_to(early, base, results[0][:1])
+    results[1], backs[1] = attend_to(late, [pages])
+    pages = pages_to(late, [pages], [*results[1][:1], *backs[0], backs[1][2]])
+    cache = lax.all_to_all(pages, "pd", split_axis=0, concat_axis=0, tiled=True)
 
     attended = [
         jnp.where(z == 3, result[3], back[0] + back[1] + back[2])
@@ -801,10 +801,10 @@
     attended = attended.reshape(heads, RP * 2, KVL).astype(F32)
     my_accepted = lax.dynamic_slice_in_dim(accepted, first_req, RP, 0)
     keep = (jnp.arange(2)[None, :] <= my_accepted[:, None]).astype(F32).reshape(RP * 2, 1)
-    answer = heads_out(attended, jnp.broadcast_to(keep, (RP * 2, DV)), kv_up, pages[1:])
-    placed = route(my_owners, answer, pd_count, cache[:1]).astype(BF)
+    answer = heads_out(attended, jnp.broadcast_to(keep, (RP * 2, DV)), kv_up, [pages])
+    placed = route(my_owners, answer, pd_count, [cache]).astype(BF)
     placed = lax.all_to_all(placed, "pd", split_axis=0, concat_axis=0, tiled=True)
-    cache = jnp.swapaxes(jnp.concatenate(cache, 1), 1, 2)
+    cache = jnp.swapaxes(cache, 1, 2)
     return (placed.reshape(pd_count * 2, heads * DV), cache)
 
 

time: 254 us -> 242 us (0.953)
  Pallas kernels: 98.9 us -> 106 us
  blocking collectives: 6.88 us -> 0 us
  waiting for transfers between devices: 60 us -> 53.5 us
    ppermute x2, waiting for transfers between devices: 27 us -> 6.17 us  [local_line(): side = [lax.ppermute(codes, 'tp', inward) for codes in side]]
    ppermute x4, starting transfers between devices: 19.4 us -> 8.93 us  [first_hop(): crossed.append(lax.ppermute(block, 'tp', across))]
    ppermute x4, starting transfers between devices: 12.4 us -> 20.5 us  [second_hop(): outer.append(lax.ppermute(block, 'tp', outward))]
    all_to_all x1 -> x0, blocking collectives: 6.88 us -> none  [local_line(): lax.all_to_all(placed, 'pd', split_axis=0, concat_axis=0, tiled=True)]
    all_to_all x2, waiting for transfers between devices: 12 us -> 17.9 us  [the longest x1 13.8 us: local_line(): cache = lax.all_to_all(pages, 'pd', split_axis=0, concat_axis=0, tiled=True)]
    ppermute x4, waiting for transfers between devices: 14.3 us -> 19.8 us  [second_hop(): outer.append(lax.ppermute(block, 'tp', outward))]
    ppermute x6, waiting for transfers between devices: 5.16 us -> 8.31 us  [attend_to(): return (result, [lax.ppermute(result[t], 'tp', [(3, t)]) for t in range(3)])]
    pallas_call x4, Pallas kernels: 22.6 us -> 25.1 us  [project_far(): pl.pallas_call(project_far_kernel, grid_spec=pltpu.PrefetchScalarGridSpec...]
  transfers between devices with their start and end apart: 25 -> 25, of which waited for: 7 -> 8; matrix products, arithmetic and copies ran while one was open for 5% -> 4% of each run, Pallas kernels for 35% -> 39%
where the time goes in v5:
time: 242 us; the launch traced here: 240 us
  Pallas kernels  106 us (44%)
  starting transfers between devices  55.1 us (23%)
  waiting for transfers between devices  53.5 us (22%)
  local copies, waits for them, and re-layouts  17.6 us (7%)
  other arithmetic  7.01 us (3%)
    pallas_call x8, Pallas kernels, add_on(): pl.pallas_call(functools.partial(add_kernel, -1 - len(carried)), grid_spe...  27.8 us
    pallas_call x4, Pallas kernels, project_far(): pl.pallas_call(project_far_kernel, grid_spec=pltpu.PrefetchScalarGridSpec...  25.1 us
    ppermute x4, starting transfers between devices, second_hop(): outer.append(lax.ppermute(block, 'tp', outward))  20.5 us
    ppermute x4, waiting for transfers between devices, second_hop(): outer.append(lax.ppermute(block, 'tp', outward))  19.8 us
    pallas_call x1, Pallas kernels, queries(): pl.pallas_call(body, grid=(heads // step,), in_specs=[pl.BlockSpec((rows,...  13.8 us
    all_to_all x1, waiting for transfers between devices, local_line(): cache = lax.all_to_all(pages, 'pd', split_axis=0, concat_axis=0, tiled=True)  13.8 us
    pallas_call x1, Pallas kernels, project_near(): pl.pallas_call(project_near_kernel, grid_spec=pltpu.PrefetchScalarGridSpe...  13.7 us
    unnamed x65, local copies, waits for them, and re-layouts  13.3 us
  transfers between devices with their start and end apart: 25, of which 8 were waited for; matrix products, arithmetic and copies ran while one was open for 4% of the time, Pallas kernels for 39%

profile of v5, /device:TPU:16, one launch (start us, length us, event | category | flops | bytes accessed | tf_op | source)
XLA Modules:
  0.0 240.0 jit_solution(10843919182310836369)
XLA Ops:
  1.3 6.3 %project_far.4 = (f32[2,3,576,128]{3,2,1,0:T(8,128)}, s16[2,3,592,128]{3,2,1,0:T(8,128)(2,1)}) custom-call(s32[2]{0:T(128)} %pad_add_fusion.rank, bf16[4,1536,1792]{2,1,0:T(8,128)(2,1)} %bitcast.18, bf16[576,1792]{1,0:T(8,128)(2,1)} %bitcast.23), custom_call_target="tpu_custom_call" | custom-call | flops 1024 | bytes 1024 | tf_op jit(solution)/shard_map/project_far/pallas_call | solution.py:268
  7.5 1.3 collective-permute-start.3
  8.8 6.3 %project_far.5 = (f32[2,3,576,128]{3,2,1,0:T(8,128)}, s16[2,3,592,128]{3,2,1,0:T(8,128)(2,1)}) custom-call(s32[2]{0:T(128)} %pad_add_fusion.rank, bf16[4,1536,1792]{2,1,0:T(8,128)(2,1)} %bitcast.19, bf16[576,1792]{1,0:T(8,128)(2,1)} %bitcast.24, f32[2,3,576,128]{3,2,1,0:T(8,128)} %get-tuple-element.25.refs_0_.own_ref), custom_call_target="tpu_custom_call" | custom-call | flops 1024 | bytes 1024 | tf_op jit(solution)/shard_map/project_far/pallas_call | solution.py:268
  15.1 1.3 collective-permute-start.5
  17.9 13.8 %queries.1 = (f32[32,8,576]{2,1,0:T(8,128)}, f32[4,8,576]{2,1,0:T(8,128)}) custom-call(bf16[8,1536]{1,0:T(8,128)(2,1)} %reshape.120.refs_0_, bf16[1536,6144]{1,0:T(8,128)(2,1)} %refs_1_.2, bf16[8,1792]{1,0:T(8,128)(2,1)} %refs_2_.2, bf16[576,1792]{1,0:T(8,128)(2,1)} %bitcast.25, bf16[512,8192]{1,0:T(8,128)(2,1)} %refs_7_.3, bf16[512,8192]{1,0:T(8,128)(2,1)} %refs_7_.3, ...), custom_call_target="tpu_custom_call" | custom-call | flops 1024 | bytes 1024 | tf_op jit(solution)/shard_map/queries/pallas_call | solution.py:484
  35.6 3.5 %add_on.8.refs_0_ = s16[2,3,592,128]{3,2,1,0:T(8,128)(2,1)} custom-call(s32[2]{0:T(128)} %pad_add_fusion.rank, f32[2,3,576,128]{3,2,1,0:T(8,128)} %get-tuple-element.25.refs_0_.own_ref, s16[2,3,592,128]{3,2,1,0:T(8,128)(2,1)} %copy-done.16, bf16[288,576]{1,0:T(8,128)(2,1)} %pad_maximum_fusion.refs_0_.refs_3_.refs_7_), custom_call_target="tpu_custom_call" | custom-call | flops 1024 | bytes 1024 | tf_op jit(solution)/shard_map/add_on/pallas_call | solution.py:357
  39.1 2.4 collective-permute-start.4
  42.8 4.3 %collective-permute-start.2 = (bf16[288,576]{1,0:T(8,128)(2,1)S(1)}, bf16[288,576]{1,0:T(8,128)(2,1)S(1)}, u32[]{:S(2)}, u32[]{:S(2)}) collective-permute-start(bf16[288,576]{1,0:T(8,128)(2,1)S(1)} %copy-done.3), channel_id=1, source_target_pairs={{8,12},{9,13},{10,14},{11,15},{24,28},{25,29},{26,30},{27,31}} | collective-permute-start | bytes 995336 | tf_op jit(solution)/shard_map/ppermute | solution.py:732
  47.2 6.3 %project_far.6 = (f32[2,3,576,128]{3,2,1,0:T(8,128)}, s16[2,3,592,128]{3,2,1,0:T(8,128)(2,1)}) custom-call(s32[2]{0:T(128)} %pad_add_fusion.rank, bf16[4,1536,1792]{2,1,0:T(8,128)(2,1)} %bitcast.20, bf16[576,1792]{1,0:T(8,128)(2,1)} %bitcast.26, s16[2,3,592,128]{3,2,1,0:T(8,128)(2,1)} %add_on.8.refs_0_), custom_call_target="tpu_custom_call" | custom-call | flops 1024 | bytes 1024 | tf_op jit(solution)/shard_map/project_far/pallas_call | solution.py:268
  53.4 13.7 %project_near.1 = (f32[3,2,4,576,128]{4,3,2,1,0:T(8,128)}, s16[1,4,592,128]{3,2,1,0:T(8,128)(2,1)}, s16[2,4,592,128]{3,2,1,0:T(8,128)(2,1)}) custom-call(s32[2]{0:T(128)} %pad_add_fusion.rank, bf16[4,1536,1792]{2,1,0:T(8,128)(2,1)} %bitcast.21, bf16[576,1792]{1,0:T(8,128)(2,1)} %bitcast.27, f32[2,3,576,128]{3,2,1,0:T(8,128)} %get-tuple-element.30.refs_0_.own_ref), custom_call_target="tpu_custom_call" | custom-call | flops 1024 | bytes 1024 | tf_op jit(solution)/shard_map/project_near/pallas_call | solution.py:311
  67.2 1.3 collective-permute-start.8
  68.5 3.5 %add_on.9.refs_0_ = s16[2,3,592,128]{3,2,1,0:T(8,128)(2,1)} custom-call(s32[2]{0:T(128)} %pad_add_fusion.rank, f32[2,3,576,128]{3,2,1,0:T(8,128)} %get-tuple-element.26.refs_10_.own_ref, s16[2,3,592,128]{3,2,1,0:T(8,128)(2,1)} %copy-done.14, f32[3,2,4,576,128]{4,3,2,1,0:T(8,128)} %get-tuple-element.31.refs_0_.own_ref.refs_8_), custom_call_target="tpu_custom_call" | custom-call | flops 1024 | bytes 1024 | tf_op jit(solution)/shard_map/add_on/pallas_call | solution.py:357
  72.0 2.8 %collective-permute-start.7 = (s16[2,3,592,128]{3,2,1,0:T(8,128)(2,1)}, s16[2,3,592,128]{3,2,1,0:T(8,128)(2,1)}, u32[]{:S(2)}, u32[]{:S(2)}) collective-permute-start(s16[2,3,592,128]{3,2,1,0:T(8,128)(2,1)} %add_on.9.refs_0_), channel_id=1, source_target_pairs={{4,8},{8,4},{5,9},{9,5},{6,10},{10,6},{7,11},{11,7},{20,24},{24,20... | collective-permute-start | bytes 2727944 | tf_op jit(solution)/shard_map/ppermute | solution.py:709
  76.6 3.5 %add_on.10.refs_0_.refs_3_ = s16[2,3,592,128]{3,2,1,0:T(8,128)(2,1)} custom-call(s32[2]{0:T(128)} %pad_add_fusion.rank, f32[3,2,4,576,128]{4,3,2,1,0:T(8,128)} %get-tuple-element.31.refs_0_.own_ref.refs_8_, s16[2,3,592,128]{3,2,1,0:T(8,128)(2,1)} %copy-done.17, s16[2,3,592,128]{3,2,1,0:T(8,128)(2,1)} %add_on.9.refs_0_, bf16[288,576]{1,0:T(8,128)(2,1)} %copy-done.4, ...), custom_call_target="tpu_custom_call" | custom-call | flops 1024 | bytes 1024 | tf_op jit(solution)/shard_map/add_on/pallas_call | solution.py:357
  80.1 8.3 %collective-permute-start.6 = (s16[2,3,592,128]{3,2,1,0:T(8,128)(2,1)}, s16[2,3,592,128]{3,2,1,0:T(8,128)(2,1)S(1)}, u32[]{:S(2)}, u32[]{:S(2)}) collective-permute-start(s16[2,3,592,128]{3,2,1,0:T(8,128)(2,1)} %add_on.10.refs_0_.refs_3_), channel_id=1, source_target_pairs={{8,12},{4,0},{9,13},{5,1},{10,14},{6,2},{11,15},{7,3},{24,28},{20,... | collective-permute-start | bytes 2727944 | tf_op jit(solution)/shard_map/ppermute | solution.py:715
  88.4 6.3 %project_far.7 = (f32[2,3,576,128]{3,2,1,0:T(8,128)}, s16[2,3,592,128]{3,2,1,0:T(8,128)(2,1)}) custom-call(s32[2]{0:T(128)} %pad_add_fusion.rank, bf16[4,1536,1792]{2,1,0:T(8,128)(2,1)} %bitcast.22, bf16[576,1792]{1,0:T(8,128)(2,1)} %bitcast.28, s16[2,3,592,128]{3,2,1,0:T(8,128)(2,1)} %add_on.10.refs_0_.refs_3_), custom_call_target="tpu_custom_call" | custom-call | flops 1024 | bytes 1024 | tf_op jit(solution)/shard_map/project_far/pallas_call | solution.py:268
  94.7 1.3 collective-permute-start.11
  96.0 3.5 %add_on.11 = (s16[2,3,592,128]{3,2,1,0:T(8,128)(2,1)}, s16[1,4,592,128]{3,2,1,0:T(8,128)(2,1)}) custom-call(s32[2]{0:T(128)} %pad_add_fusion.rank, f32[2,3,576,128]{3,2,1,0:T(8,128)} %get-tuple-element.30.refs_0_.own_ref, s16[2,3,592,128]{3,2,1,0:T(8,128)(2,1)} %collective-permute-done.8.got_ref, ...), custom_call_target="tpu_custom_call", output_to_operand_aliasing={{1}: (4, {})} | custom-call | flops 1024 | bytes 1024 | tf_op jit(solution)/shard_map/add_on/pallas_call | solution.py:357
  99.5 1.9 collective-permute-start.10
  101.4 4.7 %collective-permute-done.6.refs_1_.refs_9_.refs_0_ = s16[2,3,592,128]{3,2,1,0:T(8,128)(2,1)S(1)} collective-permute-done((s16[2,3,592,128]{3,2,1,0:T(8,128)(2,1)}, s16[2,3,592,128]{3,2,1,0:T(8,128)(2,1)S(1)}, u32[]{:S(2)}, u32[]{:S(2)}) %collective-permute-start.6) | collective-permute-done | bytes 909344 | tf_op jit(solution)/shard_map/ppermute | solution.py:715
  107.0 3.5 %add_on.12.refs_0_.refs_4_ = s16[2,3,592,128]{3,2,1,0:T(8,128)(2,1)} custom-call(s32[2]{0:T(128)} %pad_add_fusion.rank, f32[3,2,4,576,128]{4,3,2,1,0:T(8,128)} %get-tuple-element.31.refs_0_.own_ref.refs_8_, s16[2,3,592,128]{3,2,1,0:T(8,128)(2,1)} %collective-permute-done.7.got_ref, s16[2,3,592,128]{3,2,1,0:T(8,128)(2,1)} %get-tuple-element.36.refs_0_, ...), custom_call_target="tpu_custom_call" | custom-call | flops 1024 | bytes 1024 | tf_op jit(solution)/shard_map/add_on/pallas_call | solution.py:357
  110.5 4.0 %collective-permute-start.9 = (s16[2,3,592,128]{3,2,1,0:T(8,128)(2,1)}, s16[2,3,592,128]{3,2,1,0:T(8,128)(2,1)S(1)}, u32[]{:S(2)}, u32[]{:S(2)}) collective-permute-start(s16[2,3,592,128]{3,2,1,0:T(8,128)(2,1)} %add_on.12.refs_0_.refs_4_), channel_id=1, source_target_pairs={{8,12},{4,0},{9,13},{5,1},{10,14},{6,2},{11,15},{7,3},{24,28},{20,... | collective-permute-start | bytes 2727944 | tf_op jit(solution)/shard_map/ppermute | solution.py:715
  114.5 1.3 collective-permute-start.12
  117.9 3.5 %add_on.13.refs_0_ = s16[2,3,592,128]{3,2,1,0:T(8,128)(2,1)} custom-call(s32[2]{0:T(128)} %pad_add_fusion.rank, f32[2,3,576,128]{3,2,1,0:T(8,128)} %get-tuple-element.34.refs_0_.own_ref, s16[2,3,592,128]{3,2,1,0:T(8,128)(2,1)} %copy-done.13, s16[2,3,592,128]{3,2,1,0:T(8,128)(2,1)} %add_on.12.refs_0_.refs_4_), custom_call_target="tpu_custom_call" | custom-call | flops 1024 | bytes 1024 | tf_op jit(solution)/shard_map/add_on/pallas_call | solution.py:357
  121.3 1.9 collective-permute-start.14
  123.3 6.2 %collective-permute-done.12.refs_2_.refs_6_ = s16[1,4,592,128]{3,2,1,0:T(8,128)(2,1)S(1)} collective-permute-done((s16[1,4,592,128]{3,2,1,0:T(8,128)(2,1)}, s16[1,4,592,128]{3,2,1,0:T(8,128)(2,1)S(1)}, u32[]{:S(2)}, u32[]{:S(2)}) %collective-permute-start.12) | collective-permute-done | bytes 606240 | tf_op jit(solution)/shard_map/ppermute | solution.py:746
  129.4 1.8 collective-permute-done.9.refs_1_.refs_10_
  132.2 3.5 %add_on.14.refs_0_.refs_5_ = s16[2,3,592,128]{3,2,1,0:T(8,128)(2,1)} custom-call(s32[2]{0:T(128)} %pad_add_fusion.rank, f32[3,2,4,576,128]{4,3,2,1,0:T(8,128)} %get-tuple-element.31.refs_0_.own_ref.refs_8_, s16[2,3,592,128]{3,2,1,0:T(8,128)(2,1)} %copy-done.15, s16[2,3,592,128]{3,2,1,0:T(8,128)(2,1)} %add_on.13.refs_0_, s16[2,3,592,128]{3,2,1,0:T(8,128)(2,1)} %copy-done.8, ...), custom_call_target="tpu_custom_call" | custom-call | flops 1024 | bytes 1024 | tf_op jit(solution)/shard_map/add_on/pallas_call | solution.py:357
  135.7 4.0 %collective-permute-start.13 = (s16[2,3,592,128]{3,2,1,0:T(8,128)(2,1)}, s16[2,3,592,128]{3,2,1,0:T(8,128)(2,1)S(1)}, u32[]{:S(2)}, u32[]{:S(2)}) collective-permute-start(s16[2,3,592,128]{3,2,1,0:T(8,128)(2,1)} %add_on.14.refs_0_.refs_5_), channel_id=1, source_target_pairs={{8,12},{4,0},{9,13},{5,1},{10,14},{6,2},{11,15},{7,3},{24,28},{20,... | collective-permute-start | bytes 2727944 | tf_op jit(solution)/shard_map/ppermute | solution.py:715
  139.7 1.3 collective-permute-start.19
  142.2 13.3 %collective-permute-done.13.refs_1_.refs_11_.refs_2_ = s16[2,3,592,128]{3,2,1,0:T(8,128)(2,1)S(1)} collective-permute-done((s16[2,3,592,128]{3,2,1,0:T(8,128)(2,1)}, s16[2,3,592,128]{3,2,1,0:T(8,128)(2,1)S(1)}, u32[]{:S(2)}, u32[]{:S(2)}) %collective-permute-start.13) | collective-permute-done | bytes 909344 | tf_op jit(solution)/shard_map/ppermute | solution.py:715
  156.4 3.5 %add_on.15.refs_20_.refs_1_ = s16[2,3,592,128]{3,2,1,0:T(8,128)(2,1)} custom-call(s32[2]{0:T(128)} %pad_add_fusion.rank, f32[3,2,4,576,128]{4,3,2,1,0:T(8,128)} %get-tuple-element.31.refs_0_.own_ref.refs_8_, s16[2,3,592,128]{3,2,1,0:T(8,128)(2,1)} %collective-permute-done.14.got_ref, s16[2,3,592,128]{3,2,1,0:T(8,128)(2,1)} %add_on.14.refs_0_.refs_5_, ...), custom_call_target="tpu_custom_call" | custom-call | flops 1024 | bytes 1024 | tf_op jit(solution)/shard_map/add_on/pallas_call | solution.py:357
  159.9 4.2 %collective-permute-start.18 = (s16[2,3,592,128]{3,2,1,0:T(8,128)(2,1)}, s16[2,3,592,128]{3,2,1,0:T(8,128)(2,1)S(1)}, u32[]{:S(2)}, u32[]{:S(2)}) collective-permute-start(s16[2,3,592,128]{3,2,1,0:T(8,128)(2,1)} %add_on.15.refs_20_.refs_1_), channel_id=1, source_target_pairs={{8,12},{4,0},{9,13},{5,1},{10,14},{6,2},{11,15},{7,3},{24,28},{20,... | collective-permute-start | bytes 2727944 | tf_op jit(solution)/shard_map/ppermute | solution.py:715
  164.1 5.9 %attend.2 = (bf16[3,64,512]{2,1,0:T(8,128)(2,1)}, bf16[3,64,512]{2,1,0:T(8,128)(2,1)}, bf16[3,64,512]{2,1,0:T(8,128)(2,1)}, bf16[3,64,512]{2,1,0:T(8,128)(2,1)}) custom-call(s32[2]{0:T(128)} %pad_add_fusion.rank, bf16[288,576]{1,0:T(8,128)(2,1)} %copy-done.4, bf16[288,576]{1,0:T(8,128)(2,1)} %copy-done.5, bf16[288,576]{1,0:T(8,128)(2,1)} %copy-done.6, ...), custom_call_target="tpu_custom_call" | custom-call | flops 1024 | bytes 1024 | tf_op jit(solution)/shard_map/attend/pallas_call | solution.py:592
  171.4 1.3 collective-permute-start.17
  174.3 6.2 %pages.2.refs_18_.refs_7_ = bf16[4,576,384]{2,1,0:T(8,128)(2,1)} custom-call(s32[2]{0:T(128)} %pad_add_fusion.rank, s32[4]{0:T(128)} %dynamic_slice.9.slot, f32[3,2,4,576,128]{4,3,2,1,0:T(8,128)} %get-tuple-element.31.refs_0_.own_ref.refs_8_, s16[2,3,592,128]{3,2,1,0:T(8,128)(2,1)} %copy-done.7, s16[2,3,592,128]{3,2,1,0:T(8,128)(2,1)} %copy-done.8, ...), custom_call_target="tpu_custom_call" | custom-call | flops 1024 | bytes 1024 | tf_op jit(solution)/shard_map/pages/pallas_call | solution.py:419
  181.6 3.4 %attend.3 = (bf16[1,64,512]{2,1,0:T(8,128)(2,1)}, bf16[1,64,512]{2,1,0:T(8,128)(2,1)}, bf16[1,64,512]{2,1,0:T(8,128)(2,1)}, bf16[1,64,512]{2,1,0:T(8,128)(2,1)}) custom-call(s32[2]{0:T(128)} %pad_add_fusion.rank, bf16[288,576]{1,0:T(8,128)(2,1)} %copy-done.4, bf16[288,576]{1,0:T(8,128)(2,1)} %copy-done.5, bf16[288,576]{1,0:T(8,128)(2,1)} %copy-done.6, ...), custom_call_target="tpu_custom_call" | custom-call | flops 1024 | bytes 1024 | tf_op jit(solution)/shard_map/attend/pallas_call | solution.py:592
  184.9 1.3 collective-permute-start.22
  186.3 8.3 %collective-permute-done.22.refs_12_ = bf16[1,64,512]{2,1,0:T(8,128)(2,1)S(1)} collective-permute-done((bf16[1,64,512]{2,1,0:T(8,128)(2,1)}, bf16[1,64,512]{2,1,0:T(8,128)(2,1)S(1)}, u32[]{:S(2)}, u32[]{:S(2)}) %collective-permute-start.22) | collective-permute-done | bytes 65568 | tf_op jit(solution)/shard_map/ppermute | solution.py:766
  195.2 3.5 %pages.3.refs_8_ = bf16[4,576,384]{2,1,0:T(8,128)(2,1)} custom-call(s32[2]{0:T(128)} %pad_add_fusion.rank, s32[4]{0:T(128)} %dynamic_slice.9.slot, f32[3,2,4,576,128]{4,3,2,1,0:T(8,128)} %get-tuple-element.31.refs_0_.own_ref.refs_8_, s16[2,3,592,128]{3,2,1,0:T(8,128)(2,1)} %copy-done.12, ...), custom_call_target="tpu_custom_call", output_to_operand_aliasing={{}: (10, {})} | custom-call | flops 1024 | bytes 1024 | tf_op jit(solution)/shard_map/pages/pallas_call | solution.py:419
  198.8 3.7 %all-to-all-start = ((bf16[4,576,384]{2,1,0:T(8,128)(2,1)}), bf16[4,576,384]{2,1,0:T(8,128)(2,1)S(1)}, u32[]{:S(2)}, u32[]{:S(2)}) async-start(bf16[4,576,384]{2,1,0:T(8,128)(2,1)} %pages.3.refs_8_), calls=%async_computation | async-start | bytes 3538944 | tf_op jit(solution)/shard_map/all_to_all | solution.py:794
  206.5 4.4 %heads_out.1.answer_ref = f32[8,4096]{1,0:T(8,128)} custom-call(f32[32,8,512]{2,1,0:T(8,128)} %reshape.130.o_ref, f32[8,128]{1,0:T(8,128)} %broadcast_in_dim.2.keep_ref, bf16[512,8192]{1,0:T(8,128)(2,1)} %refs_7_.3, bf16[512,8192]{1,0:T(8,128)(2,1)} %refs_7_.3, bf16[512,8192]{1,0:T(8,128)(2,1)} %refs_7_.3, bf16[512,8192]{1,0:T(8,128)(2,1)} %refs_7_.3, ...), custom_call_target="tpu_custom_call" | custom-call | flops 1024 | bytes 1024 | tf_op jit(solution)/shard_map/heads_out/pallas_call | solution.py:634
  210.9 13.8 %all-to-all-done.refs_0_ = bf16[4,576,384]{2,1,0:T(8,128)(2,1)S(1)} async-done(((bf16[4,576,384]{2,1,0:T(8,128)(2,1)}), bf16[4,576,384]{2,1,0:T(8,128)(2,1)S(1)}, u32[]{:S(2)}, u32[]{:S(2)}) %all-to-all-start) | async-done | bytes 1769504 | tf_op jit(solution)/shard_map/all_to_all | solution.py:794
  225.9 1.6 route.1
  227.5 1.6 convert_element_type.88
  229.1 3.3 %all-to-all-start.1 = ((bf16[4,2,4096]{2,1,0:T(2,128)(2,1)}), bf16[4,2,4096]{2,1,0:T(2,128)(2,1)S(1)}, u32[]{:S(2)}, u32[]{:S(2)}) async-start(bf16[4,2,4096]{2,1,0:T(2,128)(2,1)} %convert_element_type.88), calls=%async_computation.1 | async-start | bytes 131072 | tf_op jit(solution)/shard_map/all_to_all | solution.py:806
  232.4 4.1 %all-to-all-done.1 = bf16[4,2,4096]{2,1,0:T(2,128)(2,1)S(1)} async-done(((bf16[4,2,4096]{2,1,0:T(2,128)(2,1)}), bf16[4,2,4096]{2,1,0:T(2,128)(2,1)S(1)}, u32[]{:S(2)}, u32[]{:S(2)}) %all-to-all-start.1) | async-done | bytes 65568 | tf_op jit(solution)/shard_map/all_to_all | solution.py:806
  237.2 2.9 %copy.24 = bf16[4,384,576]{1,2,0:T(8,128)(2,1)} copy(bf16[4,384,576]{1,2,0:T(8,128)(2,1)} %bitcast.29) | data formatting | bytes 3538944
  (114 shorter events, 25.5 us)
Async XLA Ops:
  0.6 15.8 %copy-start = (bf16[16,2,1536]{2,1,0:T(2,128)(2,1)S(1)}, bf16[16,2,1536]{2,1,0:T(2,128)(2,1)}, u32[]{:S(2)}) copy-start(bf16[16,2,1536]{2,1,0:T(2,128)(2,1)} %param.14) | copy-start | bytes 294916
  7.5 27.1 %collective-permute-start.3 = (s16[2,3,592,128]{3,2,1,0:T(8,128)(2,1)}, s16[2,3,592,128]{3,2,1,0:T(8,128)(2,1)S(1)}, u32[]{:S(2)}, u32[]{:S(2)}) collective-permute-start(s16[2,3,592,128]{3,2,1,0:T(8,128)(2,1)} %get-tuple-element.29), channel_id=1, source_target_pairs={{0,4},{12,8},{1,5},{13,9},{2,6},{14,10},{3,7},{15,11},{16,20},{28,... | collective-permute-start | bytes 2727944 | tf_op jit(solution)/shard_map/ppermute | solution.py:705
  15.1 52.0 %collective-permute-start.5 = (s16[2,3,592,128]{3,2,1,0:T(8,128)(2,1)}, s16[2,3,592,128]{3,2,1,0:T(8,128)(2,1)S(1)}, u32[]{:S(2)}, u32[]{:S(2)}) collective-permute-start(s16[2,3,592,128]{3,2,1,0:T(8,128)(2,1)} %get-tuple-element.32), channel_id=1, source_target_pairs={{0,4},{12,8},{1,5},{13,9},{2,6},{14,10},{3,7},{15,11},{16,20},{28,... | collective-permute-start | bytes 2727944 | tf_op jit(solution)/shard_map/ppermute | solution.py:705
  34.7 6.8 %copy-start.3 = (bf16[288,576]{1,0:T(8,128)(2,1)S(1)}, bf16[288,576]{1,0:T(8,128)(2,1)}, u32[]{:S(2)}) copy-start(bf16[288,576]{1,0:T(8,128)(2,1)} %pad_maximum_fusion.refs_0_.refs_3_.refs_7_) | copy-start | bytes 995332
  39.1 35.7 %collective-permute-start.4 = (s16[2,3,592,128]{3,2,1,0:T(8,128)(2,1)}, s16[2,3,592,128]{3,2,1,0:T(8,128)(2,1)S(1)}, u32[]{:S(2)}, u32[]{:S(2)}) collective-permute-start(s16[2,3,592,128]{3,2,1,0:T(8,128)(2,1)} %add_on.8.refs_0_), channel_id=1, source_target_pairs={{4,8},{8,4},{5,9},{9,5},{6,10},{10,6},{7,11},{11,7},{20,24},{24,20... | collective-permute-start | bytes 2727944 | tf_op jit(solution)/shard_map/ppermute | solution.py:709
  41.4 30.5 %collective-permute-start = (bf16[288,576]{1,0:T(8,128)(2,1)S(1)}, bf16[288,576]{1,0:T(8,128)(2,1)S(1)}, u32[]{:S(2)}, u32[]{:S(2)}) collective-permute-start(bf16[288,576]{1,0:T(8,128)(2,1)S(1)} %copy-done.3), channel_id=1, source_target_pairs={{0,12},{1,13},{2,14},{3,15},{16,28},{17,29},{18,30},{19,31}} | collective-permute-start | bytes 995336 | tf_op jit(solution)/shard_map/ppermute | solution.py:732
  42.1 32.6 %collective-permute-start.1 = (bf16[288,576]{1,0:T(8,128)(2,1)S(1)}, bf16[288,576]{1,0:T(8,128)(2,1)S(1)}, u32[]{:S(2)}, u32[]{:S(2)}) collective-permute-start(bf16[288,576]{1,0:T(8,128)(2,1)S(1)} %copy-done.3), channel_id=1, source_target_pairs={{4,12},{5,13},{6,14},{7,15},{20,28},{21,29},{22,30},{23,31}} | collective-permute-start | bytes 995336 | tf_op jit(solution)/shard_map/ppermute | solution.py:732
  42.8 32.0 %collective-permute-start.2 = (bf16[288,576]{1,0:T(8,128)(2,1)S(1)}, bf16[288,576]{1,0:T(8,128)(2,1)S(1)}, u32[]{:S(2)}, u32[]{:S(2)}) collective-permute-start(bf16[288,576]{1,0:T(8,128)(2,1)S(1)} %copy-done.3), channel_id=1, source_target_pairs={{8,12},{9,13},{10,14},{11,15},{24,28},{25,29},{26,30},{27,31}} | collective-permute-start | bytes 995336 | tf_op jit(solution)/shard_map/ppermute | solution.py:732
  67.2 1.3 copy-start.14
  67.2 28.8 %collective-permute-start.8 = (s16[2,3,592,128]{3,2,1,0:T(8,128)(2,1)}, s16[2,3,592,128]{3,2,1,0:T(8,128)(2,1)}, u32[]{:S(2)}, u32[]{:S(2)}) collective-permute-start(s16[2,3,592,128]{3,2,1,0:T(8,128)(2,1)} %get-tuple-element.33), channel_id=1, source_target_pairs={{0,4},{12,8},{1,5},{13,9},{2,6},{14,10},{3,7},{15,11},{16,20},{28,... | collective-permute-start | bytes 2727944 | tf_op jit(solution)/shard_map/ppermute | solution.py:705
  72.0 2.8 %copy-start.4 = (bf16[288,576]{1,0:T(8,128)(2,1)}, bf16[288,576]{1,0:T(8,128)(2,1)S(1)}, u32[]{:S(2)}) copy-start(bf16[288,576]{1,0:T(8,128)(2,1)S(1)} %collective-permute-done.refs_1_.refs_0_.refs_4_) | copy-start | bytes 995332
  72.0 29.4 %collective-permute-start.7 = (s16[2,3,592,128]{3,2,1,0:T(8,128)(2,1)}, s16[2,3,592,128]{3,2,1,0:T(8,128)(2,1)}, u32[]{:S(2)}, u32[]{:S(2)}) collective-permute-start(s16[2,3,592,128]{3,2,1,0:T(8,128)(2,1)} %add_on.9.refs_0_), channel_id=1, source_target_pairs={{4,8},{8,4},{5,9},{9,5},{6,10},{10,6},{7,11},{11,7},{20,24},{24,20... | collective-permute-start | bytes 2727944 | tf_op jit(solution)/shard_map/ppermute | solution.py:709
  80.1 26.0 %collective-permute-start.6 = (s16[2,3,592,128]{3,2,1,0:T(8,128)(2,1)}, s16[2,3,592,128]{3,2,1,0:T(8,128)(2,1)S(1)}, u32[]{:S(2)}, u32[]{:S(2)}) collective-permute-start(s16[2,3,592,128]{3,2,1,0:T(8,128)(2,1)} %add_on.10.refs_0_.refs_3_), channel_id=1, source_target_pairs={{8,12},{4,0},{9,13},{5,1},{10,14},{6,2},{11,15},{7,3},{24,28},{20,... | collective-permute-start | bytes 2727944 | tf_op jit(solution)/shard_map/ppermute | solution.py:715
  94.7 22.2 %collective-permute-start.11 = (s16[2,3,592,128]{3,2,1,0:T(8,128)(2,1)}, s16[2,3,592,128]{3,2,1,0:T(8,128)(2,1)S(1)}, u32[]{:S(2)}, u32[]{:S(2)}) collective-permute-start(s16[2,3,592,128]{3,2,1,0:T(8,128)(2,1)} %get-tuple-element.37), channel_id=1, source_target_pairs={{0,4},{12,8},{1,5},{13,9},{2,6},{14,10},{3,7},{15,11},{16,20},{28,... | collective-permute-start | bytes 2727944 | tf_op jit(solution)/shard_map/ppermute | solution.py:705
  99.5 29.9 %collective-permute-start.10 = (s16[2,3,592,128]{3,2,1,0:T(8,128)(2,1)}, s16[2,3,592,128]{3,2,1,0:T(8,128)(2,1)S(1)}, u32[]{:S(2)}, u32[]{:S(2)}) collective-permute-start(s16[2,3,592,128]{3,2,1,0:T(8,128)(2,1)} %get-tuple-element.36.refs_0_), channel_id=1, source_target_pairs={{4,8},{8,4},{5,9},{9,5},{6,10},{10,6},{7,11},{11,7},{20,24},{24,20... | collective-permute-start | bytes 2727944 | tf_op jit(solution)/shard_map/ppermute | solution.py:709
  110.5 20.7 %collective-permute-start.9 = (s16[2,3,592,128]{3,2,1,0:T(8,128)(2,1)}, s16[2,3,592,128]{3,2,1,0:T(8,128)(2,1)S(1)}, u32[]{:S(2)}, u32[]{:S(2)}) collective-permute-start(s16[2,3,592,128]{3,2,1,0:T(8,128)(2,1)} %add_on.12.refs_0_.refs_4_), channel_id=1, source_target_pairs={{8,12},{4,0},{9,13},{5,1},{10,14},{6,2},{11,15},{7,3},{24,28},{20,... | collective-permute-start | bytes 2727944 | tf_op jit(solution)/shard_map/ppermute | solution.py:715
  114.5 14.9 %collective-permute-start.12 = (s16[1,4,592,128]{3,2,1,0:T(8,128)(2,1)}, s16[1,4,592,128]{3,2,1,0:T(8,128)(2,1)S(1)}, u32[]{:S(2)}, u32[]{:S(2)}) collective-permute-start(s16[1,4,592,128]{3,2,1,0:T(8,128)(2,1)} %get-tuple-element.38), channel_id=1, source_target_pairs={{0,4},{12,8},{1,5},{13,9},{2,6},{14,10},{3,7},{15,11},{16,20},{28,... | collective-permute-start | bytes 1818632 | tf_op jit(solution)/shard_map/ppermute | solution.py:746
  121.3 20.9 %collective-permute-start.14 = (s16[2,3,592,128]{3,2,1,0:T(8,128)(2,1)}, s16[2,3,592,128]{3,2,1,0:T(8,128)(2,1)}, u32[]{:S(2)}, u32[]{:S(2)}) collective-permute-start(s16[2,3,592,128]{3,2,1,0:T(8,128)(2,1)} %add_on.13.refs_0_), channel_id=1, source_target_pairs={{4,8},{8,4},{5,9},{9,5},{6,10},{10,6},{7,11},{11,7},{20,24},{24,20... | collective-permute-start | bytes 2727944 | tf_op jit(solution)/shard_map/ppermute | solution.py:709
  129.4 1.8 copy-start.10
  129.4 1.8 copy-start.15
  135.7 19.8 %collective-permute-start.13 = (s16[2,3,592,128]{3,2,1,0:T(8,128)(2,1)}, s16[2,3,592,128]{3,2,1,0:T(8,128)(2,1)S(1)}, u32[]{:S(2)}, u32[]{:S(2)}) collective-permute-start(s16[2,3,592,128]{3,2,1,0:T(8,128)(2,1)} %add_on.14.refs_0_.refs_5_), channel_id=1, source_target_pairs={{8,12},{4,0},{9,13},{5,1},{10,14},{6,2},{11,15},{7,3},{24,28},{20,... | collective-permute-start | bytes 2727944 | tf_op jit(solution)/shard_map/ppermute | solution.py:715
  139.7 33.6 %collective-permute-start.19 = (s16[2,4,592,128]{3,2,1,0:T(8,128)(2,1)}, s16[2,4,592,128]{3,2,1,0:T(8,128)(2,1)S(1)}, u32[]{:S(2)}, u32[]{:S(2)}) collective-permute-start(s16[2,4,592,128]{3,2,1,0:T(8,128)(2,1)} %get-tuple-element.43), channel_id=1, source_target_pairs={{0,4},{12,8},{1,5},{13,9},{2,6},{14,10},{3,7},{15,11},{16,20},{28,... | collective-permute-start | bytes 3637256 | tf_op jit(solution)/shard_map/ppermute | solution.py:746
  159.9 20.7 %collective-permute-start.18 = (s16[2,3,592,128]{3,2,1,0:T(8,128)(2,1)}, s16[2,3,592,128]{3,2,1,0:T(8,128)(2,1)S(1)}, u32[]{:S(2)}, u32[]{:S(2)}) collective-permute-start(s16[2,3,592,128]{3,2,1,0:T(8,128)(2,1)} %add_on.15.refs_20_.refs_1_), channel_id=1, source_target_pairs={{8,12},{4,0},{9,13},{5,1},{10,14},{6,2},{11,15},{7,3},{24,28},{20,... | collective-permute-start | bytes 2727944 | tf_op jit(solution)/shard_map/ppermute | solution.py:715
  164.1 8.6 %copy-start.30 = (s32[16]{0:T(128)S(1)}, s32[16]{0:T(128)}, u32[]{:S(2)}) copy-start(s32[16]{0:T(128)} %param.17) | copy-start | bytes 196
  170.0 16.2 %collective-permute-start.15 = (bf16[3,64,512]{2,1,0:T(8,128)(2,1)}, bf16[3,64,512]{2,1,0:T(8,128)(2,1)S(1)}, u32[]{:S(2)}, u32[]{:S(2)}) collective-permute-start(bf16[3,64,512]{2,1,0:T(8,128)(2,1)} %get-tuple-element.40.refs_11_), channel_id=1, source_target_pairs={{12,0},{13,1},{14,2},{15,3},{28,16},{29,17},{30,18},{31,19}} | collective-permute-start | bytes 589832 | tf_op jit(solution)/shard_map/ppermute | solution.py:766
  170.7 15.6 %collective-permute-start.16 = (bf16[3,64,512]{2,1,0:T(8,128)(2,1)}, bf16[3,64,512]{2,1,0:T(8,128)(2,1)S(1)}, u32[]{:S(2)}, u32[]{:S(2)}) collective-permute-start(bf16[3,64,512]{2,1,0:T(8,128)(2,1)} %get-tuple-element.41), channel_id=1, source_target_pairs={{12,4},{13,5},{14,6},{15,7},{28,20},{29,21},{30,22},{31,23}} | collective-permute-start | bytes 589832 | tf_op jit(solution)/shard_map/ppermute | solution.py:766
  171.4 14.9 %collective-permute-start.17 = (bf16[3,64,512]{2,1,0:T(8,128)(2,1)}, bf16[3,64,512]{2,1,0:T(8,128)(2,1)S(1)}, u32[]{:S(2)}, u32[]{:S(2)}) collective-permute-start(bf16[3,64,512]{2,1,0:T(8,128)(2,1)} %get-tuple-element.42), channel_id=1, source_target_pairs={{12,8},{13,9},{14,10},{15,11},{28,24},{29,25},{30,26},{31,27}} | collective-permute-start | bytes 589832 | tf_op jit(solution)/shard_map/ppermute | solution.py:766
  173.3 1.1 copy-start.11
  180.6 1.0 copy-start.12
  184.9 9.6 %collective-permute-start.22 = (bf16[1,64,512]{2,1,0:T(8,128)(2,1)}, bf16[1,64,512]{2,1,0:T(8,128)(2,1)S(1)}, u32[]{:S(2)}, u32[]{:S(2)}) collective-permute-start(bf16[1,64,512]{2,1,0:T(8,128)(2,1)} %get-tuple-element.47), channel_id=1, source_target_pairs={{12,8},{13,9},{14,10},{15,11},{28,24},{29,25},{30,26},{31,27}} | collective-permute-start | bytes 196616 | tf_op jit(solution)/shard_map/ppermute | solution.py:766
  186.2 8.3 %copy-start.18 = (bf16[3,64,512]{2,1,0:T(8,128)(2,1)}, bf16[3,64,512]{2,1,0:T(8,128)(2,1)S(1)}, u32[]{:S(2)}) copy-start(bf16[3,64,512]{2,1,0:T(8,128)(2,1)S(1)} %collective-permute-done.15.refs_9_) | copy-start | bytes 589828
  186.3 8.3 %copy-start.20 = (bf16[3,64,512]{2,1,0:T(8,128)(2,1)}, bf16[3,64,512]{2,1,0:T(8,128)(2,1)S(1)}, u32[]{:S(2)}) copy-start(bf16[3,64,512]{2,1,0:T(8,128)(2,1)S(1)} %collective-permute-done.16.refs_10_) | copy-start | bytes 589828
  186.3 8.3 %copy-start.22 = (bf16[3,64,512]{2,1,0:T(8,128)(2,1)}, bf16[3,64,512]{2,1,0:T(8,128)(2,1)S(1)}, u32[]{:S(2)}) copy-start(bf16[3,64,512]{2,1,0:T(8,128)(2,1)S(1)} %collective-permute-done.17.refs_11_) | copy-start | bytes 589828
  198.8 3.8 %copy-start.31 = (s32[16]{0:T(128)S(1)}, s32[16]{0:T(128)}, u32[]{:S(2)}) copy-start(s32[16]{0:T(128)} %param.19) | copy-start | bytes 196
  198.8 4.1 %copy-start.27 = (bf16[1,64,512]{2,1,0:T(8,128)(2,1)S(1)}, bf16[1,64,512]{2,1,0:T(8,128)(2,1)}, u32[]{:S(2)}) copy-start(bf16[1,64,512]{2,1,0:T(8,128)(2,1)} %get-tuple-element.45.refs_8_) | copy-start | bytes 196612
  198.8 4.7 %copy-start.29 = (bf16[1,64,512]{2,1,0:T(8,128)(2,1)S(1)}, bf16[1,64,512]{2,1,0:T(8,128)(2,1)}, u32[]{:S(2)}) copy-start(bf16[1,64,512]{2,1,0:T(8,128)(2,1)} %get-tuple-element.46) | copy-start | bytes 196612
  198.8 5.4 %copy-start.19 = (bf16[3,64,512]{2,1,0:T(8,128)(2,1)S(1)}, bf16[3,64,512]{2,1,0:T(8,128)(2,1)}, u32[]{:S(2)}) copy-start(bf16[3,64,512]{2,1,0:T(8,128)(2,1)} %copy-done.18) | copy-start | bytes 589828
  198.8 5.4 %copy-start.21 = (bf16[3,64,512]{2,1,0:T(8,128)(2,1)S(1)}, bf16[3,64,512]{2,1,0:T(8,128)(2,1)}, u32[]{:S(2)}) copy-start(bf16[3,64,512]{2,1,0:T(8,128)(2,1)} %copy-done.20) | copy-start | bytes 589828
  198.8 5.4 %copy-start.23 = (bf16[3,64,512]{2,1,0:T(8,128)(2,1)S(1)}, bf16[3,64,512]{2,1,0:T(8,128)(2,1)}, u32[]{:S(2)}) copy-start(bf16[3,64,512]{2,1,0:T(8,128)(2,1)} %copy-done.22) | copy-start | bytes 589828
  198.8 5.4 %copy-start.26 = (bf16[3,64,512]{2,1,0:T(8,128)(2,1)S(1)}, bf16[3,64,512]{2,1,0:T(8,128)(2,1)}, u32[]{:S(2)}) copy-start(bf16[3,64,512]{2,1,0:T(8,128)(2,1)} %get-tuple-element.39) | copy-start | bytes 589828
  198.8 5.5 %copy-start.25 = (bf16[1,64,512]{2,1,0:T(8,128)(2,1)S(1)}, bf16[1,64,512]{2,1,0:T(8,128)(2,1)}, u32[]{:S(2)}) copy-start(bf16[1,64,512]{2,1,0:T(8,128)(2,1)} %copy-done.24) | copy-start | bytes 196612
  198.8 5.5 %copy-start.28 = (bf16[1,64,512]{2,1,0:T(8,128)(2,1)S(1)}, bf16[1,64,512]{2,1,0:T(8,128)(2,1)}, u32[]{:S(2)}) copy-start(bf16[1,64,512]{2,1,0:T(8,128)(2,1)} %get-tuple-element.44) | copy-start | bytes 196612
  198.8 25.9 %all-to-all-start = ((bf16[4,576,384]{2,1,0:T(8,128)(2,1)}), bf16[4,576,384]{2,1,0:T(8,128)(2,1)S(1)}, u32[]{:S(2)}, u32[]{:S(2)}) async-start(bf16[4,576,384]{2,1,0:T(8,128)(2,1)} %pages.3.refs_8_), calls=%async_computation | async-start | bytes 3538944 | tf_op jit(solution)/shard_map/all_to_all | solution.py:794
  202.8 1.4 collective-permute-start.20
  203.5 0.8 collective-permute-start.21
  224.7 1.2 copy-start.2
  229.1 7.4 %all-to-all-start.1 = ((bf16[4,2,4096]{2,1,0:T(2,128)(2,1)}), bf16[4,2,4096]{2,1,0:T(2,128)(2,1)S(1)}, u32[]{:S(2)}, u32[]{:S(2)}) async-start(bf16[4,2,4096]{2,1,0:T(2,128)(2,1)} %convert_element_type.88), calls=%async_computation.1 | async-start | bytes 131072 | tf_op jit(solution)/shard_map/all_to_all | solution.py:806
  236.5 3.5 %copy-start.1 = (bf16[16,2,1536]{2,1,0:T(2,128)(2,1)S(1)}, bf16[16,2,1536]{2,1,0:T(2,128)(2,1)}, u32[]{:S(2)}) copy-start(bf16[16,2,1536]{2,1,0:T(2,128)(2,1)} %param.14) | copy-start | bytes 294916
  (9 other events, 7.9 us)

commit v6 on v5

--- a/solution.py
+++ b/solution.py
@@ -28,6 +28,7 @@
 I16 = jnp.int16
 NT = (((1,), (1,)), ((), ()))
 ROOM = pltpu.CompilerParams(vmem_limit_bytes=60 << 20)
+SOME = pltpu.CompilerParams(vmem_limit_bytes=52 << 20)
 ANY = pl.BlockSpec(memory_space=pl.ANY)
 VMEM = pl.BlockSpec(memory_space=pltpu.VMEM)
 SMEM = pl.BlockSpec(memory_space=pltpu.SMEM)
@@ -374,7 +375,7 @@
             *[jax.ShapeDtypeStruct(c.shape, c.dtype) for c in carried],
         ],
         input_output_aliases={3 + len(after) + n: 1 + n for n in range(len(carried))},
-        compiler_params=ROOM,
+        compiler_params=SOME,
         cost_estimate=COST,
         name="add_on",
     )(rank, own, got, *after, *carried)
@@ -440,7 +441,7 @@
         ),
         out_shape=jax.ShapeDtypeStruct((count, WIDTH, SHARE), BF),
         input_output_aliases={8 + 2 * total + n: n for n in range(len(base))},
-        compiler_params=ROOM,
+        compiler_params=SOME,
         cost_estimate=COST,
         name="pages",
     )(rank, slot, own, *got, *sent, *side, gain, cosine, sine, *base, *after)
@@ -508,7 +509,7 @@
     )(latents, q_up, draft, down_t, *([kv_up] * step), cosine, sine, after)
 
 
-def attend_kernel(requests, rank, *refs):
+def attend_kernel(requests, rank, first_ref, *refs):
     count = len(requests)
     q_refs, draft_refs, refs = refs[:4], refs[4:8], refs[8:]
     own_ref, got_refs, refs = refs[0], refs[1 : 1 + count], refs[1 + count :]
@@ -557,7 +558,7 @@
         drafts = jnp.concatenate([drafts, jnp.zeros((UNIT - new, WIDTH), F32)], 0).astype(BF)
         query = jnp.concatenate([ref[...] for ref in q_refs], 0)
         scores = jnp.dot(query, keys_ref[...], preferred_element_type=F32) * scale
-        segments = segment_ref[pl.ds(rank[1] * RP + request, 1), :]
+        segments = segment_ref[pl.ds(first_ref[0] + request, 1), :]
         valid = segments[:, PRE_TOK // 2 :] == segments[:, PRE_TOK - 1 :]
         scores = jnp.where(valid, scores, -1e30)
         fresh = lax.dot_general(query, drafts, NT, preferred_element_type=F32) * scale
@@ -580,27 +581,27 @@
             ref[0] = result[t * local_rows : (t + 1) * local_rows]
 
 
-def attend(requests, rank, messages, own, got, tables, segments, gain, cosine, sine, after):
+def attend(requests, rank, first, messages, own, got, tables, segments, gain, cosine, sine, after):
     new = 2 * RP
     local_rows = (messages[0].shape[0] - 4 * new) // RP
     last = RP * local_rows // (4 * new)
     start, count = requests[0], len(requests)
     got = got[start : start + count]
     out = jax.ShapeDtypeStruct((count, local_rows, KVL), BF)
-    whole = lambda i, rank: (0, 0)
-    whole3 = lambda i, rank: (0, 0, 0)
+    whole = lambda i, *_: (0, 0)
+    whole3 = lambda i, *_: (0, 0, 0)
     return pl.pallas_call(
         functools.partial(attend_kernel, requests),
         grid_spec=pltpu.PrefetchScalarGridSpec(
-            num_scalar_prefetch=1,
+            num_scalar_prefetch=2,
             grid=(count,),
             in_specs=[
-                *([pl.BlockSpec((local_rows, WIDTH), lambda i, rank: (i + start, 0))] * 4),
-                *([pl.BlockSpec((4 * new, WIDTH), lambda i, rank: (last, 0))] * 4),
+                *([pl.BlockSpec((local_rows, WIDTH), lambda i, *_: (i + start, 0))] * 4),
+                *([pl.BlockSpec((4 * new, WIDTH), lambda i, *_: (last, 0))] * 4),
                 pl.BlockSpec(
-                    (UNITS, 2, None, WIDTH, UNIT), lambda i, rank: (0, 0, i + start, 0, 0)
+                    (UNITS, 2, None, WIDTH, UNIT), lambda i, *_: (0, 0, i + start, 0, 0)
                 ),
-                *([pl.BlockSpec((2, UNITS, CODED, UNIT), lambda i, rank: (0, 0, 0, 0))] * count),
+                *([pl.BlockSpec((2, UNITS, CODED, UNIT), lambda i, *_: (0, 0, 0, 0))] * count),
                 *([pl.BlockSpec((UNITS, HALF, UNIT), whole3)] * 4),
                 pl.BlockSpec(segments.shape, whole),
                 pl.BlockSpec((1, KVL), whole),
@@ -608,14 +609,14 @@
                 pl.BlockSpec(sine.shape, whole),
                 *([ANY] * len(after)),
             ],
-            out_specs=[pl.BlockSpec((1, local_rows, KVL), lambda i, rank: (i, 0, 0))] * 4,
+            out_specs=[pl.BlockSpec((1, local_rows, KVL), lambda i, *_: (i, 0, 0))] * 4,
             scratch_shapes=[pltpu.VMEM((WIDTH, 2 * SHARE), BF)],
         ),
         out_shape=[out] * 4,
-        compiler_params=ROOM,
+        compiler_params=SOME,
         cost_estimate=COST,
         name="attend",
-    )(rank, *messages, *messages, own, *got, *tables, segments, gain, cosine, sine, *after)
+    )(rank, first, *messages, *messages, own, *got, *tables, segments, gain, cosine, sine, *after)
 
 
 def heads_kernel(step, o_ref, keep_ref, *refs):
@@ -652,7 +653,7 @@
     out_ref = refs[-1]
     out_ref[...] = jnp.zeros_like(out_ref)
     for r in range(RP):
-        out_ref[slot[r]] = answer_ref[2 * r : 2 * r + 2, :]
+        out_ref[slot[r]] = answer_ref[2 * r : 2 * r + 2, :].astype(BF)
 
 
 def route(slot, answer, count, after):
@@ -661,8 +662,8 @@
         route_kernel,
         in_specs=[SMEM, VMEM, *([ANY] * len(after))],
         out_specs=VMEM,
-        out_shape=jax.ShapeDtypeStruct((count, 2, width), F32),
-        compiler_params=ROOM,
+        out_shape=jax.ShapeDtypeStruct((count, 2, width), BF),
+        compiler_params=SOME,
         cost_estimate=COST,
         name="route",
     )(slot, answer, *after)
@@ -692,7 +693,7 @@
     first_req = p * RP
 
     gain = kv_gain.reshape(1, KVL)
-    rank = jnp.stack([z, p]).astype(jnp.int32)
+    rank = z.astype(jnp.int32).reshape(1)
     hidden = prefill_hidden.reshape(RP, PRE_TOK, prefill_hidden.shape[1])
     down_t = kv_down.T
     inward, across, outward = [(0, 1), (3, 2)], [(1, 2), (2, 1)], [(2, 3), (1, 0)]
@@ -753,6 +754,7 @@
         result = attend(
             requests,
             rank,
+            first_req.astype(jnp.int32).reshape(1),
             messages,
             near_sums,
             outer,
@@ -790,7 +792,7 @@
     base = [jnp.zeros((pd_count, WIDTH, SHARE), BF)] if pd_count > RP else []
     pages = pages_to(early, base, results[0][:1])
     results[1], backs[1] = attend_to(late, [pages])
-    pages = pages_to(late, [pages], [*results[1][:1], *backs[0], backs[1][2]])
+    pages = pages_to(late, [pages], [*results[1][:1], *backs[0]])
     cache = lax.all_to_all(pages, "pd", split_axis=0, concat_axis=0, tiled=True)
 
     attended = [
@@ -802,7 +804,7 @@
     my_accepted = lax.dynamic_slice_in_dim(accepted, first_req, RP, 0)
     keep = (jnp.arange(2)[None, :] <= my_accepted[:, None]).astype(F32).reshape(RP * 2, 1)
     answer = heads_out(attended, jnp.broadcast_to(keep, (RP * 2, DV)), kv_up, [pages])
-    placed = route(my_owners, answer, pd_count, [cache]).astype(BF)
+    placed = route(my_owners, answer, pd_count, [lax.slice(cache, (0, 0, 0), (1, 16, UNIT))])
     placed = lax.all_to_all(placed, "pd", split_axis=0, concat_axis=0, tiled=True)
     cache = jnp.swapaxes(cache, 1, 2)
     return (placed.reshape(pd_count * 2, heads * DV), cache)

time: 242 us -> 219 us (0.905)
  the two profiles are of different devices: /device:TPU:16 before, /device:TPU:0 now
where the time goes in v6:
time: 219 us; the launch traced here: 218 us
  Pallas kernels  87.4 us (40%)
  waiting for transfers between devices  57 us (26%)
  starting transfers between devices  55.8 us (25%)
  local copies, waits for them, and re-layouts  13.2 us (6%)
  other arithmetic  3.4 us (2%)
    ppermute x4, waiting for transfers between devices, second_hop(): outer.append(lax.ppermute(block, 'tp', outward))  30.6 us
    pallas_call x4, Pallas kernels, project_far(): pl.pallas_call(project_far_kernel, grid_spec=pltpu.PrefetchScalarGridSpec...  24.3 us
    ppermute x4, starting transfers between devices, send_far(): inner.append(lax.ppermute(codes, 'tp', inward))  16.7 us
    pallas_call x8, Pallas kernels, add_on(): pl.pallas_call(functools.partial(add_kernel, -1 - len(carried)), grid_spe...  15 us
    pallas_call x1, Pallas kernels, queries(): pl.pallas_call(body, grid=(heads // step,), in_specs=[pl.BlockSpec((rows,...  13.8 us
    pallas_call x1, Pallas kernels, project_near(): pl.pallas_call(project_near_kernel, grid_spec=pltpu.PrefetchScalarGridSpe...  13.8 us
    ppermute x2, starting transfers between devices, local_line(): side = [lax.ppermute(codes, 'tp', inward) for codes in side]  9.44 us
    pallas_call x2, Pallas kernels, pages_of(): pl.pallas_call(functools.partial(page_kernel, requests), grid_spec=pltpu....  8.92 us
  transfers between devices with their start and end apart: 25, of which 9 were waited for; matrix products, arithmetic and copies ran while one was open for 3% of the time, Pallas kernels for 35%

profile of v6, /device:TPU:0, one launch (start us, length us, event | category | flops | bytes accessed | tf_op | source)
XLA Modules:
  0.0 217.8 jit_solution(16772630497923812642)
XLA Ops:
  0.7 6.1 %project_far.4 = (f32[2,3,576,128]{3,2,1,0:T(8,128)}, s16[2,3,592,128]{3,2,1,0:T(8,128)(2,1)}) custom-call(s32[1]{0:T(128)} %bitcast.rank, bf16[4,1536,1792]{2,1,0:T(8,128)(2,1)} %bitcast.22, bf16[576,1792]{1,0:T(8,128)(2,1)} %bitcast.27), custom_call_target="tpu_custom_call" | custom-call | flops 1024 | bytes 1024 | tf_op jit(solution)/shard_map/project_far/pallas_call | solution.py:269
  6.8 5.4 %collective-permute-start.3 = (s16[2,3,592,128]{3,2,1,0:T(8,128)(2,1)}, s16[2,3,592,128]{3,2,1,0:T(8,128)(2,1)}, u32[]{:S(2)}, u32[]{:S(2)}) collective-permute-start(s16[2,3,592,128]{3,2,1,0:T(8,128)(2,1)} %get-tuple-element.29), channel_id=1, source_target_pairs={{0,4},{12,8},{1,5},{13,9},{2,6},{14,10},{3,7},{15,11},{16,20},{28,... | collective-permute-start | bytes 2727944 | tf_op jit(solution)/shard_map/ppermute | solution.py:706
  12.2 6.1 %project_far.5 = (f32[2,3,576,128]{3,2,1,0:T(8,128)}, s16[2,3,592,128]{3,2,1,0:T(8,128)(2,1)}) custom-call(s32[1]{0:T(128)} %bitcast.rank, bf16[4,1536,1792]{2,1,0:T(8,128)(2,1)} %bitcast.23, bf16[576,1792]{1,0:T(8,128)(2,1)} %bitcast.28, f32[2,3,576,128]{3,2,1,0:T(8,128)} %get-tuple-element.25.refs_0_.own_ref), custom_call_target="tpu_custom_call" | custom-call | flops 1024 | bytes 1024 | tf_op jit(solution)/shard_map/project_far/pallas_call | solution.py:269
  18.2 1.3 collective-permute-start.5
  21.1 13.8 %queries.1 = (f32[32,8,576]{2,1,0:T(8,128)}, f32[4,8,576]{2,1,0:T(8,128)}) custom-call(bf16[8,1536]{1,0:T(8,128)(2,1)} %reshape.129.refs_0_, bf16[1536,6144]{1,0:T(8,128)(2,1)} %refs_1_.2, bf16[8,1792]{1,0:T(8,128)(2,1)} %refs_2_.2, bf16[576,1792]{1,0:T(8,128)(2,1)} %bitcast.29, bf16[512,8192]{1,0:T(8,128)(2,1)} %refs_7_.3, bf16[512,8192]{1,0:T(8,128)(2,1)} %refs_7_.3, ...), custom_call_target="tpu_custom_call" | custom-call | flops 1024 | bytes 1024 | tf_op jit(solution)/shard_map/queries/pallas_call | solution.py:485
  37.0 1.8 add_on.8.refs_0_
  38.9 1.6 collective-permute-start.4
  40.5 4.4 %collective-permute-start = (bf16[288,576]{1,0:T(8,128)(2,1)S(1)}, bf16[288,576]{1,0:T(8,128)(2,1)S(1)}, u32[]{:S(2)}, u32[]{:S(2)}) collective-permute-start(bf16[288,576]{1,0:T(8,128)(2,1)S(1)} %pad_maximum_fusion.refs_0_.refs_3_.refs_7_), channel_id=1, source_target_pairs={{0,12},{1,13},{2,14},{3,15},{16,28},{17,29},{18,30},{19,31}} | collective-permute-start | bytes 995336 | tf_op jit(solution)/shard_map/ppermute | solution.py:733
  46.3 6.1 %project_far.6 = (f32[2,3,576,128]{3,2,1,0:T(8,128)}, s16[2,3,592,128]{3,2,1,0:T(8,128)(2,1)}) custom-call(s32[1]{0:T(128)} %bitcast.rank, bf16[4,1536,1792]{2,1,0:T(8,128)(2,1)} %bitcast.24, bf16[576,1792]{1,0:T(8,128)(2,1)} %bitcast.30, s16[2,3,592,128]{3,2,1,0:T(8,128)(2,1)} %copy-done.11), custom_call_target="tpu_custom_call" | custom-call | flops 1024 | bytes 1024 | tf_op jit(solution)/shard_map/project_far/pallas_call | solution.py:269
  52.3 13.8 %project_near.1 = (f32[3,2,4,576,128]{4,3,2,1,0:T(8,128)}, s16[1,4,592,128]{3,2,1,0:T(8,128)(2,1)}, s16[2,4,592,128]{3,2,1,0:T(8,128)(2,1)}) custom-call(s32[1]{0:T(128)} %bitcast.rank, bf16[4,1536,1792]{2,1,0:T(8,128)(2,1)} %bitcast.25, bf16[576,1792]{1,0:T(8,128)(2,1)} %bitcast.31, f32[2,3,576,128]{3,2,1,0:T(8,128)} %get-tuple-element.30.refs_0_.own_ref), custom_call_target="tpu_custom_call" | custom-call | flops 1024 | bytes 1024 | tf_op jit(solution)/shard_map/project_near/pallas_call | solution.py:312
  66.2 2.9 %collective-permute-start.8 = (s16[2,3,592,128]{3,2,1,0:T(8,128)(2,1)}, s16[2,3,592,128]{3,2,1,0:T(8,128)(2,1)}, u32[]{:S(2)}, u32[]{:S(2)}) collective-permute-start(s16[2,3,592,128]{3,2,1,0:T(8,128)(2,1)} %get-tuple-element.33), channel_id=1, source_target_pairs={{0,4},{12,8},{1,5},{13,9},{2,6},{14,10},{3,7},{15,11},{16,20},{28,... | collective-permute-start | bytes 2727944 | tf_op jit(solution)/shard_map/ppermute | solution.py:706
  69.0 2.2 %add_on.9.refs_0_ = s16[2,3,592,128]{3,2,1,0:T(8,128)(2,1)} custom-call(s32[1]{0:T(128)} %bitcast.rank, f32[2,3,576,128]{3,2,1,0:T(8,128)} %get-tuple-element.26.refs_10_.own_ref, s16[2,3,592,128]{3,2,1,0:T(8,128)(2,1)S(1)} %collective-permute-done.5.got_ref, f32[3,2,4,576,128]{4,3,2,1,0:T(8,128)} %get-tuple-element.31.refs_0_.own_ref.refs_8_), custom_call_target="tpu_custom_call" | custom-call | flops 1024 | bytes 1024 | tf_op jit(solution)/shard_map/add_on/pallas_call | solution.py:358
  71.2 1.6 collective-permute-start.7
  72.8 1.8 add_on.10.refs_0_.refs_3_
  74.7 1.3 collective-permute-start.6
  76.0 6.1 %project_far.7 = (f32[2,3,576,128]{3,2,1,0:T(8,128)}, s16[2,3,592,128]{3,2,1,0:T(8,128)(2,1)}) custom-call(s32[1]{0:T(128)} %bitcast.rank, bf16[4,1536,1792]{2,1,0:T(8,128)(2,1)} %bitcast.26, bf16[576,1792]{1,0:T(8,128)(2,1)} %bitcast.32, s16[2,3,592,128]{3,2,1,0:T(8,128)(2,1)} %copy-done.5), custom_call_target="tpu_custom_call" | custom-call | flops 1024 | bytes 1024 | tf_op jit(solution)/shard_map/project_far/pallas_call | solution.py:269
  82.0 7.1 %collective-permute-start.11 = (s16[2,3,592,128]{3,2,1,0:T(8,128)(2,1)}, s16[2,3,592,128]{3,2,1,0:T(8,128)(2,1)}, u32[]{:S(2)}, u32[]{:S(2)}) collective-permute-start(s16[2,3,592,128]{3,2,1,0:T(8,128)(2,1)} %get-tuple-element.37), channel_id=1, source_target_pairs={{0,4},{12,8},{1,5},{13,9},{2,6},{14,10},{3,7},{15,11},{16,20},{28,... | collective-permute-start | bytes 2727944 | tf_op jit(solution)/shard_map/ppermute | solution.py:706
  89.1 2.5 %add_on.11 = (s16[2,3,592,128]{3,2,1,0:T(8,128)(2,1)}, s16[1,4,592,128]{3,2,1,0:T(8,128)(2,1)}) custom-call(s32[1]{0:T(128)} %bitcast.rank, f32[2,3,576,128]{3,2,1,0:T(8,128)} %get-tuple-element.30.refs_0_.own_ref, s16[2,3,592,128]{3,2,1,0:T(8,128)(2,1)} %collective-permute-done.8.got_ref, ...), custom_call_target="tpu_custom_call", output_to_operand_aliasing={{1}: (4, {})} | custom-call | flops 1024 | bytes 1024 | tf_op jit(solution)/shard_map/add_on/pallas_call | solution.py:358
  91.7 1.6 collective-permute-start.10
  93.3 5.5 %collective-permute-done.6.refs_1_.refs_9_.refs_0_ = s16[2,3,592,128]{3,2,1,0:T(8,128)(2,1)S(1)} collective-permute-done((s16[2,3,592,128]{3,2,1,0:T(8,128)(2,1)S(1)}, s16[2,3,592,128]{3,2,1,0:T(8,128)(2,1)S(1)}, u32[]{:S(2)}, u32[]{:S(2)}) %collective-permute-start.6) | collective-permute-done | bytes 909344 | tf_op jit(solution)/shard_map/ppermute | solution.py:716
  99.7 1.7 add_on.12.refs_0_.refs_4_
  101.4 1.3 collective-permute-start.9
  102.6 4.6 %collective-permute-start.12 = (s16[1,4,592,128]{3,2,1,0:T(8,128)(2,1)}, s16[1,4,592,128]{3,2,1,0:T(8,128)(2,1)S(1)}, u32[]{:S(2)}, u32[]{:S(2)}) collective-permute-start(s16[1,4,592,128]{3,2,1,0:T(8,128)(2,1)} %get-tuple-element.38), channel_id=1, source_target_pairs={{0,4},{12,8},{1,5},{13,9},{2,6},{14,10},{3,7},{15,11},{16,20},{28,... | collective-permute-start | bytes 1818632 | tf_op jit(solution)/shard_map/ppermute | solution.py:747
  108.8 1.7 add_on.13.refs_0_
  111.2 8.5 %collective-permute-done.12.refs_2_.refs_6_ = s16[1,4,592,128]{3,2,1,0:T(8,128)(2,1)S(1)} collective-permute-done((s16[1,4,592,128]{3,2,1,0:T(8,128)(2,1)}, s16[1,4,592,128]{3,2,1,0:T(8,128)(2,1)S(1)}, u32[]{:S(2)}, u32[]{:S(2)}) %collective-permute-start.12) | collective-permute-done | bytes 606240 | tf_op jit(solution)/shard_map/ppermute | solution.py:747
  119.7 2.8 %collective-permute-done.9.refs_1_.refs_10_ = s16[2,3,592,128]{3,2,1,0:T(8,128)(2,1)S(1)} collective-permute-done((s16[2,3,592,128]{3,2,1,0:T(8,128)(2,1)S(1)}, s16[2,3,592,128]{3,2,1,0:T(8,128)(2,1)S(1)}, u32[]{:S(2)}, u32[]{:S(2)}) %collective-permute-start.9) | collective-permute-done | bytes 909344 | tf_op jit(solution)/shard_map/ppermute | solution.py:716
  123.4 1.8 add_on.14.refs_0_.refs_5_
  125.2 1.3 collective-permute-start.13
  126.5 4.8 %collective-permute-start.19 = (s16[2,4,592,128]{3,2,1,0:T(8,128)(2,1)S(1)}, s16[2,4,592,128]{3,2,1,0:T(8,128)(2,1)S(1)}, u32[]{:S(2)}, u32[]{:S(2)}) collective-permute-start(s16[2,4,592,128]{3,2,1,0:T(8,128)(2,1)S(1)} %copy-done.22), channel_id=1, source_target_pairs={{0,4},{12,8},{1,5},{13,9},{2,6},{14,10},{3,7},{15,11},{16,20},{28,... | collective-permute-start | bytes 3637256 | tf_op jit(solution)/shard_map/ppermute | solution.py:747
  131.4 14.0 %collective-permute-done.13.refs_1_.refs_11_.refs_2_ = s16[2,3,592,128]{3,2,1,0:T(8,128)(2,1)S(1)} collective-permute-done((s16[2,3,592,128]{3,2,1,0:T(8,128)(2,1)S(1)}, s16[2,3,592,128]{3,2,1,0:T(8,128)(2,1)S(1)}, u32[]{:S(2)}, u32[]{:S(2)}) %collective-permute-start.13) | collective-permute-done | bytes 909344 | tf_op jit(solution)/shard_map/ppermute | solution.py:716
  146.4 1.4 add_on.15.refs_20_.refs_1_
  147.8 1.5 collective-permute-start.18
  149.4 4.1 %attend.2 = (bf16[3,64,512]{2,1,0:T(8,128)(2,1)S(1)}, bf16[3,64,512]{2,1,0:T(8,128)(2,1)S(1)}, bf16[3,64,512]{2,1,0:T(8,128)(2,1)S(1)}, bf16[3,64,512]{2,1,0:T(8,128)(2,1)S(1)}) custom-call(s32[1]{0:T(128)} %bitcast.rank, s32[1]{0:T(128)} %bitcast.1.first_ref, bf16[288,576]{1,0:T(8,128)(2,1)S(1)} %collective-permute-done.refs_1_.refs_0_.refs_4_, ...), custom_call_target="tpu_custom_call" | custom-call | flops 1024 | bytes 1024 | tf_op jit(solution)/shard_map/attend/pallas_call | solution.py:593
  153.5 1.3 collective-permute-start.15
  157.4 5.6 %pages.2.refs_18_.refs_7_ = bf16[4,576,384]{2,1,0:T(8,128)(2,1)} custom-call(s32[1]{0:T(128)} %bitcast.rank, s32[4]{0:T(128)S(1)} %dynamic_slice.9.slot, f32[3,2,4,576,128]{4,3,2,1,0:T(8,128)} %get-tuple-element.31.refs_0_.own_ref.refs_8_, s16[2,3,592,128]{3,2,1,0:T(8,128)(2,1)S(1)} %copy-done.8, s16[2,3,592,128]{3,2,1,0:T(8,128)(2,1)} %copy-done.18, ...), custom_call_target="tpu_custom_call" | custom-call | flops 1024 | bytes 1024 | tf_op jit(solution)/shard_map/pages/pallas_call | solution.py:420
  163.0 8.3 %collective-permute-done.18.refs_9_.refs_0_ = s16[2,3,592,128]{3,2,1,0:T(8,128)(2,1)S(1)} collective-permute-done((s16[2,3,592,128]{3,2,1,0:T(8,128)(2,1)S(1)}, s16[2,3,592,128]{3,2,1,0:T(8,128)(2,1)S(1)}, u32[]{:S(2)}, u32[]{:S(2)}) %collective-permute-start.18) | collective-permute-done | bytes 909344 | tf_op jit(solution)/shard_map/ppermute | solution.py:716
  172.3 1.8 attend.3
  174.1 3.3 %pages.3.refs_8_ = bf16[4,576,384]{2,1,0:T(8,128)(2,1)} custom-call(s32[1]{0:T(128)} %bitcast.rank, s32[4]{0:T(128)S(1)} %dynamic_slice.9.slot, f32[3,2,4,576,128]{4,3,2,1,0:T(8,128)} %get-tuple-element.31.refs_0_.own_ref.refs_8_, s16[2,3,592,128]{3,2,1,0:T(8,128)(2,1)} %copy-done.21, ...), custom_call_target="tpu_custom_call", output_to_operand_aliasing={{}: (10, {})} | custom-call | flops 1024 | bytes 1024 | tf_op jit(solution)/shard_map/pages/pallas_call | solution.py:420
  177.4 4.5 %all-to-all-start = ((bf16[4,576,384]{2,1,0:T(8,128)(2,1)}), bf16[4,576,384]{2,1,0:T(8,128)(2,1)}, u32[]{:S(2)}, u32[]{:S(2)}) async-start(bf16[4,576,384]{2,1,0:T(8,128)(2,1)} %pages.3.refs_8_), calls=%async_computation | async-start | bytes 3538944 | tf_op jit(solution)/shard_map/all_to_all | solution.py:796
  182.2 1.3 collective-permute-start.20
  184.8 5.6 %collective-permute-done.20 = bf16[1,64,512]{2,1,0:T(8,128)(2,1)S(1)} collective-permute-done((bf16[1,64,512]{2,1,0:T(8,128)(2,1)S(1)}, bf16[1,64,512]{2,1,0:T(8,128)(2,1)S(1)}, u32[]{:S(2)}, u32[]{:S(2)}) %collective-permute-start.20) | collective-permute-done | bytes 65568 | tf_op jit(solution)/shard_map/ppermute | solution.py:768
  190.7 1.2 reshape.139.o_ref
  192.6 4.4 %heads_out.1.answer_ref = f32[8,4096]{1,0:T(8,128)} custom-call(f32[32,8,512]{2,1,0:T(8,128)} %reshape.139.o_ref, f32[8,128]{1,0:T(8,128)} %broadcast_in_dim.2.keep_ref, bf16[512,8192]{1,0:T(8,128)(2,1)} %refs_7_.3, bf16[512,8192]{1,0:T(8,128)(2,1)} %refs_7_.3, bf16[512,8192]{1,0:T(8,128)(2,1)} %refs_7_.3, bf16[512,8192]{1,0:T(8,128)(2,1)} %refs_7_.3, ...), custom_call_target="tpu_custom_call" | custom-call | flops 1024 | bytes 1024 | tf_op jit(solution)/shard_map/heads_out/pallas_call | solution.py:635
  197.0 7.2 %all-to-all-done = bf16[4,576,384]{2,1,0:T(8,128)(2,1)} async-done(((bf16[4,576,384]{2,1,0:T(8,128)(2,1)}), bf16[4,576,384]{2,1,0:T(8,128)(2,1)}, u32[]{:S(2)}, u32[]{:S(2)}) %all-to-all-start) | async-done | bytes 1769504 | tf_op jit(solution)/shard_map/all_to_all | solution.py:796
  205.7 1.2 route.1
  206.9 3.3 %all-to-all-start.1 = ((bf16[4,2,4096]{2,1,0:T(2,128)(2,1)}), bf16[4,2,4096]{2,1,0:T(2,128)(2,1)S(1)}, u32[]{:S(2)}, u32[]{:S(2)}) async-start(bf16[4,2,4096]{2,1,0:T(2,128)(2,1)} %route.1), calls=%async_computation.1 | async-start | bytes 131072 | tf_op jit(solution)/shard_map/all_to_all | solution.py:808
  210.2 4.1 %all-to-all-done.1 = bf16[4,2,4096]{2,1,0:T(2,128)(2,1)S(1)} async-done(((bf16[4,2,4096]{2,1,0:T(2,128)(2,1)}), bf16[4,2,4096]{2,1,0:T(2,128)(2,1)S(1)}, u32[]{:S(2)}, u32[]{:S(2)}) %all-to-all-start.1) | async-done | bytes 65568 | tf_op jit(solution)/shard_map/all_to_all | solution.py:808
  215.0 2.9 %copy.24 = bf16[4,384,576]{1,2,0:T(8,128)(2,1)} copy(bf16[4,384,576]{1,2,0:T(8,128)(2,1)} %bitcast.11) | data formatting | bytes 3538944
  (99 shorter events, 18.4 us)
Async XLA Ops:
  0.6 19.0 %copy-start = (bf16[16,2,1536]{2,1,0:T(2,128)(2,1)S(1)}, bf16[16,2,1536]{2,1,0:T(2,128)(2,1)}, u32[]{:S(2)}) copy-start(bf16[16,2,1536]{2,1,0:T(2,128)(2,1)} %param.14) | copy-start | bytes 294916
  6.8 30.3 %collective-permute-start.3 = (s16[2,3,592,128]{3,2,1,0:T(8,128)(2,1)}, s16[2,3,592,128]{3,2,1,0:T(8,128)(2,1)}, u32[]{:S(2)}, u32[]{:S(2)}) collective-permute-start(s16[2,3,592,128]{3,2,1,0:T(8,128)(2,1)} %get-tuple-element.29), channel_id=1, source_target_pairs={{0,4},{12,8},{1,5},{13,9},{2,6},{14,10},{3,7},{15,11},{16,20},{28,... | collective-permute-start | bytes 2727944 | tf_op jit(solution)/shard_map/ppermute | solution.py:706
  18.2 47.9 %collective-permute-start.5 = (s16[2,3,592,128]{3,2,1,0:T(8,128)(2,1)}, s16[2,3,592,128]{3,2,1,0:T(8,128)(2,1)S(1)}, u32[]{:S(2)}, u32[]{:S(2)}) collective-permute-start(s16[2,3,592,128]{3,2,1,0:T(8,128)(2,1)} %get-tuple-element.32), channel_id=1, source_target_pairs={{0,4},{12,8},{1,5},{13,9},{2,6},{14,10},{3,7},{15,11},{16,20},{28,... | collective-permute-start | bytes 2727944 | tf_op jit(solution)/shard_map/ppermute | solution.py:706
  37.0 8.5 %copy-start.2 = (bf16[288,576]{1,0:T(8,128)(2,1)}, bf16[288,576]{1,0:T(8,128)(2,1)S(1)}, u32[]{:S(2)}) copy-start(bf16[288,576]{1,0:T(8,128)(2,1)S(1)} %pad_maximum_fusion.refs_0_.refs_3_.refs_7_) | copy-start | bytes 995332
  38.9 7.4 %copy-start.11 = (s16[2,3,592,128]{3,2,1,0:T(8,128)(2,1)}, s16[2,3,592,128]{3,2,1,0:T(8,128)(2,1)S(1)}, u32[]{:S(2)}) copy-start(s16[2,3,592,128]{3,2,1,0:T(8,128)(2,1)S(1)} %add_on.8.refs_0_) | copy-start | bytes 2727940
  38.9 34.0 %collective-permute-start.4 = (s16[2,3,592,128]{3,2,1,0:T(8,128)(2,1)S(1)}, s16[2,3,592,128]{3,2,1,0:T(8,128)(2,1)}, u32[]{:S(2)}, u32[]{:S(2)}) collective-permute-start(s16[2,3,592,128]{3,2,1,0:T(8,128)(2,1)S(1)} %add_on.8.refs_0_), channel_id=1, source_target_pairs={{4,8},{8,4},{5,9},{9,5},{6,10},{10,6},{7,11},{11,7},{20,24},{24,20... | collective-permute-start | bytes 2727944 | tf_op jit(solution)/shard_map/ppermute | solution.py:710
  40.5 30.8 %collective-permute-start = (bf16[288,576]{1,0:T(8,128)(2,1)S(1)}, bf16[288,576]{1,0:T(8,128)(2,1)S(1)}, u32[]{:S(2)}, u32[]{:S(2)}) collective-permute-start(bf16[288,576]{1,0:T(8,128)(2,1)S(1)} %pad_maximum_fusion.refs_0_.refs_3_.refs_7_), channel_id=1, source_target_pairs={{0,12},{1,13},{2,14},{3,15},{16,28},{17,29},{18,30},{19,31}} | collective-permute-start | bytes 995336 | tf_op jit(solution)/shard_map/ppermute | solution.py:733
  44.9 28.0 %collective-permute-start.1 = (bf16[288,576]{1,0:T(8,128)(2,1)S(1)}, bf16[288,576]{1,0:T(8,128)(2,1)S(1)}, u32[]{:S(2)}, u32[]{:S(2)}) collective-permute-start(bf16[288,576]{1,0:T(8,128)(2,1)S(1)} %pad_maximum_fusion.refs_0_.refs_3_.refs_7_), channel_id=1, source_target_pairs={{4,12},{5,13},{6,14},{7,15},{20,28},{21,29},{22,30},{23,31}} | collective-permute-start | bytes 995336 | tf_op jit(solution)/shard_map/ppermute | solution.py:733
  45.6 27.3 %collective-permute-start.2 = (bf16[288,576]{1,0:T(8,128)(2,1)S(1)}, bf16[288,576]{1,0:T(8,128)(2,1)S(1)}, u32[]{:S(2)}, u32[]{:S(2)}) collective-permute-start(bf16[288,576]{1,0:T(8,128)(2,1)S(1)} %pad_maximum_fusion.refs_0_.refs_3_.refs_7_), channel_id=1, source_target_pairs={{8,12},{9,13},{10,14},{11,15},{24,28},{25,29},{26,30},{27,31}} | collective-permute-start | bytes 995336 | tf_op jit(solution)/shard_map/ppermute | solution.py:733
  66.2 23.0 %collective-permute-start.8 = (s16[2,3,592,128]{3,2,1,0:T(8,128)(2,1)}, s16[2,3,592,128]{3,2,1,0:T(8,128)(2,1)}, u32[]{:S(2)}, u32[]{:S(2)}) collective-permute-start(s16[2,3,592,128]{3,2,1,0:T(8,128)(2,1)} %get-tuple-element.33), channel_id=1, source_target_pairs={{0,4},{12,8},{1,5},{13,9},{2,6},{14,10},{3,7},{15,11},{16,20},{28,... | collective-permute-start | bytes 2727944 | tf_op jit(solution)/shard_map/ppermute | solution.py:706
  71.2 22.1 %collective-permute-start.7 = (s16[2,3,592,128]{3,2,1,0:T(8,128)(2,1)}, s16[2,3,592,128]{3,2,1,0:T(8,128)(2,1)}, u32[]{:S(2)}, u32[]{:S(2)}) collective-permute-start(s16[2,3,592,128]{3,2,1,0:T(8,128)(2,1)} %add_on.9.refs_0_), channel_id=1, source_target_pairs={{4,8},{8,4},{5,9},{9,5},{6,10},{10,6},{7,11},{11,7},{20,24},{24,20... | collective-permute-start | bytes 2727944 | tf_op jit(solution)/shard_map/ppermute | solution.py:710
  72.8 1.8 copy-start.3
  74.7 1.3 copy-start.5
  74.7 24.1 %collective-permute-start.6 = (s16[2,3,592,128]{3,2,1,0:T(8,128)(2,1)S(1)}, s16[2,3,592,128]{3,2,1,0:T(8,128)(2,1)S(1)}, u32[]{:S(2)}, u32[]{:S(2)}) collective-permute-start(s16[2,3,592,128]{3,2,1,0:T(8,128)(2,1)S(1)} %add_on.10.refs_0_.refs_3_), channel_id=1, source_target_pairs={{8,12},{4,0},{9,13},{5,1},{10,14},{6,2},{11,15},{7,3},{24,28},{20,... | collective-permute-start | bytes 2727944 | tf_op jit(solution)/shard_map/ppermute | solution.py:716
  82.0 26.7 %collective-permute-start.11 = (s16[2,3,592,128]{3,2,1,0:T(8,128)(2,1)}, s16[2,3,592,128]{3,2,1,0:T(8,128)(2,1)}, u32[]{:S(2)}, u32[]{:S(2)}) collective-permute-start(s16[2,3,592,128]{3,2,1,0:T(8,128)(2,1)} %get-tuple-element.37), channel_id=1, source_target_pairs={{0,4},{12,8},{1,5},{13,9},{2,6},{14,10},{3,7},{15,11},{16,20},{28,... | collective-permute-start | bytes 2727944 | tf_op jit(solution)/shard_map/ppermute | solution.py:706
  91.7 28.0 %collective-permute-start.10 = (s16[2,3,592,128]{3,2,1,0:T(8,128)(2,1)}, s16[2,3,592,128]{3,2,1,0:T(8,128)(2,1)}, u32[]{:S(2)}, u32[]{:S(2)}) collective-permute-start(s16[2,3,592,128]{3,2,1,0:T(8,128)(2,1)} %get-tuple-element.36.refs_0_), channel_id=1, source_target_pairs={{4,8},{8,4},{5,9},{9,5},{6,10},{10,6},{7,11},{11,7},{20,24},{24,20... | collective-permute-start | bytes 2727944 | tf_op jit(solution)/shard_map/ppermute | solution.py:710
  101.3 7.4 %copy-start.6 = (s16[2,3,592,128]{3,2,1,0:T(8,128)(2,1)}, s16[2,3,592,128]{3,2,1,0:T(8,128)(2,1)S(1)}, u32[]{:S(2)}) copy-start(s16[2,3,592,128]{3,2,1,0:T(8,128)(2,1)S(1)} %add_on.12.refs_0_.refs_4_) | copy-start | bytes 2727940
  101.4 21.1 %collective-permute-start.9 = (s16[2,3,592,128]{3,2,1,0:T(8,128)(2,1)S(1)}, s16[2,3,592,128]{3,2,1,0:T(8,128)(2,1)S(1)}, u32[]{:S(2)}, u32[]{:S(2)}) collective-permute-start(s16[2,3,592,128]{3,2,1,0:T(8,128)(2,1)S(1)} %add_on.12.refs_0_.refs_4_), channel_id=1, source_target_pairs={{8,12},{4,0},{9,13},{5,1},{10,14},{6,2},{11,15},{7,3},{24,28},{20,... | collective-permute-start | bytes 2727944 | tf_op jit(solution)/shard_map/ppermute | solution.py:716
  102.6 17.0 %collective-permute-start.12 = (s16[1,4,592,128]{3,2,1,0:T(8,128)(2,1)}, s16[1,4,592,128]{3,2,1,0:T(8,128)(2,1)S(1)}, u32[]{:S(2)}, u32[]{:S(2)}) collective-permute-start(s16[1,4,592,128]{3,2,1,0:T(8,128)(2,1)} %get-tuple-element.38), channel_id=1, source_target_pairs={{0,4},{12,8},{1,5},{13,9},{2,6},{14,10},{3,7},{15,11},{16,20},{28,... | collective-permute-start | bytes 1818632 | tf_op jit(solution)/shard_map/ppermute | solution.py:747
  110.5 12.0 %copy-start.12 = (s16[2,3,592,128]{3,2,1,0:T(8,128)(2,1)}, s16[2,3,592,128]{3,2,1,0:T(8,128)(2,1)S(1)}, u32[]{:S(2)}) copy-start(s16[2,3,592,128]{3,2,1,0:T(8,128)(2,1)S(1)} %add_on.13.refs_0_) | copy-start | bytes 2727940
  110.5 20.9 %collective-permute-start.14 = (s16[2,3,592,128]{3,2,1,0:T(8,128)(2,1)S(1)}, s16[2,3,592,128]{3,2,1,0:T(8,128)(2,1)S(1)}, u32[]{:S(2)}, u32[]{:S(2)}) collective-permute-start(s16[2,3,592,128]{3,2,1,0:T(8,128)(2,1)S(1)} %add_on.13.refs_0_), channel_id=1, source_target_pairs={{4,8},{8,4},{5,9},{9,5},{6,10},{10,6},{7,11},{11,7},{20,24},{24,20... | collective-permute-start | bytes 2727944 | tf_op jit(solution)/shard_map/ppermute | solution.py:710
  122.5 0.9 copy-start.18
  123.4 3.1 %copy-start.22 = (s16[2,4,592,128]{3,2,1,0:T(8,128)(2,1)S(1)}, s16[2,4,592,128]{3,2,1,0:T(8,128)(2,1)}, u32[]{:S(2)}) copy-start(s16[2,4,592,128]{3,2,1,0:T(8,128)(2,1)} %get-tuple-element.43) | copy-start | bytes 3637252
  125.2 20.2 %copy-start.9 = (s16[2,3,592,128]{3,2,1,0:T(8,128)(2,1)}, s16[2,3,592,128]{3,2,1,0:T(8,128)(2,1)S(1)}, u32[]{:S(2)}) copy-start(s16[2,3,592,128]{3,2,1,0:T(8,128)(2,1)S(1)} %add_on.14.refs_0_.refs_5_) | copy-start | bytes 2727940
  125.2 20.2 %collective-permute-start.13 = (s16[2,3,592,128]{3,2,1,0:T(8,128)(2,1)S(1)}, s16[2,3,592,128]{3,2,1,0:T(8,128)(2,1)S(1)}, u32[]{:S(2)}, u32[]{:S(2)}) collective-permute-start(s16[2,3,592,128]{3,2,1,0:T(8,128)(2,1)S(1)} %add_on.14.refs_0_.refs_5_), channel_id=1, source_target_pairs={{8,12},{4,0},{9,13},{5,1},{10,14},{6,2},{11,15},{7,3},{24,28},{20,... | collective-permute-start | bytes 2727944 | tf_op jit(solution)/shard_map/ppermute | solution.py:716
  126.5 22.8 %copy-start.14 = (s32[16,1536]{1,0:T(8,128)S(1)}, s32[16,1536]{1,0:T(8,128)}, u32[]{:S(2)}) copy-start(s32[16,1536]{1,0:T(8,128)} %refs_14_.1) | copy-start | bytes 294916
  126.5 22.8 %copy-start.15 = (f32[8,32]{1,0:T(8,128)S(1)}, f32[8,32]{1,0:T(8,128)}, u32[]{:S(2)}) copy-start(f32[8,32]{1,0:T(8,128)} %get-tuple-element.52.refs_9_.refs_19_.refs_17_) | copy-start | bytes 3076
  126.5 22.8 %copy-start.16 = (f32[8,32]{1,0:T(8,128)S(1)}, f32[8,32]{1,0:T(8,128)}, u32[]{:S(2)}) copy-start(f32[8,32]{1,0:T(8,128)} %get-tuple-element.53.refs_8_.refs_18_.refs_16_) | copy-start | bytes 3076
  126.5 22.8 %copy-start.17 = (f32[512]{0:T(512)S(1)}, f32[512]{0:T(512)}, u32[]{:S(2)}) copy-start(f32[512]{0:T(512)} %param.13) | copy-start | bytes 6148
  126.5 29.7 %collective-permute-start.19 = (s16[2,4,592,128]{3,2,1,0:T(8,128)(2,1)S(1)}, s16[2,4,592,128]{3,2,1,0:T(8,128)(2,1)S(1)}, u32[]{:S(2)}, u32[]{:S(2)}) collective-permute-start(s16[2,4,592,128]{3,2,1,0:T(8,128)(2,1)S(1)} %copy-done.22), channel_id=1, source_target_pairs={{0,4},{12,8},{1,5},{13,9},{2,6},{14,10},{3,7},{15,11},{16,20},{28,... | collective-permute-start | bytes 3637256 | tf_op jit(solution)/shard_map/ppermute | solution.py:747
  145.4 1.0 copy-start.19
  147.8 1.5 copy-start.10
  147.8 23.5 %collective-permute-start.18 = (s16[2,3,592,128]{3,2,1,0:T(8,128)(2,1)S(1)}, s16[2,3,592,128]{3,2,1,0:T(8,128)(2,1)S(1)}, u32[]{:S(2)}, u32[]{:S(2)}) collective-permute-start(s16[2,3,592,128]{3,2,1,0:T(8,128)(2,1)S(1)} %add_on.15.refs_20_.refs_1_), channel_id=1, source_target_pairs={{8,12},{4,0},{9,13},{5,1},{10,14},{6,2},{11,15},{7,3},{24,28},{20,... | collective-permute-start | bytes 2727944 | tf_op jit(solution)/shard_map/ppermute | solution.py:716
  149.4 6.8 %copy-start.23 = (s32[16]{0:T(128)S(1)}, s32[16]{0:T(128)}, u32[]{:S(2)}) copy-start(s32[16]{0:T(128)} %param.17) | copy-start | bytes 196
  149.4 8.0 %copy-start.8 = (s16[2,3,592,128]{3,2,1,0:T(8,128)(2,1)S(1)}, s16[2,3,592,128]{3,2,1,0:T(8,128)(2,1)}, u32[]{:S(2)}) copy-start(s16[2,3,592,128]{3,2,1,0:T(8,128)(2,1)} %copy-done.7) | copy-start | bytes 2727940
  153.5 20.5 %collective-permute-start.15 = (bf16[3,64,512]{2,1,0:T(8,128)(2,1)S(1)}, bf16[3,64,512]{2,1,0:T(8,128)(2,1)S(1)}, u32[]{:S(2)}, u32[]{:S(2)}) collective-permute-start(bf16[3,64,512]{2,1,0:T(8,128)(2,1)S(1)} %get-tuple-element.40.refs_11_), channel_id=1, source_target_pairs={{12,0},{13,1},{14,2},{15,3},{28,16},{29,17},{30,18},{31,19}} | collective-permute-start | bytes 589832 | tf_op jit(solution)/shard_map/ppermute | solution.py:768
  154.8 19.3 %collective-permute-start.16 = (bf16[3,64,512]{2,1,0:T(8,128)(2,1)S(1)}, bf16[3,64,512]{2,1,0:T(8,128)(2,1)S(1)}, u32[]{:S(2)}, u32[]{:S(2)}) collective-permute-start(bf16[3,64,512]{2,1,0:T(8,128)(2,1)S(1)} %get-tuple-element.41), channel_id=1, source_target_pairs={{12,4},{13,5},{14,6},{15,7},{28,20},{29,21},{30,22},{31,23}} | collective-permute-start | bytes 589832 | tf_op jit(solution)/shard_map/ppermute | solution.py:768
  155.5 18.6 %collective-permute-start.17 = (bf16[3,64,512]{2,1,0:T(8,128)(2,1)S(1)}, bf16[3,64,512]{2,1,0:T(8,128)(2,1)S(1)}, u32[]{:S(2)}, u32[]{:S(2)}) collective-permute-start(bf16[3,64,512]{2,1,0:T(8,128)(2,1)S(1)} %get-tuple-element.42), channel_id=1, source_target_pairs={{12,8},{13,9},{14,10},{15,11},{28,24},{29,25},{30,26},{31,27}} | collective-permute-start | bytes 589832 | tf_op jit(solution)/shard_map/ppermute | solution.py:768
  156.3 16.0 %copy-start.4 = (bf16[288,576]{1,0:T(8,128)(2,1)S(1)}, bf16[288,576]{1,0:T(8,128)(2,1)}, u32[]{:S(2)}) copy-start(bf16[288,576]{1,0:T(8,128)(2,1)} %copy-done.3) | copy-start | bytes 995332
  156.3 1.1 copy-start.20
  171.3 0.9 copy-start.21
  177.4 4.5 %copy-start.24 = (s32[16]{0:T(128)S(1)}, s32[16]{0:T(128)}, u32[]{:S(2)}) copy-start(s32[16]{0:T(128)} %param.19) | copy-start | bytes 196
  177.4 26.8 %all-to-all-start = ((bf16[4,576,384]{2,1,0:T(8,128)(2,1)}), bf16[4,576,384]{2,1,0:T(8,128)(2,1)}, u32[]{:S(2)}, u32[]{:S(2)}) async-start(bf16[4,576,384]{2,1,0:T(8,128)(2,1)} %pages.3.refs_8_), calls=%async_computation | async-start | bytes 3538944 | tf_op jit(solution)/shard_map/all_to_all | solution.py:796
  182.2 8.3 %collective-permute-start.20 = (bf16[1,64,512]{2,1,0:T(8,128)(2,1)S(1)}, bf16[1,64,512]{2,1,0:T(8,128)(2,1)S(1)}, u32[]{:S(2)}, u32[]{:S(2)}) collective-permute-start(bf16[1,64,512]{2,1,0:T(8,128)(2,1)S(1)} %get-tuple-element.45.refs_8_), channel_id=1, source_target_pairs={{12,0},{13,1},{14,2},{15,3},{28,16},{29,17},{30,18},{31,19}} | collective-permute-start | bytes 196616 | tf_op jit(solution)/shard_map/ppermute | solution.py:768
  183.4 7.0 %collective-permute-start.21 = (bf16[1,64,512]{2,1,0:T(8,128)(2,1)S(1)}, bf16[1,64,512]{2,1,0:T(8,128)(2,1)S(1)}, u32[]{:S(2)}, u32[]{:S(2)}) collective-permute-start(bf16[1,64,512]{2,1,0:T(8,128)(2,1)S(1)} %get-tuple-element.46), channel_id=1, source_target_pairs={{12,4},{13,5},{14,6},{15,7},{28,20},{29,21},{30,22},{31,23}} | collective-permute-start | bytes 196616 | tf_op jit(solution)/shard_map/ppermute | solution.py:768
  184.1 6.3 %collective-permute-start.22 = (bf16[1,64,512]{2,1,0:T(8,128)(2,1)S(1)}, bf16[1,64,512]{2,1,0:T(8,128)(2,1)S(1)}, u32[]{:S(2)}, u32[]{:S(2)}) collective-permute-start(bf16[1,64,512]{2,1,0:T(8,128)(2,1)S(1)} %get-tuple-element.47), channel_id=1, source_target_pairs={{12,8},{13,9},{14,10},{15,11},{28,24},{29,25},{30,26},{31,27}} | collective-permute-start | bytes 196616 | tf_op jit(solution)/shard_map/ppermute | solution.py:768
  206.9 7.4 %all-to-all-start.1 = ((bf16[4,2,4096]{2,1,0:T(2,128)(2,1)}), bf16[4,2,4096]{2,1,0:T(2,128)(2,1)S(1)}, u32[]{:S(2)}, u32[]{:S(2)}) async-start(bf16[4,2,4096]{2,1,0:T(2,128)(2,1)} %route.1), calls=%async_computation.1 | async-start | bytes 131072 | tf_op jit(solution)/shard_map/all_to_all | solution.py:808
  214.3 3.5 %copy-start.1 = (bf16[16,2,1536]{2,1,0:T(2,128)(2,1)S(1)}, bf16[16,2,1536]{2,1,0:T(2,128)(2,1)}, u32[]{:S(2)}) copy-start(bf16[16,2,1536]{2,1,0:T(2,128)(2,1)} %param.14) | copy-start | bytes 294916
  (2 other events, 1.8 us)

commit v7 on v6

--- a/solution.py
+++ b/solution.py
@@ -619,54 +619,69 @@
     )(rank, first, *messages, *messages, own, *got, *tables, segments, gain, cosine, sine, *after)
 
 
-def heads_kernel(step, o_ref, keep_ref, *refs):
+def heads_kernel(step, slot, o_ref, keep_ref, *refs):
     out_ref = refs[-1]
+    out_ref[...] = jnp.zeros_like(out_ref)
     for h, value_ref in enumerate(refs[:step]):
         row = jnp.dot(o_ref[h].astype(BF), value_ref[...], preferred_element_type=F32)
-        out_ref[:, h * DV : (h + 1) * DV] = row * keep_ref[...]
-
-
-def heads_out(attended, keep, kv_up, after):
+        row = (row * keep_ref[...]).astype(BF)
+        for r in range(RP):
+            out_ref[slot[r], :, h * DV : (h + 1) * DV] = row[2 * r : 2 * r + 2]
+
+
+def heads_out(slot, attended, keep, kv_up, count, after):
     heads, rows, _ = attended.shape
     step = 8
     value_spec = [
-        pl.BlockSpec((KVL, DV), lambda i, h=h: (0, 2 * (step * i + h) + 1)) for h in range(step)
+        pl.BlockSpec((KVL, DV), lambda i, slot, h=h: (0, 2 * (step * i + h) + 1))
+        for h in range(step)
     ]
     return pl.pallas_call(
         functools.partial(heads_kernel, step),
-        grid=(heads // step,),
-        in_specs=[
-            pl.BlockSpec((step, rows, KVL), lambda i: (i, 0, 0)),
-            pl.BlockSpec((rows, DV), lambda i: (0, 0)),
-            *value_spec,
-            *([ANY] * len(after)),
-        ],
-        out_specs=pl.BlockSpec((rows, step * DV), lambda i: (0, i)),
-        out_shape=jax.ShapeDtypeStruct((rows, heads * DV), F32),
+        grid_spec=pltpu.PrefetchScalarGridSpec(
+            num_scalar_prefetch=1,
+            grid=(heads // step,),
+            in_specs=[
+                pl.BlockSpec((step, rows, KVL), lambda i, slot: (i, 0, 0)),
+                pl.BlockSpec((rows, DV), lambda i, slot: (0, 0)),
+                *value_spec,
+                *([ANY] * len(after)),
+            ],
+            out_specs=pl.BlockSpec((count, 2, step * DV), lambda i, slot: (0, 0, i)),
+        ),
+        out_shape=jax.ShapeDtypeStruct((count, 2, heads * DV), BF),
         compiler_params=ROOM,
         cost_estimate=COST,
         name="heads_out",
-    )(attended, keep, *([kv_up] * step), *after)
-
-
-def route_kernel(slot, answer_ref, *refs):
-    out_ref = refs[-1]
-    out_ref[...] = jnp.zeros_like(out_ref)
-    for r in range(RP):
-        out_ref[slot[r]] = answer_ref[2 * r : 2 * r + 2, :].astype(BF)
-
-
-def route(slot, answer, count, after):
-    width = answer.shape[1]
+    )(slot, attended, keep, *([kv_up] * step), *after)
+
+
+def emit_kernel(pages_ref, placed_ref, out_ref, same_ref, done):
+    copies = [
+        pltpu.make_async_copy(pages_ref.at[n], out_ref.at[n], done.at[n])
+        for n in range(pages_ref.shape[0])
+    ]
+    for copy in copies:
+        copy.start()
+    for copy in copies:
+        copy.wait()
+
+
+def emit(pages, placed):
     return pl.pallas_call(
-        route_kernel,
-        in_specs=[SMEM, VMEM, *([ANY] * len(after))],
-        out_specs=VMEM,
-        out_shape=jax.ShapeDtypeStruct((count, 2, width), BF),
+        emit_kernel,
+        in_specs=[ANY, ANY],
+        out_specs=[ANY, ANY],
+        out_shape=[
+            jax.ShapeDtypeStruct(pages.shape, pages.dtype),
+            jax.ShapeDtypeStruct(placed.shape, placed.dtype),
+        ],
+        scratch_shapes=[pltpu.SemaphoreType.DMA((pages.shape[0],))],
+        input_output_aliases={1: 1},
         compiler_params=SOME,
         cost_estimate=COST,
-        name="route",
-    )(slot, answer, *after)
+        name="emit",
+    )(pages, placed)
 
 
 def rope_tables(position):
@@ -791,8 +806,8 @@
     results[0], backs[0] = attend_to(early, done)
     base = [jnp.zeros((pd_count, WIDTH, SHARE), BF)] if pd_count > RP else []
     pages = pages_to(early, base, results[0][:1])
+    pages = pages_to(late, [pages], backs[0])
     results[1], backs[1] = attend_to(late, [pages])
-    pages = pages_to(late, [pages], [*results[1][:1], *backs[0]])
     cache = lax.all_to_all(pages, "pd", split_axis=0, concat_axis=0, tiled=True)
 
     attended = [
@@ -803,11 +818,17 @@
     attended = attended.reshape(heads, RP * 2, KVL).astype(F32)
     my_accepted = lax.dynamic_slice_in_dim(accepted, first_req, RP, 0)
     keep = (jnp.arange(2)[None, :] <= my_accepted[:, None]).astype(F32).reshape(RP * 2, 1)
-    answer = heads_out(attended, jnp.broadcast_to(keep, (RP * 2, DV)), kv_up, [pages])
-    placed = route(my_owners, answer, pd_count, [lax.slice(cache, (0, 0, 0), (1, 16, UNIT))])
+    placed = heads_out(
+        my_owners,
+        attended,
+        jnp.broadcast_to(keep, (RP * 2, DV)),
+        kv_up,
+        pd_count,
+        [pages],
+    )
+    cache, placed = emit(cache, placed)
     placed = lax.all_to_all(placed, "pd", split_axis=0, concat_axis=0, tiled=True)
-    cache = jnp.swapaxes(cache, 1, 2)
-    return (placed.reshape(pd_count * 2, heads * DV), cache)
+    return (placed.reshape(pd_count * 2, heads * DV), jnp.swapaxes(cache, 1, 2))
 
 
 def solution(mesh):

time: 219 us -> 211 us (0.963)
  the two profiles are of different devices: /device:TPU:0 before, /device:TPU:16 now
where the time goes in v7:
time: 211 us; the launch traced here: 207 us
  Pallas kernels  89.1 us (42%)
  starting transfers between devices  55.6 us (26%)
  waiting for transfers between devices  41.2 us (20%)
  local copies, waits for them, and re-layouts  10.2 us (5%)
  blocking collectives  6.49 us (3%)
  other arithmetic  3.4 us (2%)
    pallas_call x4, Pallas kernels, project_far(): pl.pallas_call(project_far_kernel, grid_spec=pltpu.PrefetchScalarGridSpec...  22.6 us
    ppermute x4, starting transfers between devices, second_hop(): outer.append(lax.ppermute(block, 'tp', outward))  21.8 us
    pallas_call x8, Pallas kernels, add_on(): pl.pallas_call(functools.partial(add_kernel, -1 - len(carried)), grid_spe...  17.9 us
    ppermute x4, waiting for transfers between devices, second_hop(): outer.append(lax.ppermute(block, 'tp', outward))  14.2 us
    pallas_call x1, Pallas kernels, queries(): pl.pallas_call(body, grid=(heads // step,), in_specs=[pl.BlockSpec((rows,...  13.8 us
    pallas_call x1, Pallas kernels, project_near(): pl.pallas_call(project_near_kernel, grid_spec=pltpu.PrefetchScalarGridSpe...  13.1 us
    ppermute x6, waiting for transfers between devices, attend_to(): return (result, [lax.ppermute(result[t], 'tp', [(3, t)]) for t in range(3)])  10.6 us
    ppermute x4, starting transfers between devices, first_hop(): crossed.append(lax.ppermute(block, 'tp', across))  9.57 us
  transfers between devices with their start and end apart: 24, of which 10 were waited for; matrix products, arithmetic and copies ran while one was open for 3% of the time, Pallas kernels for 38%

profile of v7, /device:TPU:16, one launch (start us, length us, event | category | flops | bytes accessed | tf_op | source)
XLA Modules:
  0.0 207.3 jit_solution(7677816348500810213)
XLA Ops:
  0.7 5.7 %project_far.4 = (f32[2,3,576,128]{3,2,1,0:T(8,128)}, s16[2,3,592,128]{3,2,1,0:T(8,128)(2,1)}) custom-call(s32[1]{0:T(128)} %bitcast.rank, bf16[4,1536,1792]{2,1,0:T(8,128)(2,1)} %bitcast.22, bf16[576,1792]{1,0:T(8,128)(2,1)} %bitcast.27), custom_call_target="tpu_custom_call" | custom-call | flops 1024 | bytes 1024 | tf_op jit(solution)/shard_map/project_far/pallas_call | solution.py:269
  6.3 1.3 collective-permute-start
  7.6 5.6 %project_far.5 = (f32[2,3,576,128]{3,2,1,0:T(8,128)}, s16[2,3,592,128]{3,2,1,0:T(8,128)(2,1)}) custom-call(s32[1]{0:T(128)} %bitcast.rank, bf16[4,1536,1792]{2,1,0:T(8,128)(2,1)} %bitcast.23, bf16[576,1792]{1,0:T(8,128)(2,1)} %bitcast.28, f32[2,3,576,128]{3,2,1,0:T(8,128)} %get-tuple-element.27.refs_0_.own_ref), custom_call_target="tpu_custom_call" | custom-call | flops 1024 | bytes 1024 | tf_op jit(solution)/shard_map/project_far/pallas_call | solution.py:269
  13.2 1.3 collective-permute-start.2
  16.0 13.8 %queries.1 = (f32[32,8,576]{2,1,0:T(8,128)}, f32[4,8,576]{2,1,0:T(8,128)}) custom-call(bf16[8,1536]{1,0:T(8,128)(2,1)} %reshape.129.refs_0_, bf16[1536,6144]{1,0:T(8,128)(2,1)} %refs_1_.2, bf16[8,1792]{1,0:T(8,128)(2,1)} %refs_2_.2, bf16[576,1792]{1,0:T(8,128)(2,1)} %bitcast.29, bf16[512,8192]{1,0:T(8,128)(2,1)} %refs_7_.3, bf16[512,8192]{1,0:T(8,128)(2,1)} %refs_7_.3, ...), custom_call_target="tpu_custom_call" | custom-call | flops 1024 | bytes 1024 | tf_op jit(solution)/shard_map/queries/pallas_call | solution.py:485
  32.0 2.2 %add_on.8.refs_0_ = s16[2,3,592,128]{3,2,1,0:T(8,128)(2,1)S(1)} custom-call(s32[1]{0:T(128)} %bitcast.rank, f32[2,3,576,128]{3,2,1,0:T(8,128)} %get-tuple-element.27.refs_0_.own_ref, s16[2,3,592,128]{3,2,1,0:T(8,128)(2,1)} %collective-permute-done.got_ref, bf16[288,576]{1,0:T(8,128)(2,1)S(1)} %pad_maximum_fusion.refs_0_.refs_3_.refs_7_), custom_call_target="tpu_custom_call" | custom-call | flops 1024 | bytes 1024 | tf_op jit(solution)/shard_map/add_on/pallas_call | solution.py:358
  34.1 2.4 %collective-permute-start.1 = (s16[2,3,592,128]{3,2,1,0:T(8,128)(2,1)S(1)}, s16[2,3,592,128]{3,2,1,0:T(8,128)(2,1)}, u32[]{:S(2)}, u32[]{:S(2)}) collective-permute-start(s16[2,3,592,128]{3,2,1,0:T(8,128)(2,1)S(1)} %add_on.8.refs_0_), channel_id=1, source_target_pairs={{4,8},{8,4},{5,9},{9,5},{6,10},{10,6},{7,11},{11,7},{20,24},{24,20... | collective-permute-start | bytes 2727944 | tf_op jit(solution)/shard_map/ppermute | solution.py:725
  37.9 6.1 %collective-permute-start.5 = (bf16[288,576]{1,0:T(8,128)(2,1)S(1)}, bf16[288,576]{1,0:T(8,128)(2,1)S(1)}, u32[]{:S(2)}, u32[]{:S(2)}) collective-permute-start(bf16[288,576]{1,0:T(8,128)(2,1)S(1)} %pad_maximum_fusion.refs_0_.refs_3_.refs_7_), channel_id=1, source_target_pairs={{8,12},{9,13},{10,14},{11,15},{24,28},{25,29},{26,30},{27,31}} | collective-permute-start | bytes 995336 | tf_op jit(solution)/shard_map/ppermute | solution.py:748
  44.0 5.6 %project_far.6 = (f32[2,3,576,128]{3,2,1,0:T(8,128)}, s16[2,3,592,128]{3,2,1,0:T(8,128)(2,1)}) custom-call(s32[1]{0:T(128)} %bitcast.rank, bf16[4,1536,1792]{2,1,0:T(8,128)(2,1)} %bitcast.24, bf16[576,1792]{1,0:T(8,128)(2,1)} %bitcast.30, s16[2,3,592,128]{3,2,1,0:T(8,128)(2,1)} %copy-done.11), custom_call_target="tpu_custom_call" | custom-call | flops 1024 | bytes 1024 | tf_op jit(solution)/shard_map/project_far/pallas_call | solution.py:269
  49.6 13.1 %project_near.1 = (f32[3,2,4,576,128]{4,3,2,1,0:T(8,128)}, s16[1,4,592,128]{3,2,1,0:T(8,128)(2,1)}, s16[2,4,592,128]{3,2,1,0:T(8,128)(2,1)}) custom-call(s32[1]{0:T(128)} %bitcast.rank, bf16[4,1536,1792]{2,1,0:T(8,128)(2,1)} %bitcast.25, bf16[576,1792]{1,0:T(8,128)(2,1)} %bitcast.31, f32[2,3,576,128]{3,2,1,0:T(8,128)} %get-tuple-element.32.refs_0_.own_ref), custom_call_target="tpu_custom_call" | custom-call | flops 1024 | bytes 1024 | tf_op jit(solution)/shard_map/project_near/pallas_call | solution.py:312
  62.7 1.3 collective-permute-start.8
  64.0 2.7 %add_on.9.refs_0_ = s16[2,3,592,128]{3,2,1,0:T(8,128)(2,1)} custom-call(s32[1]{0:T(128)} %bitcast.rank, f32[2,3,576,128]{3,2,1,0:T(8,128)} %get-tuple-element.29.refs_10_.own_ref, s16[2,3,592,128]{3,2,1,0:T(8,128)(2,1)S(1)} %collective-permute-done.2.got_ref, f32[3,2,4,576,128]{4,3,2,1,0:T(8,128)} %get-tuple-element.33.refs_0_.own_ref.refs_8_), custom_call_target="tpu_custom_call" | custom-call | flops 1024 | bytes 1024 | tf_op jit(solution)/shard_map/add_on/pallas_call | solution.py:358
  66.7 2.8 %collective-permute-start.7 = (s16[2,3,592,128]{3,2,1,0:T(8,128)(2,1)}, s16[2,3,592,128]{3,2,1,0:T(8,128)(2,1)}, u32[]{:S(2)}, u32[]{:S(2)}) collective-permute-start(s16[2,3,592,128]{3,2,1,0:T(8,128)(2,1)} %add_on.9.refs_0_), channel_id=1, source_target_pairs={{4,8},{8,4},{5,9},{9,5},{6,10},{10,6},{7,11},{11,7},{20,24},{24,20... | collective-permute-start | bytes 2727944 | tf_op jit(solution)/shard_map/ppermute | solution.py:725
  69.5 2.2 %add_on.10.refs_0_.refs_3_ = s16[2,3,592,128]{3,2,1,0:T(8,128)(2,1)S(1)} custom-call(s32[1]{0:T(128)} %bitcast.rank, f32[3,2,4,576,128]{4,3,2,1,0:T(8,128)} %get-tuple-element.33.refs_0_.own_ref.refs_8_, s16[2,3,592,128]{3,2,1,0:T(8,128)(2,1)} %collective-permute-done.1.got_ref, s16[2,3,592,128]{3,2,1,0:T(8,128)(2,1)} %add_on.9.refs_0_, ...), custom_call_target="tpu_custom_call" | custom-call | flops 1024 | bytes 1024 | tf_op jit(solution)/shard_map/add_on/pallas_call | solution.py:358
  71.7 8.5 %collective-permute-start.9 = (s16[2,3,592,128]{3,2,1,0:T(8,128)(2,1)S(1)}, s16[2,3,592,128]{3,2,1,0:T(8,128)(2,1)S(1)}, u32[]{:S(2)}, u32[]{:S(2)}) collective-permute-start(s16[2,3,592,128]{3,2,1,0:T(8,128)(2,1)S(1)} %add_on.10.refs_0_.refs_3_), channel_id=1, source_target_pairs={{8,12},{4,0},{9,13},{5,1},{10,14},{6,2},{11,15},{7,3},{24,28},{20,... | collective-permute-start | bytes 2727944 | tf_op jit(solution)/shard_map/ppermute | solution.py:731
  80.2 5.7 %project_far.7 = (f32[2,3,576,128]{3,2,1,0:T(8,128)}, s16[2,3,592,128]{3,2,1,0:T(8,128)(2,1)}) custom-call(s32[1]{0:T(128)} %bitcast.rank, bf16[4,1536,1792]{2,1,0:T(8,128)(2,1)} %bitcast.26, bf16[576,1792]{1,0:T(8,128)(2,1)} %bitcast.32, s16[2,3,592,128]{3,2,1,0:T(8,128)(2,1)} %copy-done.5), custom_call_target="tpu_custom_call" | custom-call | flops 1024 | bytes 1024 | tf_op jit(solution)/shard_map/project_far/pallas_call | solution.py:269
  85.9 1.3 collective-permute-start.6
  87.2 2.8 %add_on.11 = (s16[2,3,592,128]{3,2,1,0:T(8,128)(2,1)}, s16[1,4,592,128]{3,2,1,0:T(8,128)(2,1)}) custom-call(s32[1]{0:T(128)} %bitcast.rank, f32[2,3,576,128]{3,2,1,0:T(8,128)} %get-tuple-element.32.refs_0_.own_ref, s16[2,3,592,128]{3,2,1,0:T(8,128)(2,1)} %collective-permute-done.8.got_ref, ...), custom_call_target="tpu_custom_call", output_to_operand_aliasing={{1}: (4, {})} | custom-call | flops 1024 | bytes 1024 | tf_op jit(solution)/shard_map/add_on/pallas_call | solution.py:358
  90.0 2.5 %collective-permute-start.11 = (s16[2,3,592,128]{3,2,1,0:T(8,128)(2,1)}, s16[2,3,592,128]{3,2,1,0:T(8,128)(2,1)}, u32[]{:S(2)}, u32[]{:S(2)}) collective-permute-start(s16[2,3,592,128]{3,2,1,0:T(8,128)(2,1)} %get-tuple-element.39.refs_0_), channel_id=1, source_target_pairs={{4,8},{8,4},{5,9},{9,5},{6,10},{10,6},{7,11},{11,7},{20,24},{24,20... | collective-permute-start | bytes 2727944 | tf_op jit(solution)/shard_map/ppermute | solution.py:725
  92.6 1.7 collective-permute-done.7.got_ref
  94.3 3.2 %collective-permute-done.9.refs_1_.refs_9_.refs_0_ = s16[2,3,592,128]{3,2,1,0:T(8,128)(2,1)S(1)} collective-permute-done((s16[2,3,592,128]{3,2,1,0:T(8,128)(2,1)S(1)}, s16[2,3,592,128]{3,2,1,0:T(8,128)(2,1)S(1)}, u32[]{:S(2)}, u32[]{:S(2)}) %collective-permute-start.9) | collective-permute-done | bytes 909344 | tf_op jit(solution)/shard_map/ppermute | solution.py:731
  98.4 2.0 add_on.12.refs_0_.refs_4_
  100.5 5.0 %collective-permute-start.12 = (s16[2,3,592,128]{3,2,1,0:T(8,128)(2,1)S(1)}, s16[2,3,592,128]{3,2,1,0:T(8,128)(2,1)}, u32[]{:S(2)}, u32[]{:S(2)}) collective-permute-start(s16[2,3,592,128]{3,2,1,0:T(8,128)(2,1)S(1)} %add_on.12.refs_0_.refs_4_), channel_id=1, source_target_pairs={{8,12},{4,0},{9,13},{5,1},{10,14},{6,2},{11,15},{7,3},{24,28},{20,... | collective-permute-start | bytes 2727944 | tf_op jit(solution)/shard_map/ppermute | solution.py:731
  105.5 1.3 collective-permute-start.13
  107.2 1.2 collective-permute-done.6.got_ref
  108.5 2.0 add_on.13.refs_0_
  110.5 1.9 collective-permute-start.10
  112.4 8.2 %collective-permute-done.13.refs_2_.refs_6_ = s16[1,4,592,128]{3,2,1,0:T(8,128)(2,1)S(1)} collective-permute-done((s16[1,4,592,128]{3,2,1,0:T(8,128)(2,1)}, s16[1,4,592,128]{3,2,1,0:T(8,128)(2,1)S(1)}, u32[]{:S(2)}, u32[]{:S(2)}) %collective-permute-start.13) | collective-permute-done | bytes 606240 | tf_op jit(solution)/shard_map/ppermute | solution.py:762
  121.0 2.1 %add_on.14.refs_0_.refs_5_ = s16[2,3,592,128]{3,2,1,0:T(8,128)(2,1)S(1)} custom-call(s32[1]{0:T(128)} %bitcast.rank, f32[3,2,4,576,128]{4,3,2,1,0:T(8,128)} %get-tuple-element.33.refs_0_.own_ref.refs_8_, s16[2,3,592,128]{3,2,1,0:T(8,128)(2,1)} %collective-permute-done.11.got_ref, s16[2,3,592,128]{3,2,1,0:T(8,128)(2,1)} %copy-done.12, ...), custom_call_target="tpu_custom_call" | custom-call | flops 1024 | bytes 1024 | tf_op jit(solution)/shard_map/add_on/pallas_call | solution.py:358
  123.1 4.2 %collective-permute-start.14 = (s16[2,3,592,128]{3,2,1,0:T(8,128)(2,1)S(1)}, s16[2,3,592,128]{3,2,1,0:T(8,128)(2,1)S(1)}, u32[]{:S(2)}, u32[]{:S(2)}) collective-permute-start(s16[2,3,592,128]{3,2,1,0:T(8,128)(2,1)S(1)} %add_on.14.refs_0_.refs_5_), channel_id=1, source_target_pairs={{8,12},{4,0},{9,13},{5,1},{10,14},{6,2},{11,15},{7,3},{24,28},{20,... | collective-permute-start | bytes 2727944 | tf_op jit(solution)/shard_map/ppermute | solution.py:731
  127.4 1.4 collective-permute-start.16
  128.8 3.4 %collective-permute-done.10.got_ref = s16[2,3,592,128]{3,2,1,0:T(8,128)(2,1)S(1)} collective-permute-done((s16[2,3,592,128]{3,2,1,0:T(8,128)(2,1)S(1)}, s16[2,3,592,128]{3,2,1,0:T(8,128)(2,1)S(1)}, u32[]{:S(2)}, u32[]{:S(2)}) %collective-permute-start.10) | collective-permute-done | bytes 909344 | tf_op jit(solution)/shard_map/ppermute | solution.py:725
  132.2 10.6 %collective-permute-done.14.refs_1_.refs_11_.refs_2_ = s16[2,3,592,128]{3,2,1,0:T(8,128)(2,1)S(1)} collective-permute-done((s16[2,3,592,128]{3,2,1,0:T(8,128)(2,1)S(1)}, s16[2,3,592,128]{3,2,1,0:T(8,128)(2,1)S(1)}, u32[]{:S(2)}, u32[]{:S(2)}) %collective-permute-start.14) | collective-permute-done | bytes 909344 | tf_op jit(solution)/shard_map/ppermute | solution.py:731
  143.8 1.9 add_on.15.refs_20_.refs_1_
  145.7 4.2 %collective-permute-start.15 = (s16[2,3,592,128]{3,2,1,0:T(8,128)(2,1)S(1)}, s16[2,3,592,128]{3,2,1,0:T(8,128)(2,1)S(1)}, u32[]{:S(2)}, u32[]{:S(2)}) collective-permute-start(s16[2,3,592,128]{3,2,1,0:T(8,128)(2,1)S(1)} %add_on.15.refs_20_.refs_1_), channel_id=1, source_target_pairs={{8,12},{4,0},{9,13},{5,1},{10,14},{6,2},{11,15},{7,3},{24,28},{20,... | collective-permute-start | bytes 2727944 | tf_op jit(solution)/shard_map/ppermute | solution.py:731
  149.9 4.1 %attend.2 = (bf16[3,64,512]{2,1,0:T(8,128)(2,1)S(1)}, bf16[3,64,512]{2,1,0:T(8,128)(2,1)S(1)}, bf16[3,64,512]{2,1,0:T(8,128)(2,1)S(1)}, bf16[3,64,512]{2,1,0:T(8,128)(2,1)S(1)}) custom-call(s32[1]{0:T(128)} %bitcast.rank, s32[1]{0:T(128)} %bitcast.8.first_ref, bf16[288,576]{1,0:T(8,128)(2,1)S(1)} %collective-permute-done.3.refs_1_.refs_0_.refs_4_, ...), custom_call_target="tpu_custom_call" | custom-call | flops 1024 | bytes 1024 | tf_op jit(solution)/shard_map/attend/pallas_call | solution.py:593
  156.1 1.3 collective-permute-start.19
  158.6 5.8 %pages.2.refs_7_ = bf16[4,576,384]{2,1,0:T(8,128)(2,1)} custom-call(s32[1]{0:T(128)} %bitcast.rank, s32[4]{0:T(128)S(1)} %dynamic_slice.9.slot, f32[3,2,4,576,128]{4,3,2,1,0:T(8,128)} %get-tuple-element.33.refs_0_.own_ref.refs_8_, s16[2,3,592,128]{3,2,1,0:T(8,128)(2,1)S(1)} %copy-done.8, s16[2,3,592,128]{3,2,1,0:T(8,128)(2,1)} %collective-permute-done.12.refs_1_.refs_10_, ...), custom_call_target="tpu_custom_call" | custom-call | flops 1024 | bytes 1024 | tf_op jit(solution)/shard_map/pages/pallas_call | solution.py:420
  164.4 3.4 %collective-permute-done.19.refs_10_ = bf16[3,64,512]{2,1,0:T(8,128)(2,1)S(1)} collective-permute-done((bf16[3,64,512]{2,1,0:T(8,128)(2,1)S(1)}, bf16[3,64,512]{2,1,0:T(8,128)(2,1)S(1)}, u32[]{:S(2)}, u32[]{:S(2)}) %collective-permute-start.19) | collective-permute-done | bytes 196640 | tf_op jit(solution)/shard_map/ppermute | solution.py:783
  168.8 3.4 %pages.3.refs_18_.refs_8_ = bf16[4,576,384]{2,1,0:T(8,128)(2,1)} custom-call(s32[1]{0:T(128)} %bitcast.rank, s32[4]{0:T(128)S(1)} %dynamic_slice.9.slot, f32[3,2,4,576,128]{4,3,2,1,0:T(8,128)} %get-tuple-element.33.refs_0_.own_ref.refs_8_, s16[2,3,592,128]{3,2,1,0:T(8,128)(2,1)} %copy-done.26, ...), custom_call_target="tpu_custom_call", output_to_operand_aliasing={{}: (10, {})} | custom-call | flops 1024 | bytes 1024 | tf_op jit(solution)/shard_map/pages/pallas_call | solution.py:420
  172.2 3.7 %all-to-all-start = ((bf16[4,576,384]{2,1,0:T(8,128)(2,1)}), bf16[4,576,384]{2,1,0:T(8,128)(2,1)S(1)}, u32[]{:S(2)}, u32[]{:S(2)}) async-start(bf16[4,576,384]{2,1,0:T(8,128)(2,1)} %pages.3.refs_18_.refs_8_), calls=%async_computation | async-start | bytes 3538944 | tf_op jit(solution)/shard_map/all_to_all | solution.py:811
  177.1 1.8 attend.3
  180.3 1.3 collective-permute-start.22
  181.7 7.2 %collective-permute-done.22 = bf16[1,64,512]{2,1,0:T(8,128)(2,1)S(1)} collective-permute-done((bf16[1,64,512]{2,1,0:T(8,128)(2,1)S(1)}, bf16[1,64,512]{2,1,0:T(8,128)(2,1)S(1)}, u32[]{:S(2)}, u32[]{:S(2)}) %collective-permute-start.22) | collective-permute-done | bytes 65568 | tf_op jit(solution)/shard_map/ppermute | solution.py:783
  191.0 5.2 %heads_out.1.placed_ref = bf16[4,2,4096]{2,1,0:T(2,128)(2,1)} custom-call(s32[4]{0:T(128)} %copy-done.23, f32[32,8,512]{2,1,0:T(8,128)} %reshape.139.o_ref, f32[8,128]{1,0:T(8,128)} %broadcast_in_dim.2.keep_ref, bf16[512,8192]{1,0:T(8,128)(2,1)} %refs_7_.3, bf16[512,8192]{1,0:T(8,128)(2,1)} %refs_7_.3, bf16[512,8192]{1,0:T(8,128)(2,1)} %refs_7_.3, ...), custom_call_target="tpu_custom_call" | custom-call | flops 1024 | bytes 1024 | tf_op jit(solution)/shard_map/heads_out/pallas_call | solution.py:639
  196.2 1.9 all-to-all-done.pages_ref
  198.9 1.2 emit.1
  200.2 6.5 %all_to_all.10 = bf16[4,2,4096]{2,1,0:T(2,128)(2,1)S(1)} all-to-all(bf16[4,2,4096]{2,1,0:T(2,128)(2,1)S(1)} %get-tuple-element.50), channel_id=1, replica_groups=mesh['groups'=2,'tp'=4,'pd'=4] {'pd'}, dimensions={0} | all-to-all | bytes 131072 | tf_op jit(solution)/shard_map/all_to_all | solution.py:830
  (106 shorter events, 18.1 us)
Async XLA Ops:
  0.6 13.9 %copy-start = (bf16[16,2,1536]{2,1,0:T(2,128)(2,1)S(1)}, bf16[16,2,1536]{2,1,0:T(2,128)(2,1)}, u32[]{:S(2)}) copy-start(bf16[16,2,1536]{2,1,0:T(2,128)(2,1)} %param.14) | copy-start | bytes 294916
  6.3 25.6 %collective-permute-start = (s16[2,3,592,128]{3,2,1,0:T(8,128)(2,1)}, s16[2,3,592,128]{3,2,1,0:T(8,128)(2,1)}, u32[]{:S(2)}, u32[]{:S(2)}) collective-permute-start(s16[2,3,592,128]{3,2,1,0:T(8,128)(2,1)} %get-tuple-element.28), channel_id=1, source_target_pairs={{0,4},{12,8},{1,5},{13,9},{2,6},{14,10},{3,7},{15,11},{16,20},{28,... | collective-permute-start | bytes 2727944 | tf_op jit(solution)/shard_map/ppermute | solution.py:721
  13.2 49.5 %collective-permute-start.2 = (s16[2,3,592,128]{3,2,1,0:T(8,128)(2,1)}, s16[2,3,592,128]{3,2,1,0:T(8,128)(2,1)S(1)}, u32[]{:S(2)}, u32[]{:S(2)}) collective-permute-start(s16[2,3,592,128]{3,2,1,0:T(8,128)(2,1)} %get-tuple-element.34), channel_id=1, source_target_pairs={{0,4},{12,8},{1,5},{13,9},{2,6},{14,10},{3,7},{15,11},{16,20},{28,... | collective-permute-start | bytes 2727944 | tf_op jit(solution)/shard_map/ppermute | solution.py:721
  31.9 6.0 %copy-start.2 = (bf16[288,576]{1,0:T(8,128)(2,1)}, bf16[288,576]{1,0:T(8,128)(2,1)S(1)}, u32[]{:S(2)}) copy-start(bf16[288,576]{1,0:T(8,128)(2,1)S(1)} %pad_maximum_fusion.refs_0_.refs_3_.refs_7_) | copy-start | bytes 995332
  34.1 9.9 %copy-start.11 = (s16[2,3,592,128]{3,2,1,0:T(8,128)(2,1)}, s16[2,3,592,128]{3,2,1,0:T(8,128)(2,1)S(1)}, u32[]{:S(2)}) copy-start(s16[2,3,592,128]{3,2,1,0:T(8,128)(2,1)S(1)} %add_on.8.refs_0_) | copy-start | bytes 2727940
  34.1 35.4 %collective-permute-start.1 = (s16[2,3,592,128]{3,2,1,0:T(8,128)(2,1)S(1)}, s16[2,3,592,128]{3,2,1,0:T(8,128)(2,1)}, u32[]{:S(2)}, u32[]{:S(2)}) collective-permute-start(s16[2,3,592,128]{3,2,1,0:T(8,128)(2,1)S(1)} %add_on.8.refs_0_), channel_id=1, source_target_pairs={{4,8},{8,4},{5,9},{9,5},{6,10},{10,6},{7,11},{11,7},{20,24},{24,20... | collective-permute-start | bytes 2727944 | tf_op jit(solution)/shard_map/ppermute | solution.py:725
  36.5 30.2 %collective-permute-start.3 = (bf16[288,576]{1,0:T(8,128)(2,1)S(1)}, bf16[288,576]{1,0:T(8,128)(2,1)S(1)}, u32[]{:S(2)}, u32[]{:S(2)}) collective-permute-start(bf16[288,576]{1,0:T(8,128)(2,1)S(1)} %pad_maximum_fusion.refs_0_.refs_3_.refs_7_), channel_id=1, source_target_pairs={{0,12},{1,13},{2,14},{3,15},{16,28},{17,29},{18,30},{19,31}} | collective-permute-start | bytes 995336 | tf_op jit(solution)/shard_map/ppermute | solution.py:748
  37.2 32.3 %collective-permute-start.4 = (bf16[288,576]{1,0:T(8,128)(2,1)S(1)}, bf16[288,576]{1,0:T(8,128)(2,1)S(1)}, u32[]{:S(2)}, u32[]{:S(2)}) collective-permute-start(bf16[288,576]{1,0:T(8,128)(2,1)S(1)} %pad_maximum_fusion.refs_0_.refs_3_.refs_7_), channel_id=1, source_target_pairs={{4,12},{5,13},{6,14},{7,15},{20,28},{21,29},{22,30},{23,31}} | collective-permute-start | bytes 995336 | tf_op jit(solution)/shard_map/ppermute | solution.py:748
  37.9 31.6 %collective-permute-start.5 = (bf16[288,576]{1,0:T(8,128)(2,1)S(1)}, bf16[288,576]{1,0:T(8,128)(2,1)S(1)}, u32[]{:S(2)}, u32[]{:S(2)}) collective-permute-start(bf16[288,576]{1,0:T(8,128)(2,1)S(1)} %pad_maximum_fusion.refs_0_.refs_3_.refs_7_), channel_id=1, source_target_pairs={{8,12},{9,13},{10,14},{11,15},{24,28},{25,29},{26,30},{27,31}} | collective-permute-start | bytes 995336 | tf_op jit(solution)/shard_map/ppermute | solution.py:748
  62.7 24.5 %collective-permute-start.8 = (s16[2,3,592,128]{3,2,1,0:T(8,128)(2,1)}, s16[2,3,592,128]{3,2,1,0:T(8,128)(2,1)}, u32[]{:S(2)}, u32[]{:S(2)}) collective-permute-start(s16[2,3,592,128]{3,2,1,0:T(8,128)(2,1)} %get-tuple-element.37), channel_id=1, source_target_pairs={{0,4},{12,8},{1,5},{13,9},{2,6},{14,10},{3,7},{15,11},{16,20},{28,... | collective-permute-start | bytes 2727944 | tf_op jit(solution)/shard_map/ppermute | solution.py:721
  66.7 27.6 %collective-permute-start.7 = (s16[2,3,592,128]{3,2,1,0:T(8,128)(2,1)}, s16[2,3,592,128]{3,2,1,0:T(8,128)(2,1)}, u32[]{:S(2)}, u32[]{:S(2)}) collective-permute-start(s16[2,3,592,128]{3,2,1,0:T(8,128)(2,1)} %add_on.9.refs_0_), channel_id=1, source_target_pairs={{4,8},{8,4},{5,9},{9,5},{6,10},{10,6},{7,11},{11,7},{20,24},{24,20... | collective-permute-start | bytes 2727944 | tf_op jit(solution)/shard_map/ppermute | solution.py:725
  69.5 2.2 %copy-start.3 = (bf16[288,576]{1,0:T(8,128)(2,1)}, bf16[288,576]{1,0:T(8,128)(2,1)S(1)}, u32[]{:S(2)}) copy-start(bf16[288,576]{1,0:T(8,128)(2,1)S(1)} %collective-permute-done.5.refs_3_.refs_2_.refs_6_) | copy-start | bytes 995332
  71.7 8.5 %copy-start.5 = (s16[2,3,592,128]{3,2,1,0:T(8,128)(2,1)}, s16[2,3,592,128]{3,2,1,0:T(8,128)(2,1)S(1)}, u32[]{:S(2)}) copy-start(s16[2,3,592,128]{3,2,1,0:T(8,128)(2,1)S(1)} %add_on.10.refs_0_.refs_3_) | copy-start | bytes 2727940
  71.7 25.8 %collective-permute-start.9 = (s16[2,3,592,128]{3,2,1,0:T(8,128)(2,1)S(1)}, s16[2,3,592,128]{3,2,1,0:T(8,128)(2,1)S(1)}, u32[]{:S(2)}, u32[]{:S(2)}) collective-permute-start(s16[2,3,592,128]{3,2,1,0:T(8,128)(2,1)S(1)} %add_on.10.refs_0_.refs_3_), channel_id=1, source_target_pairs={{8,12},{4,0},{9,13},{5,1},{10,14},{6,2},{11,15},{7,3},{24,28},{20,... | collective-permute-start | bytes 2727944 | tf_op jit(solution)/shard_map/ppermute | solution.py:731
  85.9 22.6 %collective-permute-start.6 = (s16[2,3,592,128]{3,2,1,0:T(8,128)(2,1)}, s16[2,3,592,128]{3,2,1,0:T(8,128)(2,1)}, u32[]{:S(2)}, u32[]{:S(2)}) collective-permute-start(s16[2,3,592,128]{3,2,1,0:T(8,128)(2,1)} %get-tuple-element.36), channel_id=1, source_target_pairs={{0,4},{12,8},{1,5},{13,9},{2,6},{14,10},{3,7},{15,11},{16,20},{28,... | collective-permute-start | bytes 2727944 | tf_op jit(solution)/shard_map/ppermute | solution.py:721
  90.0 30.6 %collective-permute-start.11 = (s16[2,3,592,128]{3,2,1,0:T(8,128)(2,1)}, s16[2,3,592,128]{3,2,1,0:T(8,128)(2,1)}, u32[]{:S(2)}, u32[]{:S(2)}) collective-permute-start(s16[2,3,592,128]{3,2,1,0:T(8,128)(2,1)} %get-tuple-element.39.refs_0_), channel_id=1, source_target_pairs={{4,8},{8,4},{5,9},{9,5},{6,10},{10,6},{7,11},{11,7},{20,24},{24,20... | collective-permute-start | bytes 2727944 | tf_op jit(solution)/shard_map/ppermute | solution.py:725
  100.5 8.0 %copy-start.6 = (s16[2,3,592,128]{3,2,1,0:T(8,128)(2,1)}, s16[2,3,592,128]{3,2,1,0:T(8,128)(2,1)S(1)}, u32[]{:S(2)}) copy-start(s16[2,3,592,128]{3,2,1,0:T(8,128)(2,1)S(1)} %add_on.12.refs_0_.refs_4_) | copy-start | bytes 2727940
  100.5 20.5 %collective-permute-start.12 = (s16[2,3,592,128]{3,2,1,0:T(8,128)(2,1)S(1)}, s16[2,3,592,128]{3,2,1,0:T(8,128)(2,1)}, u32[]{:S(2)}, u32[]{:S(2)}) collective-permute-start(s16[2,3,592,128]{3,2,1,0:T(8,128)(2,1)S(1)} %add_on.12.refs_0_.refs_4_), channel_id=1, source_target_pairs={{8,12},{4,0},{9,13},{5,1},{10,14},{6,2},{11,15},{7,3},{24,28},{20,... | collective-permute-start | bytes 2727944 | tf_op jit(solution)/shard_map/ppermute | solution.py:731
  105.5 15.1 %collective-permute-start.13 = (s16[1,4,592,128]{3,2,1,0:T(8,128)(2,1)}, s16[1,4,592,128]{3,2,1,0:T(8,128)(2,1)S(1)}, u32[]{:S(2)}, u32[]{:S(2)}) collective-permute-start(s16[1,4,592,128]{3,2,1,0:T(8,128)(2,1)} %get-tuple-element.40), channel_id=1, source_target_pairs={{0,4},{12,8},{1,5},{13,9},{2,6},{14,10},{3,7},{15,11},{16,20},{28,... | collective-permute-start | bytes 1818632 | tf_op jit(solution)/shard_map/ppermute | solution.py:762
  110.5 10.5 %copy-start.12 = (s16[2,3,592,128]{3,2,1,0:T(8,128)(2,1)}, s16[2,3,592,128]{3,2,1,0:T(8,128)(2,1)S(1)}, u32[]{:S(2)}) copy-start(s16[2,3,592,128]{3,2,1,0:T(8,128)(2,1)S(1)} %add_on.13.refs_0_) | copy-start | bytes 2727940
  110.5 21.7 %collective-permute-start.10 = (s16[2,3,592,128]{3,2,1,0:T(8,128)(2,1)S(1)}, s16[2,3,592,128]{3,2,1,0:T(8,128)(2,1)S(1)}, u32[]{:S(2)}, u32[]{:S(2)}) collective-permute-start(s16[2,3,592,128]{3,2,1,0:T(8,128)(2,1)S(1)} %add_on.13.refs_0_), channel_id=1, source_target_pairs={{4,8},{8,4},{5,9},{9,5},{6,10},{10,6},{7,11},{11,7},{20,24},{24,20... | collective-permute-start | bytes 2727944 | tf_op jit(solution)/shard_map/ppermute | solution.py:725
  121.0 6.3 %copy-start.27 = (s16[2,4,592,128]{3,2,1,0:T(8,128)(2,1)S(1)}, s16[2,4,592,128]{3,2,1,0:T(8,128)(2,1)}, u32[]{:S(2)}) copy-start(s16[2,4,592,128]{3,2,1,0:T(8,128)(2,1)} %get-tuple-element.41) | copy-start | bytes 3637252
  123.1 19.7 %copy-start.9 = (s16[2,3,592,128]{3,2,1,0:T(8,128)(2,1)}, s16[2,3,592,128]{3,2,1,0:T(8,128)(2,1)S(1)}, u32[]{:S(2)}) copy-start(s16[2,3,592,128]{3,2,1,0:T(8,128)(2,1)S(1)} %add_on.14.refs_0_.refs_5_) | copy-start | bytes 2727940
  123.1 19.7 %collective-permute-start.14 = (s16[2,3,592,128]{3,2,1,0:T(8,128)(2,1)S(1)}, s16[2,3,592,128]{3,2,1,0:T(8,128)(2,1)S(1)}, u32[]{:S(2)}, u32[]{:S(2)}) collective-permute-start(s16[2,3,592,128]{3,2,1,0:T(8,128)(2,1)S(1)} %add_on.14.refs_0_.refs_5_), channel_id=1, source_target_pairs={{8,12},{4,0},{9,13},{5,1},{10,14},{6,2},{11,15},{7,3},{24,28},{20,... | collective-permute-start | bytes 2727944 | tf_op jit(solution)/shard_map/ppermute | solution.py:731
  127.3 22.5 %copy-start.16 = (s32[16,1536]{1,0:T(8,128)S(1)}, s32[16,1536]{1,0:T(8,128)}, u32[]{:S(2)}) copy-start(s32[16,1536]{1,0:T(8,128)} %refs_14_.1) | copy-start | bytes 294916
  127.3 22.5 %copy-start.20 = (f32[8,32]{1,0:T(8,128)S(1)}, f32[8,32]{1,0:T(8,128)}, u32[]{:S(2)}) copy-start(f32[8,32]{1,0:T(8,128)} %get-tuple-element.56.refs_9_.refs_19_.refs_17_) | copy-start | bytes 3076
  127.4 22.5 %copy-start.21 = (f32[8,32]{1,0:T(8,128)S(1)}, f32[8,32]{1,0:T(8,128)}, u32[]{:S(2)}) copy-start(f32[8,32]{1,0:T(8,128)} %get-tuple-element.57.refs_8_.refs_18_.refs_16_) | copy-start | bytes 3076
  127.4 22.5 %copy-start.22 = (f32[512]{0:T(512)S(1)}, f32[512]{0:T(512)}, u32[]{:S(2)}) copy-start(f32[512]{0:T(512)} %param.13) | copy-start | bytes 6148
  127.4 30.1 %collective-permute-start.16 = (s16[2,4,592,128]{3,2,1,0:T(8,128)(2,1)S(1)}, s16[2,4,592,128]{3,2,1,0:T(8,128)(2,1)S(1)}, u32[]{:S(2)}, u32[]{:S(2)}) collective-permute-start(s16[2,4,592,128]{3,2,1,0:T(8,128)(2,1)S(1)} %copy-done.27), channel_id=1, source_target_pairs={{0,4},{12,8},{1,5},{13,9},{2,6},{14,10},{3,7},{15,11},{16,20},{28,... | collective-permute-start | bytes 3637256 | tf_op jit(solution)/shard_map/ppermute | solution.py:762
  145.7 4.2 %copy-start.10 = (s16[2,3,592,128]{3,2,1,0:T(8,128)(2,1)}, s16[2,3,592,128]{3,2,1,0:T(8,128)(2,1)S(1)}, u32[]{:S(2)}) copy-start(s16[2,3,592,128]{3,2,1,0:T(8,128)(2,1)S(1)} %add_on.15.refs_20_.refs_1_) | copy-start | bytes 2727940
  145.7 22.2 %collective-permute-start.15 = (s16[2,3,592,128]{3,2,1,0:T(8,128)(2,1)S(1)}, s16[2,3,592,128]{3,2,1,0:T(8,128)(2,1)S(1)}, u32[]{:S(2)}, u32[]{:S(2)}) collective-permute-start(s16[2,3,592,128]{3,2,1,0:T(8,128)(2,1)S(1)} %add_on.15.refs_20_.refs_1_), channel_id=1, source_target_pairs={{8,12},{4,0},{9,13},{5,1},{10,14},{6,2},{11,15},{7,3},{24,28},{20,... | collective-permute-start | bytes 2727944 | tf_op jit(solution)/shard_map/ppermute | solution.py:731
  149.9 7.5 %copy-start.28 = (s32[16]{0:T(128)S(1)}, s32[16]{0:T(128)}, u32[]{:S(2)}) copy-start(s32[16]{0:T(128)} %param.17) | copy-start | bytes 196
  149.9 8.7 %copy-start.8 = (s16[2,3,592,128]{3,2,1,0:T(8,128)(2,1)S(1)}, s16[2,3,592,128]{3,2,1,0:T(8,128)(2,1)}, u32[]{:S(2)}) copy-start(s16[2,3,592,128]{3,2,1,0:T(8,128)(2,1)} %copy-done.7) | copy-start | bytes 2727940
  154.7 9.7 %collective-permute-start.17 = (bf16[3,64,512]{2,1,0:T(8,128)(2,1)S(1)}, bf16[3,64,512]{2,1,0:T(8,128)(2,1)S(1)}, u32[]{:S(2)}, u32[]{:S(2)}) collective-permute-start(bf16[3,64,512]{2,1,0:T(8,128)(2,1)S(1)} %get-tuple-element.42.refs_11_), channel_id=1, source_target_pairs={{12,0},{13,1},{14,2},{15,3},{28,16},{29,17},{30,18},{31,19}} | collective-permute-start | bytes 589832 | tf_op jit(solution)/shard_map/ppermute | solution.py:783
  155.4 9.0 %collective-permute-start.18 = (bf16[3,64,512]{2,1,0:T(8,128)(2,1)S(1)}, bf16[3,64,512]{2,1,0:T(8,128)(2,1)S(1)}, u32[]{:S(2)}, u32[]{:S(2)}) collective-permute-start(bf16[3,64,512]{2,1,0:T(8,128)(2,1)S(1)} %get-tuple-element.43), channel_id=1, source_target_pairs={{12,4},{13,5},{14,6},{15,7},{28,20},{29,21},{30,22},{31,23}} | collective-permute-start | bytes 589832 | tf_op jit(solution)/shard_map/ppermute | solution.py:783
  156.1 11.8 %collective-permute-start.19 = (bf16[3,64,512]{2,1,0:T(8,128)(2,1)S(1)}, bf16[3,64,512]{2,1,0:T(8,128)(2,1)S(1)}, u32[]{:S(2)}, u32[]{:S(2)}) collective-permute-start(bf16[3,64,512]{2,1,0:T(8,128)(2,1)S(1)} %get-tuple-element.44), channel_id=1, source_target_pairs={{12,8},{13,9},{14,10},{15,11},{28,24},{29,25},{30,26},{31,27}} | collective-permute-start | bytes 589832 | tf_op jit(solution)/shard_map/ppermute | solution.py:783
  157.5 10.4 %copy-start.23 = (s32[4]{0:T(128)}, s32[4]{0:T(128)S(1)}, u32[]{:S(2)}) copy-start(s32[4]{0:T(128)S(1)} %dynamic_slice.9.slot) | copy-start | bytes 52
  157.5 1.1 copy-start.25
  167.9 4.3 %copy-start.13 = (bf16[3,64,512]{2,1,0:T(8,128)(2,1)}, bf16[3,64,512]{2,1,0:T(8,128)(2,1)S(1)}, u32[]{:S(2)}) copy-start(bf16[3,64,512]{2,1,0:T(8,128)(2,1)S(1)} %collective-permute-done.19.refs_10_) | copy-start | bytes 589828
  172.2 3.7 %copy-start.29 = (s32[16]{0:T(128)S(1)}, s32[16]{0:T(128)}, u32[]{:S(2)}) copy-start(s32[16]{0:T(128)} %param.19) | copy-start | bytes 196
  172.2 4.0 %copy-start.4 = (bf16[288,576]{1,0:T(8,128)(2,1)S(1)}, bf16[288,576]{1,0:T(8,128)(2,1)}, u32[]{:S(2)}) copy-start(bf16[288,576]{1,0:T(8,128)(2,1)} %copy-done.3) | copy-start | bytes 995332
  172.2 25.9 %all-to-all-start = ((bf16[4,576,384]{2,1,0:T(8,128)(2,1)}), bf16[4,576,384]{2,1,0:T(8,128)(2,1)S(1)}, u32[]{:S(2)}, u32[]{:S(2)}) async-start(bf16[4,576,384]{2,1,0:T(8,128)(2,1)} %pages.3.refs_18_.refs_8_), calls=%async_computation | async-start | bytes 3538944 | tf_op jit(solution)/shard_map/all_to_all | solution.py:811
  177.1 4.5 %copy-start.14 = (bf16[3,64,512]{2,1,0:T(8,128)(2,1)S(1)}, bf16[3,64,512]{2,1,0:T(8,128)(2,1)}, u32[]{:S(2)}) copy-start(bf16[3,64,512]{2,1,0:T(8,128)(2,1)} %copy-done.13) | copy-start | bytes 589828
  177.1 4.5 %copy-start.19 = (bf16[3,64,512]{2,1,0:T(8,128)(2,1)S(1)}, bf16[3,64,512]{2,1,0:T(8,128)(2,1)}, u32[]{:S(2)}) copy-start(bf16[3,64,512]{2,1,0:T(8,128)(2,1)} %copy-done.18) | copy-start | bytes 589828
  178.9 2.7 %collective-permute-start.20 = (bf16[1,64,512]{2,1,0:T(8,128)(2,1)S(1)}, bf16[1,64,512]{2,1,0:T(8,128)(2,1)S(1)}, u32[]{:S(2)}, u32[]{:S(2)}) collective-permute-start(bf16[1,64,512]{2,1,0:T(8,128)(2,1)S(1)} %get-tuple-element.47), channel_id=1, source_target_pairs={{12,0},{13,1},{14,2},{15,3},{28,16},{29,17},{30,18},{31,19}} | collective-permute-start | bytes 196616 | tf_op jit(solution)/shard_map/ppermute | solution.py:783
  179.6 2.1 collective-permute-start.21
  180.3 8.6 %collective-permute-start.22 = (bf16[1,64,512]{2,1,0:T(8,128)(2,1)S(1)}, bf16[1,64,512]{2,1,0:T(8,128)(2,1)S(1)}, u32[]{:S(2)}, u32[]{:S(2)}) collective-permute-start(bf16[1,64,512]{2,1,0:T(8,128)(2,1)S(1)} %get-tuple-element.49), channel_id=1, source_target_pairs={{12,8},{13,9},{14,10},{15,11},{28,24},{29,25},{30,26},{31,27}} | collective-permute-start | bytes 196616 | tf_op jit(solution)/shard_map/ppermute | solution.py:783
  191.0 16.4 %copy-start.1 = (bf16[16,2,1536]{2,1,0:T(2,128)(2,1)S(1)}, bf16[16,2,1536]{2,1,0:T(2,128)(2,1)}, u32[]{:S(2)}) copy-start(bf16[16,2,1536]{2,1,0:T(2,128)(2,1)} %param.14) | copy-start | bytes 294916
  (6 other events, 5.2 us)

commit v8 on v7

--- a/solution.py
+++ b/solution.py
@@ -381,6 +381,23 @@
     )(rank, own, got, *after, *carried)
 
 
+def hold_kernel(*refs):
+    pass
+
+
+def hold(block, after):
+    return pl.pallas_call(
+        hold_kernel,
+        in_specs=[ANY] * (1 + len(after)),
+        out_specs=ANY,
+        out_shape=jax.ShapeDtypeStruct(block.shape, block.dtype),
+        input_output_aliases={0: 0},
+        compiler_params=SOME,
+        cost_estimate=COST,
+        name="hold",
+    )(block, *after)
+
+
 def gain_column(gain_ref):
     return jnp.broadcast_to(gain_ref[...], (UNIT, KVL)).T
 
@@ -725,8 +742,10 @@
         crossed.append(lax.ppermute(block, "tp", across))
         return [block, *carried]
 
-    def second_hop(r, after):
+    def second_hop(r, after, awaited=()):
         (block,) = add_on(rank, near_sums, crossed[r], r, after)
+        if awaited:
+            block = hold(block, awaited)
         sent.append(block)
         outer.append(lax.ppermute(block, "tp", outward))
         return [block]
@@ -760,10 +779,10 @@
     ]
     block, side[0] = first_hop(2, far_sums[3:], side[:1])
     side = [lax.ppermute(codes, "tp", inward) for codes in side]
-    done = second_hop(1, [block, outer[0]])
+    done = second_hop(1, [block], outer[:1])
     done = first_hop(3, done)
-    done = second_hop(2, [*done, outer[1], side[0], *tables])
-    done = second_hop(3, [*done, outer[2]])
+    done = second_hop(2, [*done, *tables], [outer[1], side[0]])
+    done = second_hop(3, done, outer[2:])
 
     def attend_to(requests, after):
         result = attend(
@@ -806,8 +825,8 @@
     results[0], backs[0] = attend_to(early, done)
     base = [jnp.zeros((pd_count, WIDTH, SHARE), BF)] if pd_count > RP else []
     pages = pages_to(early, base, results[0][:1])
-    pages = pages_to(late, [pages], backs[0])
-    results[1], backs[1] = attend_to(late, [pages])
+    pages = pages_to(late, [pages], [])
+    results[1], backs[1] = attend_to(late, [pages, *backs[0]])
     cache = lax.all_to_all(pages, "pd", split_axis=0, concat_axis=0, tiled=True)
 
     attended = [

time: 211 us -> 268 us (1.27)
  Pallas kernels: 89.1 us -> 142 us
  waiting for transfers between devices: 41.2 us -> 50.7 us
  local copies, waits for them, and re-layouts: 10.2 us -> 6.74 us
    pallas_call x1, Pallas kernels: 1.23 us -> 54.7 us  [emit(): pl.pallas_call(emit_kernel, in_specs=[ANY, ANY], out_specs=[ANY, ANY], ou...]
    ppermute x6, waiting for transfers between devices: 10.6 us -> 19.7 us  [attend_to(): return (result, [lax.ppermute(result[t], 'tp', [(3, t)]) for t in range(3)])]
    ppermute x4, waiting for transfers between devices: 1.22 us -> 8.39 us  [send_far(): inner.append(lax.ppermute(codes, 'tp', inward))]
    ppermute x4, waiting for transfers between devices: 14.2 us -> 9.85 us  [second_hop(): outer.append(lax.ppermute(block, 'tp', outward))]
    unnamed x60 -> x46, local copies, waits for them, and re-layouts: 6.44 us -> 2.96 us
    ppermute x2, waiting for transfers between devices: 8.16 us -> 5.13 us  [local_line(): side = [lax.ppermute(codes, 'tp', inward) for codes in side]]
  transfers between devices with their start and end apart: 24 -> 24, of which waited for: 10 -> 11; matrix products, arithmetic and copies ran while one was open for 3% -> 2% of each run, Pallas kernels for 38% -> 30%
where the time goes in v8:
time: 268 us; the launch traced here: 265 us
  Pallas kernels  142 us (53%)
  starting transfers between devices  53.8 us (20%)
  waiting for transfers between devices  50.7 us (19%)
  blocking collectives  6.86 us (3%)
  local copies, waits for them, and re-layouts  6.74 us (3%)
  other arithmetic  3.38 us (1%)
    pallas_call x1, Pallas kernels, emit(): pl.pallas_call(emit_kernel, in_specs=[ANY, ANY], out_specs=[ANY, ANY], ou...  54.7 us
    pallas_call x4, Pallas kernels, project_far(): pl.pallas_call(project_far_kernel, grid_spec=pltpu.PrefetchScalarGridSpec...  22.6 us
    ppermute x6, waiting for transfers between devices, attend_to(): return (result, [lax.ppermute(result[t], 'tp', [(3, t)]) for t in range(3)])  19.7 us
    ppermute x4, starting transfers between devices, second_hop(): outer.append(lax.ppermute(block, 'tp', outward))  19.2 us
    pallas_call x8, Pallas kernels, add_on(): pl.pallas_call(functools.partial(add_kernel, -1 - len(carried)), grid_spe...  17.8 us
    pallas_call x1, Pallas kernels, queries(): pl.pallas_call(body, grid=(heads // step,), in_specs=[pl.BlockSpec((rows,...  13.8 us
    pallas_call x1, Pallas kernels, project_near(): pl.pallas_call(project_near_kernel, grid_spec=pltpu.PrefetchScalarGridSpe...  13.1 us
    ppermute x4, waiting for transfers between devices, second_hop(): outer.append(lax.ppermute(block, 'tp', outward))  9.85 us
  transfers between devices with their start and end apart: 24, of which 11 were waited for; matrix products, arithmetic and copies ran while one was open for 2% of the time, Pallas kernels for 30%

profile of v8, /device:TPU:16, one launch (start us, length us, event | category | flops | bytes accessed | tf_op | source)
XLA Modules:
  0.0 265.3 jit_solution(14584499340335726376)
XLA Ops:
  0.7 5.6 %project_far.4 = (f32[2,3,576,128]{3,2,1,0:T(8,128)}, s16[2,3,592,128]{3,2,1,0:T(8,128)(2,1)}) custom-call(s32[1]{0:T(128)} %bitcast.rank, bf16[4,1536,1792]{2,1,0:T(8,128)(2,1)} %bitcast.22, bf16[576,1792]{1,0:T(8,128)(2,1)} %bitcast.27), custom_call_target="tpu_custom_call" | custom-call | flops 1024 | bytes 1024 | tf_op jit(solution)/shard_map/project_far/pallas_call | solution.py:269
  6.3 1.3 collective-permute-start
  7.6 5.7 %project_far.5 = (f32[2,3,576,128]{3,2,1,0:T(8,128)}, s16[2,3,592,128]{3,2,1,0:T(8,128)(2,1)}) custom-call(s32[1]{0:T(128)} %bitcast.rank, bf16[4,1536,1792]{2,1,0:T(8,128)(2,1)} %bitcast.23, bf16[576,1792]{1,0:T(8,128)(2,1)} %bitcast.28, f32[2,3,576,128]{3,2,1,0:T(8,128)} %get-tuple-element.27.refs_0_.own_ref), custom_call_target="tpu_custom_call" | custom-call | flops 1024 | bytes 1024 | tf_op jit(solution)/shard_map/project_far/pallas_call | solution.py:269
  13.2 1.3 collective-permute-start.2
  16.0 13.8 %queries.1 = (f32[32,8,576]{2,1,0:T(8,128)}, f32[4,8,576]{2,1,0:T(8,128)}) custom-call(bf16[8,1536]{1,0:T(8,128)(2,1)} %reshape.129.refs_0_, bf16[1536,6144]{1,0:T(8,128)(2,1)} %refs_1_.2, bf16[8,1792]{1,0:T(8,128)(2,1)} %refs_2_.2, bf16[576,1792]{1,0:T(8,128)(2,1)} %bitcast.29, bf16[512,8192]{1,0:T(8,128)(2,1)} %refs_7_.3, bf16[512,8192]{1,0:T(8,128)(2,1)} %refs_7_.3, ...), custom_call_target="tpu_custom_call" | custom-call | flops 1024 | bytes 1024 | tf_op jit(solution)/shard_map/queries/pallas_call | solution.py:502
  32.0 2.2 add_on.8.refs_0_
  34.2 2.4 collective-permute-start.1
  37.9 6.0 %collective-permute-start.5 = (bf16[288,576]{1,0:T(8,128)(2,1)S(1)}, bf16[288,576]{1,0:T(8,128)(2,1)S(1)}, u32[]{:S(2)}, u32[]{:S(2)}) collective-permute-start(bf16[288,576]{1,0:T(8,128)(2,1)S(1)} %pad_maximum_fusion.refs_0_.refs_3_.refs_7_), channel_id=1, source_target_pairs={{8,12},{9,13},{10,14},{11,15},{24,28},{25,29},{26,30},{27,31}} | collective-permute-start | bytes 995336 | tf_op jit(solution)/shard_map/ppermute | solution.py:767
  44.0 5.6 %project_far.6 = (f32[2,3,576,128]{3,2,1,0:T(8,128)}, s16[2,3,592,128]{3,2,1,0:T(8,128)(2,1)}) custom-call(s32[1]{0:T(128)} %bitcast.rank, bf16[4,1536,1792]{2,1,0:T(8,128)(2,1)} %bitcast.24, bf16[576,1792]{1,0:T(8,128)(2,1)} %bitcast.30, s16[2,3,592,128]{3,2,1,0:T(8,128)(2,1)} %copy-done.9), custom_call_target="tpu_custom_call" | custom-call | flops 1024 | bytes 1024 | tf_op jit(solution)/shard_map/project_far/pallas_call | solution.py:269
  49.8 1.3 collective-permute-start.8
  51.1 13.1 %project_near.1 = (f32[3,2,4,576,128]{4,3,2,1,0:T(8,128)}, s16[1,4,592,128]{3,2,1,0:T(8,128)(2,1)}, s16[2,4,592,128]{3,2,1,0:T(8,128)(2,1)}) custom-call(s32[1]{0:T(128)} %bitcast.rank, bf16[4,1536,1792]{2,1,0:T(8,128)(2,1)} %bitcast.25, bf16[576,1792]{1,0:T(8,128)(2,1)} %bitcast.31, f32[2,3,576,128]{3,2,1,0:T(8,128)} %get-tuple-element.32.refs_0_.own_ref), custom_call_target="tpu_custom_call" | custom-call | flops 1024 | bytes 1024 | tf_op jit(solution)/shard_map/project_near/pallas_call | solution.py:312
  64.2 2.6 add_on.9.refs_0_
  66.9 3.5 %collective-permute-start.7 = (s16[2,3,592,128]{3,2,1,0:T(8,128)(2,1)}, s16[2,3,592,128]{3,2,1,0:T(8,128)(2,1)}, u32[]{:S(2)}, u32[]{:S(2)}) collective-permute-start(s16[2,3,592,128]{3,2,1,0:T(8,128)(2,1)} %add_on.9.refs_0_), channel_id=1, source_target_pairs={{4,8},{8,4},{5,9},{9,5},{6,10},{10,6},{7,11},{11,7},{20,24},{24,20... | collective-permute-start | bytes 2727944 | tf_op jit(solution)/shard_map/ppermute | solution.py:742
  70.4 2.2 add_on.10.refs_0_.refs_3_
  72.6 8.5 %collective-permute-start.9 = (s16[2,3,592,128]{3,2,1,0:T(8,128)(2,1)S(1)}, s16[2,3,592,128]{3,2,1,0:T(8,128)(2,1)}, u32[]{:S(2)}, u32[]{:S(2)}) collective-permute-start(s16[2,3,592,128]{3,2,1,0:T(8,128)(2,1)S(1)} %add_on.10.refs_0_.refs_3_), channel_id=1, source_target_pairs={{8,12},{4,0},{9,13},{5,1},{10,14},{6,2},{11,15},{7,3},{24,28},{20,... | collective-permute-start | bytes 2727944 | tf_op jit(solution)/shard_map/ppermute | solution.py:750
  81.1 5.6 %project_far.7 = (f32[2,3,576,128]{3,2,1,0:T(8,128)}, s16[2,3,592,128]{3,2,1,0:T(8,128)(2,1)}) custom-call(s32[1]{0:T(128)} %bitcast.rank, bf16[4,1536,1792]{2,1,0:T(8,128)(2,1)} %bitcast.26, bf16[576,1792]{1,0:T(8,128)(2,1)} %bitcast.32, s16[2,3,592,128]{3,2,1,0:T(8,128)(2,1)} %copy-done.7), custom_call_target="tpu_custom_call" | custom-call | flops 1024 | bytes 1024 | tf_op jit(solution)/shard_map/project_far/pallas_call | solution.py:269
  86.7 1.3 collective-permute-start.6
  88.0 2.8 %add_on.11 = (s16[2,3,592,128]{3,2,1,0:T(8,128)(2,1)}, s16[1,4,592,128]{3,2,1,0:T(8,128)(2,1)}) custom-call(s32[1]{0:T(128)} %bitcast.rank, f32[2,3,576,128]{3,2,1,0:T(8,128)} %get-tuple-element.32.refs_0_.own_ref, s16[2,3,592,128]{3,2,1,0:T(8,128)(2,1)} %collective-permute-done.8.got_ref, ...), custom_call_target="tpu_custom_call", output_to_operand_aliasing={{1}: (4, {})} | custom-call | flops 1024 | bytes 1024 | tf_op jit(solution)/shard_map/add_on/pallas_call | solution.py:358
  90.8 1.9 collective-permute-start.11
  93.5 2.0 add_on.12.refs_0_
  95.6 2.0 collective-permute-done.9.refs_1_.refs_9_.refs_0_
  97.5 4.5 %collective-permute-start.12 = (s16[2,3,592,128]{3,2,1,0:T(8,128)(2,1)S(1)}, s16[2,3,592,128]{3,2,1,0:T(8,128)(2,1)S(1)}, u32[]{:S(2)}, u32[]{:S(2)}) collective-permute-start(s16[2,3,592,128]{3,2,1,0:T(8,128)(2,1)S(1)} %hold.3.refs_0_.refs_4_), channel_id=1, source_target_pairs={{8,12},{4,0},{9,13},{5,1},{10,14},{6,2},{11,15},{7,3},{24,28},{20,... | collective-permute-start | bytes 2727944 | tf_op jit(solution)/shard_map/ppermute | solution.py:750
  102.1 1.3 collective-permute-start.13
  103.8 8.2 %collective-permute-done.6.got_ref = s16[2,3,592,128]{3,2,1,0:T(8,128)(2,1)} collective-permute-done((s16[2,3,592,128]{3,2,1,0:T(8,128)(2,1)}, s16[2,3,592,128]{3,2,1,0:T(8,128)(2,1)}, u32[]{:S(2)}, u32[]{:S(2)}) %collective-permute-start.6) | collective-permute-done | bytes 909344 | tf_op jit(solution)/shard_map/ppermute | solution.py:738
  112.1 2.0 add_on.13.refs_0_
  114.1 1.9 collective-permute-start.10
  116.1 2.1 add_on.14.refs_0_
  118.1 3.3 %collective-permute-done.13.refs_2_.refs_6_ = s16[1,4,592,128]{3,2,1,0:T(8,128)(2,1)S(1)} collective-permute-done((s16[1,4,592,128]{3,2,1,0:T(8,128)(2,1)}, s16[1,4,592,128]{3,2,1,0:T(8,128)(2,1)S(1)}, u32[]{:S(2)}, u32[]{:S(2)}) %collective-permute-start.13) | collective-permute-done | bytes 606240 | tf_op jit(solution)/shard_map/ppermute | solution.py:781
  122.4 1.6 collective-permute-start.14
  124.0 1.3 collective-permute-start.16
  125.3 6.9 %collective-permute-done.10.got_ref = s16[2,3,592,128]{3,2,1,0:T(8,128)(2,1)S(1)} collective-permute-done((s16[2,3,592,128]{3,2,1,0:T(8,128)(2,1)S(1)}, s16[2,3,592,128]{3,2,1,0:T(8,128)(2,1)S(1)}, u32[]{:S(2)}, u32[]{:S(2)}) %collective-permute-start.10) | collective-permute-done | bytes 909344 | tf_op jit(solution)/shard_map/ppermute | solution.py:742
  132.2 1.9 add_on.15.refs_0_
  134.2 5.9 %collective-permute-done.14.refs_1_.refs_11_.refs_2_ = s16[2,3,592,128]{3,2,1,0:T(8,128)(2,1)S(1)} collective-permute-done((s16[2,3,592,128]{3,2,1,0:T(8,128)(2,1)S(1)}, s16[2,3,592,128]{3,2,1,0:T(8,128)(2,1)S(1)}, u32[]{:S(2)}, u32[]{:S(2)}) %collective-permute-start.14) | collective-permute-done | bytes 909344 | tf_op jit(solution)/shard_map/ppermute | solution.py:750
  140.1 4.6 %collective-permute-start.15 = (s16[2,3,592,128]{3,2,1,0:T(8,128)(2,1)S(1)}, s16[2,3,592,128]{3,2,1,0:T(8,128)(2,1)S(1)}, u32[]{:S(2)}, u32[]{:S(2)}) collective-permute-start(s16[2,3,592,128]{3,2,1,0:T(8,128)(2,1)S(1)} %hold.5.refs_20_.refs_1_), channel_id=1, source_target_pairs={{8,12},{4,0},{9,13},{5,1},{10,14},{6,2},{11,15},{7,3},{24,28},{20,... | collective-permute-start | bytes 2727944 | tf_op jit(solution)/shard_map/ppermute | solution.py:750
  144.9 4.1 %attend.2 = (bf16[3,64,512]{2,1,0:T(8,128)(2,1)S(1)}, bf16[3,64,512]{2,1,0:T(8,128)(2,1)S(1)}, bf16[3,64,512]{2,1,0:T(8,128)(2,1)S(1)}, bf16[3,64,512]{2,1,0:T(8,128)(2,1)S(1)}) custom-call(s32[1]{0:T(128)} %bitcast.rank, s32[1]{0:T(128)} %bitcast.8.first_ref, bf16[288,576]{1,0:T(8,128)(2,1)S(1)} %collective-permute-done.3.refs_1_.refs_0_.refs_4_, ...), custom_call_target="tpu_custom_call" | custom-call | flops 1024 | bytes 1024 | tf_op jit(solution)/shard_map/attend/pallas_call | solution.py:610
  149.0 1.8 collective-permute-done.16.refs_7_.refs_3_
  151.9 6.0 %pages.2.refs_7_ = bf16[4,576,384]{2,1,0:T(8,128)(2,1)} custom-call(s32[1]{0:T(128)} %bitcast.rank, s32[4]{0:T(128)S(1)} %dynamic_slice.9.slot, f32[3,2,4,576,128]{4,3,2,1,0:T(8,128)} %get-tuple-element.33.refs_0_.own_ref.refs_8_, s16[2,3,592,128]{3,2,1,0:T(8,128)(2,1)} %collective-permute-done.9.refs_1_.refs_9_.refs_0_, s16[2,3,592,128]{3,2,1,0:T(8,128)(2,1)} %copy-done.18, ...), custom_call_target="tpu_custom_call" | custom-call | flops 1024 | bytes 1024 | tf_op jit(solution)/shard_map/pages/pallas_call | solution.py:437
  157.9 1.9 collective-permute-done.15.refs_0_.refs_9_
  159.8 3.2 %pages.3.refs_18_.refs_8_ = bf16[4,576,384]{2,1,0:T(8,128)(2,1)} custom-call(s32[1]{0:T(128)} %bitcast.rank, s32[4]{0:T(128)S(1)} %dynamic_slice.9.slot, f32[3,2,4,576,128]{4,3,2,1,0:T(8,128)} %get-tuple-element.33.refs_0_.own_ref.refs_8_, s16[2,3,592,128]{3,2,1,0:T(8,128)(2,1)S(1)} %collective-permute-done.15.refs_0_.refs_9_, ...), custom_call_target="tpu_custom_call", output_to_operand_aliasing={{}: (10, {})} | custom-call | flops 1024 | bytes 1024 | tf_op jit(solution)/shard_map/pages/pallas_call | solution.py:437
  163.1 4.6 %all-to-all-start = ((bf16[4,576,384]{2,1,0:T(8,128)(2,1)}), bf16[4,576,384]{2,1,0:T(8,128)(2,1)}, u32[]{:S(2)}, u32[]{:S(2)}) async-start(bf16[4,576,384]{2,1,0:T(8,128)(2,1)} %pages.3.refs_18_.refs_8_), calls=%async_computation | async-start | bytes 3538944 | tf_op jit(solution)/shard_map/all_to_all | solution.py:830
  169.1 1.3 collective-permute-start.19
  170.5 14.8 %collective-permute-done.19.refs_21_ = bf16[3,64,512]{2,1,0:T(8,128)(2,1)S(1)} collective-permute-done((bf16[3,64,512]{2,1,0:T(8,128)(2,1)S(1)}, bf16[3,64,512]{2,1,0:T(8,128)(2,1)S(1)}, u32[]{:S(2)}, u32[]{:S(2)}) %collective-permute-start.19) | collective-permute-done | bytes 196640 | tf_op jit(solution)/shard_map/ppermute | solution.py:802
  185.3 1.9 attend.3
  188.5 1.3 collective-permute-start.22
  189.9 4.9 %collective-permute-done.22 = bf16[1,64,512]{2,1,0:T(8,128)(2,1)S(1)} collective-permute-done((bf16[1,64,512]{2,1,0:T(8,128)(2,1)S(1)}, bf16[1,64,512]{2,1,0:T(8,128)(2,1)S(1)}, u32[]{:S(2)}, u32[]{:S(2)}) %collective-permute-start.22) | collective-permute-done | bytes 65568 | tf_op jit(solution)/shard_map/ppermute | solution.py:802
  196.9 5.2 %heads_out.1.placed_ref = bf16[4,2,4096]{2,1,0:T(2,128)(2,1)} custom-call(s32[4]{0:T(128)} %copy-done.17, f32[32,8,512]{2,1,0:T(8,128)} %reshape.139.o_ref, f32[8,128]{1,0:T(8,128)} %broadcast_in_dim.2.keep_ref, bf16[512,8192]{1,0:T(8,128)(2,1)} %refs_7_.3, bf16[512,8192]{1,0:T(8,128)(2,1)} %refs_7_.3, bf16[512,8192]{1,0:T(8,128)(2,1)} %refs_7_.3, ...), custom_call_target="tpu_custom_call" | custom-call | flops 1024 | bytes 1024 | tf_op jit(solution)/shard_map/heads_out/pallas_call | solution.py:656
  203.0 54.7 %emit.1 = (bf16[4,576,384]{2,1,0:T(8,128)(2,1)}, bf16[4,2,4096]{2,1,0:T(2,128)(2,1)S(1)}) custom-call(bf16[4,576,384]{2,1,0:T(8,128)(2,1)} %all-to-all-done.pages_ref, bf16[4,2,4096]{2,1,0:T(2,128)(2,1)S(1)} %copy-done.12), custom_call_target="tpu_custom_call", output_to_operand_aliasing={{1}: (1, {})} | custom-call | flops 1024 | bytes 1024 | tf_op jit(solution)/shard_map/emit/pallas_call | solution.py:688
  257.7 6.9 %all_to_all.10 = bf16[4,2,4096]{2,1,0:T(2,128)(2,1)S(1)} all-to-all(bf16[4,2,4096]{2,1,0:T(2,128)(2,1)S(1)} %get-tuple-element.50), channel_id=1, replica_groups=mesh['groups'=2,'tp'=4,'pd'=4] {'pd'}, dimensions={0} | all-to-all | bytes 131072 | tf_op jit(solution)/shard_map/all_to_all | solution.py:849
  (95 shorter events, 15.1 us)
Async XLA Ops:
  0.6 13.9 %copy-start = (bf16[16,2,1536]{2,1,0:T(2,128)(2,1)S(1)}, bf16[16,2,1536]{2,1,0:T(2,128)(2,1)}, u32[]{:S(2)}) copy-start(bf16[16,2,1536]{2,1,0:T(2,128)(2,1)} %param.14) | copy-start | bytes 294916
  6.3 25.7 %collective-permute-start = (s16[2,3,592,128]{3,2,1,0:T(8,128)(2,1)}, s16[2,3,592,128]{3,2,1,0:T(8,128)(2,1)}, u32[]{:S(2)}, u32[]{:S(2)}) collective-permute-start(s16[2,3,592,128]{3,2,1,0:T(8,128)(2,1)} %get-tuple-element.28), channel_id=1, source_target_pairs={{0,4},{12,8},{1,5},{13,9},{2,6},{14,10},{3,7},{15,11},{16,20},{28,... | collective-permute-start | bytes 2727944 | tf_op jit(solution)/shard_map/ppermute | solution.py:738
  13.2 36.6 %collective-permute-start.2 = (s16[2,3,592,128]{3,2,1,0:T(8,128)(2,1)}, s16[2,3,592,128]{3,2,1,0:T(8,128)(2,1)S(1)}, u32[]{:S(2)}, u32[]{:S(2)}) collective-permute-start(s16[2,3,592,128]{3,2,1,0:T(8,128)(2,1)} %get-tuple-element.34), channel_id=1, source_target_pairs={{0,4},{12,8},{1,5},{13,9},{2,6},{14,10},{3,7},{15,11},{16,20},{28,... | collective-permute-start | bytes 2727944 | tf_op jit(solution)/shard_map/ppermute | solution.py:738
  32.0 6.0 %copy-start.5 = (bf16[288,576]{1,0:T(8,128)(2,1)}, bf16[288,576]{1,0:T(8,128)(2,1)S(1)}, u32[]{:S(2)}) copy-start(bf16[288,576]{1,0:T(8,128)(2,1)S(1)} %pad_maximum_fusion.refs_0_.refs_3_.refs_7_) | copy-start | bytes 995332
  34.2 9.8 %copy-start.9 = (s16[2,3,592,128]{3,2,1,0:T(8,128)(2,1)}, s16[2,3,592,128]{3,2,1,0:T(8,128)(2,1)S(1)}, u32[]{:S(2)}) copy-start(s16[2,3,592,128]{3,2,1,0:T(8,128)(2,1)S(1)} %add_on.8.refs_0_) | copy-start | bytes 2727940
  34.2 36.2 %collective-permute-start.1 = (s16[2,3,592,128]{3,2,1,0:T(8,128)(2,1)S(1)}, s16[2,3,592,128]{3,2,1,0:T(8,128)(2,1)}, u32[]{:S(2)}, u32[]{:S(2)}) collective-permute-start(s16[2,3,592,128]{3,2,1,0:T(8,128)(2,1)S(1)} %add_on.8.refs_0_), channel_id=1, source_target_pairs={{4,8},{8,4},{5,9},{9,5},{6,10},{10,6},{7,11},{11,7},{20,24},{24,20... | collective-permute-start | bytes 2727944 | tf_op jit(solution)/shard_map/ppermute | solution.py:742
  36.5 30.3 %collective-permute-start.3 = (bf16[288,576]{1,0:T(8,128)(2,1)S(1)}, bf16[288,576]{1,0:T(8,128)(2,1)S(1)}, u32[]{:S(2)}, u32[]{:S(2)}) collective-permute-start(bf16[288,576]{1,0:T(8,128)(2,1)S(1)} %pad_maximum_fusion.refs_0_.refs_3_.refs_7_), channel_id=1, source_target_pairs={{0,12},{1,13},{2,14},{3,15},{16,28},{17,29},{18,30},{19,31}} | collective-permute-start | bytes 995336 | tf_op jit(solution)/shard_map/ppermute | solution.py:767
  37.2 33.1 %collective-permute-start.4 = (bf16[288,576]{1,0:T(8,128)(2,1)S(1)}, bf16[288,576]{1,0:T(8,128)(2,1)S(1)}, u32[]{:S(2)}, u32[]{:S(2)}) collective-permute-start(bf16[288,576]{1,0:T(8,128)(2,1)S(1)} %pad_maximum_fusion.refs_0_.refs_3_.refs_7_), channel_id=1, source_target_pairs={{4,12},{5,13},{6,14},{7,15},{20,28},{21,29},{22,30},{23,31}} | collective-permute-start | bytes 995336 | tf_op jit(solution)/shard_map/ppermute | solution.py:767
  37.9 32.5 %collective-permute-start.5 = (bf16[288,576]{1,0:T(8,128)(2,1)S(1)}, bf16[288,576]{1,0:T(8,128)(2,1)S(1)}, u32[]{:S(2)}, u32[]{:S(2)}) collective-permute-start(bf16[288,576]{1,0:T(8,128)(2,1)S(1)} %pad_maximum_fusion.refs_0_.refs_3_.refs_7_), channel_id=1, source_target_pairs={{8,12},{9,13},{10,14},{11,15},{24,28},{25,29},{26,30},{27,31}} | collective-permute-start | bytes 995336 | tf_op jit(solution)/shard_map/ppermute | solution.py:767
  49.8 38.2 %collective-permute-start.8 = (s16[2,3,592,128]{3,2,1,0:T(8,128)(2,1)}, s16[2,3,592,128]{3,2,1,0:T(8,128)(2,1)}, u32[]{:S(2)}, u32[]{:S(2)}) collective-permute-start(s16[2,3,592,128]{3,2,1,0:T(8,128)(2,1)} %get-tuple-element.37), channel_id=1, source_target_pairs={{0,4},{12,8},{1,5},{13,9},{2,6},{14,10},{3,7},{15,11},{16,20},{28,... | collective-permute-start | bytes 2727944 | tf_op jit(solution)/shard_map/ppermute | solution.py:738
  66.9 26.6 %collective-permute-start.7 = (s16[2,3,592,128]{3,2,1,0:T(8,128)(2,1)}, s16[2,3,592,128]{3,2,1,0:T(8,128)(2,1)}, u32[]{:S(2)}, u32[]{:S(2)}) collective-permute-start(s16[2,3,592,128]{3,2,1,0:T(8,128)(2,1)} %add_on.9.refs_0_), channel_id=1, source_target_pairs={{4,8},{8,4},{5,9},{9,5},{6,10},{10,6},{7,11},{11,7},{20,24},{24,20... | collective-permute-start | bytes 2727944 | tf_op jit(solution)/shard_map/ppermute | solution.py:742
  70.4 2.2 copy-start.6
  72.6 8.5 %copy-start.7 = (s16[2,3,592,128]{3,2,1,0:T(8,128)(2,1)}, s16[2,3,592,128]{3,2,1,0:T(8,128)(2,1)S(1)}, u32[]{:S(2)}) copy-start(s16[2,3,592,128]{3,2,1,0:T(8,128)(2,1)S(1)} %add_on.10.refs_0_.refs_3_) | copy-start | bytes 2727940
  72.6 24.9 %collective-permute-start.9 = (s16[2,3,592,128]{3,2,1,0:T(8,128)(2,1)S(1)}, s16[2,3,592,128]{3,2,1,0:T(8,128)(2,1)}, u32[]{:S(2)}, u32[]{:S(2)}) collective-permute-start(s16[2,3,592,128]{3,2,1,0:T(8,128)(2,1)S(1)} %add_on.10.refs_0_.refs_3_), channel_id=1, source_target_pairs={{8,12},{4,0},{9,13},{5,1},{10,14},{6,2},{11,15},{7,3},{24,28},{20,... | collective-permute-start | bytes 2727944 | tf_op jit(solution)/shard_map/ppermute | solution.py:750
  86.7 25.3 %collective-permute-start.6 = (s16[2,3,592,128]{3,2,1,0:T(8,128)(2,1)}, s16[2,3,592,128]{3,2,1,0:T(8,128)(2,1)}, u32[]{:S(2)}, u32[]{:S(2)}) collective-permute-start(s16[2,3,592,128]{3,2,1,0:T(8,128)(2,1)} %get-tuple-element.36), channel_id=1, source_target_pairs={{0,4},{12,8},{1,5},{13,9},{2,6},{14,10},{3,7},{15,11},{16,20},{28,... | collective-permute-start | bytes 2727944 | tf_op jit(solution)/shard_map/ppermute | solution.py:738
  90.8 25.2 %collective-permute-start.11 = (s16[2,3,592,128]{3,2,1,0:T(8,128)(2,1)}, s16[2,3,592,128]{3,2,1,0:T(8,128)(2,1)}, u32[]{:S(2)}, u32[]{:S(2)}) collective-permute-start(s16[2,3,592,128]{3,2,1,0:T(8,128)(2,1)} %get-tuple-element.39.refs_0_), channel_id=1, source_target_pairs={{4,8},{8,4},{5,9},{9,5},{6,10},{10,6},{7,11},{11,7},{20,24},{24,20... | collective-permute-start | bytes 2727944 | tf_op jit(solution)/shard_map/ppermute | solution.py:742
  97.5 14.5 %copy-start.3 = (s16[2,3,592,128]{3,2,1,0:T(8,128)(2,1)}, s16[2,3,592,128]{3,2,1,0:T(8,128)(2,1)S(1)}, u32[]{:S(2)}) copy-start(s16[2,3,592,128]{3,2,1,0:T(8,128)(2,1)S(1)} %hold.3.refs_0_.refs_4_) | copy-start | bytes 2727940
  97.5 23.9 %collective-permute-start.12 = (s16[2,3,592,128]{3,2,1,0:T(8,128)(2,1)S(1)}, s16[2,3,592,128]{3,2,1,0:T(8,128)(2,1)S(1)}, u32[]{:S(2)}, u32[]{:S(2)}) collective-permute-start(s16[2,3,592,128]{3,2,1,0:T(8,128)(2,1)S(1)} %hold.3.refs_0_.refs_4_), channel_id=1, source_target_pairs={{8,12},{4,0},{9,13},{5,1},{10,14},{6,2},{11,15},{7,3},{24,28},{20,... | collective-permute-start | bytes 2727944 | tf_op jit(solution)/shard_map/ppermute | solution.py:750
  102.1 19.4 %collective-permute-start.13 = (s16[1,4,592,128]{3,2,1,0:T(8,128)(2,1)}, s16[1,4,592,128]{3,2,1,0:T(8,128)(2,1)S(1)}, u32[]{:S(2)}, u32[]{:S(2)}) collective-permute-start(s16[1,4,592,128]{3,2,1,0:T(8,128)(2,1)} %get-tuple-element.40), channel_id=1, source_target_pairs={{0,4},{12,8},{1,5},{13,9},{2,6},{14,10},{3,7},{15,11},{16,20},{28,... | collective-permute-start | bytes 1818632 | tf_op jit(solution)/shard_map/ppermute | solution.py:781
  114.1 2.0 copy-start.10
  114.1 18.1 %collective-permute-start.10 = (s16[2,3,592,128]{3,2,1,0:T(8,128)(2,1)S(1)}, s16[2,3,592,128]{3,2,1,0:T(8,128)(2,1)S(1)}, u32[]{:S(2)}, u32[]{:S(2)}) collective-permute-start(s16[2,3,592,128]{3,2,1,0:T(8,128)(2,1)S(1)} %add_on.13.refs_0_), channel_id=1, source_target_pairs={{4,8},{8,4},{5,9},{9,5},{6,10},{10,6},{7,11},{11,7},{20,24},{24,20... | collective-permute-start | bytes 2727944 | tf_op jit(solution)/shard_map/ppermute | solution.py:742
  118.1 5.9 %copy-start.20 = (s16[2,4,592,128]{3,2,1,0:T(8,128)(2,1)S(1)}, s16[2,4,592,128]{3,2,1,0:T(8,128)(2,1)}, u32[]{:S(2)}) copy-start(s16[2,4,592,128]{3,2,1,0:T(8,128)(2,1)} %get-tuple-element.41) | copy-start | bytes 3637252
  121.4 0.9 copy-start.18
  122.4 9.9 %copy-start.2 = (s16[2,3,592,128]{3,2,1,0:T(8,128)(2,1)}, s16[2,3,592,128]{3,2,1,0:T(8,128)(2,1)S(1)}, u32[]{:S(2)}) copy-start(s16[2,3,592,128]{3,2,1,0:T(8,128)(2,1)S(1)} %hold.4.refs_0_.refs_5_) | copy-start | bytes 2727940
  122.4 17.8 %collective-permute-start.14 = (s16[2,3,592,128]{3,2,1,0:T(8,128)(2,1)S(1)}, s16[2,3,592,128]{3,2,1,0:T(8,128)(2,1)S(1)}, u32[]{:S(2)}, u32[]{:S(2)}) collective-permute-start(s16[2,3,592,128]{3,2,1,0:T(8,128)(2,1)S(1)} %hold.4.refs_0_.refs_5_), channel_id=1, source_target_pairs={{8,12},{4,0},{9,13},{5,1},{10,14},{6,2},{11,15},{7,3},{24,28},{20,... | collective-permute-start | bytes 2727944 | tf_op jit(solution)/shard_map/ppermute | solution.py:750
  124.0 26.8 %collective-permute-start.16 = (s16[2,4,592,128]{3,2,1,0:T(8,128)(2,1)S(1)}, s16[2,4,592,128]{3,2,1,0:T(8,128)(2,1)S(1)}, u32[]{:S(2)}, u32[]{:S(2)}) collective-permute-start(s16[2,4,592,128]{3,2,1,0:T(8,128)(2,1)S(1)} %copy-done.20), channel_id=1, source_target_pairs={{0,4},{12,8},{1,5},{13,9},{2,6},{14,10},{3,7},{15,11},{16,20},{28,... | collective-permute-start | bytes 3637256 | tf_op jit(solution)/shard_map/ppermute | solution.py:781
  134.1 10.6 %copy-start.21 = (s32[16]{0:T(128)S(1)}, s32[16]{0:T(128)}, u32[]{:S(2)}) copy-start(s32[16]{0:T(128)} %param.17) | copy-start | bytes 196
  134.2 10.7 %copy-start.13 = (s32[16,1536]{1,0:T(8,128)S(1)}, s32[16,1536]{1,0:T(8,128)}, u32[]{:S(2)}) copy-start(s32[16,1536]{1,0:T(8,128)} %refs_14_.1) | copy-start | bytes 294916
  134.2 10.7 %copy-start.14 = (f32[8,32]{1,0:T(8,128)S(1)}, f32[8,32]{1,0:T(8,128)}, u32[]{:S(2)}) copy-start(f32[8,32]{1,0:T(8,128)} %get-tuple-element.56.refs_9_.refs_19_.refs_17_) | copy-start | bytes 3076
  134.2 10.7 %copy-start.15 = (f32[8,32]{1,0:T(8,128)S(1)}, f32[8,32]{1,0:T(8,128)}, u32[]{:S(2)}) copy-start(f32[8,32]{1,0:T(8,128)} %get-tuple-element.57.refs_8_.refs_18_.refs_16_) | copy-start | bytes 3076
  134.2 10.7 %copy-start.16 = (f32[512]{0:T(512)S(1)}, f32[512]{0:T(512)}, u32[]{:S(2)}) copy-start(f32[512]{0:T(512)} %param.13) | copy-start | bytes 6148
  140.1 4.7 %copy-start.8 = (s16[2,3,592,128]{3,2,1,0:T(8,128)(2,1)}, s16[2,3,592,128]{3,2,1,0:T(8,128)(2,1)S(1)}, u32[]{:S(2)}) copy-start(s16[2,3,592,128]{3,2,1,0:T(8,128)(2,1)S(1)} %collective-permute-done.14.refs_1_.refs_11_.refs_2_) | copy-start | bytes 2727940
  140.1 4.7 %copy-start.4 = (s16[2,3,592,128]{3,2,1,0:T(8,128)(2,1)}, s16[2,3,592,128]{3,2,1,0:T(8,128)(2,1)S(1)}, u32[]{:S(2)}) copy-start(s16[2,3,592,128]{3,2,1,0:T(8,128)(2,1)S(1)} %hold.5.refs_20_.refs_1_) | copy-start | bytes 2727940
  140.1 19.7 %collective-permute-start.15 = (s16[2,3,592,128]{3,2,1,0:T(8,128)(2,1)S(1)}, s16[2,3,592,128]{3,2,1,0:T(8,128)(2,1)S(1)}, u32[]{:S(2)}, u32[]{:S(2)}) collective-permute-start(s16[2,3,592,128]{3,2,1,0:T(8,128)(2,1)S(1)} %hold.5.refs_20_.refs_1_), channel_id=1, source_target_pairs={{8,12},{4,0},{9,13},{5,1},{10,14},{6,2},{11,15},{7,3},{24,28},{20,... | collective-permute-start | bytes 2727944 | tf_op jit(solution)/shard_map/ppermute | solution.py:750
  144.9 15.0 %copy-start.17 = (s32[4]{0:T(128)}, s32[4]{0:T(128)S(1)}, u32[]{:S(2)}) copy-start(s32[4]{0:T(128)S(1)} %dynamic_slice.9.slot) | copy-start | bytes 52
  150.8 1.1 copy-start.19
  159.8 3.2 %copy-start.11 = (s16[2,3,592,128]{3,2,1,0:T(8,128)(2,1)}, s16[2,3,592,128]{3,2,1,0:T(8,128)(2,1)S(1)}, u32[]{:S(2)}) copy-start(s16[2,3,592,128]{3,2,1,0:T(8,128)(2,1)S(1)} %collective-permute-done.15.refs_0_.refs_9_) | copy-start | bytes 2727940
  163.1 4.6 %copy-start.22 = (s32[16]{0:T(128)S(1)}, s32[16]{0:T(128)}, u32[]{:S(2)}) copy-start(s32[16]{0:T(128)} %param.19) | copy-start | bytes 196
  163.1 39.1 %all-to-all-start = ((bf16[4,576,384]{2,1,0:T(8,128)(2,1)}), bf16[4,576,384]{2,1,0:T(8,128)(2,1)}, u32[]{:S(2)}, u32[]{:S(2)}) async-start(bf16[4,576,384]{2,1,0:T(8,128)(2,1)} %pages.3.refs_18_.refs_8_), calls=%async_computation | async-start | bytes 3538944 | tf_op jit(solution)/shard_map/all_to_all | solution.py:830
  167.7 2.8 %collective-permute-start.17 = (bf16[3,64,512]{2,1,0:T(8,128)(2,1)S(1)}, bf16[3,64,512]{2,1,0:T(8,128)(2,1)S(1)}, u32[]{:S(2)}, u32[]{:S(2)}) collective-permute-start(bf16[3,64,512]{2,1,0:T(8,128)(2,1)S(1)} %get-tuple-element.42.refs_11_), channel_id=1, source_target_pairs={{12,0},{13,1},{14,2},{15,3},{28,16},{29,17},{30,18},{31,19}} | collective-permute-start | bytes 589832 | tf_op jit(solution)/shard_map/ppermute | solution.py:802
  168.4 2.1 collective-permute-start.18
  169.1 16.2 %collective-permute-start.19 = (bf16[3,64,512]{2,1,0:T(8,128)(2,1)S(1)}, bf16[3,64,512]{2,1,0:T(8,128)(2,1)S(1)}, u32[]{:S(2)}, u32[]{:S(2)}) collective-permute-start(bf16[3,64,512]{2,1,0:T(8,128)(2,1)S(1)} %get-tuple-element.45), channel_id=1, source_target_pairs={{12,8},{13,9},{14,10},{15,11},{28,24},{29,25},{30,26},{31,27}} | collective-permute-start | bytes 589832 | tf_op jit(solution)/shard_map/ppermute | solution.py:802
  187.2 2.7 %collective-permute-start.20 = (bf16[1,64,512]{2,1,0:T(8,128)(2,1)S(1)}, bf16[1,64,512]{2,1,0:T(8,128)(2,1)S(1)}, u32[]{:S(2)}, u32[]{:S(2)}) collective-permute-start(bf16[1,64,512]{2,1,0:T(8,128)(2,1)S(1)} %get-tuple-element.47), channel_id=1, source_target_pairs={{12,0},{13,1},{14,2},{15,3},{28,16},{29,17},{30,18},{31,19}} | collective-permute-start | bytes 196616 | tf_op jit(solution)/shard_map/ppermute | solution.py:802
  187.8 2.0 collective-permute-start.21
  188.5 6.2 %collective-permute-start.22 = (bf16[1,64,512]{2,1,0:T(8,128)(2,1)S(1)}, bf16[1,64,512]{2,1,0:T(8,128)(2,1)S(1)}, u32[]{:S(2)}, u32[]{:S(2)}) collective-permute-start(bf16[1,64,512]{2,1,0:T(8,128)(2,1)S(1)} %get-tuple-element.49), channel_id=1, source_target_pairs={{12,8},{13,9},{14,10},{15,11},{28,24},{29,25},{30,26},{31,27}} | collective-permute-start | bytes 196616 | tf_op jit(solution)/shard_map/ppermute | solution.py:802
  196.9 68.4 %copy-start.1 = (bf16[16,2,1536]{2,1,0:T(2,128)(2,1)S(1)}, bf16[16,2,1536]{2,1,0:T(2,128)(2,1)}, u32[]{:S(2)}) copy-start(bf16[16,2,1536]{2,1,0:T(2,128)(2,1)} %param.14) | copy-start | bytes 294916
  202.1 0.8 copy-start.12

commit v9 on v8

--- a/solution.py
+++ b/solution.py
@@ -673,27 +673,21 @@
     )(slot, attended, keep, *([kv_up] * step), *after)
 
 
-def emit_kernel(pages_ref, placed_ref, out_ref, same_ref, done):
-    copies = [
-        pltpu.make_async_copy(pages_ref.at[n], out_ref.at[n], done.at[n])
-        for n in range(pages_ref.shape[0])
-    ]
-    for copy in copies:
-        copy.start()
-    for copy in copies:
-        copy.wait()
+def emit_kernel(pages_ref, placed_ref, out_ref, same_ref):
+    out_ref[...] = pages_ref[...]
 
 
 def emit(pages, placed):
+    page = pl.BlockSpec((1, *pages.shape[1:]), lambda i: (i, 0, 0))
     return pl.pallas_call(
         emit_kernel,
-        in_specs=[ANY, ANY],
-        out_specs=[ANY, ANY],
+        grid=(pages.shape[0],),
+        in_specs=[page, ANY],
+        out_specs=[page, ANY],
         out_shape=[
             jax.ShapeDtypeStruct(pages.shape, pages.dtype),
             jax.ShapeDtypeStruct(placed.shape, placed.dtype),
         ],
-        scratch_shapes=[pltpu.SemaphoreType.DMA((pages.shape[0],))],
         input_output_aliases={1: 1},
         compiler_params=SOME,
         cost_estimate=COST,
@@ -825,8 +819,8 @@
     results[0], backs[0] = attend_to(early, done)
     base = [jnp.zeros((pd_count, WIDTH, SHARE), BF)] if pd_count > RP else []
     pages = pages_to(early, base, results[0][:1])
-    pages = pages_to(late, [pages], [])
-    results[1], backs[1] = attend_to(late, [pages, *backs[0]])
+    pages = pages_to(late, [pages], backs[0])
+    results[1], backs[1] = attend_to(late, [pages])
     cache = lax.all_to_all(pages, "pd", split_axis=0, concat_axis=0, tiled=True)
 
     attended = [

time: 268 us -> 210 us (0.78)
  Pallas kernels: 142 us -> 91.5 us
  waiting for transfers between devices: 50.7 us -> 42.1 us
    pallas_call x1, Pallas kernels: 54.7 us -> 3.66 us  [emit(): pl.pallas_call(emit_kernel, grid=(pages.shape[0],), in_specs=[page, ANY],...]
    ppermute x6, waiting for transfers between devices: 19.7 us -> 11.3 us  [attend_to(): return (result, [lax.ppermute(result[t], 'tp', [(3, t)]) for t in range(3)])]
    all_to_all x1, waiting for transfers between devices: 0.01 us -> 3.46 us  [local_line(): cache = lax.all_to_all(pages, 'pd', split_axis=0, concat_axis=0, tiled=True)]
  transfers between devices with their start and end apart: 24 -> 24, of which waited for: 11 -> 10; matrix products, arithmetic and copies ran while one was open for 2% -> 3% of each run, Pallas kernels for 30% -> 38%
where the time goes in v9:
time: 210 us; the launch traced here: 206 us
  Pallas kernels  91.5 us (44%)
  starting transfers between devices  53.8 us (26%)
  waiting for transfers between devices  42.1 us (20%)
  local copies, waits for them, and re-layouts  7.69 us (4%)
  blocking collectives  6.47 us (3%)
  other arithmetic  3.4 us (2%)
    pallas_call x4, Pallas kernels, project_far(): pl.pallas_call(project_far_kernel, grid_spec=pltpu.PrefetchScalarGridSpec...  22.6 us
    ppermute x4, starting transfers between devices, second_hop(): outer.append(lax.ppermute(block, 'tp', outward))  19.2 us
    pallas_call x8, Pallas kernels, add_on(): pl.pallas_call(functools.partial(add_kernel, -1 - len(carried)), grid_spe...  17.8 us
    pallas_call x1, Pallas kernels, queries(): pl.pallas_call(body, grid=(heads // step,), in_specs=[pl.BlockSpec((rows,...  13.8 us
    pallas_call x1, Pallas kernels, project_near(): pl.pallas_call(project_near_kernel, grid_spec=pltpu.PrefetchScalarGridSpe...  13.1 us
    ppermute x6, waiting for transfers between devices, attend_to(): return (result, [lax.ppermute(result[t], 'tp', [(3, t)]) for t in range(3)])  11.3 us
    ppermute x4, starting transfers between devices, first_hop(): crossed.append(lax.ppermute(block, 'tp', across))  9.68 us
    pallas_call x2, Pallas kernels, pages_of(): pl.pallas_call(functools.partial(page_kernel, requests), grid_spec=pltpu....  9.34 us
  transfers between devices with their start and end apart: 24, of which 10 were waited for; matrix products, arithmetic and copies ran while one was open for 3% of the time, Pallas kernels for 38%

profile of v9, /device:TPU:16, one launch (start us, length us, event | category | flops | bytes accessed | tf_op | source)
XLA Modules:
  0.0 206.2 jit_solution(7490241072912061771)
XLA Ops:
  0.7 5.6 %project_far.4 = (f32[2,3,576,128]{3,2,1,0:T(8,128)}, s16[2,3,592,128]{3,2,1,0:T(8,128)(2,1)}) custom-call(s32[1]{0:T(128)} %bitcast.rank, bf16[4,1536,1792]{2,1,0:T(8,128)(2,1)} %bitcast.22, bf16[576,1792]{1,0:T(8,128)(2,1)} %bitcast.27), custom_call_target="tpu_custom_call" | custom-call | flops 1024 | bytes 1024 | tf_op jit(solution)/shard_map/project_far/pallas_call | solution.py:269
  6.3 1.3 collective-permute-start
  7.6 5.7 %project_far.5 = (f32[2,3,576,128]{3,2,1,0:T(8,128)}, s16[2,3,592,128]{3,2,1,0:T(8,128)(2,1)}) custom-call(s32[1]{0:T(128)} %bitcast.rank, bf16[4,1536,1792]{2,1,0:T(8,128)(2,1)} %bitcast.23, bf16[576,1792]{1,0:T(8,128)(2,1)} %bitcast.28, f32[2,3,576,128]{3,2,1,0:T(8,128)} %get-tuple-element.27.refs_0_.own_ref), custom_call_target="tpu_custom_call" | custom-call | flops 1024 | bytes 1024 | tf_op jit(solution)/shard_map/project_far/pallas_call | solution.py:269
  13.2 1.3 collective-permute-start.2
  16.0 13.8 %queries.1 = (f32[32,8,576]{2,1,0:T(8,128)}, f32[4,8,576]{2,1,0:T(8,128)}) custom-call(bf16[8,1536]{1,0:T(8,128)(2,1)} %reshape.129.refs_0_, bf16[1536,6144]{1,0:T(8,128)(2,1)} %refs_1_.2, bf16[8,1792]{1,0:T(8,128)(2,1)} %refs_2_.2, bf16[576,1792]{1,0:T(8,128)(2,1)} %bitcast.29, bf16[512,8192]{1,0:T(8,128)(2,1)} %refs_7_.3, bf16[512,8192]{1,0:T(8,128)(2,1)} %refs_7_.3, ...), custom_call_target="tpu_custom_call" | custom-call | flops 1024 | bytes 1024 | tf_op jit(solution)/shard_map/queries/pallas_call | solution.py:502
  32.0 2.2 %add_on.8.refs_0_ = s16[2,3,592,128]{3,2,1,0:T(8,128)(2,1)S(1)} custom-call(s32[1]{0:T(128)} %bitcast.rank, f32[2,3,576,128]{3,2,1,0:T(8,128)} %get-tuple-element.27.refs_0_.own_ref, s16[2,3,592,128]{3,2,1,0:T(8,128)(2,1)} %collective-permute-done.got_ref, bf16[288,576]{1,0:T(8,128)(2,1)S(1)} %pad_maximum_fusion.refs_0_.refs_3_.refs_7_), custom_call_target="tpu_custom_call" | custom-call | flops 1024 | bytes 1024 | tf_op jit(solution)/shard_map/add_on/pallas_call | solution.py:358
  34.2 2.4 %collective-permute-start.1 = (s16[2,3,592,128]{3,2,1,0:T(8,128)(2,1)S(1)}, s16[2,3,592,128]{3,2,1,0:T(8,128)(2,1)}, u32[]{:S(2)}, u32[]{:S(2)}) collective-permute-start(s16[2,3,592,128]{3,2,1,0:T(8,128)(2,1)S(1)} %add_on.8.refs_0_), channel_id=1, source_target_pairs={{4,8},{8,4},{5,9},{9,5},{6,10},{10,6},{7,11},{11,7},{20,24},{24,20... | collective-permute-start | bytes 2727944 | tf_op jit(solution)/shard_map/ppermute | solution.py:736
  37.9 6.0 %collective-permute-start.5 = (bf16[288,576]{1,0:T(8,128)(2,1)S(1)}, bf16[288,576]{1,0:T(8,128)(2,1)S(1)}, u32[]{:S(2)}, u32[]{:S(2)}) collective-permute-start(bf16[288,576]{1,0:T(8,128)(2,1)S(1)} %pad_maximum_fusion.refs_0_.refs_3_.refs_7_), channel_id=1, source_target_pairs={{8,12},{9,13},{10,14},{11,15},{24,28},{25,29},{26,30},{27,31}} | collective-permute-start | bytes 995336 | tf_op jit(solution)/shard_map/ppermute | solution.py:761
  44.0 5.6 %project_far.6 = (f32[2,3,576,128]{3,2,1,0:T(8,128)}, s16[2,3,592,128]{3,2,1,0:T(8,128)(2,1)}) custom-call(s32[1]{0:T(128)} %bitcast.rank, bf16[4,1536,1792]{2,1,0:T(8,128)(2,1)} %bitcast.24, bf16[576,1792]{1,0:T(8,128)(2,1)} %bitcast.30, s16[2,3,592,128]{3,2,1,0:T(8,128)(2,1)} %copy-done.10), custom_call_target="tpu_custom_call" | custom-call | flops 1024 | bytes 1024 | tf_op jit(solution)/shard_map/project_far/pallas_call | solution.py:269
  49.8 1.3 collective-permute-start.8
  51.1 13.1 %project_near.1 = (f32[3,2,4,576,128]{4,3,2,1,0:T(8,128)}, s16[1,4,592,128]{3,2,1,0:T(8,128)(2,1)}, s16[2,4,592,128]{3,2,1,0:T(8,128)(2,1)}) custom-call(s32[1]{0:T(128)} %bitcast.rank, bf16[4,1536,1792]{2,1,0:T(8,128)(2,1)} %bitcast.25, bf16[576,1792]{1,0:T(8,128)(2,1)} %bitcast.31, f32[2,3,576,128]{3,2,1,0:T(8,128)} %get-tuple-element.32.refs_0_.own_ref), custom_call_target="tpu_custom_call" | custom-call | flops 1024 | bytes 1024 | tf_op jit(solution)/shard_map/project_near/pallas_call | solution.py:312
  64.2 2.7 %add_on.9.refs_0_ = s16[2,3,592,128]{3,2,1,0:T(8,128)(2,1)} custom-call(s32[1]{0:T(128)} %bitcast.rank, f32[2,3,576,128]{3,2,1,0:T(8,128)} %get-tuple-element.29.refs_10_.own_ref, s16[2,3,592,128]{3,2,1,0:T(8,128)(2,1)S(1)} %collective-permute-done.2.got_ref, f32[3,2,4,576,128]{4,3,2,1,0:T(8,128)} %get-tuple-element.33.refs_0_.own_ref.refs_8_), custom_call_target="tpu_custom_call" | custom-call | flops 1024 | bytes 1024 | tf_op jit(solution)/shard_map/add_on/pallas_call | solution.py:358
  66.9 3.5 %collective-permute-start.7 = (s16[2,3,592,128]{3,2,1,0:T(8,128)(2,1)}, s16[2,3,592,128]{3,2,1,0:T(8,128)(2,1)}, u32[]{:S(2)}, u32[]{:S(2)}) collective-permute-start(s16[2,3,592,128]{3,2,1,0:T(8,128)(2,1)} %add_on.9.refs_0_), channel_id=1, source_target_pairs={{4,8},{8,4},{5,9},{9,5},{6,10},{10,6},{7,11},{11,7},{20,24},{24,20... | collective-permute-start | bytes 2727944 | tf_op jit(solution)/shard_map/ppermute | solution.py:736
  70.4 2.2 %add_on.10.refs_0_.refs_3_ = s16[2,3,592,128]{3,2,1,0:T(8,128)(2,1)S(1)} custom-call(s32[1]{0:T(128)} %bitcast.rank, f32[3,2,4,576,128]{4,3,2,1,0:T(8,128)} %get-tuple-element.33.refs_0_.own_ref.refs_8_, s16[2,3,592,128]{3,2,1,0:T(8,128)(2,1)} %collective-permute-done.1.got_ref, s16[2,3,592,128]{3,2,1,0:T(8,128)(2,1)} %add_on.9.refs_0_, ...), custom_call_target="tpu_custom_call" | custom-call | flops 1024 | bytes 1024 | tf_op jit(solution)/shard_map/add_on/pallas_call | solution.py:358
  72.6 8.5 %collective-permute-start.9 = (s16[2,3,592,128]{3,2,1,0:T(8,128)(2,1)S(1)}, s16[2,3,592,128]{3,2,1,0:T(8,128)(2,1)}, u32[]{:S(2)}, u32[]{:S(2)}) collective-permute-start(s16[2,3,592,128]{3,2,1,0:T(8,128)(2,1)S(1)} %add_on.10.refs_0_.refs_3_), channel_id=1, source_target_pairs={{8,12},{4,0},{9,13},{5,1},{10,14},{6,2},{11,15},{7,3},{24,28},{20,... | collective-permute-start | bytes 2727944 | tf_op jit(solution)/shard_map/ppermute | solution.py:744
  81.1 5.6 %project_far.7 = (f32[2,3,576,128]{3,2,1,0:T(8,128)}, s16[2,3,592,128]{3,2,1,0:T(8,128)(2,1)}) custom-call(s32[1]{0:T(128)} %bitcast.rank, bf16[4,1536,1792]{2,1,0:T(8,128)(2,1)} %bitcast.26, bf16[576,1792]{1,0:T(8,128)(2,1)} %bitcast.32, s16[2,3,592,128]{3,2,1,0:T(8,128)(2,1)} %copy-done.8), custom_call_target="tpu_custom_call" | custom-call | flops 1024 | bytes 1024 | tf_op jit(solution)/shard_map/project_far/pallas_call | solution.py:269
  86.7 1.3 collective-permute-start.6
  88.0 2.8 %add_on.11 = (s16[2,3,592,128]{3,2,1,0:T(8,128)(2,1)}, s16[1,4,592,128]{3,2,1,0:T(8,128)(2,1)}) custom-call(s32[1]{0:T(128)} %bitcast.rank, f32[2,3,576,128]{3,2,1,0:T(8,128)} %get-tuple-element.32.refs_0_.own_ref, s16[2,3,592,128]{3,2,1,0:T(8,128)(2,1)} %collective-permute-done.8.got_ref, ...), custom_call_target="tpu_custom_call", output_to_operand_aliasing={{1}: (4, {})} | custom-call | flops 1024 | bytes 1024 | tf_op jit(solution)/shard_map/add_on/pallas_call | solution.py:358
  90.8 1.9 collective-permute-start.11
  93.5 2.0 add_on.12.refs_0_
  95.6 2.0 collective-permute-done.9.refs_1_.refs_9_.refs_0_
  97.5 4.5 %collective-permute-start.12 = (s16[2,3,592,128]{3,2,1,0:T(8,128)(2,1)S(1)}, s16[2,3,592,128]{3,2,1,0:T(8,128)(2,1)S(1)}, u32[]{:S(2)}, u32[]{:S(2)}) collective-permute-start(s16[2,3,592,128]{3,2,1,0:T(8,128)(2,1)S(1)} %hold.3.refs_0_.refs_4_), channel_id=1, source_target_pairs={{8,12},{4,0},{9,13},{5,1},{10,14},{6,2},{11,15},{7,3},{24,28},{20,... | collective-permute-start | bytes 2727944 | tf_op jit(solution)/shard_map/ppermute | solution.py:744
  102.1 1.3 collective-permute-start.13
  103.8 8.2 %collective-permute-done.6.got_ref = s16[2,3,592,128]{3,2,1,0:T(8,128)(2,1)} collective-permute-done((s16[2,3,592,128]{3,2,1,0:T(8,128)(2,1)}, s16[2,3,592,128]{3,2,1,0:T(8,128)(2,1)}, u32[]{:S(2)}, u32[]{:S(2)}) %collective-permute-start.6) | collective-permute-done | bytes 909344 | tf_op jit(solution)/shard_map/ppermute | solution.py:732
  112.0 2.0 add_on.13.refs_0_
  114.1 1.9 collective-permute-start.10
  116.0 2.1 add_on.14.refs_0_
  118.1 3.3 %collective-permute-done.13.refs_2_.refs_6_ = s16[1,4,592,128]{3,2,1,0:T(8,128)(2,1)S(1)} collective-permute-done((s16[1,4,592,128]{3,2,1,0:T(8,128)(2,1)}, s16[1,4,592,128]{3,2,1,0:T(8,128)(2,1)S(1)}, u32[]{:S(2)}, u32[]{:S(2)}) %collective-permute-start.13) | collective-permute-done | bytes 606240 | tf_op jit(solution)/shard_map/ppermute | solution.py:775
  122.4 1.6 collective-permute-start.14
  124.0 1.3 collective-permute-start.16
  125.3 7.0 %collective-permute-done.10.got_ref = s16[2,3,592,128]{3,2,1,0:T(8,128)(2,1)S(1)} collective-permute-done((s16[2,3,592,128]{3,2,1,0:T(8,128)(2,1)S(1)}, s16[2,3,592,128]{3,2,1,0:T(8,128)(2,1)S(1)}, u32[]{:S(2)}, u32[]{:S(2)}) %collective-permute-start.10) | collective-permute-done | bytes 909344 | tf_op jit(solution)/shard_map/ppermute | solution.py:736
  132.2 1.9 add_on.15.refs_0_
  134.2 5.9 %collective-permute-done.14.refs_1_.refs_11_.refs_2_ = s16[2,3,592,128]{3,2,1,0:T(8,128)(2,1)S(1)} collective-permute-done((s16[2,3,592,128]{3,2,1,0:T(8,128)(2,1)S(1)}, s16[2,3,592,128]{3,2,1,0:T(8,128)(2,1)S(1)}, u32[]{:S(2)}, u32[]{:S(2)}) %collective-permute-start.14) | collective-permute-done | bytes 909344 | tf_op jit(solution)/shard_map/ppermute | solution.py:744
  140.1 4.6 %collective-permute-start.15 = (s16[2,3,592,128]{3,2,1,0:T(8,128)(2,1)S(1)}, s16[2,3,592,128]{3,2,1,0:T(8,128)(2,1)S(1)}, u32[]{:S(2)}, u32[]{:S(2)}) collective-permute-start(s16[2,3,592,128]{3,2,1,0:T(8,128)(2,1)S(1)} %hold.5.refs_20_.refs_1_), channel_id=1, source_target_pairs={{8,12},{4,0},{9,13},{5,1},{10,14},{6,2},{11,15},{7,3},{24,28},{20,... | collective-permute-start | bytes 2727944 | tf_op jit(solution)/shard_map/ppermute | solution.py:744
  144.8 4.1 %attend.2 = (bf16[3,64,512]{2,1,0:T(8,128)(2,1)S(1)}, bf16[3,64,512]{2,1,0:T(8,128)(2,1)S(1)}, bf16[3,64,512]{2,1,0:T(8,128)(2,1)S(1)}, bf16[3,64,512]{2,1,0:T(8,128)(2,1)S(1)}) custom-call(s32[1]{0:T(128)} %bitcast.rank, s32[1]{0:T(128)} %bitcast.8.first_ref, bf16[288,576]{1,0:T(8,128)(2,1)S(1)} %collective-permute-done.3.refs_1_.refs_0_.refs_4_, ...), custom_call_target="tpu_custom_call" | custom-call | flops 1024 | bytes 1024 | tf_op jit(solution)/shard_map/attend/pallas_call | solution.py:610
  150.3 1.3 collective-permute-start.19
  152.7 6.0 %pages.2.refs_7_ = bf16[4,576,384]{2,1,0:T(8,128)(2,1)} custom-call(s32[1]{0:T(128)} %bitcast.rank, s32[4]{0:T(128)S(1)} %dynamic_slice.9.slot, f32[3,2,4,576,128]{4,3,2,1,0:T(8,128)} %get-tuple-element.33.refs_0_.own_ref.refs_8_, s16[2,3,592,128]{3,2,1,0:T(8,128)(2,1)} %collective-permute-done.9.refs_1_.refs_9_.refs_0_, s16[2,3,592,128]{3,2,1,0:T(8,128)(2,1)} %copy-done.18, ...), custom_call_target="tpu_custom_call" | custom-call | flops 1024 | bytes 1024 | tf_op jit(solution)/shard_map/pages/pallas_call | solution.py:437
  158.7 4.7 %collective-permute-done.19.refs_10_ = bf16[3,64,512]{2,1,0:T(8,128)(2,1)S(1)} collective-permute-done((bf16[3,64,512]{2,1,0:T(8,128)(2,1)S(1)}, bf16[3,64,512]{2,1,0:T(8,128)(2,1)S(1)}, u32[]{:S(2)}, u32[]{:S(2)}) %collective-permute-start.19) | collective-permute-done | bytes 196640 | tf_op jit(solution)/shard_map/ppermute | solution.py:796
  164.4 3.4 %pages.3.refs_18_.refs_8_ = bf16[4,576,384]{2,1,0:T(8,128)(2,1)} custom-call(s32[1]{0:T(128)} %bitcast.rank, s32[4]{0:T(128)S(1)} %dynamic_slice.9.slot, f32[3,2,4,576,128]{4,3,2,1,0:T(8,128)} %get-tuple-element.33.refs_0_.own_ref.refs_8_, s16[2,3,592,128]{3,2,1,0:T(8,128)(2,1)} %copy-done.20, ...), custom_call_target="tpu_custom_call", output_to_operand_aliasing={{}: (10, {})} | custom-call | flops 1024 | bytes 1024 | tf_op jit(solution)/shard_map/pages/pallas_call | solution.py:437
  167.8 4.6 %all-to-all-start = ((bf16[4,576,384]{2,1,0:T(8,128)(2,1)}), bf16[4,576,384]{2,1,0:T(8,128)(2,1)}, u32[]{:S(2)}, u32[]{:S(2)}) async-start(bf16[4,576,384]{2,1,0:T(8,128)(2,1)} %pages.3.refs_18_.refs_8_), calls=%async_computation | async-start | bytes 3538944 | tf_op jit(solution)/shard_map/all_to_all | solution.py:824
  172.6 1.8 attend.3
  175.7 1.3 collective-permute-start.22
  177.1 6.6 %collective-permute-done.22 = bf16[1,64,512]{2,1,0:T(8,128)(2,1)S(1)} collective-permute-done((bf16[1,64,512]{2,1,0:T(8,128)(2,1)S(1)}, bf16[1,64,512]{2,1,0:T(8,128)(2,1)S(1)}, u32[]{:S(2)}, u32[]{:S(2)}) %collective-permute-start.22) | collective-permute-done | bytes 65568 | tf_op jit(solution)/shard_map/ppermute | solution.py:796
  184.0 1.2 reshape.139.o_ref
  185.9 5.2 %heads_out.1.placed_ref = bf16[4,2,4096]{2,1,0:T(2,128)(2,1)} custom-call(s32[4]{0:T(128)} %copy-done.17, f32[32,8,512]{2,1,0:T(8,128)} %reshape.139.o_ref, f32[8,128]{1,0:T(8,128)} %broadcast_in_dim.2.keep_ref, bf16[512,8192]{1,0:T(8,128)(2,1)} %refs_7_.3, bf16[512,8192]{1,0:T(8,128)(2,1)} %refs_7_.3, bf16[512,8192]{1,0:T(8,128)(2,1)} %refs_7_.3, ...), custom_call_target="tpu_custom_call" | custom-call | flops 1024 | bytes 1024 | tf_op jit(solution)/shard_map/heads_out/pallas_call | solution.py:656
  191.1 3.5 %all-to-all-done.pages_ref = bf16[4,576,384]{2,1,0:T(8,128)(2,1)} async-done(((bf16[4,576,384]{2,1,0:T(8,128)(2,1)}), bf16[4,576,384]{2,1,0:T(8,128)(2,1)}, u32[]{:S(2)}, u32[]{:S(2)}) %all-to-all-start) | async-done | bytes 1769504 | tf_op jit(solution)/shard_map/all_to_all | solution.py:824
  195.4 3.7 %emit.1 = (bf16[4,576,384]{2,1,0:T(8,128)(2,1)}, bf16[4,2,4096]{2,1,0:T(2,128)(2,1)S(1)}) custom-call(bf16[4,576,384]{2,1,0:T(8,128)(2,1)} %all-to-all-done.pages_ref, bf16[4,2,4096]{2,1,0:T(2,128)(2,1)S(1)} %copy-done.12), custom_call_target="tpu_custom_call", output_to_operand_aliasing={{1}: (1, {})} | custom-call | flops 1024 | bytes 1024 | tf_op jit(solution)/shard_map/emit/pallas_call | solution.py:682
  199.1 6.5 %all_to_all.10 = bf16[4,2,4096]{2,1,0:T(2,128)(2,1)S(1)} all-to-all(bf16[4,2,4096]{2,1,0:T(2,128)(2,1)S(1)} %get-tuple-element.50), channel_id=1, replica_groups=mesh['groups'=2,'tp'=4,'pd'=4] {'pd'}, dimensions={0} | all-to-all | bytes 131072 | tf_op jit(solution)/shard_map/all_to_all | solution.py:843
  (97 shorter events, 14.9 us)
Async XLA Ops:
  0.6 13.9 %copy-start = (bf16[16,2,1536]{2,1,0:T(2,128)(2,1)S(1)}, bf16[16,2,1536]{2,1,0:T(2,128)(2,1)}, u32[]{:S(2)}) copy-start(bf16[16,2,1536]{2,1,0:T(2,128)(2,1)} %param.14) | copy-start | bytes 294916
  6.3 25.7 %collective-permute-start = (s16[2,3,592,128]{3,2,1,0:T(8,128)(2,1)}, s16[2,3,592,128]{3,2,1,0:T(8,128)(2,1)}, u32[]{:S(2)}, u32[]{:S(2)}) collective-permute-start(s16[2,3,592,128]{3,2,1,0:T(8,128)(2,1)} %get-tuple-element.28), channel_id=1, source_target_pairs={{0,4},{12,8},{1,5},{13,9},{2,6},{14,10},{3,7},{15,11},{16,20},{28,... | collective-permute-start | bytes 2727944 | tf_op jit(solution)/shard_map/ppermute | solution.py:732
  13.2 36.5 %collective-permute-start.2 = (s16[2,3,592,128]{3,2,1,0:T(8,128)(2,1)}, s16[2,3,592,128]{3,2,1,0:T(8,128)(2,1)S(1)}, u32[]{:S(2)}, u32[]{:S(2)}) collective-permute-start(s16[2,3,592,128]{3,2,1,0:T(8,128)(2,1)} %get-tuple-element.34), channel_id=1, source_target_pairs={{0,4},{12,8},{1,5},{13,9},{2,6},{14,10},{3,7},{15,11},{16,20},{28,... | collective-permute-start | bytes 2727944 | tf_op jit(solution)/shard_map/ppermute | solution.py:732
  32.0 6.0 %copy-start.5 = (bf16[288,576]{1,0:T(8,128)(2,1)}, bf16[288,576]{1,0:T(8,128)(2,1)S(1)}, u32[]{:S(2)}) copy-start(bf16[288,576]{1,0:T(8,128)(2,1)S(1)} %pad_maximum_fusion.refs_0_.refs_3_.refs_7_) | copy-start | bytes 995332
  34.2 9.8 %copy-start.10 = (s16[2,3,592,128]{3,2,1,0:T(8,128)(2,1)}, s16[2,3,592,128]{3,2,1,0:T(8,128)(2,1)S(1)}, u32[]{:S(2)}) copy-start(s16[2,3,592,128]{3,2,1,0:T(8,128)(2,1)S(1)} %add_on.8.refs_0_) | copy-start | bytes 2727940
  34.2 36.2 %collective-permute-start.1 = (s16[2,3,592,128]{3,2,1,0:T(8,128)(2,1)S(1)}, s16[2,3,592,128]{3,2,1,0:T(8,128)(2,1)}, u32[]{:S(2)}, u32[]{:S(2)}) collective-permute-start(s16[2,3,592,128]{3,2,1,0:T(8,128)(2,1)S(1)} %add_on.8.refs_0_), channel_id=1, source_target_pairs={{4,8},{8,4},{5,9},{9,5},{6,10},{10,6},{7,11},{11,7},{20,24},{24,20... | collective-permute-start | bytes 2727944 | tf_op jit(solution)/shard_map/ppermute | solution.py:736
  36.5 30.3 %collective-permute-start.3 = (bf16[288,576]{1,0:T(8,128)(2,1)S(1)}, bf16[288,576]{1,0:T(8,128)(2,1)S(1)}, u32[]{:S(2)}, u32[]{:S(2)}) collective-permute-start(bf16[288,576]{1,0:T(8,128)(2,1)S(1)} %pad_maximum_fusion.refs_0_.refs_3_.refs_7_), channel_id=1, source_target_pairs={{0,12},{1,13},{2,14},{3,15},{16,28},{17,29},{18,30},{19,31}} | collective-permute-start | bytes 995336 | tf_op jit(solution)/shard_map/ppermute | solution.py:761
  37.2 33.1 %collective-permute-start.4 = (bf16[288,576]{1,0:T(8,128)(2,1)S(1)}, bf16[288,576]{1,0:T(8,128)(2,1)S(1)}, u32[]{:S(2)}, u32[]{:S(2)}) collective-permute-start(bf16[288,576]{1,0:T(8,128)(2,1)S(1)} %pad_maximum_fusion.refs_0_.refs_3_.refs_7_), channel_id=1, source_target_pairs={{4,12},{5,13},{6,14},{7,15},{20,28},{21,29},{22,30},{23,31}} | collective-permute-start | bytes 995336 | tf_op jit(solution)/shard_map/ppermute | solution.py:761
  37.9 32.5 %collective-permute-start.5 = (bf16[288,576]{1,0:T(8,128)(2,1)S(1)}, bf16[288,576]{1,0:T(8,128)(2,1)S(1)}, u32[]{:S(2)}, u32[]{:S(2)}) collective-permute-start(bf16[288,576]{1,0:T(8,128)(2,1)S(1)} %pad_maximum_fusion.refs_0_.refs_3_.refs_7_), channel_id=1, source_target_pairs={{8,12},{9,13},{10,14},{11,15},{24,28},{25,29},{26,30},{27,31}} | collective-permute-start | bytes 995336 | tf_op jit(solution)/shard_map/ppermute | solution.py:761
  49.8 38.2 %collective-permute-start.8 = (s16[2,3,592,128]{3,2,1,0:T(8,128)(2,1)}, s16[2,3,592,128]{3,2,1,0:T(8,128)(2,1)}, u32[]{:S(2)}, u32[]{:S(2)}) collective-permute-start(s16[2,3,592,128]{3,2,1,0:T(8,128)(2,1)} %get-tuple-element.37), channel_id=1, source_target_pairs={{0,4},{12,8},{1,5},{13,9},{2,6},{14,10},{3,7},{15,11},{16,20},{28,... | collective-permute-start | bytes 2727944 | tf_op jit(solution)/shard_map/ppermute | solution.py:732
  66.9 26.7 %collective-permute-start.7 = (s16[2,3,592,128]{3,2,1,0:T(8,128)(2,1)}, s16[2,3,592,128]{3,2,1,0:T(8,128)(2,1)}, u32[]{:S(2)}, u32[]{:S(2)}) collective-permute-start(s16[2,3,592,128]{3,2,1,0:T(8,128)(2,1)} %add_on.9.refs_0_), channel_id=1, source_target_pairs={{4,8},{8,4},{5,9},{9,5},{6,10},{10,6},{7,11},{11,7},{20,24},{24,20... | collective-permute-start | bytes 2727944 | tf_op jit(solution)/shard_map/ppermute | solution.py:736
  70.4 2.2 %copy-start.6 = (bf16[288,576]{1,0:T(8,128)(2,1)}, bf16[288,576]{1,0:T(8,128)(2,1)S(1)}, u32[]{:S(2)}) copy-start(bf16[288,576]{1,0:T(8,128)(2,1)S(1)} %collective-permute-done.5.refs_3_.refs_2_.refs_6_) | copy-start | bytes 995332
  72.6 8.5 %copy-start.8 = (s16[2,3,592,128]{3,2,1,0:T(8,128)(2,1)}, s16[2,3,592,128]{3,2,1,0:T(8,128)(2,1)S(1)}, u32[]{:S(2)}) copy-start(s16[2,3,592,128]{3,2,1,0:T(8,128)(2,1)S(1)} %add_on.10.refs_0_.refs_3_) | copy-start | bytes 2727940
  72.6 24.9 %collective-permute-start.9 = (s16[2,3,592,128]{3,2,1,0:T(8,128)(2,1)S(1)}, s16[2,3,592,128]{3,2,1,0:T(8,128)(2,1)}, u32[]{:S(2)}, u32[]{:S(2)}) collective-permute-start(s16[2,3,592,128]{3,2,1,0:T(8,128)(2,1)S(1)} %add_on.10.refs_0_.refs_3_), channel_id=1, source_target_pairs={{8,12},{4,0},{9,13},{5,1},{10,14},{6,2},{11,15},{7,3},{24,28},{20,... | collective-permute-start | bytes 2727944 | tf_op jit(solution)/shard_map/ppermute | solution.py:744
  86.7 25.3 %collective-permute-start.6 = (s16[2,3,592,128]{3,2,1,0:T(8,128)(2,1)}, s16[2,3,592,128]{3,2,1,0:T(8,128)(2,1)}, u32[]{:S(2)}, u32[]{:S(2)}) collective-permute-start(s16[2,3,592,128]{3,2,1,0:T(8,128)(2,1)} %get-tuple-element.36), channel_id=1, source_target_pairs={{0,4},{12,8},{1,5},{13,9},{2,6},{14,10},{3,7},{15,11},{16,20},{28,... | collective-permute-start | bytes 2727944 | tf_op jit(solution)/shard_map/ppermute | solution.py:732
  90.8 25.2 %collective-permute-start.11 = (s16[2,3,592,128]{3,2,1,0:T(8,128)(2,1)}, s16[2,3,592,128]{3,2,1,0:T(8,128)(2,1)}, u32[]{:S(2)}, u32[]{:S(2)}) collective-permute-start(s16[2,3,592,128]{3,2,1,0:T(8,128)(2,1)} %get-tuple-element.39.refs_0_), channel_id=1, source_target_pairs={{4,8},{8,4},{5,9},{9,5},{6,10},{10,6},{7,11},{11,7},{20,24},{24,20... | collective-permute-start | bytes 2727944 | tf_op jit(solution)/shard_map/ppermute | solution.py:736
  97.5 14.5 %copy-start.3 = (s16[2,3,592,128]{3,2,1,0:T(8,128)(2,1)}, s16[2,3,592,128]{3,2,1,0:T(8,128)(2,1)S(1)}, u32[]{:S(2)}) copy-start(s16[2,3,592,128]{3,2,1,0:T(8,128)(2,1)S(1)} %hold.3.refs_0_.refs_4_) | copy-start | bytes 2727940
  97.5 23.9 %collective-permute-start.12 = (s16[2,3,592,128]{3,2,1,0:T(8,128)(2,1)S(1)}, s16[2,3,592,128]{3,2,1,0:T(8,128)(2,1)S(1)}, u32[]{:S(2)}, u32[]{:S(2)}) collective-permute-start(s16[2,3,592,128]{3,2,1,0:T(8,128)(2,1)S(1)} %hold.3.refs_0_.refs_4_), channel_id=1, source_target_pairs={{8,12},{4,0},{9,13},{5,1},{10,14},{6,2},{11,15},{7,3},{24,28},{20,... | collective-permute-start | bytes 2727944 | tf_op jit(solution)/shard_map/ppermute | solution.py:744
  102.1 19.3 %collective-permute-start.13 = (s16[1,4,592,128]{3,2,1,0:T(8,128)(2,1)}, s16[1,4,592,128]{3,2,1,0:T(8,128)(2,1)S(1)}, u32[]{:S(2)}, u32[]{:S(2)}) collective-permute-start(s16[1,4,592,128]{3,2,1,0:T(8,128)(2,1)} %get-tuple-element.40), channel_id=1, source_target_pairs={{0,4},{12,8},{1,5},{13,9},{2,6},{14,10},{3,7},{15,11},{16,20},{28,... | collective-permute-start | bytes 1818632 | tf_op jit(solution)/shard_map/ppermute | solution.py:775
  114.1 2.0 copy-start.11
  114.1 18.1 %collective-permute-start.10 = (s16[2,3,592,128]{3,2,1,0:T(8,128)(2,1)S(1)}, s16[2,3,592,128]{3,2,1,0:T(8,128)(2,1)S(1)}, u32[]{:S(2)}, u32[]{:S(2)}) collective-permute-start(s16[2,3,592,128]{3,2,1,0:T(8,128)(2,1)S(1)} %add_on.13.refs_0_), channel_id=1, source_target_pairs={{4,8},{8,4},{5,9},{9,5},{6,10},{10,6},{7,11},{11,7},{20,24},{24,20... | collective-permute-start | bytes 2727944 | tf_op jit(solution)/shard_map/ppermute | solution.py:736
  118.1 5.9 %copy-start.21 = (s16[2,4,592,128]{3,2,1,0:T(8,128)(2,1)S(1)}, s16[2,4,592,128]{3,2,1,0:T(8,128)(2,1)}, u32[]{:S(2)}) copy-start(s16[2,4,592,128]{3,2,1,0:T(8,128)(2,1)} %get-tuple-element.41) | copy-start | bytes 3637252
  121.4 0.9 copy-start.18
  122.4 9.9 %copy-start.2 = (s16[2,3,592,128]{3,2,1,0:T(8,128)(2,1)}, s16[2,3,592,128]{3,2,1,0:T(8,128)(2,1)S(1)}, u32[]{:S(2)}) copy-start(s16[2,3,592,128]{3,2,1,0:T(8,128)(2,1)S(1)} %hold.4.refs_0_.refs_5_) | copy-start | bytes 2727940
  122.4 17.8 %collective-permute-start.14 = (s16[2,3,592,128]{3,2,1,0:T(8,128)(2,1)S(1)}, s16[2,3,592,128]{3,2,1,0:T(8,128)(2,1)S(1)}, u32[]{:S(2)}, u32[]{:S(2)}) collective-permute-start(s16[2,3,592,128]{3,2,1,0:T(8,128)(2,1)S(1)} %hold.4.refs_0_.refs_5_), channel_id=1, source_target_pairs={{8,12},{4,0},{9,13},{5,1},{10,14},{6,2},{11,15},{7,3},{24,28},{20,... | collective-permute-start | bytes 2727944 | tf_op jit(solution)/shard_map/ppermute | solution.py:744
  124.0 27.7 %collective-permute-start.16 = (s16[2,4,592,128]{3,2,1,0:T(8,128)(2,1)S(1)}, s16[2,4,592,128]{3,2,1,0:T(8,128)(2,1)S(1)}, u32[]{:S(2)}, u32[]{:S(2)}) collective-permute-start(s16[2,4,592,128]{3,2,1,0:T(8,128)(2,1)S(1)} %copy-done.21), channel_id=1, source_target_pairs={{0,4},{12,8},{1,5},{13,9},{2,6},{14,10},{3,7},{15,11},{16,20},{28,... | collective-permute-start | bytes 3637256 | tf_op jit(solution)/shard_map/ppermute | solution.py:775
  134.1 10.6 %copy-start.13 = (s32[16,1536]{1,0:T(8,128)S(1)}, s32[16,1536]{1,0:T(8,128)}, u32[]{:S(2)}) copy-start(s32[16,1536]{1,0:T(8,128)} %refs_14_.1) | copy-start | bytes 294916
  134.1 10.6 %copy-start.14 = (f32[8,32]{1,0:T(8,128)S(1)}, f32[8,32]{1,0:T(8,128)}, u32[]{:S(2)}) copy-start(f32[8,32]{1,0:T(8,128)} %get-tuple-element.56.refs_9_.refs_19_.refs_17_) | copy-start | bytes 3076
  134.2 10.6 %copy-start.15 = (f32[8,32]{1,0:T(8,128)S(1)}, f32[8,32]{1,0:T(8,128)}, u32[]{:S(2)}) copy-start(f32[8,32]{1,0:T(8,128)} %get-tuple-element.57.refs_8_.refs_18_.refs_16_) | copy-start | bytes 3076
  134.2 10.6 %copy-start.16 = (f32[512]{0:T(512)S(1)}, f32[512]{0:T(512)}, u32[]{:S(2)}) copy-start(f32[512]{0:T(512)} %param.13) | copy-start | bytes 6148
  140.1 4.6 %copy-start.9 = (s16[2,3,592,128]{3,2,1,0:T(8,128)(2,1)}, s16[2,3,592,128]{3,2,1,0:T(8,128)(2,1)S(1)}, u32[]{:S(2)}) copy-start(s16[2,3,592,128]{3,2,1,0:T(8,128)(2,1)S(1)} %collective-permute-done.14.refs_1_.refs_11_.refs_2_) | copy-start | bytes 2727940
  140.1 4.6 %copy-start.4 = (s16[2,3,592,128]{3,2,1,0:T(8,128)(2,1)}, s16[2,3,592,128]{3,2,1,0:T(8,128)(2,1)S(1)}, u32[]{:S(2)}) copy-start(s16[2,3,592,128]{3,2,1,0:T(8,128)(2,1)S(1)} %hold.5.refs_20_.refs_1_) | copy-start | bytes 2727940
  140.1 23.3 %collective-permute-start.15 = (s16[2,3,592,128]{3,2,1,0:T(8,128)(2,1)S(1)}, s16[2,3,592,128]{3,2,1,0:T(8,128)(2,1)S(1)}, u32[]{:S(2)}, u32[]{:S(2)}) collective-permute-start(s16[2,3,592,128]{3,2,1,0:T(8,128)(2,1)S(1)} %hold.5.refs_20_.refs_1_), channel_id=1, source_target_pairs={{8,12},{4,0},{9,13},{5,1},{10,14},{6,2},{11,15},{7,3},{24,28},{20,... | collective-permute-start | bytes 2727944 | tf_op jit(solution)/shard_map/ppermute | solution.py:744
  144.8 6.8 %copy-start.22 = (s32[16]{0:T(128)S(1)}, s32[16]{0:T(128)}, u32[]{:S(2)}) copy-start(s32[16]{0:T(128)} %param.17) | copy-start | bytes 196
  148.9 9.8 %collective-permute-start.17 = (bf16[3,64,512]{2,1,0:T(8,128)(2,1)S(1)}, bf16[3,64,512]{2,1,0:T(8,128)(2,1)S(1)}, u32[]{:S(2)}, u32[]{:S(2)}) collective-permute-start(bf16[3,64,512]{2,1,0:T(8,128)(2,1)S(1)} %get-tuple-element.42.refs_11_), channel_id=1, source_target_pairs={{12,0},{13,1},{14,2},{15,3},{28,16},{29,17},{30,18},{31,19}} | collective-permute-start | bytes 589832 | tf_op jit(solution)/shard_map/ppermute | solution.py:796
  149.6 9.2 %collective-permute-start.18 = (bf16[3,64,512]{2,1,0:T(8,128)(2,1)S(1)}, bf16[3,64,512]{2,1,0:T(8,128)(2,1)S(1)}, u32[]{:S(2)}, u32[]{:S(2)}) collective-permute-start(bf16[3,64,512]{2,1,0:T(8,128)(2,1)S(1)} %get-tuple-element.43), channel_id=1, source_target_pairs={{12,4},{13,5},{14,6},{15,7},{28,20},{29,21},{30,22},{31,23}} | collective-permute-start | bytes 589832 | tf_op jit(solution)/shard_map/ppermute | solution.py:796
  150.3 13.2 %collective-permute-start.19 = (bf16[3,64,512]{2,1,0:T(8,128)(2,1)S(1)}, bf16[3,64,512]{2,1,0:T(8,128)(2,1)S(1)}, u32[]{:S(2)}, u32[]{:S(2)}) collective-permute-start(bf16[3,64,512]{2,1,0:T(8,128)(2,1)S(1)} %get-tuple-element.44), channel_id=1, source_target_pairs={{12,8},{13,9},{14,10},{15,11},{28,24},{29,25},{30,26},{31,27}} | collective-permute-start | bytes 589832 | tf_op jit(solution)/shard_map/ppermute | solution.py:796
  151.6 11.8 %copy-start.17 = (s32[4]{0:T(128)}, s32[4]{0:T(128)S(1)}, u32[]{:S(2)}) copy-start(s32[4]{0:T(128)S(1)} %dynamic_slice.9.slot) | copy-start | bytes 52
  151.7 1.1 copy-start.19
  163.4 1.0 copy-start.20
  167.8 4.6 %copy-start.23 = (s32[16]{0:T(128)S(1)}, s32[16]{0:T(128)}, u32[]{:S(2)}) copy-start(s32[16]{0:T(128)} %param.19) | copy-start | bytes 196
  167.8 4.8 %copy-start.7 = (bf16[288,576]{1,0:T(8,128)(2,1)S(1)}, bf16[288,576]{1,0:T(8,128)(2,1)}, u32[]{:S(2)}) copy-start(bf16[288,576]{1,0:T(8,128)(2,1)} %copy-done.6) | copy-start | bytes 995332
  167.8 26.8 %all-to-all-start = ((bf16[4,576,384]{2,1,0:T(8,128)(2,1)}), bf16[4,576,384]{2,1,0:T(8,128)(2,1)}, u32[]{:S(2)}, u32[]{:S(2)}) async-start(bf16[4,576,384]{2,1,0:T(8,128)(2,1)} %pages.3.refs_18_.refs_8_), calls=%async_computation | async-start | bytes 3538944 | tf_op jit(solution)/shard_map/all_to_all | solution.py:824
  174.4 2.7 %collective-permute-start.20 = (bf16[1,64,512]{2,1,0:T(8,128)(2,1)S(1)}, bf16[1,64,512]{2,1,0:T(8,128)(2,1)S(1)}, u32[]{:S(2)}, u32[]{:S(2)}) collective-permute-start(bf16[1,64,512]{2,1,0:T(8,128)(2,1)S(1)} %get-tuple-element.47), channel_id=1, source_target_pairs={{12,0},{13,1},{14,2},{15,3},{28,16},{29,17},{30,18},{31,19}} | collective-permute-start | bytes 196616 | tf_op jit(solution)/shard_map/ppermute | solution.py:796
  175.0 2.0 collective-permute-start.21
  175.7 8.0 %collective-permute-start.22 = (bf16[1,64,512]{2,1,0:T(8,128)(2,1)S(1)}, bf16[1,64,512]{2,1,0:T(8,128)(2,1)S(1)}, u32[]{:S(2)}, u32[]{:S(2)}) collective-permute-start(bf16[1,64,512]{2,1,0:T(8,128)(2,1)S(1)} %get-tuple-element.49), channel_id=1, source_target_pairs={{12,8},{13,9},{14,10},{15,11},{28,24},{29,25},{30,26},{31,27}} | collective-permute-start | bytes 196616 | tf_op jit(solution)/shard_map/ppermute | solution.py:796
  185.9 20.3 %copy-start.1 = (bf16[16,2,1536]{2,1,0:T(2,128)(2,1)S(1)}, bf16[16,2,1536]{2,1,0:T(2,128)(2,1)}, u32[]{:S(2)}) copy-start(bf16[16,2,1536]{2,1,0:T(2,128)(2,1)} %param.14) | copy-start | bytes 294916
  194.6 0.8 copy-start.12

commit v10 on v9

--- a/solution.py
+++ b/solution.py
@@ -673,21 +673,22 @@
     )(slot, attended, keep, *([kv_up] * step), *after)
 
 
-def emit_kernel(pages_ref, placed_ref, out_ref, same_ref):
-    out_ref[...] = pages_ref[...]
+def emit_kernel(pages_ref, placed_ref, out_ref, same_ref, done):
+    copy = pltpu.make_async_copy(pages_ref, out_ref, done)
+    copy.start()
+    copy.wait()
 
 
 def emit(pages, placed):
-    page = pl.BlockSpec((1, *pages.shape[1:]), lambda i: (i, 0, 0))
     return pl.pallas_call(
         emit_kernel,
-        grid=(pages.shape[0],),
-        in_specs=[page, ANY],
-        out_specs=[page, ANY],
+        in_specs=[VMEM, ANY],
+        out_specs=[ANY, ANY],
         out_shape=[
             jax.ShapeDtypeStruct(pages.shape, pages.dtype),
             jax.ShapeDtypeStruct(placed.shape, placed.dtype),
         ],
+        scratch_shapes=[pltpu.SemaphoreType.DMA],
         input_output_aliases={1: 1},
         compiler_params=SOME,
         cost_estimate=COST,
@@ -764,7 +765,7 @@
     send_far(2, done)
     near_sums, *side = project_near(rank, hidden, down_t, far_sums[2:])
     done = first_hop(1, [near_sums])
-    done = second_hop(0, [*done, *messages[:3]])
+    done = second_hop(0, done, messages[:3])
     send_far(3, done)
     steps = jnp.arange(SHARE, dtype=jnp.int32).reshape(UNITS, UNIT)
     tables = [

time: 210 us -> 206 us (0.981)
  the two profiles are of different devices: /device:TPU:16 before, /device:TPU:0 now
where the time goes in v10:
time: 206 us; the launch traced here: 204 us
  Pallas kernels  87.2 us (42%)
  starting transfers between devices  52 us (25%)
  waiting for transfers between devices  42.8 us (21%)
  local copies, waits for them, and re-layouts  11.4 us (6%)
  blocking collectives  6.49 us (3%)
  other arithmetic  3.4 us (2%)
    pallas_call x4, Pallas kernels, project_far(): pl.pallas_call(project_far_kernel, grid_spec=pltpu.PrefetchScalarGridSpec...  24.3 us
    ppermute x4, waiting for transfers between devices, second_hop(): outer.append(lax.ppermute(block, 'tp', outward))  19.9 us
    ppermute x4, starting transfers between devices, send_far(): inner.append(lax.ppermute(codes, 'tp', inward))  16.3 us
    pallas_call x1, Pallas kernels, queries(): pl.pallas_call(body, grid=(heads // step,), in_specs=[pl.BlockSpec((rows,...  13.8 us
    pallas_call x8, Pallas kernels, add_on(): pl.pallas_call(functools.partial(add_kernel, -1 - len(carried)), grid_spe...  13.8 us
    pallas_call x1, Pallas kernels, project_near(): pl.pallas_call(project_near_kernel, grid_spec=pltpu.PrefetchScalarGridSpe...  13.8 us
    ppermute x2, starting transfers between devices, local_line(): side = [lax.ppermute(codes, 'tp', inward) for codes in side]  10.2 us
    ppermute x6, waiting for transfers between devices, attend_to(): return (result, [lax.ppermute(result[t], 'tp', [(3, t)]) for t in range(3)])  9.98 us
  transfers between devices with their start and end apart: 24, of which 9 were waited for; matrix products, arithmetic and copies ran while one was open for 3% of the time, Pallas kernels for 38%

profile of v10, /device:TPU:0, one launch (start us, length us, event | category | flops | bytes accessed | tf_op | source)
XLA Modules:
  0.0 204.4 jit_solution(1179247503468009492)
XLA Ops:
  0.7 6.1 %project_far.4 = (f32[2,3,576,128]{3,2,1,0:T(8,128)}, s16[2,3,592,128]{3,2,1,0:T(8,128)(2,1)}) custom-call(s32[1]{0:T(128)} %bitcast.rank, bf16[4,1536,1792]{2,1,0:T(8,128)(2,1)} %bitcast.22, bf16[576,1792]{1,0:T(8,128)(2,1)} %bitcast.27), custom_call_target="tpu_custom_call" | custom-call | flops 1024 | bytes 1024 | tf_op jit(solution)/shard_map/project_far/pallas_call | solution.py:269
  6.7 4.5 %collective-permute-start = (s16[2,3,592,128]{3,2,1,0:T(8,128)(2,1)}, s16[2,3,592,128]{3,2,1,0:T(8,128)(2,1)S(1)}, u32[]{:S(2)}, u32[]{:S(2)}) collective-permute-start(s16[2,3,592,128]{3,2,1,0:T(8,128)(2,1)} %get-tuple-element.28), channel_id=1, source_target_pairs={{0,4},{12,8},{1,5},{13,9},{2,6},{14,10},{3,7},{15,11},{16,20},{28,... | collective-permute-start | bytes 2727944 | tf_op jit(solution)/shard_map/ppermute | solution.py:733
  11.3 6.1 %project_far.5 = (f32[2,3,576,128]{3,2,1,0:T(8,128)}, s16[2,3,592,128]{3,2,1,0:T(8,128)(2,1)}) custom-call(s32[1]{0:T(128)} %bitcast.rank, bf16[4,1536,1792]{2,1,0:T(8,128)(2,1)} %bitcast.23, bf16[576,1792]{1,0:T(8,128)(2,1)} %bitcast.28, f32[2,3,576,128]{3,2,1,0:T(8,128)} %get-tuple-element.27.refs_0_.own_ref), custom_call_target="tpu_custom_call" | custom-call | flops 1024 | bytes 1024 | tf_op jit(solution)/shard_map/project_far/pallas_call | solution.py:269
  17.4 1.3 collective-permute-start.2
  20.2 13.8 %queries.1 = (f32[32,8,576]{2,1,0:T(8,128)}, f32[4,8,576]{2,1,0:T(8,128)}) custom-call(bf16[8,1536]{1,0:T(8,128)(2,1)} %reshape.129.refs_0_, bf16[1536,6144]{1,0:T(8,128)(2,1)} %refs_1_.2, bf16[8,1792]{1,0:T(8,128)(2,1)} %refs_2_.2, bf16[576,1792]{1,0:T(8,128)(2,1)} %bitcast.29, bf16[512,8192]{1,0:T(8,128)(2,1)} %refs_7_.3, bf16[512,8192]{1,0:T(8,128)(2,1)} %refs_7_.3, ...), custom_call_target="tpu_custom_call" | custom-call | flops 1024 | bytes 1024 | tf_op jit(solution)/shard_map/queries/pallas_call | solution.py:502
  37.2 1.7 add_on.8.refs_0_
  38.9 1.6 collective-permute-start.1
  40.4 4.4 %collective-permute-start.3 = (bf16[288,576]{1,0:T(8,128)(2,1)S(1)}, bf16[288,576]{1,0:T(8,128)(2,1)S(1)}, u32[]{:S(2)}, u32[]{:S(2)}) collective-permute-start(bf16[288,576]{1,0:T(8,128)(2,1)S(1)} %pad_maximum_fusion.refs_0_.refs_3_.refs_7_), channel_id=1, source_target_pairs={{0,12},{1,13},{2,14},{3,15},{16,28},{17,29},{18,30},{19,31}} | collective-permute-start | bytes 995336 | tf_op jit(solution)/shard_map/ppermute | solution.py:762
  46.2 6.1 %project_far.6 = (f32[2,3,576,128]{3,2,1,0:T(8,128)}, s16[2,3,592,128]{3,2,1,0:T(8,128)(2,1)}) custom-call(s32[1]{0:T(128)} %bitcast.rank, bf16[4,1536,1792]{2,1,0:T(8,128)(2,1)} %bitcast.24, bf16[576,1792]{1,0:T(8,128)(2,1)} %bitcast.30, s16[2,3,592,128]{3,2,1,0:T(8,128)(2,1)} %copy-done.10), custom_call_target="tpu_custom_call" | custom-call | flops 1024 | bytes 1024 | tf_op jit(solution)/shard_map/project_far/pallas_call | solution.py:269
  52.3 4.5 %collective-permute-start.8 = (s16[2,3,592,128]{3,2,1,0:T(8,128)(2,1)}, s16[2,3,592,128]{3,2,1,0:T(8,128)(2,1)}, u32[]{:S(2)}, u32[]{:S(2)}) collective-permute-start(s16[2,3,592,128]{3,2,1,0:T(8,128)(2,1)} %get-tuple-element.37), channel_id=1, source_target_pairs={{0,4},{12,8},{1,5},{13,9},{2,6},{14,10},{3,7},{15,11},{16,20},{28,... | collective-permute-start | bytes 2727944 | tf_op jit(solution)/shard_map/ppermute | solution.py:733
  56.8 13.8 %project_near.1 = (f32[3,2,4,576,128]{4,3,2,1,0:T(8,128)}, s16[1,4,592,128]{3,2,1,0:T(8,128)(2,1)}, s16[2,4,592,128]{3,2,1,0:T(8,128)(2,1)}) custom-call(s32[1]{0:T(128)} %bitcast.rank, bf16[4,1536,1792]{2,1,0:T(8,128)(2,1)} %bitcast.25, bf16[576,1792]{1,0:T(8,128)(2,1)} %bitcast.31, f32[2,3,576,128]{3,2,1,0:T(8,128)} %get-tuple-element.32.refs_0_.own_ref), custom_call_target="tpu_custom_call" | custom-call | flops 1024 | bytes 1024 | tf_op jit(solution)/shard_map/project_near/pallas_call | solution.py:312
  70.6 1.2 copy-done.14
  71.8 1.4 add_on.9.refs_0_
  73.2 1.6 collective-permute-start.7
  74.8 1.7 add_on.10.refs_0_
  76.5 1.3 collective-permute-start.9
  77.9 6.1 %project_far.7 = (f32[2,3,576,128]{3,2,1,0:T(8,128)}, s16[2,3,592,128]{3,2,1,0:T(8,128)(2,1)}) custom-call(s32[1]{0:T(128)} %bitcast.rank, bf16[4,1536,1792]{2,1,0:T(8,128)(2,1)} %bitcast.26, bf16[576,1792]{1,0:T(8,128)(2,1)} %bitcast.32, s16[2,3,592,128]{3,2,1,0:T(8,128)(2,1)} %copy-done.2), custom_call_target="tpu_custom_call" | custom-call | flops 1024 | bytes 1024 | tf_op jit(solution)/shard_map/project_far/pallas_call | solution.py:269
  84.0 5.9 %collective-permute-start.6 = (s16[2,3,592,128]{3,2,1,0:T(8,128)(2,1)}, s16[2,3,592,128]{3,2,1,0:T(8,128)(2,1)}, u32[]{:S(2)}, u32[]{:S(2)}) collective-permute-start(s16[2,3,592,128]{3,2,1,0:T(8,128)(2,1)} %get-tuple-element.36), channel_id=1, source_target_pairs={{0,4},{12,8},{1,5},{13,9},{2,6},{14,10},{3,7},{15,11},{16,20},{28,... | collective-permute-start | bytes 2727944 | tf_op jit(solution)/shard_map/ppermute | solution.py:733
  89.9 2.5 %add_on.11 = (s16[2,3,592,128]{3,2,1,0:T(8,128)(2,1)}, s16[1,4,592,128]{3,2,1,0:T(8,128)(2,1)}) custom-call(s32[1]{0:T(128)} %bitcast.rank, f32[2,3,576,128]{3,2,1,0:T(8,128)} %get-tuple-element.32.refs_0_.own_ref, s16[2,3,592,128]{3,2,1,0:T(8,128)(2,1)} %collective-permute-done.8.got_ref, ...), custom_call_target="tpu_custom_call", output_to_operand_aliasing={{1}: (4, {})} | custom-call | flops 1024 | bytes 1024 | tf_op jit(solution)/shard_map/add_on/pallas_call | solution.py:358
  92.4 1.6 collective-permute-start.11
  94.0 1.7 add_on.12.refs_0_
  95.7 3.0 %collective-permute-done.9.refs_1_.refs_9_.refs_0_ = s16[2,3,592,128]{3,2,1,0:T(8,128)(2,1)} collective-permute-done((s16[2,3,592,128]{3,2,1,0:T(8,128)(2,1)S(1)}, s16[2,3,592,128]{3,2,1,0:T(8,128)(2,1)}, u32[]{:S(2)}, u32[]{:S(2)}) %collective-permute-start.9) | collective-permute-done | bytes 909344 | tf_op jit(solution)/shard_map/ppermute | solution.py:745
  98.7 1.3 collective-permute-start.12
  100.0 5.5 %collective-permute-start.13 = (s16[1,4,592,128]{3,2,1,0:T(8,128)(2,1)}, s16[1,4,592,128]{3,2,1,0:T(8,128)(2,1)S(1)}, u32[]{:S(2)}, u32[]{:S(2)}) collective-permute-start(s16[1,4,592,128]{3,2,1,0:T(8,128)(2,1)} %get-tuple-element.40), channel_id=1, source_target_pairs={{0,4},{12,8},{1,5},{13,9},{2,6},{14,10},{3,7},{15,11},{16,20},{28,... | collective-permute-start | bytes 1818632 | tf_op jit(solution)/shard_map/ppermute | solution.py:776
  106.0 4.0 %collective-permute-done.6.got_ref = s16[2,3,592,128]{3,2,1,0:T(8,128)(2,1)} collective-permute-done((s16[2,3,592,128]{3,2,1,0:T(8,128)(2,1)}, s16[2,3,592,128]{3,2,1,0:T(8,128)(2,1)}, u32[]{:S(2)}, u32[]{:S(2)}) %collective-permute-start.6) | collective-permute-done | bytes 909344 | tf_op jit(solution)/shard_map/ppermute | solution.py:733
  109.9 1.7 add_on.13.refs_0_
  112.5 1.7 add_on.14.refs_0_
  114.2 5.4 %collective-permute-done.13.refs_2_.refs_6_ = s16[1,4,592,128]{3,2,1,0:T(8,128)(2,1)S(1)} collective-permute-done((s16[1,4,592,128]{3,2,1,0:T(8,128)(2,1)}, s16[1,4,592,128]{3,2,1,0:T(8,128)(2,1)S(1)}, u32[]{:S(2)}, u32[]{:S(2)}) %collective-permute-start.13) | collective-permute-done | bytes 606240 | tf_op jit(solution)/shard_map/ppermute | solution.py:776
  119.9 1.3 collective-permute-start.14
  121.2 4.7 %collective-permute-start.16 = (s16[2,4,592,128]{3,2,1,0:T(8,128)(2,1)S(1)}, s16[2,4,592,128]{3,2,1,0:T(8,128)(2,1)S(1)}, u32[]{:S(2)}, u32[]{:S(2)}) collective-permute-start(s16[2,4,592,128]{3,2,1,0:T(8,128)(2,1)S(1)} %copy-done.29), channel_id=1, source_target_pairs={{0,4},{12,8},{1,5},{13,9},{2,6},{14,10},{3,7},{15,11},{16,20},{28,... | collective-permute-start | bytes 3637256 | tf_op jit(solution)/shard_map/ppermute | solution.py:776
  125.9 1.5 add_on.15.refs_0_
  127.4 13.1 %collective-permute-done.14.refs_1_.refs_11_.refs_2_ = s16[2,3,592,128]{3,2,1,0:T(8,128)(2,1)S(1)} collective-permute-done((s16[2,3,592,128]{3,2,1,0:T(8,128)(2,1)S(1)}, s16[2,3,592,128]{3,2,1,0:T(8,128)(2,1)S(1)}, u32[]{:S(2)}, u32[]{:S(2)}) %collective-permute-start.14) | collective-permute-done | bytes 909344 | tf_op jit(solution)/shard_map/ppermute | solution.py:745
  140.5 1.5 collective-permute-start.15
  142.1 4.1 %attend.2 = (bf16[3,64,512]{2,1,0:T(8,128)(2,1)S(1)}, bf16[3,64,512]{2,1,0:T(8,128)(2,1)S(1)}, bf16[3,64,512]{2,1,0:T(8,128)(2,1)S(1)}, bf16[3,64,512]{2,1,0:T(8,128)(2,1)S(1)}) custom-call(s32[1]{0:T(128)} %bitcast.rank, s32[1]{0:T(128)} %bitcast.8.first_ref, bf16[288,576]{1,0:T(8,128)(2,1)S(1)} %collective-permute-done.3.refs_1_.refs_0_.refs_4_, ...), custom_call_target="tpu_custom_call" | custom-call | flops 1024 | bytes 1024 | tf_op jit(solution)/shard_map/attend/pallas_call | solution.py:610
  146.9 1.3 collective-permute-start.17
  150.7 5.8 %pages.2.refs_7_ = bf16[4,576,384]{2,1,0:T(8,128)(2,1)} custom-call(s32[1]{0:T(128)} %bitcast.rank, s32[4]{0:T(128)S(1)} %dynamic_slice.9.slot, f32[3,2,4,576,128]{4,3,2,1,0:T(8,128)} %get-tuple-element.33.refs_0_.own_ref.refs_8_, s16[2,3,592,128]{3,2,1,0:T(8,128)(2,1)} %collective-permute-done.9.refs_1_.refs_9_.refs_0_, ...), custom_call_target="tpu_custom_call" | custom-call | flops 1024 | bytes 1024 | tf_op jit(solution)/shard_map/pages/pallas_call | solution.py:437
  156.5 4.4 %collective-permute-done.17.refs_8_ = bf16[3,64,512]{2,1,0:T(8,128)(2,1)S(1)} collective-permute-done((bf16[3,64,512]{2,1,0:T(8,128)(2,1)S(1)}, bf16[3,64,512]{2,1,0:T(8,128)(2,1)S(1)}, u32[]{:S(2)}, u32[]{:S(2)}) %collective-permute-start.17) | collective-permute-done | bytes 196640 | tf_op jit(solution)/shard_map/ppermute | solution.py:797
  160.9 3.5 %collective-permute-done.15.refs_0_.refs_9_ = s16[2,3,592,128]{3,2,1,0:T(8,128)(2,1)S(1)} collective-permute-done((s16[2,3,592,128]{3,2,1,0:T(8,128)(2,1)S(1)}, s16[2,3,592,128]{3,2,1,0:T(8,128)(2,1)S(1)}, u32[]{:S(2)}, u32[]{:S(2)}) %collective-permute-start.15) | collective-permute-done | bytes 909344 | tf_op jit(solution)/shard_map/ppermute | solution.py:745
  165.4 3.3 %pages.3.refs_18_.refs_8_ = bf16[4,576,384]{2,1,0:T(8,128)(2,1)} custom-call(s32[1]{0:T(128)} %bitcast.rank, s32[4]{0:T(128)S(1)} %dynamic_slice.9.slot, f32[3,2,4,576,128]{4,3,2,1,0:T(8,128)} %get-tuple-element.33.refs_0_.own_ref.refs_8_, s16[2,3,592,128]{3,2,1,0:T(8,128)(2,1)} %copy-done.27, ...), custom_call_target="tpu_custom_call", output_to_operand_aliasing={{}: (10, {})} | custom-call | flops 1024 | bytes 1024 | tf_op jit(solution)/shard_map/pages/pallas_call | solution.py:437
  169.3 3.7 %all-to-all-start = ((bf16[4,576,384]{2,1,0:T(8,128)(2,1)}), bf16[4,576,384]{2,1,0:T(8,128)(2,1)S(1)}, u32[]{:S(2)}, u32[]{:S(2)}) async-start(bf16[4,576,384]{2,1,0:T(8,128)(2,1)} %pages.3.refs_18_.refs_8_), calls=%async_computation | async-start | bytes 3538944 | tf_op jit(solution)/shard_map/all_to_all | solution.py:825
  174.2 1.8 attend.3
  176.0 1.3 collective-permute-start.20
  178.7 5.6 %collective-permute-done.20 = bf16[1,64,512]{2,1,0:T(8,128)(2,1)S(1)} collective-permute-done((bf16[1,64,512]{2,1,0:T(8,128)(2,1)S(1)}, bf16[1,64,512]{2,1,0:T(8,128)(2,1)S(1)}, u32[]{:S(2)}, u32[]{:S(2)}) %collective-permute-start.20) | collective-permute-done | bytes 65568 | tf_op jit(solution)/shard_map/ppermute | solution.py:797
  184.6 1.2 reshape.139.o_ref
  186.5 5.2 %heads_out.1.placed_ref = bf16[4,2,4096]{2,1,0:T(2,128)(2,1)} custom-call(s32[4]{0:T(128)} %copy-done.25, f32[32,8,512]{2,1,0:T(8,128)} %reshape.139.o_ref, f32[8,128]{1,0:T(8,128)} %broadcast_in_dim.2.keep_ref, bf16[512,8192]{1,0:T(8,128)(2,1)} %refs_7_.3, bf16[512,8192]{1,0:T(8,128)(2,1)} %refs_7_.3, bf16[512,8192]{1,0:T(8,128)(2,1)} %refs_7_.3, ...), custom_call_target="tpu_custom_call" | custom-call | flops 1024 | bytes 1024 | tf_op jit(solution)/shard_map/heads_out/pallas_call | solution.py:656
  191.7 3.5 %all-to-all-done.pages_ref = bf16[4,576,384]{2,1,0:T(8,128)(2,1)S(1)} async-done(((bf16[4,576,384]{2,1,0:T(8,128)(2,1)}), bf16[4,576,384]{2,1,0:T(8,128)(2,1)S(1)}, u32[]{:S(2)}, u32[]{:S(2)}) %all-to-all-start) | async-done | bytes 1769504 | tf_op jit(solution)/shard_map/all_to_all | solution.py:825
  196.0 1.2 emit.1
  197.3 6.5 %all_to_all.10 = bf16[4,2,4096]{2,1,0:T(2,128)(2,1)S(1)} all-to-all(bf16[4,2,4096]{2,1,0:T(2,128)(2,1)S(1)} %get-tuple-element.50), channel_id=1, replica_groups=mesh['groups'=2,'tp'=4,'pd'=4] {'pd'}, dimensions={0} | all-to-all | bytes 131072 | tf_op jit(solution)/shard_map/all_to_all | solution.py:844
  (114 shorter events, 17.5 us)
Async XLA Ops:
  0.6 18.1 %copy-start = (bf16[16,2,1536]{2,1,0:T(2,128)(2,1)S(1)}, bf16[16,2,1536]{2,1,0:T(2,128)(2,1)}, u32[]{:S(2)}) copy-start(bf16[16,2,1536]{2,1,0:T(2,128)(2,1)} %param.14) | copy-start | bytes 294916
  6.7 29.4 %collective-permute-start = (s16[2,3,592,128]{3,2,1,0:T(8,128)(2,1)}, s16[2,3,592,128]{3,2,1,0:T(8,128)(2,1)S(1)}, u32[]{:S(2)}, u32[]{:S(2)}) collective-permute-start(s16[2,3,592,128]{3,2,1,0:T(8,128)(2,1)} %get-tuple-element.28), channel_id=1, source_target_pairs={{0,4},{12,8},{1,5},{13,9},{2,6},{14,10},{3,7},{15,11},{16,20},{28,... | collective-permute-start | bytes 2727944 | tf_op jit(solution)/shard_map/ppermute | solution.py:733
  17.4 34.9 %collective-permute-start.2 = (s16[2,3,592,128]{3,2,1,0:T(8,128)(2,1)}, s16[2,3,592,128]{3,2,1,0:T(8,128)(2,1)S(1)}, u32[]{:S(2)}, u32[]{:S(2)}) collective-permute-start(s16[2,3,592,128]{3,2,1,0:T(8,128)(2,1)} %get-tuple-element.34), channel_id=1, source_target_pairs={{0,4},{12,8},{1,5},{13,9},{2,6},{14,10},{3,7},{15,11},{16,20},{28,... | collective-permute-start | bytes 2727944 | tf_op jit(solution)/shard_map/ppermute | solution.py:733
  36.1 9.4 %copy-start.6 = (bf16[288,576]{1,0:T(8,128)(2,1)}, bf16[288,576]{1,0:T(8,128)(2,1)S(1)}, u32[]{:S(2)}) copy-start(bf16[288,576]{1,0:T(8,128)(2,1)S(1)} %pad_maximum_fusion.refs_0_.refs_3_.refs_7_) | copy-start | bytes 995332
  38.9 7.4 %copy-start.10 = (s16[2,3,592,128]{3,2,1,0:T(8,128)(2,1)}, s16[2,3,592,128]{3,2,1,0:T(8,128)(2,1)S(1)}, u32[]{:S(2)}) copy-start(s16[2,3,592,128]{3,2,1,0:T(8,128)(2,1)S(1)} %add_on.8.refs_0_) | copy-start | bytes 2727940
  38.9 34.3 %collective-permute-start.1 = (s16[2,3,592,128]{3,2,1,0:T(8,128)(2,1)S(1)}, s16[2,3,592,128]{3,2,1,0:T(8,128)(2,1)}, u32[]{:S(2)}, u32[]{:S(2)}) collective-permute-start(s16[2,3,592,128]{3,2,1,0:T(8,128)(2,1)S(1)} %add_on.8.refs_0_), channel_id=1, source_target_pairs={{4,8},{8,4},{5,9},{9,5},{6,10},{10,6},{7,11},{11,7},{20,24},{24,20... | collective-permute-start | bytes 2727944 | tf_op jit(solution)/shard_map/ppermute | solution.py:737
  40.4 36.1 %collective-permute-start.3 = (bf16[288,576]{1,0:T(8,128)(2,1)S(1)}, bf16[288,576]{1,0:T(8,128)(2,1)S(1)}, u32[]{:S(2)}, u32[]{:S(2)}) collective-permute-start(bf16[288,576]{1,0:T(8,128)(2,1)S(1)} %pad_maximum_fusion.refs_0_.refs_3_.refs_7_), channel_id=1, source_target_pairs={{0,12},{1,13},{2,14},{3,15},{16,28},{17,29},{18,30},{19,31}} | collective-permute-start | bytes 995336 | tf_op jit(solution)/shard_map/ppermute | solution.py:762
  44.8 31.7 %collective-permute-start.4 = (bf16[288,576]{1,0:T(8,128)(2,1)S(1)}, bf16[288,576]{1,0:T(8,128)(2,1)S(1)}, u32[]{:S(2)}, u32[]{:S(2)}) collective-permute-start(bf16[288,576]{1,0:T(8,128)(2,1)S(1)} %pad_maximum_fusion.refs_0_.refs_3_.refs_7_), channel_id=1, source_target_pairs={{4,12},{5,13},{6,14},{7,15},{20,28},{21,29},{22,30},{23,31}} | collective-permute-start | bytes 995336 | tf_op jit(solution)/shard_map/ppermute | solution.py:762
  45.5 31.0 %collective-permute-start.5 = (bf16[288,576]{1,0:T(8,128)(2,1)S(1)}, bf16[288,576]{1,0:T(8,128)(2,1)S(1)}, u32[]{:S(2)}, u32[]{:S(2)}) collective-permute-start(bf16[288,576]{1,0:T(8,128)(2,1)S(1)} %pad_maximum_fusion.refs_0_.refs_3_.refs_7_), channel_id=1, source_target_pairs={{8,12},{9,13},{10,14},{11,15},{24,28},{25,29},{26,30},{27,31}} | collective-permute-start | bytes 995336 | tf_op jit(solution)/shard_map/ppermute | solution.py:762
  52.3 18.3 %copy-start.13 = (s16[2,3,592,128]{3,2,1,0:T(8,128)(2,1)}, s16[2,3,592,128]{3,2,1,0:T(8,128)(2,1)S(1)}, u32[]{:S(2)}) copy-start(s16[2,3,592,128]{3,2,1,0:T(8,128)(2,1)S(1)} %collective-permute-done.2.got_ref) | copy-start | bytes 2727940
  52.3 37.6 %collective-permute-start.8 = (s16[2,3,592,128]{3,2,1,0:T(8,128)(2,1)}, s16[2,3,592,128]{3,2,1,0:T(8,128)(2,1)}, u32[]{:S(2)}, u32[]{:S(2)}) collective-permute-start(s16[2,3,592,128]{3,2,1,0:T(8,128)(2,1)} %get-tuple-element.37), channel_id=1, source_target_pairs={{0,4},{12,8},{1,5},{13,9},{2,6},{14,10},{3,7},{15,11},{16,20},{28,... | collective-permute-start | bytes 2727944 | tf_op jit(solution)/shard_map/ppermute | solution.py:733
  70.6 1.2 copy-start.14
  73.2 1.6 copy-start.12
  73.2 20.8 %collective-permute-start.7 = (s16[2,3,592,128]{3,2,1,0:T(8,128)(2,1)S(1)}, s16[2,3,592,128]{3,2,1,0:T(8,128)(2,1)}, u32[]{:S(2)}, u32[]{:S(2)}) collective-permute-start(s16[2,3,592,128]{3,2,1,0:T(8,128)(2,1)S(1)} %add_on.9.refs_0_), channel_id=1, source_target_pairs={{4,8},{8,4},{5,9},{9,5},{6,10},{10,6},{7,11},{11,7},{20,24},{24,20... | collective-permute-start | bytes 2727944 | tf_op jit(solution)/shard_map/ppermute | solution.py:737
  76.5 7.5 %copy-start.7 = (bf16[288,576]{1,0:T(8,128)(2,1)}, bf16[288,576]{1,0:T(8,128)(2,1)S(1)}, u32[]{:S(2)}) copy-start(bf16[288,576]{1,0:T(8,128)(2,1)S(1)} %collective-permute-done.5.refs_3_.refs_2_.refs_6_) | copy-start | bytes 995332
  76.5 1.3 copy-start.2
  76.5 22.2 %collective-permute-start.9 = (s16[2,3,592,128]{3,2,1,0:T(8,128)(2,1)S(1)}, s16[2,3,592,128]{3,2,1,0:T(8,128)(2,1)}, u32[]{:S(2)}, u32[]{:S(2)}) collective-permute-start(s16[2,3,592,128]{3,2,1,0:T(8,128)(2,1)S(1)} %hold.4.refs_0_.refs_3_), channel_id=1, source_target_pairs={{8,12},{4,0},{9,13},{5,1},{10,14},{6,2},{11,15},{7,3},{24,28},{20,... | collective-permute-start | bytes 2727944 | tf_op jit(solution)/shard_map/ppermute | solution.py:745
  84.0 25.9 %collective-permute-start.6 = (s16[2,3,592,128]{3,2,1,0:T(8,128)(2,1)}, s16[2,3,592,128]{3,2,1,0:T(8,128)(2,1)}, u32[]{:S(2)}, u32[]{:S(2)}) collective-permute-start(s16[2,3,592,128]{3,2,1,0:T(8,128)(2,1)} %get-tuple-element.36), channel_id=1, source_target_pairs={{0,4},{12,8},{1,5},{13,9},{2,6},{14,10},{3,7},{15,11},{16,20},{28,... | collective-permute-start | bytes 2727944 | tf_op jit(solution)/shard_map/ppermute | solution.py:733
  92.4 19.9 %collective-permute-start.11 = (s16[2,3,592,128]{3,2,1,0:T(8,128)(2,1)}, s16[2,3,592,128]{3,2,1,0:T(8,128)(2,1)}, u32[]{:S(2)}, u32[]{:S(2)}) collective-permute-start(s16[2,3,592,128]{3,2,1,0:T(8,128)(2,1)} %get-tuple-element.39.refs_0_), channel_id=1, source_target_pairs={{4,8},{8,4},{5,9},{9,5},{6,10},{10,6},{7,11},{11,7},{20,24},{24,20... | collective-permute-start | bytes 2727944 | tf_op jit(solution)/shard_map/ppermute | solution.py:737
  98.7 11.2 %copy-start.4 = (s16[2,3,592,128]{3,2,1,0:T(8,128)(2,1)}, s16[2,3,592,128]{3,2,1,0:T(8,128)(2,1)S(1)}, u32[]{:S(2)}) copy-start(s16[2,3,592,128]{3,2,1,0:T(8,128)(2,1)S(1)} %hold.5.refs_0_.refs_4_) | copy-start | bytes 2727940
  98.7 21.2 %collective-permute-start.12 = (s16[2,3,592,128]{3,2,1,0:T(8,128)(2,1)S(1)}, s16[2,3,592,128]{3,2,1,0:T(8,128)(2,1)}, u32[]{:S(2)}, u32[]{:S(2)}) collective-permute-start(s16[2,3,592,128]{3,2,1,0:T(8,128)(2,1)S(1)} %hold.5.refs_0_.refs_4_), channel_id=1, source_target_pairs={{8,12},{4,0},{9,13},{5,1},{10,14},{6,2},{11,15},{7,3},{24,28},{20,... | collective-permute-start | bytes 2727944 | tf_op jit(solution)/shard_map/ppermute | solution.py:745
  100.0 19.7 %collective-permute-start.13 = (s16[1,4,592,128]{3,2,1,0:T(8,128)(2,1)}, s16[1,4,592,128]{3,2,1,0:T(8,128)(2,1)S(1)}, u32[]{:S(2)}, u32[]{:S(2)}) collective-permute-start(s16[1,4,592,128]{3,2,1,0:T(8,128)(2,1)} %get-tuple-element.40), channel_id=1, source_target_pairs={{0,4},{12,8},{1,5},{13,9},{2,6},{14,10},{3,7},{15,11},{16,20},{28,... | collective-permute-start | bytes 1818632 | tf_op jit(solution)/shard_map/ppermute | solution.py:776
  111.6 14.3 %collective-permute-start.10 = (s16[2,3,592,128]{3,2,1,0:T(8,128)(2,1)S(1)}, s16[2,3,592,128]{3,2,1,0:T(8,128)(2,1)S(1)}, u32[]{:S(2)}, u32[]{:S(2)}) collective-permute-start(s16[2,3,592,128]{3,2,1,0:T(8,128)(2,1)S(1)} %add_on.13.refs_0_), channel_id=1, source_target_pairs={{4,8},{8,4},{5,9},{9,5},{6,10},{10,6},{7,11},{11,7},{20,24},{24,20... | collective-permute-start | bytes 2727944 | tf_op jit(solution)/shard_map/ppermute | solution.py:737
  114.2 7.0 %copy-start.29 = (s16[2,4,592,128]{3,2,1,0:T(8,128)(2,1)S(1)}, s16[2,4,592,128]{3,2,1,0:T(8,128)(2,1)}, u32[]{:S(2)}) copy-start(s16[2,4,592,128]{3,2,1,0:T(8,128)(2,1)} %get-tuple-element.41) | copy-start | bytes 3637252
  119.9 6.0 %copy-start.3 = (s16[2,3,592,128]{3,2,1,0:T(8,128)(2,1)}, s16[2,3,592,128]{3,2,1,0:T(8,128)(2,1)S(1)}, u32[]{:S(2)}) copy-start(s16[2,3,592,128]{3,2,1,0:T(8,128)(2,1)S(1)} %hold.6.refs_0_.refs_5_) | copy-start | bytes 2727940
  119.9 20.6 %collective-permute-start.14 = (s16[2,3,592,128]{3,2,1,0:T(8,128)(2,1)S(1)}, s16[2,3,592,128]{3,2,1,0:T(8,128)(2,1)S(1)}, u32[]{:S(2)}, u32[]{:S(2)}) collective-permute-start(s16[2,3,592,128]{3,2,1,0:T(8,128)(2,1)S(1)} %hold.6.refs_0_.refs_5_), channel_id=1, source_target_pairs={{8,12},{4,0},{9,13},{5,1},{10,14},{6,2},{11,15},{7,3},{24,28},{20,... | collective-permute-start | bytes 2727944 | tf_op jit(solution)/shard_map/ppermute | solution.py:745
  121.2 28.4 %collective-permute-start.16 = (s16[2,4,592,128]{3,2,1,0:T(8,128)(2,1)S(1)}, s16[2,4,592,128]{3,2,1,0:T(8,128)(2,1)S(1)}, u32[]{:S(2)}, u32[]{:S(2)}) collective-permute-start(s16[2,4,592,128]{3,2,1,0:T(8,128)(2,1)S(1)} %copy-done.29), channel_id=1, source_target_pairs={{0,4},{12,8},{1,5},{13,9},{2,6},{14,10},{3,7},{15,11},{16,20},{28,... | collective-permute-start | bytes 3637256 | tf_op jit(solution)/shard_map/ppermute | solution.py:776
  127.4 14.6 %copy-start.18 = (s32[16,1536]{1,0:T(8,128)S(1)}, s32[16,1536]{1,0:T(8,128)}, u32[]{:S(2)}) copy-start(s32[16,1536]{1,0:T(8,128)} %refs_14_.1) | copy-start | bytes 294916
  127.4 14.6 %copy-start.22 = (f32[8,32]{1,0:T(8,128)S(1)}, f32[8,32]{1,0:T(8,128)}, u32[]{:S(2)}) copy-start(f32[8,32]{1,0:T(8,128)} %get-tuple-element.56.refs_9_.refs_19_.refs_17_) | copy-start | bytes 3076
  127.4 14.7 %copy-start.23 = (f32[8,32]{1,0:T(8,128)S(1)}, f32[8,32]{1,0:T(8,128)}, u32[]{:S(2)}) copy-start(f32[8,32]{1,0:T(8,128)} %get-tuple-element.57.refs_8_.refs_18_.refs_16_) | copy-start | bytes 3076
  127.4 14.7 %copy-start.24 = (f32[512]{0:T(512)S(1)}, f32[512]{0:T(512)}, u32[]{:S(2)}) copy-start(f32[512]{0:T(512)} %param.13) | copy-start | bytes 6148
  140.5 1.5 copy-start.9
  140.5 1.5 copy-start.5
  140.5 23.9 %collective-permute-start.15 = (s16[2,3,592,128]{3,2,1,0:T(8,128)(2,1)S(1)}, s16[2,3,592,128]{3,2,1,0:T(8,128)(2,1)S(1)}, u32[]{:S(2)}, u32[]{:S(2)}) collective-permute-start(s16[2,3,592,128]{3,2,1,0:T(8,128)(2,1)S(1)} %hold.7.refs_20_.refs_1_), channel_id=1, source_target_pairs={{8,12},{4,0},{9,13},{5,1},{10,14},{6,2},{11,15},{7,3},{24,28},{20,... | collective-permute-start | bytes 2727944 | tf_op jit(solution)/shard_map/ppermute | solution.py:745
  142.1 7.4 %copy-start.30 = (s32[16]{0:T(128)S(1)}, s32[16]{0:T(128)}, u32[]{:S(2)}) copy-start(s32[16]{0:T(128)} %param.17) | copy-start | bytes 196
  146.9 14.1 %collective-permute-start.17 = (bf16[3,64,512]{2,1,0:T(8,128)(2,1)S(1)}, bf16[3,64,512]{2,1,0:T(8,128)(2,1)S(1)}, u32[]{:S(2)}, u32[]{:S(2)}) collective-permute-start(bf16[3,64,512]{2,1,0:T(8,128)(2,1)S(1)} %get-tuple-element.42.refs_11_), channel_id=1, source_target_pairs={{12,0},{13,1},{14,2},{15,3},{28,16},{29,17},{30,18},{31,19}} | collective-permute-start | bytes 589832 | tf_op jit(solution)/shard_map/ppermute | solution.py:797
  148.1 12.8 %collective-permute-start.18 = (bf16[3,64,512]{2,1,0:T(8,128)(2,1)S(1)}, bf16[3,64,512]{2,1,0:T(8,128)(2,1)S(1)}, u32[]{:S(2)}, u32[]{:S(2)}) collective-permute-start(bf16[3,64,512]{2,1,0:T(8,128)(2,1)S(1)} %get-tuple-element.43), channel_id=1, source_target_pairs={{12,4},{13,5},{14,6},{15,7},{28,20},{29,21},{30,22},{31,23}} | collective-permute-start | bytes 589832 | tf_op jit(solution)/shard_map/ppermute | solution.py:797
  148.8 12.1 %collective-permute-start.19 = (bf16[3,64,512]{2,1,0:T(8,128)(2,1)S(1)}, bf16[3,64,512]{2,1,0:T(8,128)(2,1)S(1)}, u32[]{:S(2)}, u32[]{:S(2)}) collective-permute-start(bf16[3,64,512]{2,1,0:T(8,128)(2,1)S(1)} %get-tuple-element.44), channel_id=1, source_target_pairs={{12,8},{13,9},{14,10},{15,11},{28,24},{29,25},{30,26},{31,27}} | collective-permute-start | bytes 589832 | tf_op jit(solution)/shard_map/ppermute | solution.py:797
  149.6 14.8 %copy-start.25 = (s32[4]{0:T(128)}, s32[4]{0:T(128)S(1)}, u32[]{:S(2)}) copy-start(s32[4]{0:T(128)S(1)} %dynamic_slice.9.slot) | copy-start | bytes 52
  169.3 3.7 %copy-start.31 = (s32[16]{0:T(128)S(1)}, s32[16]{0:T(128)}, u32[]{:S(2)}) copy-start(s32[16]{0:T(128)} %param.19) | copy-start | bytes 196
  169.3 4.0 %copy-start.8 = (bf16[288,576]{1,0:T(8,128)(2,1)S(1)}, bf16[288,576]{1,0:T(8,128)(2,1)}, u32[]{:S(2)}) copy-start(bf16[288,576]{1,0:T(8,128)(2,1)} %copy-done.7) | copy-start | bytes 995332
  169.3 25.9 %all-to-all-start = ((bf16[4,576,384]{2,1,0:T(8,128)(2,1)}), bf16[4,576,384]{2,1,0:T(8,128)(2,1)S(1)}, u32[]{:S(2)}, u32[]{:S(2)}) async-start(bf16[4,576,384]{2,1,0:T(8,128)(2,1)} %pages.3.refs_18_.refs_8_), calls=%async_computation | async-start | bytes 3538944 | tf_op jit(solution)/shard_map/all_to_all | solution.py:825
  174.2 4.5 %copy-start.16 = (bf16[3,64,512]{2,1,0:T(8,128)(2,1)S(1)}, bf16[3,64,512]{2,1,0:T(8,128)(2,1)}, u32[]{:S(2)}) copy-start(bf16[3,64,512]{2,1,0:T(8,128)(2,1)} %copy-done.15) | copy-start | bytes 589828
  174.2 4.5 %copy-start.21 = (bf16[3,64,512]{2,1,0:T(8,128)(2,1)S(1)}, bf16[3,64,512]{2,1,0:T(8,128)(2,1)}, u32[]{:S(2)}) copy-start(bf16[3,64,512]{2,1,0:T(8,128)(2,1)} %copy-done.20) | copy-start | bytes 589828
  176.0 8.3 %collective-permute-start.20 = (bf16[1,64,512]{2,1,0:T(8,128)(2,1)S(1)}, bf16[1,64,512]{2,1,0:T(8,128)(2,1)S(1)}, u32[]{:S(2)}, u32[]{:S(2)}) collective-permute-start(bf16[1,64,512]{2,1,0:T(8,128)(2,1)S(1)} %get-tuple-element.47), channel_id=1, source_target_pairs={{12,0},{13,1},{14,2},{15,3},{28,16},{29,17},{30,18},{31,19}} | collective-permute-start | bytes 196616 | tf_op jit(solution)/shard_map/ppermute | solution.py:797
  177.3 7.0 %collective-permute-start.21 = (bf16[1,64,512]{2,1,0:T(8,128)(2,1)S(1)}, bf16[1,64,512]{2,1,0:T(8,128)(2,1)S(1)}, u32[]{:S(2)}, u32[]{:S(2)}) collective-permute-start(bf16[1,64,512]{2,1,0:T(8,128)(2,1)S(1)} %get-tuple-element.48), channel_id=1, source_target_pairs={{12,4},{13,5},{14,6},{15,7},{28,20},{29,21},{30,22},{31,23}} | collective-permute-start | bytes 196616 | tf_op jit(solution)/shard_map/ppermute | solution.py:797
  178.0 6.3 %collective-permute-start.22 = (bf16[1,64,512]{2,1,0:T(8,128)(2,1)S(1)}, bf16[1,64,512]{2,1,0:T(8,128)(2,1)S(1)}, u32[]{:S(2)}, u32[]{:S(2)}) collective-permute-start(bf16[1,64,512]{2,1,0:T(8,128)(2,1)S(1)} %get-tuple-element.49), channel_id=1, source_target_pairs={{12,8},{13,9},{14,10},{15,11},{28,24},{29,25},{30,26},{31,27}} | collective-permute-start | bytes 196616 | tf_op jit(solution)/shard_map/ppermute | solution.py:797
  186.5 17.9 %copy-start.1 = (bf16[16,2,1536]{2,1,0:T(2,128)(2,1)S(1)}, bf16[16,2,1536]{2,1,0:T(2,128)(2,1)}, u32[]{:S(2)}) copy-start(bf16[16,2,1536]{2,1,0:T(2,128)(2,1)} %param.14) | copy-start | bytes 294916
  (8 other events, 7.1 us)

commit v11 on v10

--- a/solution.py
+++ b/solution.py
@@ -761,7 +761,7 @@
     ).astype(BF)
     messages = [lax.ppermute(message, "tp", [(t, 3)]) for t in range(3)] + [message]
 
-    done = first_hop(0, [message])
+    done = first_hop(0, [terms])
     send_far(2, done)
     near_sums, *side = project_near(rank, hidden, down_t, far_sums[2:])
     done = first_hop(1, [near_sums])

time: 206 us -> 207 us (level)
  waiting for transfers between devices: 42.8 us -> 46.1 us
  local copies, waits for them, and re-layouts: 11.4 us -> 9 us
    unnamed x64 -> x56, local copies, waits for them, and re-layouts: 7.66 us -> 5.21 us
  transfers between devices with their start and end apart: 24 -> 24, of which waited for: 9 -> 9; matrix products, arithmetic and copies ran while one was open for 3% -> 2% of each run, Pallas kernels for 38% -> 37%
where the time goes in v11:
time: 207 us; the launch traced here: 205 us
  Pallas kernels  88.3 us (43%)
  starting transfers between devices  52.7 us (25%)
  waiting for transfers between devices  46.1 us (22%)
  local copies, waits for them, and re-layouts  9 us (4%)
  blocking collectives  6.49 us (3%)
    pallas_call x4, Pallas kernels, project_far(): pl.pallas_call(project_far_kernel, grid_spec=pltpu.PrefetchScalarGridSpec...  24.4 us
    ppermute x4, waiting for transfers between devices, second_hop(): outer.append(lax.ppermute(block, 'tp', outward))  20.6 us
    ppermute x4, starting transfers between devices, send_far(): inner.append(lax.ppermute(codes, 'tp', inward))  16.2 us
    pallas_call x1, Pallas kernels, queries(): pl.pallas_call(body, grid=(heads // step,), in_specs=[pl.BlockSpec((rows,...  13.8 us
    pallas_call x1, Pallas kernels, project_near(): pl.pallas_call(project_near_kernel, grid_spec=pltpu.PrefetchScalarGridSpe...  13.8 us
    pallas_call x8, Pallas kernels, add_on(): pl.pallas_call(functools.partial(add_kernel, -1 - len(carried)), grid_spe...  13.4 us
    ppermute x2, starting transfers between devices, local_line(): side = [lax.ppermute(codes, 'tp', inward) for codes in side]  10.2 us
    ppermute x6, waiting for transfers between devices, attend_to(): return (result, [lax.ppermute(result[t], 'tp', [(3, t)]) for t in range(3)])  9.83 us
  transfers between devices with their start and end apart: 24, of which 9 were waited for; matrix products, arithmetic and copies ran while one was open for 2% of the time, Pallas kernels for 37%

profile of v11, /device:TPU:0, one launch (start us, length us, event | category | flops | bytes accessed | tf_op | source)
XLA Modules:
  0.0 205.1 jit_solution(10884405105064772068)
XLA Ops:
  0.7 6.1 %project_far.4 = (f32[2,3,576,128]{3,2,1,0:T(8,128)}, s16[2,3,592,128]{3,2,1,0:T(8,128)(2,1)}) custom-call(s32[1]{0:T(128)} %bitcast.rank, bf16[4,1536,1792]{2,1,0:T(8,128)(2,1)} %bitcast.22, bf16[576,1792]{1,0:T(8,128)(2,1)} %bitcast.27), custom_call_target="tpu_custom_call" | custom-call | flops 1024 | bytes 1024 | tf_op jit(solution)/shard_map/project_far/pallas_call | solution.py:269
  6.7 4.5 %collective-permute-start = (s16[2,3,592,128]{3,2,1,0:T(8,128)(2,1)}, s16[2,3,592,128]{3,2,1,0:T(8,128)(2,1)S(1)}, u32[]{:S(2)}, u32[]{:S(2)}) collective-permute-start(s16[2,3,592,128]{3,2,1,0:T(8,128)(2,1)} %get-tuple-element.28), channel_id=1, source_target_pairs={{0,4},{12,8},{1,5},{13,9},{2,6},{14,10},{3,7},{15,11},{16,20},{28,... | collective-permute-start | bytes 2727944 | tf_op jit(solution)/shard_map/ppermute | solution.py:733
  11.3 6.1 %project_far.5 = (f32[2,3,576,128]{3,2,1,0:T(8,128)}, s16[2,3,592,128]{3,2,1,0:T(8,128)(2,1)}) custom-call(s32[1]{0:T(128)} %bitcast.rank, bf16[4,1536,1792]{2,1,0:T(8,128)(2,1)} %bitcast.23, bf16[576,1792]{1,0:T(8,128)(2,1)} %bitcast.28, f32[2,3,576,128]{3,2,1,0:T(8,128)} %get-tuple-element.27.refs_0_.own_ref), custom_call_target="tpu_custom_call" | custom-call | flops 1024 | bytes 1024 | tf_op jit(solution)/shard_map/project_far/pallas_call | solution.py:269
  17.4 1.3 collective-permute-start.2
  20.2 13.8 %queries.1 = (f32[32,8,576]{2,1,0:T(8,128)}, f32[4,8,576]{2,1,0:T(8,128)}) custom-call(bf16[8,1536]{1,0:T(8,128)(2,1)} %reshape.129.refs_0_, bf16[1536,6144]{1,0:T(8,128)(2,1)} %refs_1_.2, bf16[8,1792]{1,0:T(8,128)(2,1)} %refs_2_.2, bf16[576,1792]{1,0:T(8,128)(2,1)} %bitcast.29, bf16[512,8192]{1,0:T(8,128)(2,1)} %refs_7_.3, bf16[512,8192]{1,0:T(8,128)(2,1)} %refs_7_.3, ...), custom_call_target="tpu_custom_call" | custom-call | flops 1024 | bytes 1024 | tf_op jit(solution)/shard_map/queries/pallas_call | solution.py:502
  34.9 1.5 add_on.8.refs_0_
  36.4 1.6 collective-permute-start.1
  38.2 4.4 %collective-permute-start.3 = (bf16[288,576]{1,0:T(8,128)(2,1)S(1)}, bf16[288,576]{1,0:T(8,128)(2,1)S(1)}, u32[]{:S(2)}, u32[]{:S(2)}) collective-permute-start(bf16[288,576]{1,0:T(8,128)(2,1)S(1)} %pad_maximum_fusion.refs_3_.refs_7_), channel_id=1, source_target_pairs={{0,12},{1,13},{2,14},{3,15},{16,28},{17,29},{18,30},{19,31}} | collective-permute-start | bytes 995336 | tf_op jit(solution)/shard_map/ppermute | solution.py:762
  44.0 6.1 %project_far.6 = (f32[2,3,576,128]{3,2,1,0:T(8,128)}, s16[2,3,592,128]{3,2,1,0:T(8,128)(2,1)}) custom-call(s32[1]{0:T(128)} %bitcast.rank, bf16[4,1536,1792]{2,1,0:T(8,128)(2,1)} %bitcast.24, bf16[576,1792]{1,0:T(8,128)(2,1)} %bitcast.30, s16[2,3,592,128]{3,2,1,0:T(8,128)(2,1)} %copy-done.9), custom_call_target="tpu_custom_call" | custom-call | flops 1024 | bytes 1024 | tf_op jit(solution)/shard_map/project_far/pallas_call | solution.py:269
  50.1 1.5 collective-permute-done.2.got_ref
  51.6 5.2 %collective-permute-start.8 = (s16[2,3,592,128]{3,2,1,0:T(8,128)(2,1)}, s16[2,3,592,128]{3,2,1,0:T(8,128)(2,1)}, u32[]{:S(2)}, u32[]{:S(2)}) collective-permute-start(s16[2,3,592,128]{3,2,1,0:T(8,128)(2,1)} %get-tuple-element.37), channel_id=1, source_target_pairs={{0,4},{12,8},{1,5},{13,9},{2,6},{14,10},{3,7},{15,11},{16,20},{28,... | collective-permute-start | bytes 2727944 | tf_op jit(solution)/shard_map/ppermute | solution.py:733
  56.8 13.8 %project_near.1 = (f32[3,2,4,576,128]{4,3,2,1,0:T(8,128)}, s16[1,4,592,128]{3,2,1,0:T(8,128)(2,1)}, s16[2,4,592,128]{3,2,1,0:T(8,128)(2,1)}) custom-call(s32[1]{0:T(128)} %bitcast.rank, bf16[4,1536,1792]{2,1,0:T(8,128)(2,1)} %bitcast.25, bf16[576,1792]{1,0:T(8,128)(2,1)} %bitcast.31, f32[2,3,576,128]{3,2,1,0:T(8,128)} %get-tuple-element.31.refs_0_.own_ref), custom_call_target="tpu_custom_call" | custom-call | flops 1024 | bytes 1024 | tf_op jit(solution)/shard_map/project_near/pallas_call | solution.py:312
  71.8 1.4 add_on.9.refs_0_
  73.2 1.6 collective-permute-start.7
  74.8 1.7 add_on.10.refs_0_
  76.5 1.3 collective-permute-start.9
  77.9 6.1 %project_far.7 = (f32[2,3,576,128]{3,2,1,0:T(8,128)}, s16[2,3,592,128]{3,2,1,0:T(8,128)(2,1)}) custom-call(s32[1]{0:T(128)} %bitcast.rank, bf16[4,1536,1792]{2,1,0:T(8,128)(2,1)} %bitcast.26, bf16[576,1792]{1,0:T(8,128)(2,1)} %bitcast.32, s16[2,3,592,128]{3,2,1,0:T(8,128)(2,1)} %copy-done.2), custom_call_target="tpu_custom_call" | custom-call | flops 1024 | bytes 1024 | tf_op jit(solution)/shard_map/project_far/pallas_call | solution.py:269
  84.0 5.1 %collective-permute-start.6 = (s16[2,3,592,128]{3,2,1,0:T(8,128)(2,1)}, s16[2,3,592,128]{3,2,1,0:T(8,128)(2,1)S(1)}, u32[]{:S(2)}, u32[]{:S(2)}) collective-permute-start(s16[2,3,592,128]{3,2,1,0:T(8,128)(2,1)} %get-tuple-element.36), channel_id=1, source_target_pairs={{0,4},{12,8},{1,5},{13,9},{2,6},{14,10},{3,7},{15,11},{16,20},{28,... | collective-permute-start | bytes 2727944 | tf_op jit(solution)/shard_map/ppermute | solution.py:733
  89.1 2.5 %add_on.11 = (s16[2,3,592,128]{3,2,1,0:T(8,128)(2,1)}, s16[1,4,592,128]{3,2,1,0:T(8,128)(2,1)}) custom-call(s32[1]{0:T(128)} %bitcast.rank, f32[2,3,576,128]{3,2,1,0:T(8,128)} %get-tuple-element.31.refs_0_.own_ref, s16[2,3,592,128]{3,2,1,0:T(8,128)(2,1)} %collective-permute-done.8.got_ref, ...), custom_call_target="tpu_custom_call", output_to_operand_aliasing={{1}: (4, {})} | custom-call | flops 1024 | bytes 1024 | tf_op jit(solution)/shard_map/add_on/pallas_call | solution.py:358
  91.6 1.6 collective-permute-start.11
  93.1 1.7 add_on.12.refs_0_
  94.8 3.4 %collective-permute-done.9.refs_1_.refs_9_.refs_0_ = s16[2,3,592,128]{3,2,1,0:T(8,128)(2,1)} collective-permute-done((s16[2,3,592,128]{3,2,1,0:T(8,128)(2,1)S(1)}, s16[2,3,592,128]{3,2,1,0:T(8,128)(2,1)}, u32[]{:S(2)}, u32[]{:S(2)}) %collective-permute-start.9) | collective-permute-done | bytes 909344 | tf_op jit(solution)/shard_map/ppermute | solution.py:745
  98.3 1.3 collective-permute-start.12
  99.6 5.5 %collective-permute-start.13 = (s16[1,4,592,128]{3,2,1,0:T(8,128)(2,1)}, s16[1,4,592,128]{3,2,1,0:T(8,128)(2,1)S(1)}, u32[]{:S(2)}, u32[]{:S(2)}) collective-permute-start(s16[1,4,592,128]{3,2,1,0:T(8,128)(2,1)} %get-tuple-element.40), channel_id=1, source_target_pairs={{0,4},{12,8},{1,5},{13,9},{2,6},{14,10},{3,7},{15,11},{16,20},{28,... | collective-permute-start | bytes 1818632 | tf_op jit(solution)/shard_map/ppermute | solution.py:776
  105.5 4.4 %collective-permute-done.6.got_ref = s16[2,3,592,128]{3,2,1,0:T(8,128)(2,1)S(1)} collective-permute-done((s16[2,3,592,128]{3,2,1,0:T(8,128)(2,1)}, s16[2,3,592,128]{3,2,1,0:T(8,128)(2,1)S(1)}, u32[]{:S(2)}, u32[]{:S(2)}) %collective-permute-start.6) | collective-permute-done | bytes 909344 | tf_op jit(solution)/shard_map/ppermute | solution.py:733
  109.9 1.4 add_on.13.refs_0_
  112.3 1.7 add_on.14.refs_0_
  114.0 5.3 %collective-permute-done.13.refs_2_.refs_6_ = s16[1,4,592,128]{3,2,1,0:T(8,128)(2,1)S(1)} collective-permute-done((s16[1,4,592,128]{3,2,1,0:T(8,128)(2,1)}, s16[1,4,592,128]{3,2,1,0:T(8,128)(2,1)S(1)}, u32[]{:S(2)}, u32[]{:S(2)}) %collective-permute-start.13) | collective-permute-done | bytes 606240 | tf_op jit(solution)/shard_map/ppermute | solution.py:776
  119.3 1.3 collective-permute-start.14
  120.6 4.7 %collective-permute-start.16 = (s16[2,4,592,128]{3,2,1,0:T(8,128)(2,1)S(1)}, s16[2,4,592,128]{3,2,1,0:T(8,128)(2,1)S(1)}, u32[]{:S(2)}, u32[]{:S(2)}) collective-permute-start(s16[2,4,592,128]{3,2,1,0:T(8,128)(2,1)S(1)} %copy-done.25), channel_id=1, source_target_pairs={{0,4},{12,8},{1,5},{13,9},{2,6},{14,10},{3,7},{15,11},{16,20},{28,... | collective-permute-start | bytes 3637256 | tf_op jit(solution)/shard_map/ppermute | solution.py:776
  125.3 1.5 add_on.15.refs_0_
  126.7 12.9 %collective-permute-done.14.refs_1_.refs_11_.refs_2_ = s16[2,3,592,128]{3,2,1,0:T(8,128)(2,1)S(1)} collective-permute-done((s16[2,3,592,128]{3,2,1,0:T(8,128)(2,1)S(1)}, s16[2,3,592,128]{3,2,1,0:T(8,128)(2,1)S(1)}, u32[]{:S(2)}, u32[]{:S(2)}) %collective-permute-start.14) | collective-permute-done | bytes 909344 | tf_op jit(solution)/shard_map/ppermute | solution.py:745
  139.7 1.5 collective-permute-start.15
  141.2 4.1 %attend.2 = (bf16[3,64,512]{2,1,0:T(8,128)(2,1)S(1)}, bf16[3,64,512]{2,1,0:T(8,128)(2,1)S(1)}, bf16[3,64,512]{2,1,0:T(8,128)(2,1)S(1)}, bf16[3,64,512]{2,1,0:T(8,128)(2,1)S(1)}) custom-call(s32[1]{0:T(128)} %bitcast.rank, s32[1]{0:T(128)} %bitcast.8.first_ref, bf16[288,576]{1,0:T(8,128)(2,1)S(1)} %collective-permute-done.3.refs_1_.refs_0_.refs_4_, ...), custom_call_target="tpu_custom_call" | custom-call | flops 1024 | bytes 1024 | tf_op jit(solution)/shard_map/attend/pallas_call | solution.py:610
  145.3 1.3 collective-permute-start.17
  149.2 5.8 %pages.2.refs_7_ = bf16[4,576,384]{2,1,0:T(8,128)(2,1)} custom-call(s32[1]{0:T(128)} %bitcast.rank, s32[4]{0:T(128)S(1)} %dynamic_slice.9.slot, f32[3,2,4,576,128]{4,3,2,1,0:T(8,128)} %get-tuple-element.32.refs_0_.own_ref.refs_8_, s16[2,3,592,128]{3,2,1,0:T(8,128)(2,1)} %collective-permute-done.9.refs_1_.refs_9_.refs_0_, ...), custom_call_target="tpu_custom_call" | custom-call | flops 1024 | bytes 1024 | tf_op jit(solution)/shard_map/pages/pallas_call | solution.py:437
  154.9 4.3 %collective-permute-done.17.refs_8_ = bf16[3,64,512]{2,1,0:T(8,128)(2,1)S(1)} collective-permute-done((bf16[3,64,512]{2,1,0:T(8,128)(2,1)S(1)}, bf16[3,64,512]{2,1,0:T(8,128)(2,1)S(1)}, u32[]{:S(2)}, u32[]{:S(2)}) %collective-permute-start.17) | collective-permute-done | bytes 196640 | tf_op jit(solution)/shard_map/ppermute | solution.py:797
  159.2 4.2 %collective-permute-done.15.refs_0_.refs_9_ = s16[2,3,592,128]{3,2,1,0:T(8,128)(2,1)S(1)} collective-permute-done((s16[2,3,592,128]{3,2,1,0:T(8,128)(2,1)S(1)}, s16[2,3,592,128]{3,2,1,0:T(8,128)(2,1)S(1)}, u32[]{:S(2)}, u32[]{:S(2)}) %collective-permute-start.15) | collective-permute-done | bytes 909344 | tf_op jit(solution)/shard_map/ppermute | solution.py:745
  164.3 3.3 %pages.3.refs_18_.refs_8_ = bf16[4,576,384]{2,1,0:T(8,128)(2,1)} custom-call(s32[1]{0:T(128)} %bitcast.rank, s32[4]{0:T(128)S(1)} %dynamic_slice.9.slot, f32[3,2,4,576,128]{4,3,2,1,0:T(8,128)} %get-tuple-element.32.refs_0_.own_ref.refs_8_, s16[2,3,592,128]{3,2,1,0:T(8,128)(2,1)} %copy-done.23, ...), custom_call_target="tpu_custom_call", output_to_operand_aliasing={{}: (10, {})} | custom-call | flops 1024 | bytes 1024 | tf_op jit(solution)/shard_map/pages/pallas_call | solution.py:437
  167.6 4.6 %all-to-all-start = ((bf16[4,576,384]{2,1,0:T(8,128)(2,1)}), bf16[4,576,384]{2,1,0:T(8,128)(2,1)}, u32[]{:S(2)}, u32[]{:S(2)}) async-start(bf16[4,576,384]{2,1,0:T(8,128)(2,1)} %pages.3.refs_18_.refs_8_), calls=%async_computation | async-start | bytes 3538944 | tf_op jit(solution)/shard_map/all_to_all | solution.py:825
  172.4 1.8 attend.3
  174.2 1.3 collective-permute-start.20
  176.9 5.6 %collective-permute-done.20 = bf16[1,64,512]{2,1,0:T(8,128)(2,1)S(1)} collective-permute-done((bf16[1,64,512]{2,1,0:T(8,128)(2,1)S(1)}, bf16[1,64,512]{2,1,0:T(8,128)(2,1)S(1)}, u32[]{:S(2)}, u32[]{:S(2)}) %collective-permute-start.20) | collective-permute-done | bytes 65568 | tf_op jit(solution)/shard_map/ppermute | solution.py:797
  182.8 1.2 reshape.139.o_ref
  184.7 5.2 %heads_out.1.placed_ref = bf16[4,2,4096]{2,1,0:T(2,128)(2,1)} custom-call(s32[4]{0:T(128)} %copy-done.20, f32[32,8,512]{2,1,0:T(8,128)} %reshape.139.o_ref, f32[8,128]{1,0:T(8,128)} %broadcast_in_dim.2.keep_ref, bf16[512,8192]{1,0:T(8,128)(2,1)} %refs_7_.3, bf16[512,8192]{1,0:T(8,128)(2,1)} %refs_7_.3, bf16[512,8192]{1,0:T(8,128)(2,1)} %refs_7_.3, ...), custom_call_target="tpu_custom_call" | custom-call | flops 1024 | bytes 1024 | tf_op jit(solution)/shard_map/heads_out/pallas_call | solution.py:656
  189.9 4.5 %all-to-all-done.pages_ref = bf16[4,576,384]{2,1,0:T(8,128)(2,1)} async-done(((bf16[4,576,384]{2,1,0:T(8,128)(2,1)}), bf16[4,576,384]{2,1,0:T(8,128)(2,1)}, u32[]{:S(2)}, u32[]{:S(2)}) %all-to-all-start) | async-done | bytes 1769504 | tf_op jit(solution)/shard_map/all_to_all | solution.py:825
  195.3 2.7 %emit.1 = (bf16[4,576,384]{2,1,0:T(8,128)(2,1)}, bf16[4,2,4096]{2,1,0:T(2,128)(2,1)S(1)}) custom-call(bf16[4,576,384]{2,1,0:T(8,128)(2,1)} %all-to-all-done.pages_ref, bf16[4,2,4096]{2,1,0:T(2,128)(2,1)S(1)} %copy-done.14), custom_call_target="tpu_custom_call", output_to_operand_aliasing={{1}: (1, {})} | custom-call | flops 1024 | bytes 1024 | tf_op jit(solution)/shard_map/emit/pallas_call | solution.py:683
  198.0 6.5 %all_to_all.10 = bf16[4,2,4096]{2,1,0:T(2,128)(2,1)S(1)} all-to-all(bf16[4,2,4096]{2,1,0:T(2,128)(2,1)S(1)} %get-tuple-element.50), channel_id=1, replica_groups=mesh['groups'=2,'tp'=4,'pd'=4] {'pd'}, dimensions={0} | all-to-all | bytes 131072 | tf_op jit(solution)/shard_map/all_to_all | solution.py:844
  (106 shorter events, 14.0 us)
Async XLA Ops:
  0.6 18.1 %copy-start = (bf16[16,2,1536]{2,1,0:T(2,128)(2,1)S(1)}, bf16[16,2,1536]{2,1,0:T(2,128)(2,1)}, u32[]{:S(2)}) copy-start(bf16[16,2,1536]{2,1,0:T(2,128)(2,1)} %param.14) | copy-start | bytes 294916
  6.7 27.3 %collective-permute-start = (s16[2,3,592,128]{3,2,1,0:T(8,128)(2,1)}, s16[2,3,592,128]{3,2,1,0:T(8,128)(2,1)S(1)}, u32[]{:S(2)}, u32[]{:S(2)}) collective-permute-start(s16[2,3,592,128]{3,2,1,0:T(8,128)(2,1)} %get-tuple-element.28), channel_id=1, source_target_pairs={{0,4},{12,8},{1,5},{13,9},{2,6},{14,10},{3,7},{15,11},{16,20},{28,... | collective-permute-start | bytes 2727944 | tf_op jit(solution)/shard_map/ppermute | solution.py:733
  17.4 34.2 %collective-permute-start.2 = (s16[2,3,592,128]{3,2,1,0:T(8,128)(2,1)}, s16[2,3,592,128]{3,2,1,0:T(8,128)(2,1)S(1)}, u32[]{:S(2)}, u32[]{:S(2)}) collective-permute-start(s16[2,3,592,128]{3,2,1,0:T(8,128)(2,1)} %get-tuple-element.33), channel_id=1, source_target_pairs={{0,4},{12,8},{1,5},{13,9},{2,6},{14,10},{3,7},{15,11},{16,20},{28,... | collective-permute-start | bytes 2727944 | tf_op jit(solution)/shard_map/ppermute | solution.py:733
  34.9 3.1 %copy-start.24 = (f32[32,8,576]{2,1,0:T(8,128)S(1)}, f32[32,8,576]{2,1,0:T(8,128)}, u32[]{:S(2)}) copy-start(f32[32,8,576]{2,1,0:T(8,128)} %get-tuple-element.34) | copy-start | bytes 1769476
  36.4 7.6 %copy-start.9 = (s16[2,3,592,128]{3,2,1,0:T(8,128)(2,1)}, s16[2,3,592,128]{3,2,1,0:T(8,128)(2,1)S(1)}, u32[]{:S(2)}) copy-start(s16[2,3,592,128]{3,2,1,0:T(8,128)(2,1)S(1)} %add_on.8.refs_0_) | copy-start | bytes 2727940
  36.4 36.8 %collective-permute-start.1 = (s16[2,3,592,128]{3,2,1,0:T(8,128)(2,1)S(1)}, s16[2,3,592,128]{3,2,1,0:T(8,128)(2,1)}, u32[]{:S(2)}, u32[]{:S(2)}) collective-permute-start(s16[2,3,592,128]{3,2,1,0:T(8,128)(2,1)S(1)} %add_on.8.refs_0_), channel_id=1, source_target_pairs={{4,8},{8,4},{5,9},{9,5},{6,10},{10,6},{7,11},{11,7},{20,24},{24,20... | collective-permute-start | bytes 2727944 | tf_op jit(solution)/shard_map/ppermute | solution.py:737
  38.2 11.9 %copy-start.21 = (bf16[288,576]{1,0:T(8,128)(2,1)}, bf16[288,576]{1,0:T(8,128)(2,1)S(1)}, u32[]{:S(2)}) copy-start(bf16[288,576]{1,0:T(8,128)(2,1)S(1)} %pad_maximum_fusion.refs_3_.refs_7_) | copy-start | bytes 995332
  38.2 38.3 %collective-permute-start.3 = (bf16[288,576]{1,0:T(8,128)(2,1)S(1)}, bf16[288,576]{1,0:T(8,128)(2,1)S(1)}, u32[]{:S(2)}, u32[]{:S(2)}) collective-permute-start(bf16[288,576]{1,0:T(8,128)(2,1)S(1)} %pad_maximum_fusion.refs_3_.refs_7_), channel_id=1, source_target_pairs={{0,12},{1,13},{2,14},{3,15},{16,28},{17,29},{18,30},{19,31}} | collective-permute-start | bytes 995336 | tf_op jit(solution)/shard_map/ppermute | solution.py:762
  42.6 33.9 %collective-permute-start.4 = (bf16[288,576]{1,0:T(8,128)(2,1)S(1)}, bf16[288,576]{1,0:T(8,128)(2,1)S(1)}, u32[]{:S(2)}, u32[]{:S(2)}) collective-permute-start(bf16[288,576]{1,0:T(8,128)(2,1)S(1)} %pad_maximum_fusion.refs_3_.refs_7_), channel_id=1, source_target_pairs={{4,12},{5,13},{6,14},{7,15},{20,28},{21,29},{22,30},{23,31}} | collective-permute-start | bytes 995336 | tf_op jit(solution)/shard_map/ppermute | solution.py:762
  43.3 33.2 %collective-permute-start.5 = (bf16[288,576]{1,0:T(8,128)(2,1)S(1)}, bf16[288,576]{1,0:T(8,128)(2,1)S(1)}, u32[]{:S(2)}, u32[]{:S(2)}) collective-permute-start(bf16[288,576]{1,0:T(8,128)(2,1)S(1)} %pad_maximum_fusion.refs_3_.refs_7_), channel_id=1, source_target_pairs={{8,12},{9,13},{10,14},{11,15},{24,28},{25,29},{26,30},{27,31}} | collective-permute-start | bytes 995336 | tf_op jit(solution)/shard_map/ppermute | solution.py:762
  51.6 19.0 %copy-start.12 = (s16[2,3,592,128]{3,2,1,0:T(8,128)(2,1)}, s16[2,3,592,128]{3,2,1,0:T(8,128)(2,1)S(1)}, u32[]{:S(2)}) copy-start(s16[2,3,592,128]{3,2,1,0:T(8,128)(2,1)S(1)} %collective-permute-done.2.got_ref) | copy-start | bytes 2727940
  51.6 37.5 %collective-permute-start.8 = (s16[2,3,592,128]{3,2,1,0:T(8,128)(2,1)}, s16[2,3,592,128]{3,2,1,0:T(8,128)(2,1)}, u32[]{:S(2)}, u32[]{:S(2)}) collective-permute-start(s16[2,3,592,128]{3,2,1,0:T(8,128)(2,1)} %get-tuple-element.37), channel_id=1, source_target_pairs={{0,4},{12,8},{1,5},{13,9},{2,6},{14,10},{3,7},{15,11},{16,20},{28,... | collective-permute-start | bytes 2727944 | tf_op jit(solution)/shard_map/ppermute | solution.py:733
  70.6 1.2 copy-start.13
  73.2 1.6 copy-start.11
  73.2 19.9 %collective-permute-start.7 = (s16[2,3,592,128]{3,2,1,0:T(8,128)(2,1)S(1)}, s16[2,3,592,128]{3,2,1,0:T(8,128)(2,1)}, u32[]{:S(2)}, u32[]{:S(2)}) collective-permute-start(s16[2,3,592,128]{3,2,1,0:T(8,128)(2,1)S(1)} %add_on.9.refs_0_), channel_id=1, source_target_pairs={{4,8},{8,4},{5,9},{9,5},{6,10},{10,6},{7,11},{11,7},{20,24},{24,20... | collective-permute-start | bytes 2727944 | tf_op jit(solution)/shard_map/ppermute | solution.py:737
  76.5 7.5 %copy-start.6 = (bf16[288,576]{1,0:T(8,128)(2,1)}, bf16[288,576]{1,0:T(8,128)(2,1)S(1)}, u32[]{:S(2)}) copy-start(bf16[288,576]{1,0:T(8,128)(2,1)S(1)} %collective-permute-done.5.refs_3_.refs_2_.refs_6_) | copy-start | bytes 995332
  76.5 1.3 copy-start.2
  76.5 21.7 %collective-permute-start.9 = (s16[2,3,592,128]{3,2,1,0:T(8,128)(2,1)S(1)}, s16[2,3,592,128]{3,2,1,0:T(8,128)(2,1)}, u32[]{:S(2)}, u32[]{:S(2)}) collective-permute-start(s16[2,3,592,128]{3,2,1,0:T(8,128)(2,1)S(1)} %hold.4.refs_0_.refs_3_), channel_id=1, source_target_pairs={{8,12},{4,0},{9,13},{5,1},{10,14},{6,2},{11,15},{7,3},{24,28},{20,... | collective-permute-start | bytes 2727944 | tf_op jit(solution)/shard_map/ppermute | solution.py:745
  84.0 25.9 %collective-permute-start.6 = (s16[2,3,592,128]{3,2,1,0:T(8,128)(2,1)}, s16[2,3,592,128]{3,2,1,0:T(8,128)(2,1)S(1)}, u32[]{:S(2)}, u32[]{:S(2)}) collective-permute-start(s16[2,3,592,128]{3,2,1,0:T(8,128)(2,1)} %get-tuple-element.36), channel_id=1, source_target_pairs={{0,4},{12,8},{1,5},{13,9},{2,6},{14,10},{3,7},{15,11},{16,20},{28,... | collective-permute-start | bytes 2727944 | tf_op jit(solution)/shard_map/ppermute | solution.py:733
  91.6 20.5 %collective-permute-start.11 = (s16[2,3,592,128]{3,2,1,0:T(8,128)(2,1)}, s16[2,3,592,128]{3,2,1,0:T(8,128)(2,1)}, u32[]{:S(2)}, u32[]{:S(2)}) collective-permute-start(s16[2,3,592,128]{3,2,1,0:T(8,128)(2,1)} %get-tuple-element.39.refs_0_), channel_id=1, source_target_pairs={{4,8},{8,4},{5,9},{9,5},{6,10},{10,6},{7,11},{11,7},{20,24},{24,20... | collective-permute-start | bytes 2727944 | tf_op jit(solution)/shard_map/ppermute | solution.py:737
  98.3 11.7 %copy-start.4 = (s16[2,3,592,128]{3,2,1,0:T(8,128)(2,1)}, s16[2,3,592,128]{3,2,1,0:T(8,128)(2,1)S(1)}, u32[]{:S(2)}) copy-start(s16[2,3,592,128]{3,2,1,0:T(8,128)(2,1)S(1)} %hold.5.refs_0_.refs_4_) | copy-start | bytes 2727940
  98.3 21.0 %collective-permute-start.12 = (s16[2,3,592,128]{3,2,1,0:T(8,128)(2,1)S(1)}, s16[2,3,592,128]{3,2,1,0:T(8,128)(2,1)}, u32[]{:S(2)}, u32[]{:S(2)}) collective-permute-start(s16[2,3,592,128]{3,2,1,0:T(8,128)(2,1)S(1)} %hold.5.refs_0_.refs_4_), channel_id=1, source_target_pairs={{8,12},{4,0},{9,13},{5,1},{10,14},{6,2},{11,15},{7,3},{24,28},{20,... | collective-permute-start | bytes 2727944 | tf_op jit(solution)/shard_map/ppermute | solution.py:745
  99.6 19.7 %collective-permute-start.13 = (s16[1,4,592,128]{3,2,1,0:T(8,128)(2,1)}, s16[1,4,592,128]{3,2,1,0:T(8,128)(2,1)S(1)}, u32[]{:S(2)}, u32[]{:S(2)}) collective-permute-start(s16[1,4,592,128]{3,2,1,0:T(8,128)(2,1)} %get-tuple-element.40), channel_id=1, source_target_pairs={{0,4},{12,8},{1,5},{13,9},{2,6},{14,10},{3,7},{15,11},{16,20},{28,... | collective-permute-start | bytes 1818632 | tf_op jit(solution)/shard_map/ppermute | solution.py:776
  111.4 13.9 %collective-permute-start.10 = (s16[2,3,592,128]{3,2,1,0:T(8,128)(2,1)S(1)}, s16[2,3,592,128]{3,2,1,0:T(8,128)(2,1)S(1)}, u32[]{:S(2)}, u32[]{:S(2)}) collective-permute-start(s16[2,3,592,128]{3,2,1,0:T(8,128)(2,1)S(1)} %add_on.13.refs_0_), channel_id=1, source_target_pairs={{4,8},{8,4},{5,9},{9,5},{6,10},{10,6},{7,11},{11,7},{20,24},{24,20... | collective-permute-start | bytes 2727944 | tf_op jit(solution)/shard_map/ppermute | solution.py:737
  114.0 6.6 %copy-start.25 = (s16[2,4,592,128]{3,2,1,0:T(8,128)(2,1)S(1)}, s16[2,4,592,128]{3,2,1,0:T(8,128)(2,1)}, u32[]{:S(2)}) copy-start(s16[2,4,592,128]{3,2,1,0:T(8,128)(2,1)} %get-tuple-element.41) | copy-start | bytes 3637252
  119.3 6.0 %copy-start.3 = (s16[2,3,592,128]{3,2,1,0:T(8,128)(2,1)}, s16[2,3,592,128]{3,2,1,0:T(8,128)(2,1)S(1)}, u32[]{:S(2)}) copy-start(s16[2,3,592,128]{3,2,1,0:T(8,128)(2,1)S(1)} %hold.6.refs_0_.refs_5_) | copy-start | bytes 2727940
  119.3 20.4 %collective-permute-start.14 = (s16[2,3,592,128]{3,2,1,0:T(8,128)(2,1)S(1)}, s16[2,3,592,128]{3,2,1,0:T(8,128)(2,1)S(1)}, u32[]{:S(2)}, u32[]{:S(2)}) collective-permute-start(s16[2,3,592,128]{3,2,1,0:T(8,128)(2,1)S(1)} %hold.6.refs_0_.refs_5_), channel_id=1, source_target_pairs={{8,12},{4,0},{9,13},{5,1},{10,14},{6,2},{11,15},{7,3},{24,28},{20,... | collective-permute-start | bytes 2727944 | tf_op jit(solution)/shard_map/ppermute | solution.py:745
  120.6 27.5 %collective-permute-start.16 = (s16[2,4,592,128]{3,2,1,0:T(8,128)(2,1)S(1)}, s16[2,4,592,128]{3,2,1,0:T(8,128)(2,1)S(1)}, u32[]{:S(2)}, u32[]{:S(2)}) collective-permute-start(s16[2,4,592,128]{3,2,1,0:T(8,128)(2,1)S(1)} %copy-done.25), channel_id=1, source_target_pairs={{0,4},{12,8},{1,5},{13,9},{2,6},{14,10},{3,7},{15,11},{16,20},{28,... | collective-permute-start | bytes 3637256 | tf_op jit(solution)/shard_map/ppermute | solution.py:776
  126.7 14.5 %copy-start.15 = (s32[16,1536]{1,0:T(8,128)S(1)}, s32[16,1536]{1,0:T(8,128)}, u32[]{:S(2)}) copy-start(s32[16,1536]{1,0:T(8,128)} %refs_14_.1) | copy-start | bytes 294916
  126.7 14.5 %copy-start.17 = (f32[8,32]{1,0:T(8,128)S(1)}, f32[8,32]{1,0:T(8,128)}, u32[]{:S(2)}) copy-start(f32[8,32]{1,0:T(8,128)} %get-tuple-element.56.refs_9_.refs_19_.refs_17_) | copy-start | bytes 3076
  126.7 14.5 %copy-start.18 = (f32[8,32]{1,0:T(8,128)S(1)}, f32[8,32]{1,0:T(8,128)}, u32[]{:S(2)}) copy-start(f32[8,32]{1,0:T(8,128)} %get-tuple-element.57.refs_8_.refs_18_.refs_16_) | copy-start | bytes 3076
  126.7 14.5 %copy-start.19 = (f32[512]{0:T(512)S(1)}, f32[512]{0:T(512)}, u32[]{:S(2)}) copy-start(f32[512]{0:T(512)} %param.13) | copy-start | bytes 6148
  139.7 1.5 copy-start.8
  139.7 1.5 copy-start.5
  139.7 23.7 %collective-permute-start.15 = (s16[2,3,592,128]{3,2,1,0:T(8,128)(2,1)S(1)}, s16[2,3,592,128]{3,2,1,0:T(8,128)(2,1)S(1)}, u32[]{:S(2)}, u32[]{:S(2)}) collective-permute-start(s16[2,3,592,128]{3,2,1,0:T(8,128)(2,1)S(1)} %hold.7.refs_20_.refs_1_), channel_id=1, source_target_pairs={{8,12},{4,0},{9,13},{5,1},{10,14},{6,2},{11,15},{7,3},{24,28},{20,... | collective-permute-start | bytes 2727944 | tf_op jit(solution)/shard_map/ppermute | solution.py:745
  141.2 6.8 %copy-start.26 = (s32[16]{0:T(128)S(1)}, s32[16]{0:T(128)}, u32[]{:S(2)}) copy-start(s32[16]{0:T(128)} %param.17) | copy-start | bytes 196
  145.3 13.9 %collective-permute-start.17 = (bf16[3,64,512]{2,1,0:T(8,128)(2,1)S(1)}, bf16[3,64,512]{2,1,0:T(8,128)(2,1)S(1)}, u32[]{:S(2)}, u32[]{:S(2)}) collective-permute-start(bf16[3,64,512]{2,1,0:T(8,128)(2,1)S(1)} %get-tuple-element.42.refs_11_), channel_id=1, source_target_pairs={{12,0},{13,1},{14,2},{15,3},{28,16},{29,17},{30,18},{31,19}} | collective-permute-start | bytes 589832 | tf_op jit(solution)/shard_map/ppermute | solution.py:797
  146.6 12.6 %collective-permute-start.18 = (bf16[3,64,512]{2,1,0:T(8,128)(2,1)S(1)}, bf16[3,64,512]{2,1,0:T(8,128)(2,1)S(1)}, u32[]{:S(2)}, u32[]{:S(2)}) collective-permute-start(bf16[3,64,512]{2,1,0:T(8,128)(2,1)S(1)} %get-tuple-element.43), channel_id=1, source_target_pairs={{12,4},{13,5},{14,6},{15,7},{28,20},{29,21},{30,22},{31,23}} | collective-permute-start | bytes 589832 | tf_op jit(solution)/shard_map/ppermute | solution.py:797
  147.3 11.9 %collective-permute-start.19 = (bf16[3,64,512]{2,1,0:T(8,128)(2,1)S(1)}, bf16[3,64,512]{2,1,0:T(8,128)(2,1)S(1)}, u32[]{:S(2)}, u32[]{:S(2)}) collective-permute-start(bf16[3,64,512]{2,1,0:T(8,128)(2,1)S(1)} %get-tuple-element.44), channel_id=1, source_target_pairs={{12,8},{13,9},{14,10},{15,11},{28,24},{29,25},{30,26},{31,27}} | collective-permute-start | bytes 589832 | tf_op jit(solution)/shard_map/ppermute | solution.py:797
  148.1 15.3 %copy-start.20 = (s32[4]{0:T(128)}, s32[4]{0:T(128)S(1)}, u32[]{:S(2)}) copy-start(s32[4]{0:T(128)S(1)} %dynamic_slice.9.slot) | copy-start | bytes 52
  148.1 1.1 copy-start.22
  167.6 4.6 %copy-start.27 = (s32[16]{0:T(128)S(1)}, s32[16]{0:T(128)}, u32[]{:S(2)}) copy-start(s32[16]{0:T(128)} %param.19) | copy-start | bytes 196
  167.6 4.8 %copy-start.7 = (bf16[288,576]{1,0:T(8,128)(2,1)S(1)}, bf16[288,576]{1,0:T(8,128)(2,1)}, u32[]{:S(2)}) copy-start(bf16[288,576]{1,0:T(8,128)(2,1)} %copy-done.6) | copy-start | bytes 995332
  167.6 26.8 %all-to-all-start = ((bf16[4,576,384]{2,1,0:T(8,128)(2,1)}), bf16[4,576,384]{2,1,0:T(8,128)(2,1)}, u32[]{:S(2)}, u32[]{:S(2)}) async-start(bf16[4,576,384]{2,1,0:T(8,128)(2,1)} %pages.3.refs_18_.refs_8_), calls=%async_computation | async-start | bytes 3538944 | tf_op jit(solution)/shard_map/all_to_all | solution.py:825
  174.2 8.2 %collective-permute-start.20 = (bf16[1,64,512]{2,1,0:T(8,128)(2,1)S(1)}, bf16[1,64,512]{2,1,0:T(8,128)(2,1)S(1)}, u32[]{:S(2)}, u32[]{:S(2)}) collective-permute-start(bf16[1,64,512]{2,1,0:T(8,128)(2,1)S(1)} %get-tuple-element.47), channel_id=1, source_target_pairs={{12,0},{13,1},{14,2},{15,3},{28,16},{29,17},{30,18},{31,19}} | collective-permute-start | bytes 196616 | tf_op jit(solution)/shard_map/ppermute | solution.py:797
  175.5 7.0 %collective-permute-start.21 = (bf16[1,64,512]{2,1,0:T(8,128)(2,1)S(1)}, bf16[1,64,512]{2,1,0:T(8,128)(2,1)S(1)}, u32[]{:S(2)}, u32[]{:S(2)}) collective-permute-start(bf16[1,64,512]{2,1,0:T(8,128)(2,1)S(1)} %get-tuple-element.48), channel_id=1, source_target_pairs={{12,4},{13,5},{14,6},{15,7},{28,20},{29,21},{30,22},{31,23}} | collective-permute-start | bytes 196616 | tf_op jit(solution)/shard_map/ppermute | solution.py:797
  176.2 6.3 %collective-permute-start.22 = (bf16[1,64,512]{2,1,0:T(8,128)(2,1)S(1)}, bf16[1,64,512]{2,1,0:T(8,128)(2,1)S(1)}, u32[]{:S(2)}, u32[]{:S(2)}) collective-permute-start(bf16[1,64,512]{2,1,0:T(8,128)(2,1)S(1)} %get-tuple-element.49), channel_id=1, source_target_pairs={{12,8},{13,9},{14,10},{15,11},{28,24},{29,25},{30,26},{31,27}} | collective-permute-start | bytes 196616 | tf_op jit(solution)/shard_map/ppermute | solution.py:797
  184.7 20.5 %copy-start.1 = (bf16[16,2,1536]{2,1,0:T(2,128)(2,1)S(1)}, bf16[16,2,1536]{2,1,0:T(2,128)(2,1)}, u32[]{:S(2)}) copy-start(bf16[16,2,1536]{2,1,0:T(2,128)(2,1)} %param.14) | copy-start | bytes 294916
  (4 other events, 3.6 us)

commit v12 on v10

--- a/solution.py
+++ b/solution.py
@@ -252,8 +252,21 @@
     return (z == 0) | (z == 3)
 
 
-def project_far_kernel(rank, hid_ref, down_ref, *refs):
-    sum_ref, code_ref = refs[-2:]
+def project_far_kernel(new, rank, hid_ref, down_ref, *refs):
+    sum_ref, code_ref = refs[-2 - new :][:2]
+    if new:
+        @pl.when(pl.program_id(0) == 0)
+        def _():
+            split_ref = refs[-1]
+            rest = lax.dot_general(
+                refs[0][...], down_ref[...], NT, preferred_element_type=F32
+            )
+            for n in range(3):
+                term = rest.astype(BF).astype(F32)
+                split_ref[n] = term
+                rest = rest - term
+            split_ref[3] = jnp.zeros_like(rest)
+
     total = lax.dot_general(down_ref[...], hid_ref[0], NT, preferred_element_type=F32)
     for u in range(UNITS):
         sum_ref[0, u] = total[:, u * UNIT : (u + 1) * UNIT]
@@ -264,31 +277,36 @@
             code_ref[0, u] = encode(total[:, u * UNIT : (u + 1) * UNIT])
 
 
-def project_far(rank, hidden, down_t, request, after):
+def project_far(rank, hidden, down_t, request, after, draft=()):
     depth = hidden.shape[-1]
     return pl.pallas_call(
-        project_far_kernel,
+        functools.partial(project_far_kernel, len(draft)),
         grid_spec=pltpu.PrefetchScalarGridSpec(
             num_scalar_prefetch=1,
             grid=(2,),
             in_specs=[
                 pl.BlockSpec((1, SHARE, depth), lambda i, rank: (request, far(rank[0], i), 0)),
                 VMEM,
+                *([VMEM] * len(draft)),
                 *([ANY] * len(after)),
             ],
             out_specs=[
                 pl.BlockSpec((1, UNITS, WIDTH, UNIT), lambda i, rank: (i, 0, 0, 0)),
                 pl.BlockSpec((1, UNITS, CODED, UNIT), lambda i, rank: (i, 0, 0, 0)),
+                *[
+                    pl.BlockSpec((4, d.shape[0], WIDTH), lambda i, rank: (0, 0, 0)) for d in draft
+                ],
             ],
         ),
         out_shape=[
             jax.ShapeDtypeStruct((2, UNITS, WIDTH, UNIT), F32),
             jax.ShapeDtypeStruct((2, UNITS, CODED, UNIT), I16),
+            *[jax.ShapeDtypeStruct((4, d.shape[0], WIDTH), F32) for d in draft],
         ],
         compiler_params=ROOM,
         cost_estimate=COST,
         name="project_far",
-    )(rank, hidden, down_t, *after)
+    )(rank, hidden, down_t, *draft, *after)
 
 
 def project_near_kernel(rank, hid_ref, down_ref, *refs):
@@ -464,17 +482,8 @@
     )(rank, slot, own, *got, *sent, *side, gain, cosine, sine, *base, *after)
 
 
-def query_kernel(lat_ref, up_ref, draft_ref, down_ref, *refs):
-    *key_refs, cos_ref, sin_ref, out_ref, split_ref = refs
-
-    @pl.when(pl.program_id(0) == 0)
-    def _():
-        rest = lax.dot_general(draft_ref[...], down_ref[...], NT, preferred_element_type=F32)
-        for n in range(3):
-            term = rest.astype(BF).astype(F32)
-            split_ref[n] = term
-            rest = rest - term
-        split_ref[3] = jnp.zeros_like(rest)
+def query_kernel(lat_ref, up_ref, *refs):
+    *key_refs, cos_ref, sin_ref, out_ref = refs
 
     full = jnp.dot(lat_ref[...], up_ref[...], preferred_element_type=F32)
     for h, key_ref in enumerate(key_refs):
@@ -489,7 +498,7 @@
         )
 
 
-def queries(latents, q_up, kv_up, draft, down_t, cosine, sine, after):
+def queries(latents, q_up, kv_up, cosine, sine, after):
     rows = latents.shape[0]
     heads = q_up.shape[1] // (DN + DR)
     step = 4
@@ -498,32 +507,24 @@
     ]
     whole = lambda i: (0, 0)
     table = pl.BlockSpec((rows, HALF), whole)
-    body = lambda *refs: query_kernel(*refs[:-3], *refs[-2:])
+    body = lambda *refs: query_kernel(*refs[:-2], refs[-1])
     return pl.pallas_call(
         body,
         grid=(heads // step,),
         in_specs=[
             pl.BlockSpec((rows, QL), whole),
             pl.BlockSpec((QL, step * (DN + DR)), lambda i: (0, i)),
-            pl.BlockSpec(draft.shape, whole),
-            pl.BlockSpec(down_t.shape, whole),
             *key_spec,
             table,
             table,
             ANY,
         ],
-        out_specs=[
-            pl.BlockSpec((step, rows, WIDTH), lambda i: (i, 0, 0)),
-            pl.BlockSpec((4, rows, WIDTH), lambda i: (0, 0, 0)),
-        ],
-        out_shape=[
-            jax.ShapeDtypeStruct((heads, rows, WIDTH), F32),
-            jax.ShapeDtypeStruct((4, rows, WIDTH), F32),
-        ],
+        out_specs=pl.BlockSpec((step, rows, WIDTH), lambda i: (i, 0, 0)),
+        out_shape=jax.ShapeDtypeStruct((heads, rows, WIDTH), F32),
         compiler_params=ROOM,
         cost_estimate=COST,
         name="queries",
-    )(latents, q_up, draft, down_t, *([kv_up] * step), cosine, sine, after)
+    )(latents, q_up, *([kv_up] * step), cosine, sine, after)
 
 
 def attend_kernel(requests, rank, first_ref, *refs):
@@ -727,10 +728,11 @@
 
     far_sums, inner, crossed, sent, outer = [], [], [], [], []
 
-    def send_far(r, after):
-        total, codes = project_far(rank, hidden, down_t, r, after)
+    def send_far(r, after, draft=()):
+        total, codes, *terms = project_far(rank, hidden, down_t, r, after, draft)
         far_sums.append(total)
         inner.append(lax.ppermute(codes, "tp", inward))
+        return terms
 
     def first_hop(r, after, carried=()):
         block, *carried = add_on(rank, far_sums[r], inner[r], after=after, carried=carried)
@@ -746,14 +748,12 @@
         return [block]
 
     send_far(0, [])
-    send_far(1, far_sums[:1])
+    (terms,) = send_far(1, far_sums[:1], [draft_hidden])
 
     latents = lax.dynamic_slice_in_dim(query_latent, first_req, RP, 0).reshape(RP * 2, QL)
     new_pos = jnp.tile(PRE_TOK + jnp.arange(2, dtype=jnp.int32), RP)
     new_cos, new_sin = rope_tables(new_pos)
-    query, terms = queries(
-        latents, q_up, kv_up, draft_hidden, down_t, new_cos, new_sin, far_sums[1]
-    )
+    query = queries(latents, q_up, kv_up, new_cos, new_sin, far_sums[1])
     heads = query.shape[0]
     query = query.reshape(heads, RP, 2, WIDTH).transpose(1, 2, 0, 3)
     message = jnp.concatenate(

time: 206 us -> 205 us (level)
    ppermute x6, waiting for transfers between devices: 9.98 us -> 7.78 us  [attend_to(): return (result, [lax.ppermute(result[t], 'tp', [(3, t)]) for t in range(3)])]
    unnamed x64 -> x66, local copies, waits for them, and re-layouts: 7.66 us -> 7.66 us
  transfers between devices with their start and end apart: 24 -> 24, of which waited for: 9 -> 9; matrix products, arithmetic and copies ran while one was open for 3% -> 3% of each run, Pallas kernels for 38% -> 37%
where the time goes in v12:
time: 205 us; the launch traced here: 203 us
  Pallas kernels  86.4 us (42%)
  starting transfers between devices  52.7 us (26%)
  waiting for transfers between devices  42.7 us (21%)
  local copies, waits for them, and re-layouts  11.4 us (6%)
  blocking collectives  6.49 us (3%)
  other arithmetic  2.51 us (1%)
    pallas_call x4, Pallas kernels, project_far(): pl.pallas_call(functools.partial(project_far_kernel, len(draft)), grid_sp...  25.1 us
    ppermute x4, waiting for transfers between devices, second_hop(): outer.append(lax.ppermute(block, 'tp', outward))  21 us
    ppermute x4, starting transfers between devices, send_far(): inner.append(lax.ppermute(codes, 'tp', inward))  17 us
    pallas_call x8, Pallas kernels, add_on(): pl.pallas_call(functools.partial(add_kernel, -1 - len(carried)), grid_spe...  13.8 us
    pallas_call x1, Pallas kernels, project_near(): pl.pallas_call(project_near_kernel, grid_spec=pltpu.PrefetchScalarGridSpe...  13.8 us
    pallas_call x1, Pallas kernels, queries(): pl.pallas_call(body, grid=(heads // step,), in_specs=[pl.BlockSpec((rows,...  12.3 us
    ppermute x2, starting transfers between devices, local_line(): side = [lax.ppermute(codes, 'tp', inward) for codes in side]  10.2 us
    pallas_call x2, Pallas kernels, pages_of(): pl.pallas_call(functools.partial(page_kernel, requests), grid_spec=pltpu....  9.04 us
  transfers between devices with their start and end apart: 24, of which 9 were waited for; matrix products, arithmetic and copies ran while one was open for 3% of the time, Pallas kernels for 37%

profile of v12, /device:TPU:0, one launch (start us, length us, event | category | flops | bytes accessed | tf_op | source)
XLA Modules:
  0.0 203.4 jit_solution(18321102556978216705)
XLA Ops:
  0.7 6.1 %project_far.4 = (f32[2,3,576,128]{3,2,1,0:T(8,128)}, s16[2,3,592,128]{3,2,1,0:T(8,128)(2,1)}) custom-call(s32[1]{0:T(128)} %bitcast.rank, bf16[4,1536,1792]{2,1,0:T(8,128)(2,1)} %bitcast.22, bf16[576,1792]{1,0:T(8,128)(2,1)} %bitcast.27), custom_call_target="tpu_custom_call" | custom-call | flops 1024 | bytes 1024 | tf_op jit(solution)/shard_map/project_far/pallas_call | solution.py:282
  6.7 4.5 %collective-permute-start = (s16[2,3,592,128]{3,2,1,0:T(8,128)(2,1)}, s16[2,3,592,128]{3,2,1,0:T(8,128)(2,1)S(1)}, u32[]{:S(2)}, u32[]{:S(2)}) collective-permute-start(s16[2,3,592,128]{3,2,1,0:T(8,128)(2,1)} %get-tuple-element.27), channel_id=1, source_target_pairs={{0,4},{12,8},{1,5},{13,9},{2,6},{14,10},{3,7},{15,11},{16,20},{28,... | collective-permute-start | bytes 2727944 | tf_op jit(solution)/shard_map/ppermute | solution.py:734
  11.3 6.8 %project_far.5 = (f32[2,3,576,128]{3,2,1,0:T(8,128)}, s16[2,3,592,128]{3,2,1,0:T(8,128)(2,1)}, f32[4,8,576]{2,1,0:T(8,128)}) custom-call(s32[1]{0:T(128)} %bitcast.rank, bf16[4,1536,1792]{2,1,0:T(8,128)(2,1)} %bitcast.23, bf16[576,1792]{1,0:T(8,128)(2,1)} %bitcast.28, bf16[8,1792]{1,0:T(8,128)(2,1)} %refs_0_.2, ...), custom_call_target="tpu_custom_call" | custom-call | flops 1024 | bytes 1024 | tf_op jit(solution)/shard_map/project_far/pallas_call | solution.py:282
  18.1 1.3 collective-permute-start.2
  20.9 12.3 %queries.1 = f32[32,8,576]{2,1,0:T(8,128)} custom-call(bf16[8,1536]{1,0:T(8,128)(2,1)} %reshape.129.refs_0_, bf16[1536,6144]{1,0:T(8,128)(2,1)} %refs_1_.2, bf16[512,8192]{1,0:T(8,128)(2,1)} %refs_7_.1, bf16[512,8192]{1,0:T(8,128)(2,1)} %refs_7_.1, bf16[512,8192]{1,0:T(8,128)(2,1)} %refs_7_.1, bf16[512,8192]{1,0:T(8,128)(2,1)} %refs_7_.1, ...), custom_call_target="tpu_custom_call" | custom-call | flops 1024 | bytes 1024 | tf_op jit(solution)/shard_map/queries/pallas_call | solution.py:511
  35.5 1.7 add_on.8.refs_0_
  37.2 1.6 collective-permute-start.1
  38.8 4.4 %collective-permute-start.3 = (bf16[288,576]{1,0:T(8,128)(2,1)S(1)}, bf16[288,576]{1,0:T(8,128)(2,1)S(1)}, u32[]{:S(2)}, u32[]{:S(2)}) collective-permute-start(bf16[288,576]{1,0:T(8,128)(2,1)S(1)} %pad_maximum_fusion.refs_0_.refs_3_.refs_7_), channel_id=1, source_target_pairs={{0,12},{1,13},{2,14},{3,15},{16,28},{17,29},{18,30},{19,31}} | collective-permute-start | bytes 995336 | tf_op jit(solution)/shard_map/ppermute | solution.py:762
  44.6 6.1 %project_far.6 = (f32[2,3,576,128]{3,2,1,0:T(8,128)}, s16[2,3,592,128]{3,2,1,0:T(8,128)(2,1)}) custom-call(s32[1]{0:T(128)} %bitcast.rank, bf16[4,1536,1792]{2,1,0:T(8,128)(2,1)} %bitcast.24, bf16[576,1792]{1,0:T(8,128)(2,1)} %bitcast.29, s16[2,3,592,128]{3,2,1,0:T(8,128)(2,1)} %copy-done.10), custom_call_target="tpu_custom_call" | custom-call | flops 1024 | bytes 1024 | tf_op jit(solution)/shard_map/project_far/pallas_call | solution.py:282
  51.6 5.2 %collective-permute-start.8 = (s16[2,3,592,128]{3,2,1,0:T(8,128)(2,1)}, s16[2,3,592,128]{3,2,1,0:T(8,128)(2,1)}, u32[]{:S(2)}, u32[]{:S(2)}) collective-permute-start(s16[2,3,592,128]{3,2,1,0:T(8,128)(2,1)} %get-tuple-element.35), channel_id=1, source_target_pairs={{0,4},{12,8},{1,5},{13,9},{2,6},{14,10},{3,7},{15,11},{16,20},{28,... | collective-permute-start | bytes 2727944 | tf_op jit(solution)/shard_map/ppermute | solution.py:734
  56.8 13.8 %project_near.1 = (f32[3,2,4,576,128]{4,3,2,1,0:T(8,128)}, s16[1,4,592,128]{3,2,1,0:T(8,128)(2,1)}, s16[2,4,592,128]{3,2,1,0:T(8,128)(2,1)}) custom-call(s32[1]{0:T(128)} %bitcast.rank, bf16[4,1536,1792]{2,1,0:T(8,128)(2,1)} %bitcast.25, bf16[576,1792]{1,0:T(8,128)(2,1)} %bitcast.30, f32[2,3,576,128]{3,2,1,0:T(8,128)} %get-tuple-element.30.refs_0_.own_ref), custom_call_target="tpu_custom_call" | custom-call | flops 1024 | bytes 1024 | tf_op jit(solution)/shard_map/project_near/pallas_call | solution.py:330
  70.6 1.2 copy-done.14
  71.8 1.4 add_on.9.refs_0_
  73.2 1.6 collective-permute-start.7
  74.8 1.7 add_on.10.refs_0_
  76.5 1.3 collective-permute-start.9
  77.9 6.1 %project_far.7 = (f32[2,3,576,128]{3,2,1,0:T(8,128)}, s16[2,3,592,128]{3,2,1,0:T(8,128)(2,1)}) custom-call(s32[1]{0:T(128)} %bitcast.rank, bf16[4,1536,1792]{2,1,0:T(8,128)(2,1)} %bitcast.26, bf16[576,1792]{1,0:T(8,128)(2,1)} %bitcast.31, s16[2,3,592,128]{3,2,1,0:T(8,128)(2,1)} %copy-done.2), custom_call_target="tpu_custom_call" | custom-call | flops 1024 | bytes 1024 | tf_op jit(solution)/shard_map/project_far/pallas_call | solution.py:282
  84.0 5.9 %collective-permute-start.6 = (s16[2,3,592,128]{3,2,1,0:T(8,128)(2,1)}, s16[2,3,592,128]{3,2,1,0:T(8,128)(2,1)}, u32[]{:S(2)}, u32[]{:S(2)}) collective-permute-start(s16[2,3,592,128]{3,2,1,0:T(8,128)(2,1)} %get-tuple-element.34), channel_id=1, source_target_pairs={{0,4},{12,8},{1,5},{13,9},{2,6},{14,10},{3,7},{15,11},{16,20},{28,... | collective-permute-start | bytes 2727944 | tf_op jit(solution)/shard_map/ppermute | solution.py:734
  89.9 2.5 %add_on.11 = (s16[2,3,592,128]{3,2,1,0:T(8,128)(2,1)}, s16[1,4,592,128]{3,2,1,0:T(8,128)(2,1)}) custom-call(s32[1]{0:T(128)} %bitcast.rank, f32[2,3,576,128]{3,2,1,0:T(8,128)} %get-tuple-element.30.refs_0_.own_ref, s16[2,3,592,128]{3,2,1,0:T(8,128)(2,1)} %collective-permute-done.8.got_ref, ...), custom_call_target="tpu_custom_call", output_to_operand_aliasing={{1}: (4, {})} | custom-call | flops 1024 | bytes 1024 | tf_op jit(solution)/shard_map/add_on/pallas_call | solution.py:376
  92.4 1.6 collective-permute-start.11
  94.0 1.7 add_on.12.refs_0_
  95.7 2.6 %collective-permute-done.9.refs_1_.refs_9_.refs_0_ = s16[2,3,592,128]{3,2,1,0:T(8,128)(2,1)} collective-permute-done((s16[2,3,592,128]{3,2,1,0:T(8,128)(2,1)S(1)}, s16[2,3,592,128]{3,2,1,0:T(8,128)(2,1)}, u32[]{:S(2)}, u32[]{:S(2)}) %collective-permute-start.9) | collective-permute-done | bytes 909344 | tf_op jit(solution)/shard_map/ppermute | solution.py:747
  98.3 1.3 collective-permute-start.12
  99.6 5.5 %collective-permute-start.13 = (s16[1,4,592,128]{3,2,1,0:T(8,128)(2,1)}, s16[1,4,592,128]{3,2,1,0:T(8,128)(2,1)S(1)}, u32[]{:S(2)}, u32[]{:S(2)}) collective-permute-start(s16[1,4,592,128]{3,2,1,0:T(8,128)(2,1)} %get-tuple-element.38), channel_id=1, source_target_pairs={{0,4},{12,8},{1,5},{13,9},{2,6},{14,10},{3,7},{15,11},{16,20},{28,... | collective-permute-start | bytes 1818632 | tf_op jit(solution)/shard_map/ppermute | solution.py:776
  105.5 4.4 %collective-permute-done.6.got_ref = s16[2,3,592,128]{3,2,1,0:T(8,128)(2,1)} collective-permute-done((s16[2,3,592,128]{3,2,1,0:T(8,128)(2,1)}, s16[2,3,592,128]{3,2,1,0:T(8,128)(2,1)}, u32[]{:S(2)}, u32[]{:S(2)}) %collective-permute-start.6) | collective-permute-done | bytes 909344 | tf_op jit(solution)/shard_map/ppermute | solution.py:734
  109.9 1.7 add_on.13.refs_0_
  112.5 1.7 add_on.14.refs_0_
  114.2 5.0 %collective-permute-done.13.refs_2_.refs_6_ = s16[1,4,592,128]{3,2,1,0:T(8,128)(2,1)S(1)} collective-permute-done((s16[1,4,592,128]{3,2,1,0:T(8,128)(2,1)}, s16[1,4,592,128]{3,2,1,0:T(8,128)(2,1)S(1)}, u32[]{:S(2)}, u32[]{:S(2)}) %collective-permute-start.13) | collective-permute-done | bytes 606240 | tf_op jit(solution)/shard_map/ppermute | solution.py:776
  119.3 1.3 collective-permute-start.14
  120.6 4.7 %collective-permute-start.16 = (s16[2,4,592,128]{3,2,1,0:T(8,128)(2,1)S(1)}, s16[2,4,592,128]{3,2,1,0:T(8,128)(2,1)S(1)}, u32[]{:S(2)}, u32[]{:S(2)}) collective-permute-start(s16[2,4,592,128]{3,2,1,0:T(8,128)(2,1)S(1)} %copy-done.30), channel_id=1, source_target_pairs={{0,4},{12,8},{1,5},{13,9},{2,6},{14,10},{3,7},{15,11},{16,20},{28,... | collective-permute-start | bytes 3637256 | tf_op jit(solution)/shard_map/ppermute | solution.py:776
  125.3 1.5 add_on.15.refs_0_
  126.7 12.9 %collective-permute-done.14.refs_1_.refs_11_.refs_2_ = s16[2,3,592,128]{3,2,1,0:T(8,128)(2,1)S(1)} collective-permute-done((s16[2,3,592,128]{3,2,1,0:T(8,128)(2,1)S(1)}, s16[2,3,592,128]{3,2,1,0:T(8,128)(2,1)S(1)}, u32[]{:S(2)}, u32[]{:S(2)}) %collective-permute-start.14) | collective-permute-done | bytes 909344 | tf_op jit(solution)/shard_map/ppermute | solution.py:747
  139.7 1.5 collective-permute-start.15
  141.2 4.1 %attend.2 = (bf16[3,64,512]{2,1,0:T(8,128)(2,1)S(1)}, bf16[3,64,512]{2,1,0:T(8,128)(2,1)S(1)}, bf16[3,64,512]{2,1,0:T(8,128)(2,1)S(1)}, bf16[3,64,512]{2,1,0:T(8,128)(2,1)S(1)}) custom-call(s32[1]{0:T(128)} %bitcast.rank, s32[1]{0:T(128)} %bitcast.8.first_ref, bf16[288,576]{1,0:T(8,128)(2,1)S(1)} %collective-permute-done.3.refs_1_.refs_0_.refs_4_, ...), custom_call_target="tpu_custom_call" | custom-call | flops 1024 | bytes 1024 | tf_op jit(solution)/shard_map/attend/pallas_call | solution.py:611
  146.0 1.3 collective-permute-start.17
  149.9 5.8 %pages.2.refs_7_ = bf16[4,576,384]{2,1,0:T(8,128)(2,1)} custom-call(s32[1]{0:T(128)} %bitcast.rank, s32[4]{0:T(128)S(1)} %dynamic_slice.9.slot, f32[3,2,4,576,128]{4,3,2,1,0:T(8,128)} %get-tuple-element.31.refs_0_.own_ref.refs_8_, s16[2,3,592,128]{3,2,1,0:T(8,128)(2,1)} %collective-permute-done.9.refs_1_.refs_9_.refs_0_, ...), custom_call_target="tpu_custom_call" | custom-call | flops 1024 | bytes 1024 | tf_op jit(solution)/shard_map/pages/pallas_call | solution.py:455
  155.7 2.2 %collective-permute-done.17.refs_8_ = bf16[3,64,512]{2,1,0:T(8,128)(2,1)S(1)} collective-permute-done((bf16[3,64,512]{2,1,0:T(8,128)(2,1)S(1)}, bf16[3,64,512]{2,1,0:T(8,128)(2,1)S(1)}, u32[]{:S(2)}, u32[]{:S(2)}) %collective-permute-start.17) | collective-permute-done | bytes 196640 | tf_op jit(solution)/shard_map/ppermute | solution.py:797
  157.9 5.5 %collective-permute-done.15.refs_0_.refs_9_ = s16[2,3,592,128]{3,2,1,0:T(8,128)(2,1)S(1)} collective-permute-done((s16[2,3,592,128]{3,2,1,0:T(8,128)(2,1)S(1)}, s16[2,3,592,128]{3,2,1,0:T(8,128)(2,1)S(1)}, u32[]{:S(2)}, u32[]{:S(2)}) %collective-permute-start.15) | collective-permute-done | bytes 909344 | tf_op jit(solution)/shard_map/ppermute | solution.py:747
  164.3 3.3 %pages.3.refs_18_.refs_8_ = bf16[4,576,384]{2,1,0:T(8,128)(2,1)} custom-call(s32[1]{0:T(128)} %bitcast.rank, s32[4]{0:T(128)S(1)} %dynamic_slice.9.slot, f32[3,2,4,576,128]{4,3,2,1,0:T(8,128)} %get-tuple-element.31.refs_0_.own_ref.refs_8_, s16[2,3,592,128]{3,2,1,0:T(8,128)(2,1)} %copy-done.27, ...), custom_call_target="tpu_custom_call", output_to_operand_aliasing={{}: (10, {})} | custom-call | flops 1024 | bytes 1024 | tf_op jit(solution)/shard_map/pages/pallas_call | solution.py:455
  168.3 3.7 %all-to-all-start = ((bf16[4,576,384]{2,1,0:T(8,128)(2,1)}), bf16[4,576,384]{2,1,0:T(8,128)(2,1)S(1)}, u32[]{:S(2)}, u32[]{:S(2)}) async-start(bf16[4,576,384]{2,1,0:T(8,128)(2,1)} %pages.3.refs_18_.refs_8_), calls=%async_computation | async-start | bytes 3538944 | tf_op jit(solution)/shard_map/all_to_all | solution.py:825
  173.2 1.8 attend.3
  175.0 1.3 collective-permute-start.20
  177.7 5.6 %collective-permute-done.20 = bf16[1,64,512]{2,1,0:T(8,128)(2,1)S(1)} collective-permute-done((bf16[1,64,512]{2,1,0:T(8,128)(2,1)S(1)}, bf16[1,64,512]{2,1,0:T(8,128)(2,1)S(1)}, u32[]{:S(2)}, u32[]{:S(2)}) %collective-permute-start.20) | collective-permute-done | bytes 65568 | tf_op jit(solution)/shard_map/ppermute | solution.py:797
  183.6 1.2 reshape.139.o_ref
  185.4 5.2 %heads_out.1.placed_ref = bf16[4,2,4096]{2,1,0:T(2,128)(2,1)} custom-call(s32[4]{0:T(128)} %copy-done.25, f32[32,8,512]{2,1,0:T(8,128)} %reshape.139.o_ref, f32[8,128]{1,0:T(8,128)} %broadcast_in_dim.2.keep_ref, bf16[512,8192]{1,0:T(8,128)(2,1)} %refs_7_.1, bf16[512,8192]{1,0:T(8,128)(2,1)} %refs_7_.1, bf16[512,8192]{1,0:T(8,128)(2,1)} %refs_7_.1, ...), custom_call_target="tpu_custom_call" | custom-call | flops 1024 | bytes 1024 | tf_op jit(solution)/shard_map/heads_out/pallas_call | solution.py:657
  190.7 3.5 %all-to-all-done.pages_ref = bf16[4,576,384]{2,1,0:T(8,128)(2,1)S(1)} async-done(((bf16[4,576,384]{2,1,0:T(8,128)(2,1)}), bf16[4,576,384]{2,1,0:T(8,128)(2,1)S(1)}, u32[]{:S(2)}, u32[]{:S(2)}) %all-to-all-start) | async-done | bytes 1769504 | tf_op jit(solution)/shard_map/all_to_all | solution.py:825
  195.0 1.2 emit.1
  196.2 6.5 %all_to_all.10 = bf16[4,2,4096]{2,1,0:T(2,128)(2,1)S(1)} all-to-all(bf16[4,2,4096]{2,1,0:T(2,128)(2,1)S(1)} %get-tuple-element.48), channel_id=1, replica_groups=mesh['groups'=2,'tp'=4,'pd'=4] {'pd'}, dimensions={0} | all-to-all | bytes 131072 | tf_op jit(solution)/shard_map/all_to_all | solution.py:844
  (116 shorter events, 17.3 us)
Async XLA Ops:
  0.6 18.8 %copy-start = (bf16[16,2,1536]{2,1,0:T(2,128)(2,1)S(1)}, bf16[16,2,1536]{2,1,0:T(2,128)(2,1)}, u32[]{:S(2)}) copy-start(bf16[16,2,1536]{2,1,0:T(2,128)(2,1)} %param.14) | copy-start | bytes 294916
  6.7 27.8 %collective-permute-start = (s16[2,3,592,128]{3,2,1,0:T(8,128)(2,1)}, s16[2,3,592,128]{3,2,1,0:T(8,128)(2,1)S(1)}, u32[]{:S(2)}, u32[]{:S(2)}) collective-permute-start(s16[2,3,592,128]{3,2,1,0:T(8,128)(2,1)} %get-tuple-element.27), channel_id=1, source_target_pairs={{0,4},{12,8},{1,5},{13,9},{2,6},{14,10},{3,7},{15,11},{16,20},{28,... | collective-permute-start | bytes 2727944 | tf_op jit(solution)/shard_map/ppermute | solution.py:734
  18.1 33.5 %collective-permute-start.2 = (s16[2,3,592,128]{3,2,1,0:T(8,128)(2,1)}, s16[2,3,592,128]{3,2,1,0:T(8,128)(2,1)S(1)}, u32[]{:S(2)}, u32[]{:S(2)}) collective-permute-start(s16[2,3,592,128]{3,2,1,0:T(8,128)(2,1)} %get-tuple-element.32), channel_id=1, source_target_pairs={{0,4},{12,8},{1,5},{13,9},{2,6},{14,10},{3,7},{15,11},{16,20},{28,... | collective-permute-start | bytes 2727944 | tf_op jit(solution)/shard_map/ppermute | solution.py:734
  20.9 13.5 %copy-start.29 = (f32[4,8,576]{2,1,0:T(8,128)S(1)}, f32[4,8,576]{2,1,0:T(8,128)}, u32[]{:S(2)}) copy-start(f32[4,8,576]{2,1,0:T(8,128)} %get-tuple-element.29) | copy-start | bytes 221188
  34.5 9.4 %copy-start.6 = (bf16[288,576]{1,0:T(8,128)(2,1)}, bf16[288,576]{1,0:T(8,128)(2,1)S(1)}, u32[]{:S(2)}) copy-start(bf16[288,576]{1,0:T(8,128)(2,1)S(1)} %pad_maximum_fusion.refs_0_.refs_3_.refs_7_) | copy-start | bytes 995332
  37.2 7.4 %copy-start.10 = (s16[2,3,592,128]{3,2,1,0:T(8,128)(2,1)}, s16[2,3,592,128]{3,2,1,0:T(8,128)(2,1)S(1)}, u32[]{:S(2)}) copy-start(s16[2,3,592,128]{3,2,1,0:T(8,128)(2,1)S(1)} %add_on.8.refs_0_) | copy-start | bytes 2727940
  37.2 36.0 %collective-permute-start.1 = (s16[2,3,592,128]{3,2,1,0:T(8,128)(2,1)S(1)}, s16[2,3,592,128]{3,2,1,0:T(8,128)(2,1)}, u32[]{:S(2)}, u32[]{:S(2)}) collective-permute-start(s16[2,3,592,128]{3,2,1,0:T(8,128)(2,1)S(1)} %add_on.8.refs_0_), channel_id=1, source_target_pairs={{4,8},{8,4},{5,9},{9,5},{6,10},{10,6},{7,11},{11,7},{20,24},{24,20... | collective-permute-start | bytes 2727944 | tf_op jit(solution)/shard_map/ppermute | solution.py:739
  38.8 37.7 %collective-permute-start.3 = (bf16[288,576]{1,0:T(8,128)(2,1)S(1)}, bf16[288,576]{1,0:T(8,128)(2,1)S(1)}, u32[]{:S(2)}, u32[]{:S(2)}) collective-permute-start(bf16[288,576]{1,0:T(8,128)(2,1)S(1)} %pad_maximum_fusion.refs_0_.refs_3_.refs_7_), channel_id=1, source_target_pairs={{0,12},{1,13},{2,14},{3,15},{16,28},{17,29},{18,30},{19,31}} | collective-permute-start | bytes 995336 | tf_op jit(solution)/shard_map/ppermute | solution.py:762
  43.2 33.3 %collective-permute-start.4 = (bf16[288,576]{1,0:T(8,128)(2,1)S(1)}, bf16[288,576]{1,0:T(8,128)(2,1)S(1)}, u32[]{:S(2)}, u32[]{:S(2)}) collective-permute-start(bf16[288,576]{1,0:T(8,128)(2,1)S(1)} %pad_maximum_fusion.refs_0_.refs_3_.refs_7_), channel_id=1, source_target_pairs={{4,12},{5,13},{6,14},{7,15},{20,28},{21,29},{22,30},{23,31}} | collective-permute-start | bytes 995336 | tf_op jit(solution)/shard_map/ppermute | solution.py:762
  43.9 32.6 %collective-permute-start.5 = (bf16[288,576]{1,0:T(8,128)(2,1)S(1)}, bf16[288,576]{1,0:T(8,128)(2,1)S(1)}, u32[]{:S(2)}, u32[]{:S(2)}) collective-permute-start(bf16[288,576]{1,0:T(8,128)(2,1)S(1)} %pad_maximum_fusion.refs_0_.refs_3_.refs_7_), channel_id=1, source_target_pairs={{8,12},{9,13},{10,14},{11,15},{24,28},{25,29},{26,30},{27,31}} | collective-permute-start | bytes 995336 | tf_op jit(solution)/shard_map/ppermute | solution.py:762
  51.6 19.0 %copy-start.13 = (s16[2,3,592,128]{3,2,1,0:T(8,128)(2,1)}, s16[2,3,592,128]{3,2,1,0:T(8,128)(2,1)S(1)}, u32[]{:S(2)}) copy-start(s16[2,3,592,128]{3,2,1,0:T(8,128)(2,1)S(1)} %collective-permute-done.2.got_ref) | copy-start | bytes 2727940
  51.6 38.3 %collective-permute-start.8 = (s16[2,3,592,128]{3,2,1,0:T(8,128)(2,1)}, s16[2,3,592,128]{3,2,1,0:T(8,128)(2,1)}, u32[]{:S(2)}, u32[]{:S(2)}) collective-permute-start(s16[2,3,592,128]{3,2,1,0:T(8,128)(2,1)} %get-tuple-element.35), channel_id=1, source_target_pairs={{0,4},{12,8},{1,5},{13,9},{2,6},{14,10},{3,7},{15,11},{16,20},{28,... | collective-permute-start | bytes 2727944 | tf_op jit(solution)/shard_map/ppermute | solution.py:734
  73.2 1.6 copy-start.12
  73.2 20.8 %collective-permute-start.7 = (s16[2,3,592,128]{3,2,1,0:T(8,128)(2,1)S(1)}, s16[2,3,592,128]{3,2,1,0:T(8,128)(2,1)}, u32[]{:S(2)}, u32[]{:S(2)}) collective-permute-start(s16[2,3,592,128]{3,2,1,0:T(8,128)(2,1)S(1)} %add_on.9.refs_0_), channel_id=1, source_target_pairs={{4,8},{8,4},{5,9},{9,5},{6,10},{10,6},{7,11},{11,7},{20,24},{24,20... | collective-permute-start | bytes 2727944 | tf_op jit(solution)/shard_map/ppermute | solution.py:739
  76.5 7.5 %copy-start.7 = (bf16[288,576]{1,0:T(8,128)(2,1)}, bf16[288,576]{1,0:T(8,128)(2,1)S(1)}, u32[]{:S(2)}) copy-start(bf16[288,576]{1,0:T(8,128)(2,1)S(1)} %collective-permute-done.5.refs_3_.refs_2_.refs_6_) | copy-start | bytes 995332
  76.5 1.3 copy-start.2
  76.5 21.7 %collective-permute-start.9 = (s16[2,3,592,128]{3,2,1,0:T(8,128)(2,1)S(1)}, s16[2,3,592,128]{3,2,1,0:T(8,128)(2,1)}, u32[]{:S(2)}, u32[]{:S(2)}) collective-permute-start(s16[2,3,592,128]{3,2,1,0:T(8,128)(2,1)S(1)} %hold.4.refs_0_.refs_3_), channel_id=1, source_target_pairs={{8,12},{4,0},{9,13},{5,1},{10,14},{6,2},{11,15},{7,3},{24,28},{20,... | collective-permute-start | bytes 2727944 | tf_op jit(solution)/shard_map/ppermute | solution.py:747
  84.0 25.9 %collective-permute-start.6 = (s16[2,3,592,128]{3,2,1,0:T(8,128)(2,1)}, s16[2,3,592,128]{3,2,1,0:T(8,128)(2,1)}, u32[]{:S(2)}, u32[]{:S(2)}) collective-permute-start(s16[2,3,592,128]{3,2,1,0:T(8,128)(2,1)} %get-tuple-element.34), channel_id=1, source_target_pairs={{0,4},{12,8},{1,5},{13,9},{2,6},{14,10},{3,7},{15,11},{16,20},{28,... | collective-permute-start | bytes 2727944 | tf_op jit(solution)/shard_map/ppermute | solution.py:734
  92.4 19.9 %collective-permute-start.11 = (s16[2,3,592,128]{3,2,1,0:T(8,128)(2,1)}, s16[2,3,592,128]{3,2,1,0:T(8,128)(2,1)}, u32[]{:S(2)}, u32[]{:S(2)}) collective-permute-start(s16[2,3,592,128]{3,2,1,0:T(8,128)(2,1)} %get-tuple-element.37.refs_0_), channel_id=1, source_target_pairs={{4,8},{8,4},{5,9},{9,5},{6,10},{10,6},{7,11},{11,7},{20,24},{24,20... | collective-permute-start | bytes 2727944 | tf_op jit(solution)/shard_map/ppermute | solution.py:739
  98.3 11.7 %copy-start.4 = (s16[2,3,592,128]{3,2,1,0:T(8,128)(2,1)}, s16[2,3,592,128]{3,2,1,0:T(8,128)(2,1)S(1)}, u32[]{:S(2)}) copy-start(s16[2,3,592,128]{3,2,1,0:T(8,128)(2,1)S(1)} %hold.5.refs_0_.refs_4_) | copy-start | bytes 2727940
  98.3 21.0 %collective-permute-start.12 = (s16[2,3,592,128]{3,2,1,0:T(8,128)(2,1)S(1)}, s16[2,3,592,128]{3,2,1,0:T(8,128)(2,1)}, u32[]{:S(2)}, u32[]{:S(2)}) collective-permute-start(s16[2,3,592,128]{3,2,1,0:T(8,128)(2,1)S(1)} %hold.5.refs_0_.refs_4_), channel_id=1, source_target_pairs={{8,12},{4,0},{9,13},{5,1},{10,14},{6,2},{11,15},{7,3},{24,28},{20,... | collective-permute-start | bytes 2727944 | tf_op jit(solution)/shard_map/ppermute | solution.py:747
  99.6 19.7 %collective-permute-start.13 = (s16[1,4,592,128]{3,2,1,0:T(8,128)(2,1)}, s16[1,4,592,128]{3,2,1,0:T(8,128)(2,1)S(1)}, u32[]{:S(2)}, u32[]{:S(2)}) collective-permute-start(s16[1,4,592,128]{3,2,1,0:T(8,128)(2,1)} %get-tuple-element.38), channel_id=1, source_target_pairs={{0,4},{12,8},{1,5},{13,9},{2,6},{14,10},{3,7},{15,11},{16,20},{28,... | collective-permute-start | bytes 1818632 | tf_op jit(solution)/shard_map/ppermute | solution.py:776
  111.6 13.6 %collective-permute-start.10 = (s16[2,3,592,128]{3,2,1,0:T(8,128)(2,1)S(1)}, s16[2,3,592,128]{3,2,1,0:T(8,128)(2,1)S(1)}, u32[]{:S(2)}, u32[]{:S(2)}) collective-permute-start(s16[2,3,592,128]{3,2,1,0:T(8,128)(2,1)S(1)} %add_on.13.refs_0_), channel_id=1, source_target_pairs={{4,8},{8,4},{5,9},{9,5},{6,10},{10,6},{7,11},{11,7},{20,24},{24,20... | collective-permute-start | bytes 2727944 | tf_op jit(solution)/shard_map/ppermute | solution.py:739
  114.2 6.3 %copy-start.30 = (s16[2,4,592,128]{3,2,1,0:T(8,128)(2,1)S(1)}, s16[2,4,592,128]{3,2,1,0:T(8,128)(2,1)}, u32[]{:S(2)}) copy-start(s16[2,4,592,128]{3,2,1,0:T(8,128)(2,1)} %get-tuple-element.39) | copy-start | bytes 3637252
  119.3 6.0 %copy-start.3 = (s16[2,3,592,128]{3,2,1,0:T(8,128)(2,1)}, s16[2,3,592,128]{3,2,1,0:T(8,128)(2,1)S(1)}, u32[]{:S(2)}) copy-start(s16[2,3,592,128]{3,2,1,0:T(8,128)(2,1)S(1)} %hold.6.refs_0_.refs_5_) | copy-start | bytes 2727940
  119.3 20.4 %collective-permute-start.14 = (s16[2,3,592,128]{3,2,1,0:T(8,128)(2,1)S(1)}, s16[2,3,592,128]{3,2,1,0:T(8,128)(2,1)S(1)}, u32[]{:S(2)}, u32[]{:S(2)}) collective-permute-start(s16[2,3,592,128]{3,2,1,0:T(8,128)(2,1)S(1)} %hold.6.refs_0_.refs_5_), channel_id=1, source_target_pairs={{8,12},{4,0},{9,13},{5,1},{10,14},{6,2},{11,15},{7,3},{24,28},{20,... | collective-permute-start | bytes 2727944 | tf_op jit(solution)/shard_map/ppermute | solution.py:747
  120.6 28.2 %collective-permute-start.16 = (s16[2,4,592,128]{3,2,1,0:T(8,128)(2,1)S(1)}, s16[2,4,592,128]{3,2,1,0:T(8,128)(2,1)S(1)}, u32[]{:S(2)}, u32[]{:S(2)}) collective-permute-start(s16[2,4,592,128]{3,2,1,0:T(8,128)(2,1)S(1)} %copy-done.30), channel_id=1, source_target_pairs={{0,4},{12,8},{1,5},{13,9},{2,6},{14,10},{3,7},{15,11},{16,20},{28,... | collective-permute-start | bytes 3637256 | tf_op jit(solution)/shard_map/ppermute | solution.py:776
  126.7 14.5 %copy-start.18 = (s32[16,1536]{1,0:T(8,128)S(1)}, s32[16,1536]{1,0:T(8,128)}, u32[]{:S(2)}) copy-start(s32[16,1536]{1,0:T(8,128)} %refs_14_.1) | copy-start | bytes 294916
  126.7 14.5 %copy-start.22 = (f32[8,32]{1,0:T(8,128)S(1)}, f32[8,32]{1,0:T(8,128)}, u32[]{:S(2)}) copy-start(f32[8,32]{1,0:T(8,128)} %get-tuple-element.54.refs_7_.refs_19_.refs_17_) | copy-start | bytes 3076
  126.7 14.5 %copy-start.23 = (f32[8,32]{1,0:T(8,128)S(1)}, f32[8,32]{1,0:T(8,128)}, u32[]{:S(2)}) copy-start(f32[8,32]{1,0:T(8,128)} %get-tuple-element.55.refs_6_.refs_18_.refs_16_) | copy-start | bytes 3076
  126.7 14.5 %copy-start.24 = (f32[512]{0:T(512)S(1)}, f32[512]{0:T(512)}, u32[]{:S(2)}) copy-start(f32[512]{0:T(512)} %param.13) | copy-start | bytes 6148
  139.7 1.5 copy-start.9
  139.7 1.5 copy-start.5
  139.7 23.7 %collective-permute-start.15 = (s16[2,3,592,128]{3,2,1,0:T(8,128)(2,1)S(1)}, s16[2,3,592,128]{3,2,1,0:T(8,128)(2,1)S(1)}, u32[]{:S(2)}, u32[]{:S(2)}) collective-permute-start(s16[2,3,592,128]{3,2,1,0:T(8,128)(2,1)S(1)} %hold.7.refs_20_.refs_1_), channel_id=1, source_target_pairs={{8,12},{4,0},{9,13},{5,1},{10,14},{6,2},{11,15},{7,3},{24,28},{20,... | collective-permute-start | bytes 2727944 | tf_op jit(solution)/shard_map/ppermute | solution.py:747
  141.2 7.4 %copy-start.31 = (s32[16]{0:T(128)S(1)}, s32[16]{0:T(128)}, u32[]{:S(2)}) copy-start(s32[16]{0:T(128)} %param.17) | copy-start | bytes 196
  146.0 11.9 %collective-permute-start.17 = (bf16[3,64,512]{2,1,0:T(8,128)(2,1)S(1)}, bf16[3,64,512]{2,1,0:T(8,128)(2,1)S(1)}, u32[]{:S(2)}, u32[]{:S(2)}) collective-permute-start(bf16[3,64,512]{2,1,0:T(8,128)(2,1)S(1)} %get-tuple-element.40.refs_11_), channel_id=1, source_target_pairs={{12,0},{13,1},{14,2},{15,3},{28,16},{29,17},{30,18},{31,19}} | collective-permute-start | bytes 589832 | tf_op jit(solution)/shard_map/ppermute | solution.py:797
  147.3 10.6 %collective-permute-start.18 = (bf16[3,64,512]{2,1,0:T(8,128)(2,1)S(1)}, bf16[3,64,512]{2,1,0:T(8,128)(2,1)S(1)}, u32[]{:S(2)}, u32[]{:S(2)}) collective-permute-start(bf16[3,64,512]{2,1,0:T(8,128)(2,1)S(1)} %get-tuple-element.41), channel_id=1, source_target_pairs={{12,4},{13,5},{14,6},{15,7},{28,20},{29,21},{30,22},{31,23}} | collective-permute-start | bytes 589832 | tf_op jit(solution)/shard_map/ppermute | solution.py:797
  148.0 9.9 %collective-permute-start.19 = (bf16[3,64,512]{2,1,0:T(8,128)(2,1)S(1)}, bf16[3,64,512]{2,1,0:T(8,128)(2,1)S(1)}, u32[]{:S(2)}, u32[]{:S(2)}) collective-permute-start(bf16[3,64,512]{2,1,0:T(8,128)(2,1)S(1)} %get-tuple-element.42), channel_id=1, source_target_pairs={{12,8},{13,9},{14,10},{15,11},{28,24},{29,25},{30,26},{31,27}} | collective-permute-start | bytes 589832 | tf_op jit(solution)/shard_map/ppermute | solution.py:797
  148.7 14.6 %copy-start.25 = (s32[4]{0:T(128)}, s32[4]{0:T(128)S(1)}, u32[]{:S(2)}) copy-start(s32[4]{0:T(128)S(1)} %dynamic_slice.9.slot) | copy-start | bytes 52
  168.3 3.7 %copy-start.32 = (s32[16]{0:T(128)S(1)}, s32[16]{0:T(128)}, u32[]{:S(2)}) copy-start(s32[16]{0:T(128)} %param.19) | copy-start | bytes 196
  168.3 4.0 %copy-start.8 = (bf16[288,576]{1,0:T(8,128)(2,1)S(1)}, bf16[288,576]{1,0:T(8,128)(2,1)}, u32[]{:S(2)}) copy-start(bf16[288,576]{1,0:T(8,128)(2,1)} %copy-done.7) | copy-start | bytes 995332
  168.3 25.9 %all-to-all-start = ((bf16[4,576,384]{2,1,0:T(8,128)(2,1)}), bf16[4,576,384]{2,1,0:T(8,128)(2,1)S(1)}, u32[]{:S(2)}, u32[]{:S(2)}) async-start(bf16[4,576,384]{2,1,0:T(8,128)(2,1)} %pages.3.refs_18_.refs_8_), calls=%async_computation | async-start | bytes 3538944 | tf_op jit(solution)/shard_map/all_to_all | solution.py:825
  173.2 4.5 %copy-start.16 = (bf16[3,64,512]{2,1,0:T(8,128)(2,1)S(1)}, bf16[3,64,512]{2,1,0:T(8,128)(2,1)}, u32[]{:S(2)}) copy-start(bf16[3,64,512]{2,1,0:T(8,128)(2,1)} %copy-done.15) | copy-start | bytes 589828
  173.2 4.5 %copy-start.21 = (bf16[3,64,512]{2,1,0:T(8,128)(2,1)S(1)}, bf16[3,64,512]{2,1,0:T(8,128)(2,1)}, u32[]{:S(2)}) copy-start(bf16[3,64,512]{2,1,0:T(8,128)(2,1)} %copy-done.20) | copy-start | bytes 589828
  175.0 8.3 %collective-permute-start.20 = (bf16[1,64,512]{2,1,0:T(8,128)(2,1)S(1)}, bf16[1,64,512]{2,1,0:T(8,128)(2,1)S(1)}, u32[]{:S(2)}, u32[]{:S(2)}) collective-permute-start(bf16[1,64,512]{2,1,0:T(8,128)(2,1)S(1)} %get-tuple-element.45), channel_id=1, source_target_pairs={{12,0},{13,1},{14,2},{15,3},{28,16},{29,17},{30,18},{31,19}} | collective-permute-start | bytes 196616 | tf_op jit(solution)/shard_map/ppermute | solution.py:797
  176.3 7.0 %collective-permute-start.21 = (bf16[1,64,512]{2,1,0:T(8,128)(2,1)S(1)}, bf16[1,64,512]{2,1,0:T(8,128)(2,1)S(1)}, u32[]{:S(2)}, u32[]{:S(2)}) collective-permute-start(bf16[1,64,512]{2,1,0:T(8,128)(2,1)S(1)} %get-tuple-element.46), channel_id=1, source_target_pairs={{12,4},{13,5},{14,6},{15,7},{28,20},{29,21},{30,22},{31,23}} | collective-permute-start | bytes 196616 | tf_op jit(solution)/shard_map/ppermute | solution.py:797
  177.0 6.3 %collective-permute-start.22 = (bf16[1,64,512]{2,1,0:T(8,128)(2,1)S(1)}, bf16[1,64,512]{2,1,0:T(8,128)(2,1)S(1)}, u32[]{:S(2)}, u32[]{:S(2)}) collective-permute-start(bf16[1,64,512]{2,1,0:T(8,128)(2,1)S(1)} %get-tuple-element.47), channel_id=1, source_target_pairs={{12,8},{13,9},{14,10},{15,11},{28,24},{29,25},{30,26},{31,27}} | collective-permute-start | bytes 196616 | tf_op jit(solution)/shard_map/ppermute | solution.py:797
  185.4 17.9 %copy-start.1 = (bf16[16,2,1536]{2,1,0:T(2,128)(2,1)S(1)}, bf16[16,2,1536]{2,1,0:T(2,128)(2,1)}, u32[]{:S(2)}) copy-start(bf16[16,2,1536]{2,1,0:T(2,128)(2,1)} %param.14) | copy-start | bytes 294916
  (9 other events, 8.3 us)
